TPU v7x, 32 devices: a whole 2x2x4 slice. The times are simulated.
32 devices in a mesh: context: 8 (over z, core), heads: 4 (over y, x).
Axes of the slice: x: 2, y: 2, z: 4, core: 2. Of those that a mesh axis runs over, the one named last changes fastest.
Arguments:
- main_query: bfloat16 [64, 128, 576], P('context', 'heads'), may hold values from -6 to 6
- latent_keys: bfloat16 [16384, 576], P('context'), may hold values from -6 to 6
- head_lse: float32 [64, 128], P(None, 'heads'), may hold values from 4 to 8
- lengths: int32 [64], replicated, may hold values from 1 to 16384, as said below
- index_query: bfloat16 [64, 64, 128], P('heads'), may hold values from -256 to 256
- index_key: bfloat16 [16384, 128], P('context'), may hold values from -8 to 8
- index_weight: float32 [64, 64], P('heads'), may hold values from -2.4 to 2.4
Outputs:
- grad_index_query: float32 [64, 64, 128], P('heads', 'context')
- grad_index_key: float32 [16384, 128], P(('context', 'heads'))
Inputs may be any that keep to these rules, and one draw needn't show every extreme that they name: Query rows come in blocks of 16 consecutive rows whose lengths rise by one from row to row; some block ends at the last key.
All inputs are finite; a program needn't handle non-finite values.
Results may differ from a plain program's by a relative error of at most 0.0029.
Values may be sent and summed in bfloat16 or wider, within the bound.
No kernel may reach another device: no remote copies, remote signals or barrier semaphores. Data moves between devices by JAX's collectives and lax.ppermute only.
A program may use at most 64 MiB of HBM per device.

v0:
```python
import math

import jax
import jax.numpy as jnp
from jax import lax
from jax.sharding import PartitionSpec as P

main_scale = 192.0 ** (-0.5)
loss_scale = 64.0
masked_low = -1e30


def joined(part, axis, combine):
    gathered = jax.tree.map(lambda a: lax.all_gather(a, axis), part)

    def take(source):
        return jax.tree.map(lambda a: lax.dynamic_index_in_dim(a, source, 0, False), gathered)

    return lax.fori_loop(
        1, lax.axis_size(axis), lambda source, state: combine(state, take(source)), take(0)
    )


def head_mass(queries, lse_rows, len_rows, latent, first_key):
    row_count = queries.shape[0]
    block_rows = math.gcd(row_count, 64)
    steps_count = row_count // block_rows
    key_pos = first_key + jnp.arange(latent.shape[0], dtype=jnp.int32)

    def one_block(inputs):
        query_block, lse_block, len_block = inputs
        scores = (
            jnp.einsum("rhd,sd->rhs", query_block, latent, preferred_element_type=jnp.float32)
            * main_scale
        )
        summed = jnp.sum(jnp.exp(scores - lse_block[:, :, None]), axis=1)
        return jnp.where(key_pos[None, :] < len_block[:, None], summed, 0.0)

    stacked = lax.map(
        one_block,
        (
            queries.reshape((steps_count, block_rows) + queries.shape[1:]),
            lse_rows.reshape(steps_count, block_rows, lse_rows.shape[1]),
            len_rows.reshape(steps_count, block_rows),
        ),
    )
    return stacked.reshape(row_count, latent.shape[0])


def on_device(main_query, latent_keys, head_lse, lengths, index_query, index_key, index_weight):
    key_count = latent_keys.shape[0]
    first_key = lax.axis_index("context") * key_count
    own_rows = index_query.shape[0]
    row_first = lax.axis_index("heads") * own_rows
    partial_mass = head_mass(
        lax.all_gather(main_query, "context", axis=0, tiled=True),
        head_lse,
        lengths,
        latent_keys,
        first_key,
    )
    summed_mass = lax.psum(partial_mass, "heads")
    row_mass = lax.dynamic_slice_in_dim(summed_mass, row_first, own_rows, 0)
    own_len = lax.dynamic_slice_in_dim(lengths, row_first, own_rows, 0)
    visible = (first_key + jnp.arange(key_count, dtype=jnp.int32))[None, :] < own_len[:, None]
    heads_count = index_query.shape[1]
    width = index_query.shape[2]
    index_scale = width ** (-0.5)
    flat_query = index_query.reshape(own_rows * heads_count, width)
    block_keys = math.gcd(key_count, 512)
    block_total = key_count // block_keys
    key_blocks = index_key.reshape(block_total, block_keys, width)

    def block_dots(key_block):
        products = lax.dot_general(
            flat_query, key_block, (((1,), (1,)), ((), ())), preferred_element_type=jnp.float32
        )
        return products.reshape(own_rows, heads_count, key_block.shape[0])

    def block_logits(key_block):
        return (
            jnp.einsum(
                "tj,tjs->ts",
                index_weight,
                jax.nn.relu(block_dots(key_block)),
                precision=lax.Precision.HIGHEST,
            )
            * index_scale
        )

    logits = jnp.moveaxis(lax.map(block_logits, key_blocks), 0, 1).reshape(own_rows, key_count)
    local_top = jnp.max(jnp.where(visible, logits, masked_low), axis=1)
    mass_local = jnp.sum(row_mass, axis=1)
    local_exp = jnp.where(visible, jnp.exp(logits - local_top[:, None]), 0.0)

    def combine(first, second):
        highest = jnp.maximum(first[0], second[0])
        merged = first[1] * jnp.exp(first[0] - highest) + second[1] * jnp.exp(second[0] - highest)
        return (highest, merged, first[2] + second[2])

    top, share_sum, mass_total = joined(
        (local_top, jnp.sum(local_exp, axis=1), mass_local), "context", combine
    )
    weights_exp = jnp.where(visible, jnp.exp(logits - top[:, None]), 0.0)
    probability = weights_exp / share_sum[:, None]
    target = row_mass / mass_total[:, None]
    slopes = loss_scale * (probability - target)
    slope_blocks = slopes.reshape(own_rows, block_total, block_keys).transpose(1, 0, 2)

    def back_step(query_grad, inputs):
        key_block, slope_block = inputs
        products = block_dots(key_block)
        terms = jnp.where(
            products > 0, slope_block[:, None, :] * index_weight[:, :, None] * index_scale, 0.0
        )
        terms = terms.astype(jnp.bfloat16).reshape(own_rows * heads_count, key_block.shape[0])
        query_grad = query_grad + jnp.dot(terms, key_block, preferred_element_type=jnp.float32)
        key_grad = lax.dot_general(
            terms, flat_query, (((0,), (0,)), ((), ())), preferred_element_type=jnp.float32
        )
        return (query_grad, key_grad)

    start_grad = jnp.zeros((own_rows * heads_count, width), jnp.float32)
    query_grad, key_grads = lax.scan(back_step, start_grad, (key_blocks, slope_blocks))
    query_grad = query_grad.reshape(own_rows, heads_count, width)
    key_grad = key_grads.reshape(key_count, width)
    out_query = lax.psum_scatter(query_grad, "context", scatter_dimension=1, tiled=True)
    out_key = lax.psum_scatter(key_grad, "heads", scatter_dimension=0, tiled=True)
    return (out_query, out_key)


def solution(mesh):
    placed = (
        P("context", "heads", None),
        P("context", None),
        P(None, "heads"),
        P(),
        P("heads", None, None),
        P("context", None),
        P("heads", None),
    )
    return jax.shard_map(
        on_device,
        mesh=mesh,
        in_specs=placed,
        out_specs=(P("heads", "context", None), P(("context", "heads"), None)),
        check_vma=False,
    )
```

profile of v0, /device:TPU:0, one launch (start us, length us, event | category | flops | bytes accessed | tf_op | source)
XLA Modules:
  0.0 230.6 jit_solution(825711599944566176)
XLA Ops:
  8.8 37.5 %all-gather.5.cloned.1.call-done = bf16[64,32,576]{2,1,0:T(8,128)(2,1)} async-done(((bf16[8,32,576]{2,1,0:T(8,128)(2,1)}), bf16[64,32,576]{2,1,0:T(8,128)(2,1)}) %all-gather.5.cloned.1.call-update) | async-done | bytes 2359312 | tf_op jit(solution)/shard_map/all_gather | solution.py:56
  46.3 10.5 %exponential_reduce_fusion = f32[64,2048]{1,0:T(8,128)S(1)} fusion(f32[64,32]{1,0:T(8,128)S(1)} %copy.18, bf16[64,32,576]{2,1,0:T(8,128)(2,1)} %all-gather.5.cloned.1.call-done, bf16[2048,576]{0,1:T(8,128)(2,1)S(1)} %copy-done), kind=kOutput, calls=%fused_computation.27 | convolution fusion | flops 4844290048 | bytes 5251072 | tf_op jit(solution)/shard_map/while/body/eval_jaxpr/rhd,sd->rhs/dot_general | solution.py:33
  57.8 34.1 %while.47 = (s32[]{:T(128)}, f32[4,16,512]{2,1,0:T(8,128)S(1)}, bf16[4,512,128]{2,1,0:T(8,128)(2,1)}, bf16[1024,128]{1,0:T(8,128)(2,1)}, f32[16,64]{1,0:T(8,128)S(1)}, /*index=5*/s32[]{:T(128)}) while((s32[]{:T(128)}, f32[4,16,512]{2,1,0:T(8,128)S(1)}, bf16[4,512,128]{2,1,0:T(8,128)(2,1)}, bf16[1024,128]{1,0:T(8,128)(2,1)}, ...), condition=%wide.region_1.2_spmd, body=%wide.region_0.1_spmd.sunk | while | flops 141041664 | bytes 8884809 | solution.py:91
  57.8 2.8 %maximum_bitcast_fusion.2 = f32[1024,512]{0,1:T(8,128)} fusion(bf16[1024,128]{1,0:T(8,128)(2,1)} %get-tuple-element.512, bf16[4,512,128]{2,1,0:T(8,128)(2,1)} %get-tuple-element.511, s32[]{:T(128)} %get-tuple-element.503), kind=kOutput, calls=%fused_computation.clone.1 | convolution fusion | flops 134742016 | bytes 2490880 | tf_op jit(solution)/shard_map/while/body/eval_jaxpr/dot_general | solution.py:75
  60.6 2.9 %copy.32 = f32[1024,512]{1,0:T(8,128)} copy(f32[1024,512]{0,1:T(8,128)} %maximum_bitcast_fusion.2) | data formatting | bytes 4194304 | tf_op jit(solution)/shard_map/while/body/eval_jaxpr/jit(relu)/max | solution.py:85
  63.5 2.8 %fusion.55 = f32[16,1,512]{2,1,0:T(1,128)S(1)} fusion(f32[16,64,512]{2,1,0:T(8,128)} %bitcast.131, f32[16,64,1]{1,2,0:T(1,128)S(1)} %bitcast.138), kind=kOutput, calls=%fused_computation.41.clone.1 | convolution fusion | flops 6291456 | bytes 2134016 | tf_op jit(solution)/shard_map/while/body/eval_jaxpr/tj,tjs->ts/dot_general | solution.py:82
  66.3 2.8 %maximum_bitcast_fusion.2 = f32[1024,512]{0,1:T(8,128)} fusion(bf16[1024,128]{1,0:T(8,128)(2,1)} %get-tuple-element.512, bf16[4,512,128]{2,1,0:T(8,128)(2,1)} %get-tuple-element.511, s32[]{:T(128)} %get-tuple-element.503), kind=kOutput, calls=%fused_computation.clone.1 | convolution fusion | flops 134742016 | bytes 2490880 | tf_op jit(solution)/shard_map/while/body/eval_jaxpr/dot_general | solution.py:75
  69.2 2.9 %copy.32 = f32[1024,512]{1,0:T(8,128)} copy(f32[1024,512]{0,1:T(8,128)} %maximum_bitcast_fusion.2) | data formatting | bytes 4194304 | tf_op jit(solution)/shard_map/while/body/eval_jaxpr/jit(relu)/max | solution.py:85
  72.1 2.8 %fusion.55 = f32[16,1,512]{2,1,0:T(1,128)S(1)} fusion(f32[16,64,512]{2,1,0:T(8,128)} %bitcast.131, f32[16,64,1]{1,2,0:T(1,128)S(1)} %bitcast.138), kind=kOutput, calls=%fused_computation.41.clone.1 | convolution fusion | flops 6291456 | bytes 2134016 | tf_op jit(solution)/shard_map/while/body/eval_jaxpr/tj,tjs->ts/dot_general | solution.py:82
  74.9 2.8 %maximum_bitcast_fusion.2 = f32[1024,512]{0,1:T(8,128)} fusion(bf16[1024,128]{1,0:T(8,128)(2,1)} %get-tuple-element.512, bf16[4,512,128]{2,1,0:T(8,128)(2,1)} %get-tuple-element.511, s32[]{:T(128)} %get-tuple-element.503), kind=kOutput, calls=%fused_computation.clone.1 | convolution fusion | flops 134742016 | bytes 2490880 | tf_op jit(solution)/shard_map/while/body/eval_jaxpr/dot_general | solution.py:75
  77.7 2.9 %copy.32 = f32[1024,512]{1,0:T(8,128)} copy(f32[1024,512]{0,1:T(8,128)} %maximum_bitcast_fusion.2) | data formatting | bytes 4194304 | tf_op jit(solution)/shard_map/while/body/eval_jaxpr/jit(relu)/max | solution.py:85
  80.6 2.8 %fusion.55 = f32[16,1,512]{2,1,0:T(1,128)S(1)} fusion(f32[16,64,512]{2,1,0:T(8,128)} %bitcast.131, f32[16,64,1]{1,2,0:T(1,128)S(1)} %bitcast.138), kind=kOutput, calls=%fused_computation.41.clone.1 | convolution fusion | flops 6291456 | bytes 2134016 | tf_op jit(solution)/shard_map/while/body/eval_jaxpr/tj,tjs->ts/dot_general | solution.py:82
  83.4 2.8 %maximum_bitcast_fusion.2 = f32[1024,512]{0,1:T(8,128)} fusion(bf16[1024,128]{1,0:T(8,128)(2,1)} %get-tuple-element.512, bf16[4,512,128]{2,1,0:T(8,128)(2,1)} %get-tuple-element.511, s32[]{:T(128)} %get-tuple-element.503), kind=kOutput, calls=%fused_computation.clone.1 | convolution fusion | flops 134742016 | bytes 2490880 | tf_op jit(solution)/shard_map/while/body/eval_jaxpr/dot_general | solution.py:75
  86.2 2.9 %copy.32 = f32[1024,512]{1,0:T(8,128)} copy(f32[1024,512]{0,1:T(8,128)} %maximum_bitcast_fusion.2) | data formatting | bytes 4194304 | tf_op jit(solution)/shard_map/while/body/eval_jaxpr/jit(relu)/max | solution.py:85
  89.1 2.8 %fusion.55 = f32[16,1,512]{2,1,0:T(1,128)S(1)} fusion(f32[16,64,512]{2,1,0:T(8,128)} %bitcast.131, f32[16,64,1]{1,2,0:T(1,128)S(1)} %bitcast.138), kind=kOutput, calls=%fused_computation.41.clone.1 | convolution fusion | flops 6291456 | bytes 2134016 | tf_op jit(solution)/shard_map/while/body/eval_jaxpr/tj,tjs->ts/dot_general | solution.py:82
  94.4 7.9 %all-reduce.6.cloned.1.call-done = f32[64,2048]{1,0:T(8,128)} async-done(((f32[64,2048]{1,0:T(8,128)}), f32[64,2048]{1,0:T(8,128)}) %all-reduce.6.cloned.1.call-update) | async-done | bytes 524304 | tf_op jit(solution)/shard_map/psum | solution.py:62
  103.5 16.1 %all-reduce.3 = (f32[128]{0:T(128)S(1)}, f32[128]{0:T(128)S(1)}, f32[128]{0:T(128)S(1)}) all-reduce(f32[128]{0:T(128)S(1)} %dynamic-update-slice, f32[128]{0:T(128)S(1)} %dynamic-update-slice.1, f32[128]{0:T(128)S(1)} %dynamic-update-slice.2), channel_id=2, replica_groups=mesh['context'=8,'heads'=4] {'context'}, use_global_device_ids=true, to_apply=%add | all-reduce | flops 384 | bytes 3072
  121.2 44.9 %while.49 = (s32[]{:T(128)}, f32[1024,128]{1,0:T(8,128)}, f32[4,512,128]{2,1,0:T(8,128)}, bf16[4,512,128]{2,1,0:T(8,128)(2,1)}, bf16[1024,128]{1,0:T(8,128)(2,1)...) while((s32[]{:T(128)}, f32[1024,128]{1,0:T(8,128)}, ...), condition=%wide.wide.region_10.11_spmd.clone, body=%wide.wide.region_9.10_spmd.clone.sunk | while | flops 405536768 | bytes 13735539 | solution.py:124
  122.9 2.9 %copy.33 = f32[1024,512]{0,1:T(8,128)} copy(f32[1024,512]{1,0:T(8,128)} %bitcast.132) | data formatting | bytes 4194304 | tf_op jit(solution)/shard_map/while/body/eval_jaxpr/mul | solution.py:114
  125.8 2.3 select_convert_fusion.3
  128.0 2.2 convolution_add_fusion.3
  133.9 2.9 %copy.33 = f32[1024,512]{0,1:T(8,128)} copy(f32[1024,512]{1,0:T(8,128)} %bitcast.132) | data formatting | bytes 4194304 | tf_op jit(solution)/shard_map/while/body/eval_jaxpr/mul | solution.py:114
  136.8 2.3 select_convert_fusion.3
  139.1 2.4 %convolution_add_fusion.3 = f32[1024,128]{1,0:T(8,128)} fusion(bf16[1024,512]{0,1:T(8,128)(2,1)S(1)} %select_convert_fusion.3, f32[1024,128]{1,0:T(8,128)} %get-tuple-element.556, pred[]{:T(512)S(6)} %compare.4, bf16[4,512,128]{2,1,0:T(8,128)(2,1)} %get-tuple-element.568, s32[]{:T(128)} %get-tuple-element.555), kind=kOutput, calls=%fused_computation.17.clone.clone.1 | convolution fusion | flops 134479872 | bytes 2228737 | tf_op jit(solution)/shard_map/while/body/eval_jaxpr/dot_general | solution.py:117
  145.2 2.9 %copy.33 = f32[1024,512]{0,1:T(8,128)} copy(f32[1024,512]{1,0:T(8,128)} %bitcast.132) | data formatting | bytes 4194304 | tf_op jit(solution)/shard_map/while/body/eval_jaxpr/mul | solution.py:114
  148.1 2.3 select_convert_fusion.3
  150.4 2.4 %convolution_add_fusion.3 = f32[1024,128]{1,0:T(8,128)} fusion(bf16[1024,512]{0,1:T(8,128)(2,1)S(1)} %select_convert_fusion.3, f32[1024,128]{1,0:T(8,128)} %get-tuple-element.556, pred[]{:T(512)S(6)} %compare.4, bf16[4,512,128]{2,1,0:T(8,128)(2,1)} %get-tuple-element.568, s32[]{:T(128)} %get-tuple-element.555), kind=kOutput, calls=%fused_computation.17.clone.clone.1 | convolution fusion | flops 134479872 | bytes 2228737 | tf_op jit(solution)/shard_map/while/body/eval_jaxpr/dot_general | solution.py:117
  156.5 2.9 %copy.33 = f32[1024,512]{0,1:T(8,128)} copy(f32[1024,512]{1,0:T(8,128)} %bitcast.132) | data formatting | bytes 4194304 | tf_op jit(solution)/shard_map/while/body/eval_jaxpr/mul | solution.py:114
  159.4 2.3 select_convert_fusion.3
  161.6 2.4 %convolution_add_fusion.3 = f32[1024,128]{1,0:T(8,128)} fusion(bf16[1024,512]{0,1:T(8,128)(2,1)S(1)} %select_convert_fusion.3, f32[1024,128]{1,0:T(8,128)} %get-tuple-element.556, pred[]{:T(512)S(6)} %compare.4, bf16[4,512,128]{2,1,0:T(8,128)(2,1)} %get-tuple-element.568, s32[]{:T(128)} %get-tuple-element.555), kind=kOutput, calls=%fused_computation.17.clone.clone.1 | convolution fusion | flops 134479872 | bytes 2228737 | tf_op jit(solution)/shard_map/while/body/eval_jaxpr/dot_general | solution.py:117
  166.7 27.8 %reduce-scatter.3.cloned.1.call-done = f32[16,8,128]{2,1,0:T(8,128)} async-done(((f32[16,64,128]{2,1,0:T(8,128)}), f32[16,8,128]{2,1,0:T(8,128)}) %reduce-scatter.3.cloned.1.call-update) | async-done | bytes 65552 | tf_op jit(solution)/shard_map/reduce_scatter | solution.py:127
  194.5 29.5 %reduce-scatter.5.cloned.1.call-done = f32[512,128]{1,0:T(8,128)} async-done(((f32[2048,128]{1,0:T(8,128)}), f32[512,128]{1,0:T(8,128)}) %reduce-scatter.5.cloned.1.call-update) | async-done | bytes 262160 | tf_op jit(solution)/shard_map/reduce_scatter | solution.py:128
  (65 shorter events, 22.8 us)
Async XLA Ops:
  7.2 39.1 %copy-start = (bf16[2048,576]{0,1:T(8,128)(2,1)S(1)}, bf16[2048,576]{0,1:T(8,128)(2,1)}, u32[]{:S(2)}) copy-start(bf16[2048,576]{0,1:T(8,128)(2,1)} %param.14) | copy-start | bytes 7077892
  7.2 39.1 %all-gather.5.cloned.1.call-start = ((), (), s32[]{:S(2)}) async-start(), calls=%async_computation.2 | async-start | bytes 2949120 | tf_op jit(solution)/shard_map/all_gather | solution.py:56
  7.9 94.4 %all-reduce.6.cloned.1.call-start = ((), (), s32[]{:S(2)}) async-start(), calls=%async_computation.3 | async-start | bytes 1048576 | tf_op jit(solution)/shard_map/psum | solution.py:62
  8.8 48.0 %copy-start.2 = (s32[64]{0:T(128)S(1)}, s32[64]{0:T(128)}, u32[]{:S(2)}) copy-start(s32[64]{0:T(128)} %param.16) | copy-start | bytes 772
  8.8 49.0 %copy-start.1 = (f32[16,64]{1,0:T(8,128)S(1)}, f32[16,64]{1,0:T(8,128)}, u32[]{:S(2)}) copy-start(f32[16,64]{1,0:T(8,128)} %param.19) | copy-start | bytes 12292
  57.7 136.8 %reduce-scatter.3.cloned.1.call-start = ((), (), s32[]{:S(2)}) async-start(), calls=%async_computation.4 | async-start | bytes 589824 | tf_op jit(solution)/shard_map/reduce_scatter | solution.py:127
  57.8 34.3 %copy-start.3 = (u32[32]{0:T(128)S(1)}, u32[32]{0:T(128)}, u32[]{:S(2)}) copy-start(u32[32]{0:T(128)} %constant.128) | copy-start | bytes 388
  166.2 57.9 %reduce-scatter.5.cloned.1.call-start = ((), (), s32[]{:S(2)}) async-start(), calls=%async_computation.5 | async-start | bytes 1310720 | tf_op jit(solution)/shard_map/reduce_scatter | solution.py:128
Sparse Core Ops, SparseCore 0:
  9.6 36.5 all-gather.4
  57.9 44.3 all-reduce.5
  166.3 28.1 reduce-scatter.2
  198.1 25.9 reduce-scatter.4
where the time goes:
time: 232 us; the launch traced here: 231 us
  waiting for transfers between devices  104 us (45%)
  matrix products  59.7 us (26%)
  local copies, waits for them, and re-layouts  32.2 us (14%)
  blocking collectives  16.1 us (7%)
  between operations  14.6 us (6%)
  other arithmetic  3.62 us (2%)
    all_gather x1, waiting for transfers between devices, on_device(): lax.all_gather(main_query, 'context', axis=0, tiled=True)  37.5 us
    reduce_scatter x1, waiting for transfers between devices, on_device(): lax.psum_scatter(key_grad, 'heads', scatter_dimension=0, tiled=True)  29.5 us
    reduce_scatter x1, waiting for transfers between devices, on_device(): lax.psum_scatter(query_grad, 'context', scatter_dimension=1, tiled=True)  27.8 us
    dot_general x8, matrix products, block_dots(): lax.dot_general(flat_query, key_block, (((1,), (1,)), ((), ())), preferre...  20.3 us
    mul x13, local copies, waits for them, and re-layouts, back_step(): slope_block[:, None, :] * index_weight[:, :, None] * index_scale  18.1 us
    unnamed x1, blocking collectives  16.1 us
    max x4, local copies, waits for them, and re-layouts, block_logits(): jax.nn.relu(block_dots(key_block))  11.6 us
    dot_general x4, matrix products, block_logits(): jnp.einsum('tj,tjs->ts', index_weight, jax.nn.relu(block_dots(key_block))...  11.2 us
  transfers between devices with their start and end apart: 4, of which 4 were waited for; matrix products, arithmetic and copies ran while one was open for 16% of the time, Pallas kernels for 0%

commit v1 on v0

--- a/solution.py
+++ b/solution.py
@@ -1,14 +1,19 @@
+import functools
 import math
 
 import jax
 import jax.numpy as jnp
 from jax import lax
+from jax.experimental import pallas as pl
+from jax.experimental.pallas import tpu as pltpu
 from jax.sharding import PartitionSpec as P
 
 main_scale = 192.0 ** (-0.5)
 loss_scale = 64.0
 masked_low = -1e30
-
+log2_e = math.log2(math.e)
+lanes = 128
+vmem_bytes = 48 * 1024 * 1024
 
 def joined(part, axis, combine):
     gathered = jax.tree.map(lambda a: lax.all_gather(a, axis), part)
@@ -47,7 +52,7 @@
     return stacked.reshape(row_count, latent.shape[0])
 
 
-def on_device(main_query, latent_keys, head_lse, lengths, index_query, index_key, index_weight):
+def general_on_device(main_query, latent_keys, head_lse, lengths, index_query, index_key, index_weight):
     key_count = latent_keys.shape[0]
     first_key = lax.axis_index("context") * key_count
     own_rows = index_query.shape[0]
@@ -129,6 +134,423 @@
     return (out_query, out_key)
 
 
+def local_call(kernel, out_shape, name, grid=None, in_specs=None, out_specs=None, scratch=(), flops=0, moved=0):
+    settings = dict(
+        out_shape=out_shape,
+        scratch_shapes=list(scratch),
+        name=name,
+        compiler_params=pltpu.CompilerParams(vmem_limit_bytes=vmem_bytes),
+        cost_estimate=pl.CostEstimate(flops=flops, bytes_accessed=moved, transcendentals=0),
+    )
+    if grid is not None:
+        settings["grid"] = grid
+    if in_specs is not None:
+        settings["in_specs"] = in_specs
+    if out_specs is not None:
+        settings["out_specs"] = out_specs
+    return pl.pallas_call(kernel, **settings)
+
+
+def whole():
+    return pl.BlockSpec(memory_space=pltpu.VMEM)
+
+
+def scalars():
+    return pl.BlockSpec(memory_space=pltpu.SMEM)
+
+
+def fixed(shape):
+    return pl.BlockSpec(shape, lambda step: (0,) * len(shape))
+
+
+def f32(shape):
+    return jax.ShapeDtypeStruct(shape, jnp.float32)
+
+
+def bf16(shape):
+    return jax.ShapeDtypeStruct(shape, jnp.bfloat16)
+
+
+info_first, info_plane, info_core, info_heads, info_lengths = 0, 1, 2, 3, 4
+
+
+def pack_kernel(query_ref, out_ref):
+    rows, heads, width = query_ref.shape
+    total = rows * heads
+    columns = width // lanes
+    stacked = jnp.swapaxes(query_ref[...].astype(jnp.float32), 0, 1).reshape(total, width)
+    for i in range(columns):
+        out_ref[i * total : (i + 1) * total, :] = stacked[:, i * lanes : (i + 1) * lanes].astype(jnp.bfloat16)
+    rest = stacked[:, columns * lanes :]
+    out_ref[columns * total :, :] = jnp.concatenate([rest[: total // 2], rest[total // 2 :]], axis=1).astype(
+        jnp.bfloat16
+    )
+
+
+def packed_queries(queries):
+    rows, heads, width = queries.shape
+    return local_call(
+        pack_kernel,
+        bf16((rows * heads * width // lanes, lanes)),
+        "pack_queries",
+        in_specs=[whole()],
+        out_specs=whole(),
+        moved=4 * queries.size,
+    )(queries)
+
+
+def unpack(packed, wide_ref, place, total, width):
+    columns = width // lanes
+    half = total // 2
+    for i in range(columns):
+        wide_ref[place * total : (place + 1) * total, i * lanes : (i + 1) * lanes] = packed[
+            i * total : (i + 1) * total, :
+        ]
+    rest = packed[columns * total :, :]
+    wide_ref[place * total : place * total + half, columns * lanes :] = rest[:, : lanes // 2]
+    wide_ref[place * total + half : (place + 1) * total, columns * lanes :] = rest[:, lanes // 2 :]
+
+
+def length_column(info_ref, first_row, rows, width):
+    spread = lax.broadcasted_iota(jnp.int32, (rows, lanes), 0)
+    column = jnp.zeros((rows, lanes), jnp.int32)
+    for i in range(rows):
+        column = jnp.where(spread == i, info_ref[info_lengths + first_row + i], column)
+    return widened(column, width)
+
+
+def widened(column, width):
+    return jnp.concatenate([column] * (width // lanes), axis=1)
+
+
+def shard_mass(info_ref, scores, lse_ref, context, rows, heads, tile, step):
+    shifted = scores * (main_scale * log2_e) - widened(lse_ref[context], tile)
+    summed = jnp.sum(jnp.exp2(shifted).reshape(heads, rows, tile), axis=0)
+    positions = info_ref[info_first] + step * tile + lax.broadcasted_iota(jnp.int32, (rows, tile), 1)
+    visible = positions < length_column(info_ref, context * rows, rows, tile)
+    return jnp.where(visible, summed, 0.0)
+
+
+def mass_kernel(flip, places, choose, rows, heads, info_ref, *refs):
+    count = len(places)
+    packs = refs[: count * (2 if choose else 1)]
+    lse_ref, key_ref, out_ref, wide_ref = refs[len(packs) :]
+    step = pl.program_id(0)
+    tile, width = key_ref.shape
+    total = rows * heads
+
+    @pl.when(step == 0)
+    def _():
+        for n in range(count):
+            if choose:
+                inner = (info_ref[info_plane] == 1) | (info_ref[info_plane] == 2)
+                packed = jnp.where(inner, packs[2 * n][...], packs[2 * n + 1][...])
+            else:
+                packed = packs[n][...]
+            unpack(packed, wide_ref, n, total, width)
+
+    scores = lax.dot_general(
+        wide_ref[...], key_ref[...], (((1,), (1,)), ((), ())), preferred_element_type=jnp.float32
+    )
+    plane = info_ref[info_plane] ^ flip
+    for n, place in enumerate(places):
+        core = info_ref[info_core] ^ place
+        mass = shard_mass(
+            info_ref, scores[n * total : (n + 1) * total], lse_ref, 2 * plane + core, rows, heads, tile, step
+        )
+        if count == 1:
+            out_ref[...] = mass
+        else:
+            out_ref[pl.ds(pl.multiple_of(core * rows, rows), rows), :] = mass
+
+
+def chunk_mass(info, packs, lse_wide, keys, flip, places, rows, heads, name, choose=False):
+    key_count, width = keys.shape
+    tile = math.gcd(key_count, 512)
+    count = len(places)
+    total = rows * heads
+    return local_call(
+        functools.partial(mass_kernel, flip, places, choose, rows, heads),
+        f32((count * rows, key_count)),
+        name,
+        grid=(key_count // tile,),
+        in_specs=[scalars()]
+        + [fixed(p.shape) for p in packs]
+        + [fixed(lse_wide.shape), pl.BlockSpec((tile, width), lambda step: (step, 0))],
+        out_specs=pl.BlockSpec((count * rows, tile), lambda step: (0, step)),
+        scratch=[pltpu.VMEM((count * total, width), jnp.bfloat16)],
+        flops=2 * count * total * key_count * width,
+        moved=2 * keys.size,
+    )(info, *packs, lse_wide, keys)
+
+
+def share_kernel(rows, heads, info_ref, pack_ref, lse_ref, own_ref, near_ref, far_ref, half_ref, key_ref, *refs):
+    outs = refs[:-2]
+    wide_ref, chunks_ref = refs[-2:]
+    step = pl.program_id(0)
+    tile, width = key_ref.shape
+    total = rows * heads
+
+    @pl.when(step == 0)
+    def _():
+        unpack(pack_ref[...], wide_ref, 0, total, width)
+
+    scores = lax.dot_general(
+        wide_ref[...], key_ref[...], (((1,), (1,)), ((), ())), preferred_element_type=jnp.float32
+    )
+    core = info_ref[info_core]
+    plane = info_ref[info_plane]
+    other = 1 - core
+    last = shard_mass(info_ref, scores, lse_ref, 2 * (plane ^ 2) + other, rows, heads, tile, step)
+    chunks_ref[0] = own_ref[...]
+    chunks_ref[1] = near_ref[...]
+    chunks_ref[3] = far_ref[...]
+    chunks_ref[2, pl.ds(pl.multiple_of(other * rows, rows), rows), :] = last
+    chunks_ref[2, pl.ds(pl.multiple_of(core * rows, rows), rows), :] = half_ref[...]
+    for e, out_ref in enumerate(outs):
+        out_ref[...] = chunks_ref[plane ^ info_ref[info_heads] ^ e].astype(out_ref.dtype)
+
+
+def shared_mass(info, pack, lse_wide, own, near, far, half, keys, rows, heads, partners):
+    key_count, width = keys.shape
+    tile = math.gcd(key_count, 512)
+    total = rows * heads
+    both = 2 * rows
+    block = pl.BlockSpec((both, tile), lambda step: (0, step))
+    return local_call(
+        functools.partial(share_kernel, rows, heads),
+        [f32((both, key_count))] + [bf16((both, key_count))] * (partners - 1),
+        "mass_and_share",
+        grid=(key_count // tile,),
+        in_specs=[scalars(), fixed(pack.shape), fixed(lse_wide.shape), block, block, block]
+        + [pl.BlockSpec((rows, tile), lambda step: (0, step)), pl.BlockSpec((tile, width), lambda step: (step, 0))],
+        out_specs=[block] * partners,
+        scratch=[pltpu.VMEM((total, width), jnp.bfloat16), pltpu.VMEM((4, both, tile), jnp.float32)],
+        flops=2 * total * key_count * width,
+        moved=2 * keys.size,
+    )(info, pack, lse_wide, own, near, far, half, keys)
+
+
+def visible_tile(info_ref, rows, first, width):
+    positions = info_ref[info_first] + first + lax.broadcasted_iota(jnp.int32, (rows, width), 1)
+    return positions < length_column(info_ref, info_ref[info_heads] * rows, rows, width)
+
+
+def logits_kernel(info_ref, query_ref, key_ref, weight_ref, logits_ref, stats_ref):
+    rows, key_count = logits_ref.shape
+    heads = query_ref.shape[0] // rows
+    tile = math.gcd(key_count, 256)
+    best = jnp.full((rows, 1), masked_low, jnp.float32)
+    for first in range(0, key_count, tile):
+        dots = lax.dot_general(
+            query_ref[...], key_ref[first : first + tile, :], (((1,), (1,)), ((), ())),
+            preferred_element_type=jnp.float32,
+        )
+        weighed = jnp.maximum(dots, 0.0) * widened(weight_ref[...], tile)
+        logits = jnp.sum(weighed.reshape(rows, heads, tile), axis=1)
+        logits_ref[:, first : first + tile] = logits
+        seen = jnp.where(visible_tile(info_ref, rows, first, tile), logits, masked_low)
+        best = jnp.maximum(best, jnp.max(seen, axis=1, keepdims=True))
+    shares = jnp.where(visible_tile(info_ref, rows, 0, key_count), jnp.exp(logits_ref[...] - best), 0.0)
+    total = jnp.sum(shares, axis=1, keepdims=True)
+    place = lax.broadcasted_iota(jnp.int32, (rows, lanes), 1)
+    stats_ref[...] = jnp.where(place == 0, best, total)
+
+
+def index_logits(info, flat_query, index_key, weight_wide, rows):
+    key_count = index_key.shape[0]
+    return local_call(
+        logits_kernel,
+        [f32((rows, key_count)), f32((rows, lanes))],
+        "index_logits",
+        in_specs=[scalars()] + [whole()] * 3,
+        out_specs=[whole()] * 2,
+        flops=2 * flat_query.size * key_count,
+        moved=2 * index_key.size,
+    )(info, flat_query, index_key, weight_wide)
+
+
+def join_kernel(stats_ref, own_ref, *refs):
+    parts, (mass_ref, out_ref) = refs[:-2], refs[-2:]
+    mass = own_ref[...]
+    for part in parts:
+        mass = mass + part[...].astype(jnp.float32)
+    mass_ref[...] = mass
+    place = lax.broadcasted_iota(jnp.int32, out_ref.shape, 1)
+    out_ref[...] = jnp.where(place == 2, jnp.sum(mass, axis=1, keepdims=True), stats_ref[...])
+
+
+def joined_mass(stats, own, parts):
+    return local_call(
+        join_kernel,
+        [f32(own.shape), f32(stats.shape)],
+        "join_mass",
+        in_specs=[whole()] * (2 + len(parts)),
+        out_specs=[whole()] * 2,
+        moved=8 * own.size,
+    )(stats, own, *parts)
+
+
+def back_kernel(sources, info_ref, mass_ref, logits_ref, query_ref, turned_ref, key_ref, weight_ref, *refs):
+    stats = [ref[...] for ref in refs[:sources]]
+    partners = len(refs) - sources - 4
+    key_outs = refs[sources : sources + partners]
+    keep_ref, send_ref, slope_ref, grad_ref = refs[sources + partners :]
+    rows, key_count = mass_ref.shape
+    flat, width = query_ref.shape
+    heads = flat // rows
+    tile = math.gcd(key_count, 256)
+    top = functools.reduce(jnp.maximum, [s[:, 0:1] for s in stats])
+    shares = sum(s[:, 1:2] * jnp.exp(s[:, 0:1] - top) for s in stats)
+    total = sum(s[:, 2:3] for s in stats)
+    visible = visible_tile(info_ref, rows, 0, key_count)
+    weights_exp = jnp.where(visible, jnp.exp(logits_ref[...] - top), 0.0)
+    slope_ref[...] = loss_scale * (weights_exp / shares - mass_ref[...] / total)
+    query_grad = jnp.zeros((flat, width), jnp.float32)
+    for first in range(0, key_count, tile):
+        keys = key_ref[first : first + tile, :]
+        dots = lax.dot_general(query_ref[...], keys, (((1,), (1,)), ((), ())), preferred_element_type=jnp.float32)
+        slopes = jnp.broadcast_to(slope_ref[:, first : first + tile][:, None, :], (rows, heads, tile))
+        scaled = slopes.reshape(flat, tile) * widened(weight_ref[...], tile)
+        terms = jnp.where(dots > 0, scaled, 0.0).astype(jnp.bfloat16)
+        query_grad = query_grad + jnp.dot(terms, keys, preferred_element_type=jnp.float32)
+        key_grad = jnp.dot(turned_ref[...], terms, preferred_element_type=jnp.float32)
+        grad_ref[first : first + tile, :] = key_grad.T
+    block = key_count // partners
+    for e, out_ref in enumerate(key_outs):
+        begin = pl.multiple_of((info_ref[info_heads] ^ e) * block, block)
+        out_ref[...] = grad_ref[pl.ds(begin, block), :].astype(out_ref.dtype)
+    planes = keep_ref.shape[0]
+    part = heads // (2 * planes)
+    split = query_grad.reshape(rows, planes, 2, part, width)
+    first_core = info_ref[info_core] == 0
+    for plane in range(planes):
+        low, high = split[:, plane, 0], split[:, plane, 1]
+        keep_ref[plane] = jnp.where(first_core, low, high).reshape(rows * part, width)
+        send_ref[plane] = jnp.where(first_core, high, low).reshape(rows * part, width).astype(jnp.bfloat16)
+
+
+def back_pass(info, mass, logits, flat_query, turned, index_key, weight_wide, stats, partners, planes):
+    rows, key_count = mass.shape
+    flat, width = flat_query.shape
+    part = flat // (2 * planes)
+    return local_call(
+        functools.partial(back_kernel, len(stats)),
+        [f32((key_count // partners, width))]
+        + [bf16((key_count // partners, width))] * (partners - 1)
+        + [f32((planes, part, width)), bf16((planes, part, width))],
+        "index_back",
+        in_specs=[scalars()] + [whole()] * (6 + len(stats)),
+        out_specs=[whole()] * (partners + 2),
+        scratch=[pltpu.VMEM((rows, key_count), jnp.float32), pltpu.VMEM((key_count, width), jnp.float32)],
+        flops=6 * flat * width * key_count,
+        moved=8 * key_count * width,
+    )(info, mass, logits, flat_query, turned, index_key, weight_wide, *stats)
+
+
+def pair_kernel(info_ref, keep_ref, got_ref, *outs):
+    for e, out_ref in enumerate(outs):
+        plane = info_ref[info_plane] ^ e
+        out_ref[...] = (keep_ref[plane] + got_ref[plane].astype(jnp.float32)).astype(out_ref.dtype)
+
+
+def pair_sums(info, keep, got):
+    planes, part, width = keep.shape
+    return local_call(
+        pair_kernel,
+        [f32((part, width))] + [bf16((part, width))] * (planes - 1),
+        "pair_sums",
+        in_specs=[scalars(), whole(), whole()],
+        out_specs=[whole()] * planes,
+        moved=8 * keep.size,
+    )(info, keep, got)
+
+
+def last_kernel(key_parts, *refs):
+    query_out, key_out = refs[-2:]
+    key_refs, query_refs = refs[:key_parts], refs[key_parts:-2]
+    key_out[...] = sum(ref[...].astype(jnp.float32) for ref in key_refs)
+    query_out[...] = sum(ref[...].astype(jnp.float32) for ref in query_refs).reshape(query_out.shape)
+
+
+def last_sums(key_parts, query_parts, query_shape):
+    return local_call(
+        functools.partial(last_kernel, len(key_parts)),
+        [f32(query_shape), f32(key_parts[0].shape)],
+        "last_sums",
+        in_specs=[whole()] * (len(key_parts) + len(query_parts)),
+        out_specs=[whole()] * 2,
+        moved=8 * key_parts[0].size,
+    )(*key_parts, *query_parts)
+
+
+def block_device(main_query, latent_keys, head_lse, lengths, index_query, index_key, index_weight):
+    contexts = lax.axis_size("context")
+    planes = contexts // 2
+    partners = lax.axis_size("heads")
+    context = lax.axis_index("context")
+    rows, heads, _ = main_query.shape
+    own_rows, index_heads, width = index_query.shape
+    key_count = latent_keys.shape[0]
+    flat = own_rows * index_heads
+
+    def planes_move(array, pairs):
+        return lax.ppermute(array, "context", [(2 * a + k, 2 * b + k) for a, b in pairs for k in (0, 1)])
+
+    def context_flip(array, e):
+        return lax.ppermute(array, "context", [(c, c ^ e) for c in range(contexts)])
+
+    def heads_flip(array, e):
+        return lax.ppermute(array, "heads", [(h, h ^ e) for h in range(partners)])
+
+    info = jnp.concatenate(
+        [
+            jnp.stack([context * key_count, context // 2, context % 2, lax.axis_index("heads")]).astype(jnp.int32),
+            lengths,
+        ]
+    )
+    pack = packed_queries(main_query)
+    inner = planes_move(pack, [(1, 2), (2, 1), (0, 0), (3, 3)])
+    near = planes_move(pack, [(0, 1), (1, 0), (2, 3), (3, 2)])
+    ends = planes_move(pack, [(0, 3), (3, 0)])
+    far = planes_move(inner, [(0, 2), (3, 1), (1, 0), (2, 3)])
+    own_pair, near_pair, inner_pair, ends_pair, far_pair = (
+        context_flip(a, 1) for a in (pack, near, inner, ends, far)
+    )
+
+    lse_wide = head_lse.reshape(contexts, rows, heads).transpose(0, 2, 1).reshape(contexts, rows * heads, 1)
+    lse_wide = jnp.broadcast_to(lse_wide * log2_e, (contexts, rows * heads, lanes))
+    weight_wide = jnp.broadcast_to(index_weight.reshape(flat, 1) * width ** (-0.5), (flat, lanes))
+    flat_query = index_query.reshape(flat, width)
+    turned = flat_query.T
+
+    logits, stats = index_logits(info, flat_query, index_key, weight_wide, own_rows)
+    common = (lse_wide, latent_keys)
+    own_mass = chunk_mass(info, [pack, own_pair], *common, 0, (0, 1), rows, heads, "mass_own")
+    near_mass = chunk_mass(info, [near, near_pair], *common, 1, (0, 1), rows, heads, "mass_near")
+    ends_mass = chunk_mass(
+        info, [inner, ends, inner_pair, ends_pair], *common, 3, (0, 1), rows, heads, "mass_ends", choose=True
+    )
+    far_mass = chunk_mass(info, [far], *common, 2, (0,), rows, heads, "mass_far")
+    shared = shared_mass(
+        info, far_pair, lse_wide, own_mass, near_mass, ends_mass, far_mass, latent_keys, rows, heads, partners
+    )
+    mass, stats = joined_mass(stats, shared[0], [heads_flip(shared[e], e) for e in range(1, partners)])
+    every = [stats] + [context_flip(stats, e) for e in range(1, contexts)]
+    *key_grads, keep, send = back_pass(
+        info, mass, logits, flat_query, turned, index_key, weight_wide, every, partners, planes
+    )
+    got = context_flip(send, 1)
+    key_parts = [key_grads[0]] + [heads_flip(key_grads[e], e) for e in range(1, partners)]
+    sums = pair_sums(info, keep, got)
+    query_parts = [sums[0]] + [context_flip(sums[e], 2 * e) for e in range(1, planes)]
+    return last_sums(key_parts, query_parts, (own_rows, index_heads // contexts, width))
+
+
+def fits(mesh):
+    return mesh.shape["context"] == 8 and mesh.shape["heads"] == 4
+
+
 def solution(mesh):
     placed = (
         P("context", "heads", None),
@@ -140,7 +562,7 @@
         P("heads", None),
     )
     return jax.shard_map(
-        on_device,
+        block_device if fits(mesh) else general_on_device,
         mesh=mesh,
         in_specs=placed,
         out_specs=(P("heads", "context", None), P(("context", "heads"), None)),

time: 232 us -> 84.9 us (0.37)
  waiting for transfers between devices: 104 us -> 7.69 us
  matrix products: 59.7 us -> 0 us
  starting transfers between devices: 0.16 us -> 42.4 us
  Pallas kernels: 0 us -> 24.9 us
  local copies, waits for them, and re-layouts: 32.2 us -> 8.51 us
  blocking collectives: 16.1 us -> 0 us
  between operations: 14.6 us -> 0.9 us
  other arithmetic: 3.62 us -> 0.01 us
    dot_general x21 -> x0, matrix products: 59.7 us -> none  [the longest x8 20.3 us: block_dots(): lax.dot_general(flat_query, key_block, (((1,), (1,)), ((), ())), preferre...]
    reduce_scatter x2 -> x0, waiting for transfers between devices: 57.3 us -> none  [the longest x1 29.5 us: on_device(): lax.psum_scatter(key_grad, 'heads', scatter_dimension=0, tiled=True)]
    ppermute x0 -> x26, starting transfers between devices: none -> 42.4 us  [the longest x4 21.2 us: planes_move(): lax.ppermute(array, 'context', [(2 * a + k, 2 * b + k) for a, b in pairs...]
    all_gather x1 -> x0, waiting for transfers between devices: 37.5 us -> none  [on_device(): lax.all_gather(main_query, 'context', axis=0, tiled=True)]
    pallas_call x0 -> x11, Pallas kernels: none -> 24.9 us  [the longest x4 13.8 us: chunk_mass(): local_call(functools.partial(mass_kernel, flip, places, choose, rows, hea...]
    mul x13 -> x3, local copies, waits for them, and re-layouts: 18.1 us -> 1.85 us  [the longest x2 1.77 us: block_device(): lse_wide * log2_e]
    unnamed x1 -> x0, blocking collectives: 16.1 us -> none
    max x4 -> x0, local copies, waits for them, and re-layouts: 11.6 us -> none  [block_logits(): jax.nn.relu(block_dots(key_block))]
  transfers between devices with their start and end apart: 4 -> 26, of which waited for: 4 -> 7; matrix products, arithmetic and copies ran while one was open for 16% -> 8% of each run, Pallas kernels for 0% -> 19%
where the time goes in v1:
time: 84.9 us; the launch traced here: 84.4 us
  starting transfers between devices  42.4 us (50%)
  Pallas kernels  24.9 us (29%)
  local copies, waits for them, and re-layouts  8.51 us (10%)
  waiting for transfers between devices  7.69 us (9%)
  between operations  0.9 us (1%)
    ppermute x4, starting transfers between devices, planes_move(): lax.ppermute(array, 'context', [(2 * a + k, 2 * b + k) for a, b in pairs...  21.2 us
    ppermute x16, starting transfers between devices, context_flip(): return lax.ppermute(array, 'context', [(c, c ^ e) for c in range(contexts)])  14.1 us
    pallas_call x4, Pallas kernels, chunk_mass(): local_call(functools.partial(mass_kernel, flip, places, choose, rows, hea...  13.8 us
    ppermute x6, starting transfers between devices, heads_flip(): return lax.ppermute(array, 'heads', [(h, h ^ e) for h in range(partners)])  7.04 us
    unnamed x14, local copies, waits for them, and re-layouts  5.92 us
    ppermute x16, waiting for transfers between devices, context_flip(): return lax.ppermute(array, 'context', [(c, c ^ e) for c in range(contexts)])  5.8 us
    pallas_call x1, Pallas kernels, back_pass(): local_call(functools.partial(back_kernel, len(stats)), [f32((key_count //...  4.21 us
    pallas_call x1, Pallas kernels, shared_mass(): local_call(functools.partial(share_kernel, rows, heads), [f32((both, key_...  2.56 us
  transfers between devices with their start and end apart: 26, of which 7 were waited for; matrix products, arithmetic and copies ran while one was open for 8% of the time, Pallas kernels for 19%

profile of v1, /device:TPU:0, one launch (start us, length us, event | category | flops | bytes accessed | tf_op | source)
XLA Modules:
  0.0 84.4 jit_solution(7894565124467004579)
XLA Ops:
  0.6 1.0 %copy-done = bf16[8,32,576]{2,1,0:T(8,128)(2,1)S(1)} copy-done((bf16[8,32,576]{2,1,0:T(8,128)(2,1)S(1)}, bf16[8,32,576]{2,1,0:T(8,128)(2,1)}, u32[]{:S(2)}) %copy-start) | copy-done | bytes 294936
  1.6 0.9 %pack_queries.1.refs_0_ = bf16[1152,128]{1,0:T(8,128)(2,1)} custom-call(bf16[8,32,576]{2,1,0:T(8,128)(2,1)S(1)} %copy-done), custom_call_target="tpu_custom_call" | custom-call | bytes 589824 | tf_op jit(solution)/shard_map/pack_queries/pallas_call | solution.py:192
  2.5 1.6 %collective-permute-start = (bf16[1152,128]{1,0:T(8,128)(2,1)}, bf16[1152,128]{1,0:T(8,128)(2,1)S(1)}, u32[]{:S(2)}, u32[]{:S(2)}) collective-permute-start(bf16[1152,128]{1,0:T(8,128)(2,1)} %pack_queries.1.refs_0_), channel_id=1, source_target_pairs={{8,16},{12,20},{16,8},{20,12},{0,0},{4,4},{24,24},{28,28},{9,17},{... | collective-permute-start | bytes 884744 | tf_op jit(solution)/shard_map/ppermute | solution.py:498
  4.1 6.9 %collective-permute-start.6 = (bf16[1152,128]{1,0:T(8,128)(2,1)}, bf16[1152,128]{1,0:T(8,128)(2,1)S(1)}, u32[]{:S(2)}, u32[]{:S(2)}) collective-permute-start(bf16[1152,128]{1,0:T(8,128)(2,1)} %pack_queries.1.refs_0_), channel_id=1, source_target_pairs={{0,24},{4,28},{24,0},{28,4},{1,25},{5,29},{25,1},{29,5},{2,26},{6,... | collective-permute-start | bytes 884744 | tf_op jit(solution)/shard_map/ppermute | solution.py:498
  11.1 12.5 %collective-permute-start.1 = (bf16[1152,128]{1,0:T(8,128)(2,1)S(1)}, bf16[1152,128]{1,0:T(8,128)(2,1)S(1)}, u32[]{:S(2)}, u32[]{:S(2)}) collective-permute-start(bf16[1152,128]{1,0:T(8,128)(2,1)S(1)} %collective-permute-done.refs_0_), channel_id=1, source_target_pairs={{0,16},{4,20},{24,8},{28,12},{8,0},{12,4},{16,24},{20,28},{1,17},{... | collective-permute-start | bytes 884744 | tf_op jit(solution)/shard_map/ppermute | solution.py:498
  23.7 0.8 copy.18
  25.6 3.1 %copy.20.refs_3_.refs_5_.refs_2_.key_ref = bf16[2048,576]{1,0:T(8,128)(2,1)S(1)} copy(bf16[2048,576]{0,1:T(8,128)(2,1)} %param.8) | data formatting | bytes 4718592 | tf_op args[1]
  28.7 0.8 copy.19
  29.4 1.0 %mul.45 = f32[8,256]{1,0:T(8,128)S(1)} reshape(f32[8,32,8]{2,1,0:T(8,128)} %copy.19) | data formatting | bytes 16384 | tf_op jit(solution)/shard_map/mul | solution.py:522
  31.3 3.8 %mass_own.1.own_ref = f32[16,2048]{1,0:T(8,128)S(1)} custom-call(s32[68]{0:T(128)S(1)} %concatenate.3.info_ref, bf16[1152,128]{1,0:T(8,128)(2,1)} %pack_queries.1.refs_0_, bf16[1152,128]{1,0:T(8,128)(2,1)} %collective-permute-done.3.refs_1_, f32[8,256,128]{2,1,0:T(8,128)S(1)} %broadcast_in_dim.5.refs_2_.refs_4_.refs_1_.lse_ref, ...), custom_call_target="tpu_custom_call" | custom-call | flops 1207959552 | bytes 2359296 | tf_op jit(solution)/shard_map/mass_own/pallas_call | solution.py:272
  35.1 2.4 %mass_far.1.half_ref = f32[8,2048]{1,0:T(8,128)S(1)} custom-call(s32[68]{0:T(128)S(1)} %concatenate.3.info_ref, bf16[1152,128]{1,0:T(8,128)(2,1)S(1)} %collective-permute-done.1.refs_0_, f32[8,256,128]{2,1,0:T(8,128)S(1)} %broadcast_in_dim.5.refs_2_.refs_4_.refs_1_.lse_ref, bf16[2048,576]{1,0:T(8,128)(2,1)S(1)} %copy.20.refs_3_.refs_5_.refs_2_.key_ref), custom_call_target="tpu_custom_call" | custom-call | flops 603979776 | bytes 2359296 | tf_op jit(solution)/shard_map/mass_far/pallas_call | solution.py:272
  37.5 3.8 %mass_near.1.near_ref = f32[16,2048]{1,0:T(8,128)S(1)} custom-call(s32[68]{0:T(128)S(1)} %concatenate.3.info_ref, bf16[1152,128]{1,0:T(8,128)(2,1)} %collective-permute-done.4.refs_0_, bf16[1152,128]{1,0:T(8,128)(2,1)} %collective-permute-done.5.refs_1_, f32[8,256,128]{2,1,0:T(8,128)S(1)} %broadcast_in_dim.5.refs_2_.refs_4_.refs_1_.lse_ref, ...), custom_call_target="tpu_custom_call" | custom-call | flops 1207959552 | bytes 2359296 | tf_op jit(solution)/shard_map/mass_near/pallas_call | solution.py:272
  41.3 3.9 %mass_ends.1.far_ref = f32[16,2048]{1,0:T(8,128)S(1)} custom-call(s32[68]{0:T(128)S(1)} %concatenate.3.info_ref, bf16[1152,128]{1,0:T(8,128)(2,1)S(1)} %collective-permute-done.refs_0_, bf16[1152,128]{1,0:T(8,128)(2,1)S(1)} %collective-permute-done.6.refs_1_, bf16[1152,128]{1,0:T(8,128)(2,1)} %collective-permute-done.7.refs_2_, ...), custom_call_target="tpu_custom_call" | custom-call | flops 1207959552 | bytes 2359296 | tf_op jit(solution)/shard_map/mass_ends/pallas_call | solution.py:272
  45.3 2.6 %mass_and_share.1 = (f32[16,2048]{1,0:T(8,128)S(1)}, bf16[16,2048]{1,0:T(8,128)(2,1)S(1)}, bf16[16,2048]{1,0:T(8,128)(2,1)S(1)}, bf16[16,2048]{1,0:T(8,128)(2,1)S(1)}) custom-call(s32[68]{0:T(128)S(1)} %concatenate.3.info_ref, bf16[1152,128]{1,0:T(8,128)(2,1)S(1)} %collective-permute-done.2.pack_ref, ...), custom_call_target="tpu_custom_call" | custom-call | flops 603979776 | bytes 2359296 | tf_op jit(solution)/shard_map/mass_and_share/pallas_call | solution.py:320
  47.8 1.6 %collective-permute-start.10 = (bf16[16,2048]{1,0:T(8,128)(2,1)S(1)}, bf16[16,2048]{1,0:T(8,128)(2,1)S(1)}, u32[]{:S(2)}, u32[]{:S(2)}) collective-permute-start(bf16[16,2048]{1,0:T(8,128)(2,1)S(1)} %get-tuple-element.23), channel_id=1, source_target_pairs={{0,2},{1,3},{2,0},{3,1},{4,6},{5,7},{6,4},{7,5},{8,10},{9,11},{10,... | collective-permute-start | bytes 196616 | tf_op jit(solution)/shard_map/ppermute | solution.py:504
  49.4 1.4 %collective-permute-start.11 = (bf16[16,2048]{1,0:T(8,128)(2,1)S(1)}, bf16[16,2048]{1,0:T(8,128)(2,1)S(1)}, u32[]{:S(2)}, u32[]{:S(2)}) collective-permute-start(bf16[16,2048]{1,0:T(8,128)(2,1)S(1)} %get-tuple-element.24), channel_id=1, source_target_pairs={{0,3},{1,2},{2,1},{3,0},{4,7},{5,6},{6,5},{7,4},{8,11},{9,10},{10,... | collective-permute-start | bytes 196616 | tf_op jit(solution)/shard_map/ppermute | solution.py:504
  51.7 1.0 %copy-done.2 = bf16[2048,128]{1,0:T(8,128)(2,1)S(1)} copy-done((bf16[2048,128]{1,0:T(8,128)(2,1)S(1)}, bf16[2048,128]{1,0:T(8,128)(2,1)}, u32[]{:S(2)}) %copy-start.2) | copy-done | bytes 524312
  52.7 2.0 %index_logits.1 = (f32[16,2048]{1,0:T(8,128)S(1)}, f32[16,128]{1,0:T(8,128)S(1)}) custom-call(s32[68]{0:T(128)S(1)} %concatenate.3.info_ref, bf16[1024,128]{1,0:T(8,128)(2,1)S(1)} %bitcast.10, bf16[2048,128]{1,0:T(8,128)(2,1)S(1)} %copy-done.2, f32[1024,128]{1,0:T(8,128)S(1)} %broadcast_in_dim.4.weight_ref), custom_call_target="tpu_custom_call" | custom-call | flops 536870912 | bytes 524288 | tf_op jit(solution)/shard_map/index_logits/pallas_call | solution.py:362
  55.3 2.1 %collective-permute-start.13 = (f32[16,128]{1,0:T(8,128)S(1)}, f32[16,128]{1,0:T(8,128)S(1)}, u32[]{:S(2)}, u32[]{:S(2)}) collective-permute-start(f32[16,128]{1,0:T(8,128)S(1)} %get-tuple-element.27.refs_0_), channel_id=1, source_target_pairs={{0,8},{4,12},{8,0},{12,4},{16,24},{20,28},{24,16},{28,20},{1,9},{5... | collective-permute-start | bytes 24584 | tf_op jit(solution)/shard_map/ppermute | solution.py:501
  57.5 2.2 %collective-permute-start.15 = (f32[16,128]{1,0:T(8,128)S(1)}, f32[16,128]{1,0:T(8,128)S(1)}, u32[]{:S(2)}, u32[]{:S(2)}) collective-permute-start(f32[16,128]{1,0:T(8,128)S(1)} %get-tuple-element.27.refs_0_), channel_id=1, source_target_pairs={{0,16},{4,20},{8,24},{12,28},{16,0},{20,4},{24,8},{28,12},{1,17},{... | collective-permute-start | bytes 24584 | tf_op jit(solution)/shard_map/ppermute | solution.py:501
  59.8 2.3 %collective-permute-start.17 = (f32[16,128]{1,0:T(8,128)S(1)}, f32[16,128]{1,0:T(8,128)S(1)}, u32[]{:S(2)}, u32[]{:S(2)}) collective-permute-start(f32[16,128]{1,0:T(8,128)S(1)} %get-tuple-element.27.refs_0_), channel_id=1, source_target_pairs={{0,24},{4,28},{8,16},{12,20},{16,8},{20,12},{24,0},{28,4},{1,25},{... | collective-permute-start | bytes 24584 | tf_op jit(solution)/shard_map/ppermute | solution.py:501
  62.2 1.5 %collective-permute-start.18 = (f32[16,128]{1,0:T(8,128)S(1)}, f32[16,128]{1,0:T(8,128)S(1)}, u32[]{:S(2)}, u32[]{:S(2)}) collective-permute-start(f32[16,128]{1,0:T(8,128)S(1)} %get-tuple-element.27.refs_0_), channel_id=1, source_target_pairs={{0,28},{4,24},{8,20},{12,16},{16,12},{20,8},{24,4},{28,0},{1,29},{... | collective-permute-start | bytes 24584 | tf_op jit(solution)/shard_map/ppermute | solution.py:501
  63.8 1.5 %collective-permute-done.17.refs_6_ = f32[16,128]{1,0:T(8,128)S(1)} collective-permute-done((f32[16,128]{1,0:T(8,128)S(1)}, f32[16,128]{1,0:T(8,128)S(1)}, u32[]{:S(2)}, u32[]{:S(2)}) %collective-permute-start.17) | collective-permute-done | bytes 8224 | tf_op jit(solution)/shard_map/ppermute | solution.py:501
  65.3 1.7 %collective-permute-done.18.refs_7_ = f32[16,128]{1,0:T(8,128)S(1)} collective-permute-done((f32[16,128]{1,0:T(8,128)S(1)}, f32[16,128]{1,0:T(8,128)S(1)}, u32[]{:S(2)}, u32[]{:S(2)}) %collective-permute-start.18) | collective-permute-done | bytes 8224 | tf_op jit(solution)/shard_map/ppermute | solution.py:501
  67.0 4.2 %index_back.1 = (f32[512,128]{1,0:T(8,128)S(1)}, bf16[512,128]{1,0:T(8,128)(2,1)S(1)}, bf16[512,128]{1,0:T(8,128)(2,1)S(1)}, bf16[512,128]{1,0:T(8,128)(2,1)S(1)...) custom-call(s32[68]{0:T(128)S(1)} %concatenate.3.info_ref, f32[16,2048]{1,0:T(8,128)S(1)} %get-tuple-element.25.mass_ref, ...), custom_call_target="tpu_custom_call" | custom-call | flops 1610612736 | bytes 2097152 | tf_op jit(solution)/shard_map/index_back/pallas_call | solution.py:437
  71.5 1.5 %collective-permute-start.19 = (bf16[512,128]{1,0:T(8,128)(2,1)S(1)}, bf16[512,128]{1,0:T(8,128)(2,1)S(1)}, u32[]{:S(2)}, u32[]{:S(2)}) collective-permute-start(bf16[512,128]{1,0:T(8,128)(2,1)S(1)} %get-tuple-element.29), channel_id=1, source_target_pairs={{0,1},{1,0},{2,3},{3,2},{4,5},{5,4},{6,7},{7,6},{8,9},{9,8},{10,11... | collective-permute-start | bytes 393224 | tf_op jit(solution)/shard_map/ppermute | solution.py:504
  73.0 1.3 %collective-permute-start.20 = (bf16[512,128]{1,0:T(8,128)(2,1)S(1)}, bf16[512,128]{1,0:T(8,128)(2,1)S(1)}, u32[]{:S(2)}, u32[]{:S(2)}) collective-permute-start(bf16[512,128]{1,0:T(8,128)(2,1)S(1)} %get-tuple-element.30), channel_id=1, source_target_pairs={{0,2},{1,3},{2,0},{3,1},{4,6},{5,7},{6,4},{7,5},{8,10},{9,11},{10,... | collective-permute-start | bytes 393224 | tf_op jit(solution)/shard_map/ppermute | solution.py:504
  75.6 2.3 %collective-permute-start.24 = (bf16[128,128]{1,0:T(8,128)(2,1)S(1)}, bf16[128,128]{1,0:T(8,128)(2,1)S(1)}, u32[]{:S(2)}, u32[]{:S(2)}) collective-permute-start(bf16[128,128]{1,0:T(8,128)(2,1)S(1)} %get-tuple-element.36), channel_id=1, source_target_pairs={{0,16},{4,20},{8,24},{12,28},{16,0},{20,4},{24,8},{28,12},{1,17},{... | collective-permute-start | bytes 98312 | tf_op jit(solution)/shard_map/ppermute | solution.py:501
  77.9 2.1 %collective-permute-start.25 = (bf16[128,128]{1,0:T(8,128)(2,1)S(1)}, bf16[128,128]{1,0:T(8,128)(2,1)S(1)}, u32[]{:S(2)}, u32[]{:S(2)}) collective-permute-start(bf16[128,128]{1,0:T(8,128)(2,1)S(1)} %get-tuple-element.37), channel_id=1, source_target_pairs={{0,24},{4,28},{8,16},{12,20},{16,8},{20,12},{24,0},{28,4},{1,25},{... | collective-permute-start | bytes 98312 | tf_op jit(solution)/shard_map/ppermute | solution.py:501
  80.0 1.0 %collective-permute-done.20.refs_2_ = bf16[512,128]{1,0:T(8,128)(2,1)S(1)} collective-permute-done((bf16[512,128]{1,0:T(8,128)(2,1)S(1)}, bf16[512,128]{1,0:T(8,128)(2,1)S(1)}, u32[]{:S(2)}, u32[]{:S(2)}) %collective-permute-start.20) | collective-permute-done | bytes 131104 | tf_op jit(solution)/shard_map/ppermute | solution.py:504
  81.1 2.6 %collective-permute-done.25.refs_7_ = bf16[128,128]{1,0:T(8,128)(2,1)S(1)} collective-permute-done((bf16[128,128]{1,0:T(8,128)(2,1)S(1)}, bf16[128,128]{1,0:T(8,128)(2,1)S(1)}, u32[]{:S(2)}, u32[]{:S(2)}) %collective-permute-start.25) | collective-permute-done | bytes 32800 | tf_op jit(solution)/shard_map/ppermute | solution.py:501
  83.6 0.8 last_sums.1
  (54 shorter events, 5.4 us)
Async XLA Ops:
  0.6 1.0 %copy-start = (bf16[8,32,576]{2,1,0:T(8,128)(2,1)S(1)}, bf16[8,32,576]{2,1,0:T(8,128)(2,1)}, u32[]{:S(2)}) copy-start(bf16[8,32,576]{2,1,0:T(8,128)(2,1)} %query_ref.1) | copy-start | bytes 884740
  2.5 8.6 %collective-permute-start = (bf16[1152,128]{1,0:T(8,128)(2,1)}, bf16[1152,128]{1,0:T(8,128)(2,1)S(1)}, u32[]{:S(2)}, u32[]{:S(2)}) collective-permute-start(bf16[1152,128]{1,0:T(8,128)(2,1)} %pack_queries.1.refs_0_), channel_id=1, source_target_pairs={{8,16},{12,20},{16,8},{20,12},{0,0},{4,4},{24,24},{28,28},{9,17},{... | collective-permute-start | bytes 884744 | tf_op jit(solution)/shard_map/ppermute | solution.py:498
  4.1 20.9 %collective-permute-start.6 = (bf16[1152,128]{1,0:T(8,128)(2,1)}, bf16[1152,128]{1,0:T(8,128)(2,1)S(1)}, u32[]{:S(2)}, u32[]{:S(2)}) collective-permute-start(bf16[1152,128]{1,0:T(8,128)(2,1)} %pack_queries.1.refs_0_), channel_id=1, source_target_pairs={{0,24},{4,28},{24,0},{28,4},{1,25},{5,29},{25,1},{29,5},{2,26},{6,... | collective-permute-start | bytes 884744 | tf_op jit(solution)/shard_map/ppermute | solution.py:498
  11.1 14.1 %collective-permute-start.4 = (bf16[1152,128]{1,0:T(8,128)(2,1)}, bf16[1152,128]{1,0:T(8,128)(2,1)}, u32[]{:S(2)}, u32[]{:S(2)}) collective-permute-start(bf16[1152,128]{1,0:T(8,128)(2,1)} %pack_queries.1.refs_0_), channel_id=1, source_target_pairs={{0,8},{4,12},{8,0},{12,4},{16,24},{20,28},{24,16},{28,20},{1,9},{5... | collective-permute-start | bytes 884744 | tf_op jit(solution)/shard_map/ppermute | solution.py:498
  11.1 19.9 %collective-permute-start.1 = (bf16[1152,128]{1,0:T(8,128)(2,1)S(1)}, bf16[1152,128]{1,0:T(8,128)(2,1)S(1)}, u32[]{:S(2)}, u32[]{:S(2)}) collective-permute-start(bf16[1152,128]{1,0:T(8,128)(2,1)S(1)} %collective-permute-done.refs_0_), channel_id=1, source_target_pairs={{0,16},{4,20},{24,8},{28,12},{8,0},{12,4},{16,24},{20,28},{1,17},{... | collective-permute-start | bytes 884744 | tf_op jit(solution)/shard_map/ppermute | solution.py:498
  23.7 7.3 %collective-permute-start.3 = (bf16[1152,128]{1,0:T(8,128)(2,1)}, bf16[1152,128]{1,0:T(8,128)(2,1)}, u32[]{:S(2)}, u32[]{:S(2)}) collective-permute-start(bf16[1152,128]{1,0:T(8,128)(2,1)} %pack_queries.1.refs_0_), channel_id=1, source_target_pairs={{0,4},{4,0},{8,12},{12,8},{16,20},{20,16},{24,28},{28,24},{1,5},{5... | collective-permute-start | bytes 884744 | tf_op jit(solution)/shard_map/ppermute | solution.py:501
  24.5 16.8 %collective-permute-start.7 = (bf16[1152,128]{1,0:T(8,128)(2,1)S(1)}, bf16[1152,128]{1,0:T(8,128)(2,1)}, u32[]{:S(2)}, u32[]{:S(2)}) collective-permute-start(bf16[1152,128]{1,0:T(8,128)(2,1)S(1)} %collective-permute-done.refs_0_), channel_id=1, source_target_pairs={{0,4},{4,0},{8,12},{12,8},{16,20},{20,16},{24,28},{28,24},{1,5},{5... | collective-permute-start | bytes 884744 | tf_op jit(solution)/shard_map/ppermute | solution.py:501
  25.0 16.3 %collective-permute-start.8 = (bf16[1152,128]{1,0:T(8,128)(2,1)S(1)}, bf16[1152,128]{1,0:T(8,128)(2,1)}, u32[]{:S(2)}, u32[]{:S(2)}) collective-permute-start(bf16[1152,128]{1,0:T(8,128)(2,1)S(1)} %collective-permute-done.6.refs_1_), channel_id=1, source_target_pairs={{0,4},{4,0},{8,12},{12,8},{16,20},{20,16},{24,28},{28,24},{1,5},{5... | collective-permute-start | bytes 884744 | tf_op jit(solution)/shard_map/ppermute | solution.py:501
  25.1 12.4 %collective-permute-start.5 = (bf16[1152,128]{1,0:T(8,128)(2,1)}, bf16[1152,128]{1,0:T(8,128)(2,1)}, u32[]{:S(2)}, u32[]{:S(2)}) collective-permute-start(bf16[1152,128]{1,0:T(8,128)(2,1)} %collective-permute-done.4.refs_0_), channel_id=1, source_target_pairs={{0,4},{4,0},{8,12},{12,8},{16,20},{20,16},{24,28},{28,24},{1,5},{5... | collective-permute-start | bytes 884744 | tf_op jit(solution)/shard_map/ppermute | solution.py:501
  25.6 4.9 %copy-start.5 = (s32[64]{0:T(128)S(1)}, s32[64]{0:T(128)}, u32[]{:S(2)}) copy-start(s32[64]{0:T(128)} %param.10) | copy-start | bytes 772
  31.0 14.3 %collective-permute-start.2 = (bf16[1152,128]{1,0:T(8,128)(2,1)S(1)}, bf16[1152,128]{1,0:T(8,128)(2,1)S(1)}, u32[]{:S(2)}, u32[]{:S(2)}) collective-permute-start(bf16[1152,128]{1,0:T(8,128)(2,1)S(1)} %collective-permute-done.1.refs_0_), channel_id=1, source_target_pairs={{0,4},{4,0},{8,12},{12,8},{16,20},{20,16},{24,28},{28,24},{1,5},{5... | collective-permute-start | bytes 884744 | tf_op jit(solution)/shard_map/ppermute | solution.py:501
  45.2 6.2 %copy-start.4 = (f32[16,64]{1,0:T(8,128)S(1)}, f32[16,64]{1,0:T(8,128)}, u32[]{:S(2)}) copy-start(f32[16,64]{1,0:T(8,128)} %param.13) | copy-start | bytes 12292
  45.2 6.4 %copy-start.1 = (bf16[16,64,128]{2,1,0:T(8,128)(2,1)S(1)}, bf16[16,64,128]{2,1,0:T(8,128)(2,1)}, u32[]{:S(2)}) copy-start(bf16[16,64,128]{2,1,0:T(8,128)(2,1)} %param.11) | copy-start | bytes 786436
  47.8 19.2 %copy-start.3 = (bf16[2048,128]{1,0:T(8,128)(2,1)S(1)}, bf16[2048,128]{1,0:T(8,128)(2,1)}, u32[]{:S(2)}) copy-start(bf16[2048,128]{1,0:T(8,128)(2,1)} %key_ref.4) | copy-start | bytes 1572868
  47.8 6.9 %collective-permute-start.10 = (bf16[16,2048]{1,0:T(8,128)(2,1)S(1)}, bf16[16,2048]{1,0:T(8,128)(2,1)S(1)}, u32[]{:S(2)}, u32[]{:S(2)}) collective-permute-start(bf16[16,2048]{1,0:T(8,128)(2,1)S(1)} %get-tuple-element.23), channel_id=1, source_target_pairs={{0,2},{1,3},{2,0},{3,1},{4,6},{5,7},{6,4},{7,5},{8,10},{9,11},{10,... | collective-permute-start | bytes 196616 | tf_op jit(solution)/shard_map/ppermute | solution.py:504
  49.4 5.5 %collective-permute-start.11 = (bf16[16,2048]{1,0:T(8,128)(2,1)S(1)}, bf16[16,2048]{1,0:T(8,128)(2,1)S(1)}, u32[]{:S(2)}, u32[]{:S(2)}) collective-permute-start(bf16[16,2048]{1,0:T(8,128)(2,1)S(1)} %get-tuple-element.24), channel_id=1, source_target_pairs={{0,3},{1,2},{2,1},{3,0},{4,7},{5,6},{6,5},{7,4},{8,11},{9,10},{10,... | collective-permute-start | bytes 196616 | tf_op jit(solution)/shard_map/ppermute | solution.py:504
  50.9 4.3 %collective-permute-start.9 = (bf16[16,2048]{1,0:T(8,128)(2,1)S(1)}, bf16[16,2048]{1,0:T(8,128)(2,1)S(1)}, u32[]{:S(2)}, u32[]{:S(2)}) collective-permute-start(bf16[16,2048]{1,0:T(8,128)(2,1)S(1)} %get-tuple-element.22), channel_id=1, source_target_pairs={{0,1},{1,0},{2,3},{3,2},{4,5},{5,4},{6,7},{7,6},{8,9},{9,8},{10,11... | collective-permute-start | bytes 196616 | tf_op jit(solution)/shard_map/ppermute | solution.py:504
  51.7 1.0 %copy-start.2 = (bf16[2048,128]{1,0:T(8,128)(2,1)S(1)}, bf16[2048,128]{1,0:T(8,128)(2,1)}, u32[]{:S(2)}) copy-start(bf16[2048,128]{1,0:T(8,128)(2,1)} %key_ref.4) | copy-start | bytes 1572868
  55.2 4.6 %collective-permute-start.12 = (f32[16,128]{1,0:T(8,128)S(1)}, f32[16,128]{1,0:T(8,128)S(1)}, u32[]{:S(2)}, u32[]{:S(2)}) collective-permute-start(f32[16,128]{1,0:T(8,128)S(1)} %get-tuple-element.27.refs_0_), channel_id=1, source_target_pairs={{0,4},{4,0},{8,12},{12,8},{16,20},{20,16},{24,28},{28,24},{1,5},{5... | collective-permute-start | bytes 24584 | tf_op jit(solution)/shard_map/ppermute | solution.py:501
  55.3 6.9 %collective-permute-start.13 = (f32[16,128]{1,0:T(8,128)S(1)}, f32[16,128]{1,0:T(8,128)S(1)}, u32[]{:S(2)}, u32[]{:S(2)}) collective-permute-start(f32[16,128]{1,0:T(8,128)S(1)} %get-tuple-element.27.refs_0_), channel_id=1, source_target_pairs={{0,8},{4,12},{8,0},{12,4},{16,24},{20,28},{24,16},{28,20},{1,9},{5... | collective-permute-start | bytes 24584 | tf_op jit(solution)/shard_map/ppermute | solution.py:501
  57.4 6.4 %collective-permute-start.14 = (f32[16,128]{1,0:T(8,128)S(1)}, f32[16,128]{1,0:T(8,128)S(1)}, u32[]{:S(2)}, u32[]{:S(2)}) collective-permute-start(f32[16,128]{1,0:T(8,128)S(1)} %get-tuple-element.27.refs_0_), channel_id=1, source_target_pairs={{0,12},{4,8},{8,4},{12,0},{16,28},{20,24},{24,20},{28,16},{1,13},{... | collective-permute-start | bytes 24584 | tf_op jit(solution)/shard_map/ppermute | solution.py:501
  57.5 6.4 %collective-permute-start.15 = (f32[16,128]{1,0:T(8,128)S(1)}, f32[16,128]{1,0:T(8,128)S(1)}, u32[]{:S(2)}, u32[]{:S(2)}) collective-permute-start(f32[16,128]{1,0:T(8,128)S(1)} %get-tuple-element.27.refs_0_), channel_id=1, source_target_pairs={{0,16},{4,20},{8,24},{12,28},{16,0},{20,4},{24,8},{28,12},{1,17},{... | collective-permute-start | bytes 24584 | tf_op jit(solution)/shard_map/ppermute | solution.py:501
  59.7 4.1 %collective-permute-start.16 = (f32[16,128]{1,0:T(8,128)S(1)}, f32[16,128]{1,0:T(8,128)S(1)}, u32[]{:S(2)}, u32[]{:S(2)}) collective-permute-start(f32[16,128]{1,0:T(8,128)S(1)} %get-tuple-element.27.refs_0_), channel_id=1, source_target_pairs={{0,20},{4,16},{8,28},{12,24},{16,4},{20,0},{24,12},{28,8},{1,21},{... | collective-permute-start | bytes 24584 | tf_op jit(solution)/shard_map/ppermute | solution.py:501
  59.8 5.4 %collective-permute-start.17 = (f32[16,128]{1,0:T(8,128)S(1)}, f32[16,128]{1,0:T(8,128)S(1)}, u32[]{:S(2)}, u32[]{:S(2)}) collective-permute-start(f32[16,128]{1,0:T(8,128)S(1)} %get-tuple-element.27.refs_0_), channel_id=1, source_target_pairs={{0,24},{4,28},{8,16},{12,20},{16,8},{20,12},{24,0},{28,4},{1,25},{... | collective-permute-start | bytes 24584 | tf_op jit(solution)/shard_map/ppermute | solution.py:501
  62.2 4.9 %collective-permute-start.18 = (f32[16,128]{1,0:T(8,128)S(1)}, f32[16,128]{1,0:T(8,128)S(1)}, u32[]{:S(2)}, u32[]{:S(2)}) collective-permute-start(f32[16,128]{1,0:T(8,128)S(1)} %get-tuple-element.27.refs_0_), channel_id=1, source_target_pairs={{0,28},{4,24},{8,20},{12,16},{16,12},{20,8},{24,4},{28,0},{1,29},{... | collective-permute-start | bytes 24584 | tf_op jit(solution)/shard_map/ppermute | solution.py:501
  71.3 3.7 %collective-permute-start.22 = (bf16[4,128,128]{2,1,0:T(8,128)(2,1)S(1)}, bf16[4,128,128]{2,1,0:T(8,128)(2,1)S(1)}, u32[]{:S(2)}, u32[]{:S(2)}) collective-permute-start(bf16[4,128,128]{2,1,0:T(8,128)(2,1)S(1)} %get-tuple-element.33), channel_id=1, source_target_pairs={{0,4},{4,0},{8,12},{12,8},{16,20},{20,16},{24,28},{28,24},{1,5},{5... | collective-permute-start | bytes 393224 | tf_op jit(solution)/shard_map/ppermute | solution.py:501
  71.5 6.4 %collective-permute-start.19 = (bf16[512,128]{1,0:T(8,128)(2,1)S(1)}, bf16[512,128]{1,0:T(8,128)(2,1)S(1)}, u32[]{:S(2)}, u32[]{:S(2)}) collective-permute-start(bf16[512,128]{1,0:T(8,128)(2,1)S(1)} %get-tuple-element.29), channel_id=1, source_target_pairs={{0,1},{1,0},{2,3},{3,2},{4,5},{5,4},{6,7},{7,6},{8,9},{9,8},{10,11... | collective-permute-start | bytes 393224 | tf_op jit(solution)/shard_map/ppermute | solution.py:504
  73.0 8.1 %collective-permute-start.20 = (bf16[512,128]{1,0:T(8,128)(2,1)S(1)}, bf16[512,128]{1,0:T(8,128)(2,1)S(1)}, u32[]{:S(2)}, u32[]{:S(2)}) collective-permute-start(bf16[512,128]{1,0:T(8,128)(2,1)S(1)} %get-tuple-element.30), channel_id=1, source_target_pairs={{0,2},{1,3},{2,0},{3,1},{4,6},{5,7},{6,4},{7,5},{8,10},{9,11},{10,... | collective-permute-start | bytes 393224 | tf_op jit(solution)/shard_map/ppermute | solution.py:504
  74.2 6.8 %collective-permute-start.21 = (bf16[512,128]{1,0:T(8,128)(2,1)S(1)}, bf16[512,128]{1,0:T(8,128)(2,1)S(1)}, u32[]{:S(2)}, u32[]{:S(2)}) collective-permute-start(bf16[512,128]{1,0:T(8,128)(2,1)S(1)} %get-tuple-element.31), channel_id=1, source_target_pairs={{0,3},{1,2},{2,1},{3,0},{4,7},{5,6},{6,5},{7,4},{8,11},{9,10},{10,... | collective-permute-start | bytes 393224 | tf_op jit(solution)/shard_map/ppermute | solution.py:504
  75.6 5.5 %collective-permute-start.23 = (bf16[128,128]{1,0:T(8,128)(2,1)S(1)}, bf16[128,128]{1,0:T(8,128)(2,1)S(1)}, u32[]{:S(2)}, u32[]{:S(2)}) collective-permute-start(bf16[128,128]{1,0:T(8,128)(2,1)S(1)} %get-tuple-element.35), channel_id=1, source_target_pairs={{0,8},{4,12},{8,0},{12,4},{16,24},{20,28},{24,16},{28,20},{1,9},{5... | collective-permute-start | bytes 98312 | tf_op jit(solution)/shard_map/ppermute | solution.py:501
  75.6 5.4 %collective-permute-start.24 = (bf16[128,128]{1,0:T(8,128)(2,1)S(1)}, bf16[128,128]{1,0:T(8,128)(2,1)S(1)}, u32[]{:S(2)}, u32[]{:S(2)}) collective-permute-start(bf16[128,128]{1,0:T(8,128)(2,1)S(1)} %get-tuple-element.36), channel_id=1, source_target_pairs={{0,16},{4,20},{8,24},{12,28},{16,0},{20,4},{24,8},{28,12},{1,17},{... | collective-permute-start | bytes 98312 | tf_op jit(solution)/shard_map/ppermute | solution.py:501
  77.9 5.7 %collective-permute-start.25 = (bf16[128,128]{1,0:T(8,128)(2,1)S(1)}, bf16[128,128]{1,0:T(8,128)(2,1)S(1)}, u32[]{:S(2)}, u32[]{:S(2)}) collective-permute-start(bf16[128,128]{1,0:T(8,128)(2,1)S(1)} %get-tuple-element.37), channel_id=1, source_target_pairs={{0,24},{4,28},{8,16},{12,20},{16,8},{20,12},{24,0},{28,4},{1,25},{... | collective-permute-start | bytes 98312 | tf_op jit(solution)/shard_map/ppermute | solution.py:501

commit v2 on v1

v2 whole, which is shorter than its diff:
```python
import functools
import math

import jax
import jax.numpy as jnp
from jax import lax
from jax.experimental import pallas as pl
from jax.experimental.pallas import tpu as pltpu
from jax.sharding import PartitionSpec as P

main_scale = 192.0 ** (-0.5)
loss_scale = 64.0
masked_low = -1e30
log2_e = math.log2(math.e)
lanes = 128
vmem_bytes = 20 * 1024 * 1024
most_bytes = 60 * 1024 * 1024

def joined(part, axis, combine):
    gathered = jax.tree.map(lambda a: lax.all_gather(a, axis), part)

    def take(source):
        return jax.tree.map(lambda a: lax.dynamic_index_in_dim(a, source, 0, False), gathered)

    return lax.fori_loop(
        1, lax.axis_size(axis), lambda source, state: combine(state, take(source)), take(0)
    )


def head_mass(queries, lse_rows, len_rows, latent, first_key):
    row_count = queries.shape[0]
    block_rows = math.gcd(row_count, 64)
    steps_count = row_count // block_rows
    key_pos = first_key + jnp.arange(latent.shape[0], dtype=jnp.int32)

    def one_block(inputs):
        query_block, lse_block, len_block = inputs
        scores = (
            jnp.einsum("rhd,sd->rhs", query_block, latent, preferred_element_type=jnp.float32)
            * main_scale
        )
        summed = jnp.sum(jnp.exp(scores - lse_block[:, :, None]), axis=1)
        return jnp.where(key_pos[None, :] < len_block[:, None], summed, 0.0)

    stacked = lax.map(
        one_block,
        (
            queries.reshape((steps_count, block_rows) + queries.shape[1:]),
            lse_rows.reshape(steps_count, block_rows, lse_rows.shape[1]),
            len_rows.reshape(steps_count, block_rows),
        ),
    )
    return stacked.reshape(row_count, latent.shape[0])


def general_on_device(main_query, latent_keys, head_lse, lengths, index_query, index_key, index_weight):
    key_count = latent_keys.shape[0]
    first_key = lax.axis_index("context") * key_count
    own_rows = index_query.shape[0]
    row_first = lax.axis_index("heads") * own_rows
    partial_mass = head_mass(
        lax.all_gather(main_query, "context", axis=0, tiled=True),
        head_lse,
        lengths,
        latent_keys,
        first_key,
    )
    summed_mass = lax.psum(partial_mass, "heads")
    row_mass = lax.dynamic_slice_in_dim(summed_mass, row_first, own_rows, 0)
    own_len = lax.dynamic_slice_in_dim(lengths, row_first, own_rows, 0)
    visible = (first_key + jnp.arange(key_count, dtype=jnp.int32))[None, :] < own_len[:, None]
    heads_count = index_query.shape[1]
    width = index_query.shape[2]
    index_scale = width ** (-0.5)
    flat_query = index_query.reshape(own_rows * heads_count, width)
    block_keys = math.gcd(key_count, 512)
    block_total = key_count // block_keys
    key_blocks = index_key.reshape(block_total, block_keys, width)

    def block_dots(key_block):
        products = lax.dot_general(
            flat_query, key_block, (((1,), (1,)), ((), ())), preferred_element_type=jnp.float32
        )
        return products.reshape(own_rows, heads_count, key_block.shape[0])

    def block_logits(key_block):
        return (
            jnp.einsum(
                "tj,tjs->ts",
                index_weight,
                jax.nn.relu(block_dots(key_block)),
                precision=lax.Precision.HIGHEST,
            )
            * index_scale
        )

    logits = jnp.moveaxis(lax.map(block_logits, key_blocks), 0, 1).reshape(own_rows, key_count)
    local_top = jnp.max(jnp.where(visible, logits, masked_low), axis=1)
    mass_local = jnp.sum(row_mass, axis=1)
    local_exp = jnp.where(visible, jnp.exp(logits - local_top[:, None]), 0.0)

    def combine(first, second):
        highest = jnp.maximum(first[0], second[0])
        merged = first[1] * jnp.exp(first[0] - highest) + second[1] * jnp.exp(second[0] - highest)
        return (highest, merged, first[2] + second[2])

    top, share_sum, mass_total = joined(
        (local_top, jnp.sum(local_exp, axis=1), mass_local), "context", combine
    )
    weights_exp = jnp.where(visible, jnp.exp(logits - top[:, None]), 0.0)
    probability = weights_exp / share_sum[:, None]
    target = row_mass / mass_total[:, None]
    slopes = loss_scale * (probability - target)
    slope_blocks = slopes.reshape(own_rows, block_total, block_keys).transpose(1, 0, 2)

    def back_step(query_grad, inputs):
        key_block, slope_block = inputs
        products = block_dots(key_block)
        terms = jnp.where(
            products > 0, slope_block[:, None, :] * index_weight[:, :, None] * index_scale, 0.0
        )
        terms = terms.astype(jnp.bfloat16).reshape(own_rows * heads_count, key_block.shape[0])
        query_grad = query_grad + jnp.dot(terms, key_block, preferred_element_type=jnp.float32)
        key_grad = lax.dot_general(
            terms, flat_query, (((0,), (0,)), ((), ())), preferred_element_type=jnp.float32
        )
        return (query_grad, key_grad)

    start_grad = jnp.zeros((own_rows * heads_count, width), jnp.float32)
    query_grad, key_grads = lax.scan(back_step, start_grad, (key_blocks, slope_blocks))
    query_grad = query_grad.reshape(own_rows, heads_count, width)
    key_grad = key_grads.reshape(key_count, width)
    out_query = lax.psum_scatter(query_grad, "context", scatter_dimension=1, tiled=True)
    out_key = lax.psum_scatter(key_grad, "heads", scatter_dimension=0, tiled=True)
    return (out_query, out_key)


def local_call(kernel, out_shape, name, grid=None, in_specs=None, out_specs=None, scratch=(), flops=0, moved=0, room=vmem_bytes):
    settings = dict(
        out_shape=out_shape,
        scratch_shapes=list(scratch),
        name=name,
        compiler_params=pltpu.CompilerParams(vmem_limit_bytes=room),
        cost_estimate=pl.CostEstimate(flops=flops, bytes_accessed=moved, transcendentals=0),
    )
    if grid is not None:
        settings["grid"] = grid
    if in_specs is not None:
        settings["in_specs"] = in_specs
    if out_specs is not None:
        settings["out_specs"] = out_specs
    return pl.pallas_call(kernel, **settings)


def whole():
    return pl.BlockSpec(memory_space=pltpu.VMEM)


def scalars():
    return pl.BlockSpec(memory_space=pltpu.SMEM)


def fixed(shape):
    return pl.BlockSpec(shape, lambda step: (0,) * len(shape))


def f32(shape):
    return jax.ShapeDtypeStruct(shape, jnp.float32)


def bf16(shape):
    return jax.ShapeDtypeStruct(shape, jnp.bfloat16)


def place():
    context = lax.axis_index("context")
    return context >> 1, context & 1, lax.axis_index("heads")


def hbm():
    return pl.BlockSpec(memory_space=pltpu.HBM)


def pack_kernel(query_ref, out_ref):
    rows, heads, width = query_ref.shape
    total = rows * heads
    columns = width // lanes
    stacked = jnp.swapaxes(query_ref[...].astype(jnp.float32), 0, 1).reshape(total, width)
    for i in range(columns):
        out_ref[i * total : (i + 1) * total, :] = stacked[:, i * lanes : (i + 1) * lanes].astype(jnp.bfloat16)
    rest = stacked[:, columns * lanes :]
    out_ref[columns * total :, :] = jnp.concatenate([rest[: total // 2], rest[total // 2 :]], axis=1).astype(
        jnp.bfloat16
    )


def packed_queries(queries):
    rows, heads, width = queries.shape
    return local_call(
        pack_kernel,
        bf16((rows * heads * width // lanes, lanes)),
        "pack_queries",
        in_specs=[whole()],
        out_specs=whole(),
        flops=2 * queries.size * queries.size // width,
    )(queries)


def pick_kernel(own_ref, got_ref, out_ref):
    plane, _, _ = place()
    inner = (plane == 1) | (plane == 2)

    @pl.when(inner)
    def _():
        out_ref[...] = got_ref[...]

    @pl.when(jnp.logical_not(inner))
    def _():
        out_ref[...] = own_ref[...]


def picked(own, got):
    return local_call(
        pick_kernel, bf16(own.shape), "pick_queries", in_specs=[whole()] * 2, out_specs=whole(), moved=4 * own.size
    )(own, got)


def unpack(packed, wide_ref, slot, total, width):
    columns = width // lanes
    half = total // 2
    for i in range(columns):
        wide_ref[slot * total : (slot + 1) * total, i * lanes : (i + 1) * lanes] = packed[
            i * total : (i + 1) * total, :
        ]
    rest = packed[columns * total :, :]
    wide_ref[slot * total : slot * total + half, columns * lanes :] = rest[:, : lanes // 2]
    wide_ref[slot * total + half : (slot + 1) * total, columns * lanes :] = rest[:, lanes // 2 :]


def widened(column, width):
    return jnp.concatenate([column] * (width // lanes), axis=1)


def shard_mass(length_ref, wide_ref, slot, lse, key_ref, context, rows, heads, first, tile):
    total = rows * heads
    scores = jnp.dot(
        wide_ref[slot * total : (slot + 1) * total, :],
        key_ref[:, first : first + tile],
        preferred_element_type=jnp.float32,
    )
    summed = jnp.zeros((rows, tile), jnp.float32)
    for h in range(heads):
        summed = summed + jnp.exp2(scores[h * rows : (h + 1) * rows] * (main_scale * log2_e) - lse[:, h : h + 1])
    visible = visible_tile(length_ref, context, rows, first, tile, key_ref.shape[1])
    return jnp.where(visible, summed, 0.0)


def rows_at(ref, index, rows):
    return ref[pl.ds(pl.multiple_of(index * rows, rows), rows), :]


def visible_tile(length_ref, block, rows, first, width, key_count):
    positions = lax.axis_index("context") * key_count + first + lax.broadcasted_iota(jnp.int32, (rows, width), 1)
    return positions < widened(rows_at(length_ref, block, rows), width)


def mass_kernel(flip, places, rows, heads, length_ref, *refs):
    count = len(places)
    packs = refs[:count]
    lse_ref, key_ref, out_ref, wide_ref = refs[len(packs) :]
    width, key_count = key_ref.shape
    tile = math.gcd(key_count, 512)
    total = rows * heads
    own_plane, own_core, _ = place()
    plane = own_plane ^ flip
    for n, other in enumerate(places):
        unpack(packs[n][...], wide_ref, n, total, width)
        core = own_core ^ other
        context = 2 * plane + core
        lse = rows_at(lse_ref, context, rows)
        for first in range(0, key_count, tile):
            mass = shard_mass(length_ref, wide_ref, n, lse, key_ref, context, rows, heads, first, tile)
            if count == 1:
                out_ref[:, first : first + tile] = mass
            else:
                out_ref[pl.ds(pl.multiple_of(core * rows, rows), rows), first : first + tile] = mass


def chunk_mass(lengths, packs, lse, keys, flip, places, rows, heads, name):
    width, key_count = keys.shape
    count = len(places)
    total = rows * heads
    return local_call(
        functools.partial(mass_kernel, flip, places, rows, heads),
        f32((count * rows, key_count)),
        name,
        in_specs=[whole()] * (len(packs) + 3),
        out_specs=whole(),
        scratch=[pltpu.VMEM((count * total, width), jnp.bfloat16)],
        flops=2 * count * total * key_count * width,
        moved=2 * keys.size,
    )(lengths, *packs, lse, keys)


def share_kernel(rows, heads, length_ref, pack_ref, lse_ref, own_ref, near_ref, far_ref, half_ref, key_ref, *refs):
    outs = refs[:-2]
    wide_ref, chunks_ref = refs[-2:]
    width, key_count = key_ref.shape
    tile = math.gcd(key_count, 512)
    total = rows * heads
    unpack(pack_ref[...], wide_ref, 0, total, width)
    plane, core, group = place()
    other = 1 - core
    context = 2 * (plane ^ 2) + other
    lse = rows_at(lse_ref, context, rows)
    chunks_ref[0] = own_ref[...]
    chunks_ref[1] = near_ref[...]
    chunks_ref[3] = far_ref[...]
    chunks_ref[2, pl.ds(pl.multiple_of(core * rows, rows), rows), :] = half_ref[...]
    for first in range(0, key_count, tile):
        chunks_ref[2, pl.ds(pl.multiple_of(other * rows, rows), rows), first : first + tile] = shard_mass(
            length_ref, wide_ref, 0, lse, key_ref, context, rows, heads, first, tile
        )
    for e, out_ref in enumerate(outs):
        out_ref[...] = chunks_ref[plane ^ group ^ e].astype(out_ref.dtype)


def shared_mass(lengths, pack, lse, own, near, far, half, keys, rows, heads, partners):
    width, key_count = keys.shape
    total = rows * heads
    both = 2 * rows
    return local_call(
        functools.partial(share_kernel, rows, heads),
        [f32((both, key_count))] + [bf16((both, key_count))] * (partners - 1),
        "mass_and_share",
        in_specs=[whole()] * 8,
        out_specs=[whole()] * partners,
        scratch=[
            pltpu.VMEM((total, width), jnp.bfloat16),
            pltpu.VMEM((4, both, key_count), jnp.float32),
        ],
        flops=2 * total * key_count * width,
        moved=2 * keys.size,
    )(lengths, pack, lse, own, near, far, half, keys)


def logits_kernel(length_ref, query_ref, key_ref, weight_ref, logits_ref, masked_ref, stats_ref):
    rows, key_count = logits_ref.shape
    heads = query_ref.shape[0] // rows
    tile = math.gcd(key_count, 256)
    group = lax.axis_index("heads")
    best = jnp.full((rows, 1), masked_low, jnp.float32)
    weights = widened(weight_ref[...], tile)
    for first in range(0, key_count, tile):
        dots = lax.dot_general(
            query_ref[...], key_ref[first : first + tile, :], (((1,), (1,)), ((), ())),
            preferred_element_type=jnp.float32,
        )
        masked = jnp.where(dots > 0, weights, 0.0)
        masked_ref[:, first : first + tile] = masked
        logits = jnp.sum((dots * masked).reshape(rows, heads, tile), axis=1)
        logits_ref[:, first : first + tile] = logits
        visible = visible_tile(length_ref, group, rows, first, tile, key_count)
        best = jnp.maximum(best, jnp.max(jnp.where(visible, logits, masked_low), axis=1, keepdims=True))
    visible = visible_tile(length_ref, group, rows, 0, key_count, key_count)
    total = jnp.sum(jnp.where(visible, jnp.exp(logits_ref[...] - best), 0.0), axis=1, keepdims=True)
    column = lax.broadcasted_iota(jnp.int32, (rows, lanes), 1)
    stats_ref[...] = jnp.where(column == 0, best, total)


def index_logits(lengths, flat_query, index_key, weight_wide, rows):
    key_count = index_key.shape[0]
    flat = flat_query.shape[0]
    return local_call(
        logits_kernel,
        [f32((rows, key_count)), f32((flat, key_count)), f32((rows, lanes))],
        "index_logits",
        in_specs=[whole()] * 4,
        out_specs=[whole()] * 3,
        flops=2 * flat_query.size * key_count,
        moved=2 * index_key.size,
    )(lengths, flat_query, index_key, weight_wide)


def load_kernel(
    length_ref, lse_ref, weight_ref, query_hbm, key_hbm, latent_hbm,
    length_out, lse_out, weight_out, query_out, turned_out, key_out, latent_out, semaphores,
):
    copies = [
        pltpu.make_async_copy(source, target, semaphores.at[i])
        for i, (source, target) in enumerate(
            [(query_hbm, query_out), (key_hbm, key_out), (latent_hbm, latent_out)]
        )
    ]
    for copy in copies:
        copy.start()
    total = length_out.shape[0]
    spread = lax.broadcasted_iota(jnp.int32, (8, lanes), 0)
    for first in range(0, total, 8):
        column = jnp.zeros((8, lanes), jnp.int32)
        for i in range(8):
            column = jnp.where(spread == i, length_ref[first + i], column)
        length_out[first : first + 8, :] = column
    lse_out[...] = lse_ref[...].T * log2_e
    rows, heads = weight_ref.shape
    width = key_out.shape[1]
    weights = weight_ref[...].T * width ** (-0.5)
    for t in range(rows):
        weight_out[t * heads : (t + 1) * heads, :] = jnp.broadcast_to(weights[:, t : t + 1], (heads, lanes))
    copies[0].wait()
    turned_out[...] = query_out[...].reshape(rows * heads, width).astype(jnp.float32).T.astype(jnp.bfloat16)
    copies[1].wait()
    copies[2].wait()


def load_inputs(lengths, lse, weights, query, key, latent):
    rows, heads, width = query.shape
    flat = rows * heads
    return local_call(
        load_kernel,
        [
            jax.ShapeDtypeStruct((lengths.shape[0], lanes), jnp.int32),
            f32(lse.shape[::-1]),
            f32((flat, lanes)),
            bf16(query.shape),
            bf16((width, flat)),
            bf16(key.shape),
            bf16(latent.shape),
        ],
        "load_inputs",
        in_specs=[scalars(), whole(), whole(), hbm(), hbm(), hbm()],
        out_specs=[whole()] * 7,
        scratch=[pltpu.SemaphoreType.DMA((3,))],
        moved=4 * (key.size + latent.size),
    )(lengths, lse, weights, query, key, latent)


def join_kernel(stats_ref, own_ref, *refs):
    parts, (mass_ref, out_ref) = refs[:-2], refs[-2:]
    mass = own_ref[...]
    for part in parts:
        mass = mass + part[...].astype(jnp.float32)
    mass_ref[...] = mass
    column = lax.broadcasted_iota(jnp.int32, out_ref.shape, 1)
    out_ref[...] = jnp.where(column == 2, jnp.sum(mass, axis=1, keepdims=True), stats_ref[...])


def joined_mass(stats, own, parts):
    return local_call(
        join_kernel,
        [f32(own.shape), f32(stats.shape)],
        "join_mass",
        in_specs=[whole()] * (2 + len(parts)),
        out_specs=[whole()] * 2,
        moved=8 * own.size,
    )(stats, own, *parts)


def pair_stats_kernel(own_ref, got_ref, out_ref):
    own, got = own_ref[...], got_ref[...]
    top = jnp.maximum(own[:, 0:1], got[:, 0:1])
    shares = own[:, 1:2] * jnp.exp(own[:, 0:1] - top) + got[:, 1:2] * jnp.exp(got[:, 0:1] - top)
    column = lax.broadcasted_iota(jnp.int32, out_ref.shape, 1)
    out_ref[...] = jnp.where(column == 0, top, jnp.where(column == 1, shares, own + got))


def pair_stats(own, got):
    return local_call(
        pair_stats_kernel, f32(own.shape), "pair_stats", in_specs=[whole()] * 2, out_specs=whole(), moved=8 * own.size
    )(own, got)


def back_kernel(sources, length_ref, mass_ref, logits_ref, turned_ref, key_ref, masked_ref, *refs):
    stats = [ref[...] for ref in refs[:sources]]
    partners = len(refs) - sources - 4
    key_outs = refs[sources : sources + partners]
    keep_ref, send_ref, slope_ref, grad_ref = refs[sources + partners :]
    rows, key_count = mass_ref.shape
    width, flat = turned_ref.shape
    heads = flat // rows
    tile = math.gcd(key_count, 256)
    _, core, group = place()
    top = functools.reduce(jnp.maximum, [s[:, 0:1] for s in stats])
    shares = sum(s[:, 1:2] * jnp.exp(s[:, 0:1] - top) for s in stats)
    total = sum(s[:, 2:3] for s in stats)
    visible = visible_tile(length_ref, group, rows, 0, key_count, key_count)
    weights_exp = jnp.where(visible, jnp.exp(logits_ref[...] - top), 0.0)
    slope_ref[...] = loss_scale * (weights_exp / shares - mass_ref[...] / total)
    query_grad = jnp.zeros((flat, width), jnp.float32)
    for first in range(0, key_count, tile):
        keys = key_ref[first : first + tile, :]
        slopes = jnp.broadcast_to(slope_ref[:, first : first + tile][:, None, :], (rows, heads, tile))
        terms = (slopes.reshape(flat, tile) * masked_ref[:, first : first + tile]).astype(jnp.bfloat16)
        query_grad = query_grad + jnp.dot(terms, keys, preferred_element_type=jnp.float32)
        key_grad = jnp.dot(turned_ref[...], terms, preferred_element_type=jnp.float32)
        grad_ref[first : first + tile, :] = key_grad.T
    block = key_count // partners
    for e, out_ref in enumerate(key_outs):
        out_ref[...] = rows_at(grad_ref, group ^ e, block).astype(out_ref.dtype)
    planes = keep_ref.shape[0]
    part = heads // (2 * planes)
    split = query_grad.reshape(rows, planes, 2, part, width)
    first_core = core == 0
    for plane in range(planes):
        low, high = split[:, plane, 0], split[:, plane, 1]
        keep_ref[plane] = jnp.where(first_core, low, high).reshape(rows * part, width)
        send_ref[plane] = jnp.where(first_core, high, low).reshape(rows * part, width).astype(jnp.bfloat16)


def back_pass(lengths, mass, logits, turned, index_key, masked, stats, partners, planes):
    rows, key_count = mass.shape
    width, flat = turned.shape
    part = flat // (2 * planes)
    return local_call(
        functools.partial(back_kernel, len(stats)),
        [f32((key_count // partners, width))]
        + [bf16((key_count // partners, width))] * (partners - 1)
        + [f32((planes, part, width)), bf16((planes, part, width))],
        "index_back",
        in_specs=[whole()] * (6 + len(stats)),
        out_specs=[whole()] * (partners + 2),
        scratch=[pltpu.VMEM((rows, key_count), jnp.float32), pltpu.VMEM((key_count, width), jnp.float32)],
        flops=6 * flat * width * key_count,
        moved=8 * key_count * width,
    )(lengths, mass, logits, turned, index_key, masked, *stats)


def pair_kernel(keep_ref, got_ref, *outs):
    own_plane, _, _ = place()
    for e, out_ref in enumerate(outs):
        plane = own_plane ^ e
        out_ref[...] = (keep_ref[plane] + got_ref[plane].astype(jnp.float32)).astype(out_ref.dtype)


def pair_sums(keep, got):
    planes, part, width = keep.shape
    return local_call(
        pair_kernel,
        [f32((part, width))] + [bf16((part, width))] * (planes - 1),
        "pair_sums",
        in_specs=[whole(), whole()],
        out_specs=[whole()] * planes,
        moved=8 * keep.size,
    )(keep, got)


def last_kernel(key_parts, *refs):
    query_out, key_out = refs[-2:]
    key_refs, query_refs = refs[:key_parts], refs[key_parts:-2]
    key_out[...] = sum(ref[...].astype(jnp.float32) for ref in key_refs)
    query_out[...] = sum(ref[...].astype(jnp.float32) for ref in query_refs).reshape(query_out.shape)


def last_sums(key_parts, query_parts, query_shape):
    return local_call(
        functools.partial(last_kernel, len(key_parts)),
        [f32(query_shape), f32(key_parts[0].shape)],
        "last_sums",
        in_specs=[whole()] * (len(key_parts) + len(query_parts)),
        out_specs=[whole()] * 2,
        moved=8 * key_parts[0].size,
    )(*key_parts, *query_parts)


def after(array, *others):
    return lax.optimization_barrier((array, *others))[0]


def block_device(main_query, latent_keys, head_lse, lengths, index_query, index_key, index_weight):
    contexts = lax.axis_size("context")
    planes = contexts // 2
    partners = lax.axis_size("heads")
    context = lax.axis_index("context")
    rows, heads, _ = main_query.shape
    own_rows, index_heads, width = index_query.shape
    key_count = latent_keys.shape[0]
    flat = own_rows * index_heads

    def planes_move(array, pairs):
        return lax.ppermute(array, "context", [(2 * a + k, 2 * b + k) for a, b in pairs for k in (0, 1)])

    def context_flip(array, e):
        return lax.ppermute(array, "context", [(c, c ^ e) for c in range(contexts)])

    def heads_flip(array, e):
        return lax.ppermute(array, "heads", [(h, h ^ e) for h in range(partners)])

    def mass_of(packs, *rest):
        return chunk_mass(lengths, packs, lse, keys, *rest[:2], rows, heads, rest[2])

    pack = packed_queries(main_query)
    across = planes_move(pack, [(1, 2), (2, 1), (0, 3), (3, 0)])
    near = planes_move(pack, [(0, 1), (1, 0), (2, 3), (3, 2)])
    own_pair = context_flip(pack, 1)
    lengths, lse, weight_wide, query, turned, index_key, keys = load_inputs(
        lengths, head_lse.T, index_weight, index_query, index_key, after(latent_keys, pack).T
    )
    logits, masked, stats = index_logits(lengths, query.reshape(flat, width), index_key, weight_wide, own_rows)
    own_mass = mass_of([pack, after(own_pair, stats)], 0, (0, 1), "mass_own")
    across = after(across, own_mass)
    far = planes_move(picked(pack, across), [(0, 2), (3, 1), (1, 0), (2, 3)])
    near = after(near, own_mass)
    near_mass = mass_of([near, context_flip(near, 1)], 1, (0, 1), "mass_near")
    across_mass = mass_of([across, context_flip(across, 1)], 3, (0, 1), "mass_across")
    far = after(far, near_mass, across_mass)
    far_pair = context_flip(far, 1)
    far_mass = mass_of([far], 2, (0,), "mass_far")
    shared = shared_mass(
        lengths, far_pair, lse, own_mass, near_mass, across_mass, far_mass, keys, rows, heads, partners
    )
    mass, stats = joined_mass(stats, shared[0], [heads_flip(shared[e], e) for e in range(1, partners)])
    stats = pair_stats(stats, context_flip(stats, 1))
    every = [stats] + [context_flip(stats, 2 * e) for e in range(1, planes)]
    *key_grads, keep, send = back_pass(
        lengths, mass, logits, turned, index_key, masked, every, partners, planes
    )
    got = context_flip(send, 1)
    key_parts = [key_grads[0]] + [heads_flip(key_grads[e], e) for e in range(1, partners)]
    sums = pair_sums(keep, got)
    query_parts = [sums[0]] + [context_flip(sums[e], 2 * e) for e in range(1, planes)]
    return last_sums(key_parts, query_parts, (own_rows, index_heads // contexts, width))


def fits(mesh):
    return mesh.shape["context"] == 8 and mesh.shape["heads"] == 4


def solution(mesh):
    placed = (
        P("context", "heads", None),
        P("context", None),
        P(None, "heads"),
        P(),
        P("heads", None, None),
        P("context", None),
        P("heads", None),
    )
    return jax.shard_map(
        block_device if fits(mesh) else general_on_device,
        mesh=mesh,
        in_specs=placed,
        out_specs=(P("heads", "context", None), P(("context", "heads"), None)),
        check_vma=False,
    )
```

time: 84.9 us -> 66.9 us (0.79)
  starting transfers between devices: 42.4 us -> 23.2 us
  waiting for transfers between devices: 7.69 us -> 21.6 us
  Pallas kernels: 24.9 us -> 14.2 us
  local copies, waits for them, and re-layouts: 8.51 us -> 6.69 us
    ppermute x4 -> x3, starting transfers between devices: 21.2 us -> 7.12 us  [planes_move(): lax.ppermute(array, 'context', [(2 * a + k, 2 * b + k) for a, b in pairs...]
    ppermute x4 -> x3, waiting for transfers between devices: 0.45 us -> 6.91 us  [planes_move(): lax.ppermute(array, 'context', [(2 * a + k, 2 * b + k) for a, b in pairs...]
    pallas_call x5 -> x8, Pallas kernels: 15.8 us -> 9.84 us  [the longest x4 6.6 us: chunk_mass(): local_call(functools.partial(mass_kernel, flip, places, rows, heads), f32...]
    ppermute x16 -> x12, starting transfers between devices: 14.1 us -> 9.02 us  [context_flip(): return lax.ppermute(array, 'context', [(c, c ^ e) for c in range(contexts)])]
    ppermute x6, waiting for transfers between devices: 1.44 us -> 6.11 us  [heads_flip(): return lax.ppermute(array, 'heads', [(h, h ^ e) for h in range(partners)])]
    ppermute x16 -> x12, waiting for transfers between devices: 5.8 us -> 8.61 us  [context_flip(): return lax.ppermute(array, 'context', [(c, c ^ e) for c in range(contexts)])]
    pallas_call x1, Pallas kernels: 4.21 us -> 2.22 us  [back_pass(): local_call(functools.partial(back_kernel, len(stats)), [f32((key_count //...]
    mul x3 -> x0, local copies, waits for them, and re-layouts: 1.85 us -> none  [the longest x2 1.77 us: block_device(): lse_wide * log2_e]
  transfers between devices with their start and end apart: 26 -> 21, of which waited for: 7 -> 12; matrix products, arithmetic and copies ran while one was open for 8% -> 0% of each run, Pallas kernels for 19% -> 15%
where the time goes in v2:
time: 66.9 us; the launch traced here: 66.5 us
  starting transfers between devices  23.2 us (35%)
  waiting for transfers between devices  21.6 us (32%)
  Pallas kernels  14.2 us (21%)
  local copies, waits for them, and re-layouts  6.69 us (10%)
  between operations  0.77 us (1%)
    ppermute x12, starting transfers between devices, context_flip(): return lax.ppermute(array, 'context', [(c, c ^ e) for c in range(contexts)])  9.02 us
    ppermute x12, waiting for transfers between devices, context_flip(): return lax.ppermute(array, 'context', [(c, c ^ e) for c in range(contexts)])  8.61 us
    ppermute x3, starting transfers between devices, planes_move(): lax.ppermute(array, 'context', [(2 * a + k, 2 * b + k) for a, b in pairs...  7.12 us
    ppermute x6, starting transfers between devices, heads_flip(): return lax.ppermute(array, 'heads', [(h, h ^ e) for h in range(partners)])  7.11 us
    ppermute x3, waiting for transfers between devices, planes_move(): lax.ppermute(array, 'context', [(2 * a + k, 2 * b + k) for a, b in pairs...  6.91 us
    unnamed x14, local copies, waits for them, and re-layouts  6.69 us
    pallas_call x4, Pallas kernels, chunk_mass(): local_call(functools.partial(mass_kernel, flip, places, rows, heads), f32...  6.6 us
    ppermute x6, waiting for transfers between devices, heads_flip(): return lax.ppermute(array, 'heads', [(h, h ^ e) for h in range(partners)])  6.11 us
  transfers between devices with their start and end apart: 21, of which 12 were waited for; matrix products, arithmetic and copies ran while one was open for 0% of the time, Pallas kernels for 15%

profile of v2, /device:TPU:0, one launch (start us, length us, event | category | flops | bytes accessed | tf_op | source)
XLA Modules:
  0.0 66.5 jit_solution(6422376910322345460)
XLA Ops:
  0.6 1.0 %copy-done.2 = bf16[8,32,576]{2,1,0:T(8,128)(2,1)S(1)} copy-done((bf16[8,32,576]{2,1,0:T(8,128)(2,1)S(1)}, bf16[8,32,576]{2,1,0:T(8,128)(2,1)}, u32[]{:S(2)}) %copy-start.2) | copy-done | bytes 294936
  2.3 2.6 %collective-permute-start.3 = (bf16[1152,128]{1,0:T(8,128)(2,1)S(1)}, bf16[1152,128]{1,0:T(8,128)(2,1)S(1)}, u32[]{:S(2)}, u32[]{:S(2)}) collective-permute-start(bf16[1152,128]{1,0:T(8,128)(2,1)S(1)} %pack_queries.1.refs_0_.own_ref), channel_id=1, source_target_pairs={{0,8},{4,12},{8,0},{12,4},{16,24},{20,28},{24,16},{28,20},{1,9},{5... | collective-permute-start | bytes 884744 | tf_op jit(solution)/shard_map/ppermute | solution.py:580
  4.9 2.5 %collective-permute-start = (bf16[1152,128]{1,0:T(8,128)(2,1)S(1)}, bf16[1152,128]{1,0:T(8,128)(2,1)S(1)}, u32[]{:S(2)}, u32[]{:S(2)}) collective-permute-start(bf16[1152,128]{1,0:T(8,128)(2,1)S(1)} %pack_queries.1.refs_0_.own_ref), channel_id=1, source_target_pairs={{8,16},{12,20},{16,8},{20,12},{0,24},{4,28},{24,0},{28,4},{9,17},{... | collective-permute-start | bytes 884744 | tf_op jit(solution)/shard_map/ppermute | solution.py:580
  7.4 1.7 %copy-done = bf16[2048,576]{0,1:T(8,128)(2,1)S(1)} copy-done((bf16[2048,576]{0,1:T(8,128)(2,1)S(1)}, bf16[2048,576]{0,1:T(8,128)(2,1)}, u32[]{:S(2)}) %copy-start) | copy-done | bytes 2359320
  9.1 1.0 %copy-done.1 = bf16[2048,128]{1,0:T(8,128)(2,1)S(1)} copy-done((bf16[2048,128]{1,0:T(8,128)(2,1)S(1)}, bf16[2048,128]{1,0:T(8,128)(2,1)}, u32[]{:S(2)}) %copy-start.1) | copy-done | bytes 524312
  10.1 0.9 %copy-done.3 = bf16[16,64,128]{2,1,0:T(8,128)(2,1)S(1)} copy-done((bf16[16,64,128]{2,1,0:T(8,128)(2,1)S(1)}, bf16[16,64,128]{2,1,0:T(8,128)(2,1)}, u32[]{:S(2)}) %copy-start.3) | copy-done | bytes 262168
  13.1 1.2 %load_inputs.1 = (s32[64,128]{1,0:T(8,128)S(1)}, f32[64,32]{1,0:T(8,128)S(1)}, f32[1024,128]{1,0:T(8,128)S(1)}, bf16[16,64,128]{2,1,0:T(8,128)(2,1)S(1)}, bf16[1...) custom-call(s32[64]{0:T(128)S(1)} %copy-done.6, f32[32,64]{1,0:T(8,128)S(1)} %bitcast.4, ...), custom_call_target="tpu_custom_call" | custom-call | bytes 5767168 | tf_op jit(solution)/shard_map/load_inputs/pallas_call | solution.py:419
  14.4 1.8 %index_logits.1 = (f32[16,2048]{1,0:T(8,128)S(1)}, f32[1024,2048]{1,0:T(8,128)S(1)}, f32[16,128]{1,0:T(8,128)S(1)}) custom-call(s32[64,128]{1,0:T(8,128)S(1)} %get-tuple-element.34.length_ref, bf16[1024,128]{1,0:T(8,128)(2,1)S(1)} %bitcast.5, bf16[2048,128]{1,0:T(8,128)(2,1)S(1)} %get-tuple-element.36.key_ref, f32[1024,128]{1,0:T(8,128)S(1)} %get-tuple-element.37.weight_ref), custom_call_target="tpu_custom_call" | custom-call | flops 536870912 | bytes 524288 | tf_op jit(solution)/shard_map/index_logits/pallas_call | solution.py:374
  16.2 1.9 %mass_own.1.own_ref = f32[16,2048]{1,0:T(8,128)S(1)} custom-call(s32[64,128]{1,0:T(8,128)S(1)} %get-tuple-element.34.length_ref, bf16[1152,128]{1,0:T(8,128)(2,1)S(1)} %pack_queries.1.refs_0_.own_ref, bf16[1152,128]{1,0:T(8,128)(2,1)S(1)} %collective-permute-done.1.refs_1_, f32[64,32]{1,0:T(8,128)S(1)} %get-tuple-element.40.refs_2_.refs_1_.lse_ref, ...), custom_call_target="tpu_custom_call" | custom-call | flops 1207959552 | bytes 2359296 | tf_op jit(solution)/shard_map/mass_own/pallas_call | solution.py:293
  18.2 3.0 %collective-permute-done.got_ref.refs_0_ = bf16[1152,128]{1,0:T(8,128)(2,1)S(1)} collective-permute-done((bf16[1152,128]{1,0:T(8,128)(2,1)S(1)}, bf16[1152,128]{1,0:T(8,128)(2,1)S(1)}, u32[]{:S(2)}, u32[]{:S(2)}) %collective-permute-start) | collective-permute-done | bytes 294944 | tf_op jit(solution)/shard_map/ppermute | solution.py:580
  21.2 2.0 %collective-permute-start.2 = (bf16[1152,128]{1,0:T(8,128)(2,1)S(1)}, bf16[1152,128]{1,0:T(8,128)(2,1)S(1)}, u32[]{:S(2)}, u32[]{:S(2)}) collective-permute-start(bf16[1152,128]{1,0:T(8,128)(2,1)S(1)} %pick_queries.1), channel_id=1, source_target_pairs={{0,16},{4,20},{24,8},{28,12},{8,0},{12,4},{16,24},{20,28},{1,17},{... | collective-permute-start | bytes 884744 | tf_op jit(solution)/shard_map/ppermute | solution.py:580
  23.2 1.9 %mass_near.1.near_ref = f32[16,2048]{1,0:T(8,128)S(1)} custom-call(s32[64,128]{1,0:T(8,128)S(1)} %get-tuple-element.34.length_ref, bf16[1152,128]{1,0:T(8,128)(2,1)S(1)} %collective-permute-done.3.refs_0_, bf16[1152,128]{1,0:T(8,128)(2,1)S(1)} %collective-permute-done.4.refs_1_, f32[64,32]{1,0:T(8,128)S(1)} %get-tuple-element.40.refs_2_.refs_1_.lse_ref, ...), custom_call_target="tpu_custom_call" | custom-call | flops 1207959552 | bytes 2359296 | tf_op jit(solution)/shard_map/mass_near/pallas_call | solution.py:293
  25.1 1.9 %mass_across.1.far_ref = f32[16,2048]{1,0:T(8,128)S(1)} custom-call(s32[64,128]{1,0:T(8,128)S(1)} %get-tuple-element.34.length_ref, bf16[1152,128]{1,0:T(8,128)(2,1)S(1)} %collective-permute-done.got_ref.refs_0_, bf16[1152,128]{1,0:T(8,128)(2,1)S(1)} %collective-permute-done.5.refs_1_, f32[64,32]{1,0:T(8,128)S(1)} %get-tuple-element.40.refs_2_.refs_1_.lse_ref, ...), custom_call_target="tpu_custom_call" | custom-call | flops 1207959552 | bytes 2359296 | tf_op jit(solution)/shard_map/mass_across/pallas_call | solution.py:293
  26.9 3.9 %collective-permute-done.2.refs_0_ = bf16[1152,128]{1,0:T(8,128)(2,1)S(1)} collective-permute-done((bf16[1152,128]{1,0:T(8,128)(2,1)S(1)}, bf16[1152,128]{1,0:T(8,128)(2,1)S(1)}, u32[]{:S(2)}, u32[]{:S(2)}) %collective-permute-start.2) | collective-permute-done | bytes 294944 | tf_op jit(solution)/shard_map/ppermute | solution.py:580
  30.9 1.0 %mass_far.1.half_ref = f32[8,2048]{1,0:T(8,128)S(1)} custom-call(s32[64,128]{1,0:T(8,128)S(1)} %get-tuple-element.34.length_ref, bf16[1152,128]{1,0:T(8,128)(2,1)S(1)} %collective-permute-done.2.refs_0_, f32[64,32]{1,0:T(8,128)S(1)} %get-tuple-element.40.refs_2_.refs_1_.lse_ref, bf16[576,2048]{1,0:T(8,128)(2,1)S(1)} %get-tuple-element.41.refs_3_.refs_2_.key_ref), custom_call_target="tpu_custom_call" | custom-call | flops 603979776 | bytes 2359296 | tf_op jit(solution)/shard_map/mass_far/pallas_call | solution.py:293
  32.4 1.1 %mass_and_share.1 = (f32[16,2048]{1,0:T(8,128)S(1)}, bf16[16,2048]{1,0:T(8,128)(2,1)S(1)}, bf16[16,2048]{1,0:T(8,128)(2,1)S(1)}, bf16[16,2048]{1,0:T(8,128)(2,1)S(1)}) custom-call(s32[64,128]{1,0:T(8,128)S(1)} %get-tuple-element.34.length_ref, bf16[1152,128]{1,0:T(8,128)(2,1)S(1)} %collective-permute-done.6.pack_ref, ...), custom_call_target="tpu_custom_call" | custom-call | flops 603979776 | bytes 2359296 | tf_op jit(solution)/shard_map/mass_and_share/pallas_call | solution.py:332
  33.5 1.6 %collective-permute-start.7 = (bf16[16,2048]{1,0:T(8,128)(2,1)S(1)}, bf16[16,2048]{1,0:T(8,128)(2,1)S(1)}, u32[]{:S(2)}, u32[]{:S(2)}) collective-permute-start(bf16[16,2048]{1,0:T(8,128)(2,1)S(1)} %get-tuple-element.46), channel_id=1, source_target_pairs={{0,1},{1,0},{2,3},{3,2},{4,5},{5,4},{6,7},{7,6},{8,9},{9,8},{10,11... | collective-permute-start | bytes 196616 | tf_op jit(solution)/shard_map/ppermute | solution.py:586
  35.1 1.5 %collective-permute-start.8 = (bf16[16,2048]{1,0:T(8,128)(2,1)S(1)}, bf16[16,2048]{1,0:T(8,128)(2,1)S(1)}, u32[]{:S(2)}, u32[]{:S(2)}) collective-permute-start(bf16[16,2048]{1,0:T(8,128)(2,1)S(1)} %get-tuple-element.47), channel_id=1, source_target_pairs={{0,2},{1,3},{2,0},{3,1},{4,6},{5,7},{6,4},{7,5},{8,10},{9,11},{10,... | collective-permute-start | bytes 196616 | tf_op jit(solution)/shard_map/ppermute | solution.py:586
  37.8 1.5 %collective-permute-done.8.refs_1_ = bf16[16,2048]{1,0:T(8,128)(2,1)S(1)} collective-permute-done((bf16[16,2048]{1,0:T(8,128)(2,1)S(1)}, bf16[16,2048]{1,0:T(8,128)(2,1)S(1)}, u32[]{:S(2)}, u32[]{:S(2)}) %collective-permute-start.8) | collective-permute-done | bytes 65568 | tf_op jit(solution)/shard_map/ppermute | solution.py:586
  39.3 2.4 %collective-permute-done.9.refs_2_ = bf16[16,2048]{1,0:T(8,128)(2,1)S(1)} collective-permute-done((bf16[16,2048]{1,0:T(8,128)(2,1)S(1)}, bf16[16,2048]{1,0:T(8,128)(2,1)S(1)}, u32[]{:S(2)}, u32[]{:S(2)}) %collective-permute-start.9) | collective-permute-done | bytes 65568 | tf_op jit(solution)/shard_map/ppermute | solution.py:586
  41.9 1.2 %collective-permute-done.10.got_ref = f32[16,128]{1,0:T(8,128)S(1)} collective-permute-done((f32[16,128]{1,0:T(8,128)S(1)}, f32[16,128]{1,0:T(8,128)S(1)}, u32[]{:S(2)}, u32[]{:S(2)}) %collective-permute-start.10) | collective-permute-done | bytes 8224 | tf_op jit(solution)/shard_map/ppermute | solution.py:583
  43.2 1.5 %collective-permute-start.11 = (f32[16,128]{1,0:T(8,128)S(1)}, f32[16,128]{1,0:T(8,128)S(1)}, u32[]{:S(2)}, u32[]{:S(2)}) collective-permute-start(f32[16,128]{1,0:T(8,128)S(1)} %pair_stats.1.refs_0_), channel_id=1, source_target_pairs={{0,8},{4,12},{8,0},{12,4},{16,24},{20,28},{24,16},{28,20},{1,9},{5... | collective-permute-start | bytes 24584 | tf_op jit(solution)/shard_map/ppermute | solution.py:583
  44.7 1.3 %collective-permute-start.12 = (f32[16,128]{1,0:T(8,128)S(1)}, f32[16,128]{1,0:T(8,128)S(1)}, u32[]{:S(2)}, u32[]{:S(2)}) collective-permute-start(f32[16,128]{1,0:T(8,128)S(1)} %pair_stats.1.refs_0_), channel_id=1, source_target_pairs={{0,16},{4,20},{8,24},{12,28},{16,0},{20,4},{24,8},{28,12},{1,17},{... | collective-permute-start | bytes 24584 | tf_op jit(solution)/shard_map/ppermute | solution.py:583
  45.9 1.7 %collective-permute-start.13 = (f32[16,128]{1,0:T(8,128)S(1)}, f32[16,128]{1,0:T(8,128)S(1)}, u32[]{:S(2)}, u32[]{:S(2)}) collective-permute-start(f32[16,128]{1,0:T(8,128)S(1)} %pair_stats.1.refs_0_), channel_id=1, source_target_pairs={{0,24},{4,28},{8,16},{12,20},{16,8},{20,12},{24,0},{28,4},{1,25},{... | collective-permute-start | bytes 24584 | tf_op jit(solution)/shard_map/ppermute | solution.py:583
  47.6 1.7 %collective-permute-done.12.refs_2_ = f32[16,128]{1,0:T(8,128)S(1)} collective-permute-done((f32[16,128]{1,0:T(8,128)S(1)}, f32[16,128]{1,0:T(8,128)S(1)}, u32[]{:S(2)}, u32[]{:S(2)}) %collective-permute-start.12) | collective-permute-done | bytes 8224 | tf_op jit(solution)/shard_map/ppermute | solution.py:583
  49.3 2.1 %collective-permute-done.13.refs_3_ = f32[16,128]{1,0:T(8,128)S(1)} collective-permute-done((f32[16,128]{1,0:T(8,128)S(1)}, f32[16,128]{1,0:T(8,128)S(1)}, u32[]{:S(2)}, u32[]{:S(2)}) %collective-permute-start.13) | collective-permute-done | bytes 8224 | tf_op jit(solution)/shard_map/ppermute | solution.py:583
  51.4 2.2 %index_back.1 = (f32[512,128]{1,0:T(8,128)S(1)}, bf16[512,128]{1,0:T(8,128)(2,1)S(1)}, bf16[512,128]{1,0:T(8,128)(2,1)S(1)}, bf16[512,128]{1,0:T(8,128)(2,1)S(1)...) custom-call(s32[64,128]{1,0:T(8,128)S(1)} %get-tuple-element.34.length_ref, ...), custom_call_target="tpu_custom_call" | custom-call | flops 1610612736 | bytes 2097152 | tf_op jit(solution)/shard_map/index_back/pallas_call | solution.py:514
  54.8 2.4 %collective-permute-start.16 = (bf16[512,128]{1,0:T(8,128)(2,1)S(1)}, bf16[512,128]{1,0:T(8,128)(2,1)S(1)}, u32[]{:S(2)}, u32[]{:S(2)}) collective-permute-start(bf16[512,128]{1,0:T(8,128)(2,1)S(1)} %get-tuple-element.57), channel_id=1, source_target_pairs={{0,3},{1,2},{2,1},{3,0},{4,7},{5,6},{6,5},{7,4},{8,11},{9,10},{10,... | collective-permute-start | bytes 393224 | tf_op jit(solution)/shard_map/ppermute | solution.py:586
  57.5 2.1 %collective-permute-start.19 = (bf16[128,128]{1,0:T(8,128)(2,1)S(1)}, bf16[128,128]{1,0:T(8,128)(2,1)S(1)}, u32[]{:S(2)}, u32[]{:S(2)}) collective-permute-start(bf16[128,128]{1,0:T(8,128)(2,1)S(1)} %get-tuple-element.62), channel_id=1, source_target_pairs={{0,16},{4,20},{8,24},{12,28},{16,0},{20,4},{24,8},{28,12},{1,17},{... | collective-permute-start | bytes 98312 | tf_op jit(solution)/shard_map/ppermute | solution.py:583
  60.0 1.7 %collective-permute-start.20 = (bf16[128,128]{1,0:T(8,128)(2,1)S(1)}, bf16[128,128]{1,0:T(8,128)(2,1)S(1)}, u32[]{:S(2)}, u32[]{:S(2)}) collective-permute-start(bf16[128,128]{1,0:T(8,128)(2,1)S(1)} %get-tuple-element.63), channel_id=1, source_target_pairs={{0,24},{4,28},{8,16},{12,20},{16,8},{20,12},{24,0},{28,4},{1,25},{... | collective-permute-start | bytes 98312 | tf_op jit(solution)/shard_map/ppermute | solution.py:583
  61.7 0.9 %collective-permute-done.15.refs_2_ = bf16[512,128]{1,0:T(8,128)(2,1)S(1)} collective-permute-done((bf16[512,128]{1,0:T(8,128)(2,1)S(1)}, bf16[512,128]{1,0:T(8,128)(2,1)S(1)}, u32[]{:S(2)}, u32[]{:S(2)}) %collective-permute-start.15) | collective-permute-done | bytes 131104 | tf_op jit(solution)/shard_map/ppermute | solution.py:586
  62.7 3.1 %collective-permute-done.20.refs_7_ = bf16[128,128]{1,0:T(8,128)(2,1)S(1)} collective-permute-done((bf16[128,128]{1,0:T(8,128)(2,1)S(1)}, bf16[128,128]{1,0:T(8,128)(2,1)S(1)}, u32[]{:S(2)}, u32[]{:S(2)}) %collective-permute-start.20) | collective-permute-done | bytes 32800 | tf_op jit(solution)/shard_map/ppermute | solution.py:583
  (38 shorter events, 7.7 us)
Async XLA Ops:
  0.6 1.0 %copy-start.2 = (bf16[8,32,576]{2,1,0:T(8,128)(2,1)S(1)}, bf16[8,32,576]{2,1,0:T(8,128)(2,1)}, u32[]{:S(2)}) copy-start(bf16[8,32,576]{2,1,0:T(8,128)(2,1)} %query_ref.1) | copy-start | bytes 884740
  1.8 14.5 %collective-permute-start.1 = (bf16[1152,128]{1,0:T(8,128)(2,1)S(1)}, bf16[1152,128]{1,0:T(8,128)(2,1)S(1)}, u32[]{:S(2)}, u32[]{:S(2)}) collective-permute-start(bf16[1152,128]{1,0:T(8,128)(2,1)S(1)} %pack_queries.1.refs_0_.own_ref), channel_id=1, source_target_pairs={{0,4},{4,0},{8,12},{12,8},{16,20},{20,16},{24,28},{28,24},{1,5},{5... | collective-permute-start | bytes 884744 | tf_op jit(solution)/shard_map/ppermute | solution.py:583
  2.3 15.8 %collective-permute-start.3 = (bf16[1152,128]{1,0:T(8,128)(2,1)S(1)}, bf16[1152,128]{1,0:T(8,128)(2,1)S(1)}, u32[]{:S(2)}, u32[]{:S(2)}) collective-permute-start(bf16[1152,128]{1,0:T(8,128)(2,1)S(1)} %pack_queries.1.refs_0_.own_ref), channel_id=1, source_target_pairs={{0,8},{4,12},{8,0},{12,4},{16,24},{20,28},{24,16},{28,20},{1,9},{5... | collective-permute-start | bytes 884744 | tf_op jit(solution)/shard_map/ppermute | solution.py:580
  4.9 16.2 %collective-permute-start = (bf16[1152,128]{1,0:T(8,128)(2,1)S(1)}, bf16[1152,128]{1,0:T(8,128)(2,1)S(1)}, u32[]{:S(2)}, u32[]{:S(2)}) collective-permute-start(bf16[1152,128]{1,0:T(8,128)(2,1)S(1)} %pack_queries.1.refs_0_.own_ref), channel_id=1, source_target_pairs={{8,16},{12,20},{16,8},{20,12},{0,24},{4,28},{24,0},{28,4},{9,17},{... | collective-permute-start | bytes 884744 | tf_op jit(solution)/shard_map/ppermute | solution.py:580
  7.4 1.7 %copy-start = (bf16[2048,576]{0,1:T(8,128)(2,1)S(1)}, bf16[2048,576]{0,1:T(8,128)(2,1)}, u32[]{:S(2)}) copy-start(bf16[2048,576]{0,1:T(8,128)(2,1)} %param.8) | copy-start | bytes 7077892
  9.1 1.0 %copy-start.1 = (bf16[2048,128]{1,0:T(8,128)(2,1)S(1)}, bf16[2048,128]{1,0:T(8,128)(2,1)}, u32[]{:S(2)}) copy-start(bf16[2048,128]{1,0:T(8,128)(2,1)} %key_hbm.1) | copy-start | bytes 1572868
  10.1 0.9 %copy-start.3 = (bf16[16,64,128]{2,1,0:T(8,128)(2,1)S(1)}, bf16[16,64,128]{2,1,0:T(8,128)(2,1)}, u32[]{:S(2)}) copy-start(bf16[16,64,128]{2,1,0:T(8,128)(2,1)} %query_hbm.1) | copy-start | bytes 786436
  11.1 0.7 %copy-start.4 = (f32[64,32]{0,1:T(8,128)S(1)}, f32[64,32]{0,1:T(8,128)}, u32[]{:S(2)}) copy-start(f32[64,32]{0,1:T(8,128)} %param.9) | copy-start | bytes 24580
  11.8 0.7 %copy-start.5 = (f32[16,64]{1,0:T(8,128)S(1)}, f32[16,64]{1,0:T(8,128)}, u32[]{:S(2)}) copy-start(f32[16,64]{1,0:T(8,128)} %weight_ref.1) | copy-start | bytes 12292
  12.5 0.7 copy-start.6
  18.1 5.1 %collective-permute-start.4 = (bf16[1152,128]{1,0:T(8,128)(2,1)S(1)}, bf16[1152,128]{1,0:T(8,128)(2,1)S(1)}, u32[]{:S(2)}, u32[]{:S(2)}) collective-permute-start(bf16[1152,128]{1,0:T(8,128)(2,1)S(1)} %collective-permute-done.3.refs_0_), channel_id=1, source_target_pairs={{0,4},{4,0},{8,12},{12,8},{16,20},{20,16},{24,28},{28,24},{1,5},{5... | collective-permute-start | bytes 884744 | tf_op jit(solution)/shard_map/ppermute | solution.py:583
  21.2 3.9 %collective-permute-start.5 = (bf16[1152,128]{1,0:T(8,128)(2,1)S(1)}, bf16[1152,128]{1,0:T(8,128)(2,1)S(1)}, u32[]{:S(2)}, u32[]{:S(2)}) collective-permute-start(bf16[1152,128]{1,0:T(8,128)(2,1)S(1)} %collective-permute-done.got_ref.refs_0_), channel_id=1, source_target_pairs={{0,4},{4,0},{8,12},{12,8},{16,20},{20,16},{24,28},{28,24},{1,5},{5... | collective-permute-start | bytes 884744 | tf_op jit(solution)/shard_map/ppermute | solution.py:583
  21.2 9.7 %collective-permute-start.2 = (bf16[1152,128]{1,0:T(8,128)(2,1)S(1)}, bf16[1152,128]{1,0:T(8,128)(2,1)S(1)}, u32[]{:S(2)}, u32[]{:S(2)}) collective-permute-start(bf16[1152,128]{1,0:T(8,128)(2,1)S(1)} %pick_queries.1), channel_id=1, source_target_pairs={{0,16},{4,20},{24,8},{28,12},{8,0},{12,4},{16,24},{20,28},{1,17},{... | collective-permute-start | bytes 884744 | tf_op jit(solution)/shard_map/ppermute | solution.py:580
  30.9 1.6 %collective-permute-start.6 = (bf16[1152,128]{1,0:T(8,128)(2,1)S(1)}, bf16[1152,128]{1,0:T(8,128)(2,1)S(1)}, u32[]{:S(2)}, u32[]{:S(2)}) collective-permute-start(bf16[1152,128]{1,0:T(8,128)(2,1)S(1)} %collective-permute-done.2.refs_0_), channel_id=1, source_target_pairs={{0,4},{4,0},{8,12},{12,8},{16,20},{20,16},{24,28},{28,24},{1,5},{5... | collective-permute-start | bytes 884744 | tf_op jit(solution)/shard_map/ppermute | solution.py:583
  33.5 4.3 %collective-permute-start.7 = (bf16[16,2048]{1,0:T(8,128)(2,1)S(1)}, bf16[16,2048]{1,0:T(8,128)(2,1)S(1)}, u32[]{:S(2)}, u32[]{:S(2)}) collective-permute-start(bf16[16,2048]{1,0:T(8,128)(2,1)S(1)} %get-tuple-element.46), channel_id=1, source_target_pairs={{0,1},{1,0},{2,3},{3,2},{4,5},{5,4},{6,7},{7,6},{8,9},{9,8},{10,11... | collective-permute-start | bytes 196616 | tf_op jit(solution)/shard_map/ppermute | solution.py:586
  35.1 4.3 %collective-permute-start.8 = (bf16[16,2048]{1,0:T(8,128)(2,1)S(1)}, bf16[16,2048]{1,0:T(8,128)(2,1)S(1)}, u32[]{:S(2)}, u32[]{:S(2)}) collective-permute-start(bf16[16,2048]{1,0:T(8,128)(2,1)S(1)} %get-tuple-element.47), channel_id=1, source_target_pairs={{0,2},{1,3},{2,0},{3,1},{4,6},{5,7},{6,4},{7,5},{8,10},{9,11},{10,... | collective-permute-start | bytes 196616 | tf_op jit(solution)/shard_map/ppermute | solution.py:586
  36.6 5.2 %collective-permute-start.9 = (bf16[16,2048]{1,0:T(8,128)(2,1)S(1)}, bf16[16,2048]{1,0:T(8,128)(2,1)S(1)}, u32[]{:S(2)}, u32[]{:S(2)}) collective-permute-start(bf16[16,2048]{1,0:T(8,128)(2,1)S(1)} %get-tuple-element.48), channel_id=1, source_target_pairs={{0,3},{1,2},{2,1},{3,0},{4,7},{5,6},{6,5},{7,4},{8,11},{9,10},{10,... | collective-permute-start | bytes 196616 | tf_op jit(solution)/shard_map/ppermute | solution.py:586
  41.9 1.2 %collective-permute-start.10 = (f32[16,128]{1,0:T(8,128)S(1)}, f32[16,128]{1,0:T(8,128)S(1)}, u32[]{:S(2)}, u32[]{:S(2)}) collective-permute-start(f32[16,128]{1,0:T(8,128)S(1)} %get-tuple-element.53.own_ref), channel_id=1, source_target_pairs={{0,4},{4,0},{8,12},{12,8},{16,20},{20,16},{24,28},{28,24},{1,5},{5... | collective-permute-start | bytes 24584 | tf_op jit(solution)/shard_map/ppermute | solution.py:583
  43.2 4.4 %collective-permute-start.11 = (f32[16,128]{1,0:T(8,128)S(1)}, f32[16,128]{1,0:T(8,128)S(1)}, u32[]{:S(2)}, u32[]{:S(2)}) collective-permute-start(f32[16,128]{1,0:T(8,128)S(1)} %pair_stats.1.refs_0_), channel_id=1, source_target_pairs={{0,8},{4,12},{8,0},{12,4},{16,24},{20,28},{24,16},{28,20},{1,9},{5... | collective-permute-start | bytes 24584 | tf_op jit(solution)/shard_map/ppermute | solution.py:583
  44.7 4.6 %collective-permute-start.12 = (f32[16,128]{1,0:T(8,128)S(1)}, f32[16,128]{1,0:T(8,128)S(1)}, u32[]{:S(2)}, u32[]{:S(2)}) collective-permute-start(f32[16,128]{1,0:T(8,128)S(1)} %pair_stats.1.refs_0_), channel_id=1, source_target_pairs={{0,16},{4,20},{8,24},{12,28},{16,0},{20,4},{24,8},{28,12},{1,17},{... | collective-permute-start | bytes 24584 | tf_op jit(solution)/shard_map/ppermute | solution.py:583
  45.9 5.4 %collective-permute-start.13 = (f32[16,128]{1,0:T(8,128)S(1)}, f32[16,128]{1,0:T(8,128)S(1)}, u32[]{:S(2)}, u32[]{:S(2)}) collective-permute-start(f32[16,128]{1,0:T(8,128)S(1)} %pair_stats.1.refs_0_), channel_id=1, source_target_pairs={{0,24},{4,28},{8,16},{12,20},{16,8},{20,12},{24,0},{28,4},{1,25},{... | collective-permute-start | bytes 24584 | tf_op jit(solution)/shard_map/ppermute | solution.py:583
  53.6 3.6 %collective-permute-start.17 = (bf16[4,128,128]{2,1,0:T(8,128)(2,1)S(1)}, bf16[4,128,128]{2,1,0:T(8,128)(2,1)S(1)}, u32[]{:S(2)}, u32[]{:S(2)}) collective-permute-start(bf16[4,128,128]{2,1,0:T(8,128)(2,1)S(1)} %get-tuple-element.59), channel_id=1, source_target_pairs={{0,4},{4,0},{8,12},{12,8},{16,20},{20,16},{24,28},{28,24},{1,5},{5... | collective-permute-start | bytes 393224 | tf_op jit(solution)/shard_map/ppermute | solution.py:583
  53.7 6.4 %collective-permute-start.14 = (bf16[512,128]{1,0:T(8,128)(2,1)S(1)}, bf16[512,128]{1,0:T(8,128)(2,1)S(1)}, u32[]{:S(2)}, u32[]{:S(2)}) collective-permute-start(bf16[512,128]{1,0:T(8,128)(2,1)S(1)} %get-tuple-element.55), channel_id=1, source_target_pairs={{0,1},{1,0},{2,3},{3,2},{4,5},{5,4},{6,7},{7,6},{8,9},{9,8},{10,11... | collective-permute-start | bytes 393224 | tf_op jit(solution)/shard_map/ppermute | solution.py:586
  54.3 8.4 %collective-permute-start.15 = (bf16[512,128]{1,0:T(8,128)(2,1)S(1)}, bf16[512,128]{1,0:T(8,128)(2,1)S(1)}, u32[]{:S(2)}, u32[]{:S(2)}) collective-permute-start(bf16[512,128]{1,0:T(8,128)(2,1)S(1)} %get-tuple-element.56), channel_id=1, source_target_pairs={{0,2},{1,3},{2,0},{3,1},{4,6},{5,7},{6,4},{7,5},{8,10},{9,11},{10,... | collective-permute-start | bytes 393224 | tf_op jit(solution)/shard_map/ppermute | solution.py:586
  54.8 7.9 %collective-permute-start.16 = (bf16[512,128]{1,0:T(8,128)(2,1)S(1)}, bf16[512,128]{1,0:T(8,128)(2,1)S(1)}, u32[]{:S(2)}, u32[]{:S(2)}) collective-permute-start(bf16[512,128]{1,0:T(8,128)(2,1)S(1)} %get-tuple-element.57), channel_id=1, source_target_pairs={{0,3},{1,2},{2,1},{3,0},{4,7},{5,6},{6,5},{7,4},{8,11},{9,10},{10,... | collective-permute-start | bytes 393224 | tf_op jit(solution)/shard_map/ppermute | solution.py:586
  57.3 5.4 %collective-permute-start.18 = (bf16[128,128]{1,0:T(8,128)(2,1)S(1)}, bf16[128,128]{1,0:T(8,128)(2,1)S(1)}, u32[]{:S(2)}, u32[]{:S(2)}) collective-permute-start(bf16[128,128]{1,0:T(8,128)(2,1)S(1)} %get-tuple-element.61), channel_id=1, source_target_pairs={{0,8},{4,12},{8,0},{12,4},{16,24},{20,28},{24,16},{28,20},{1,9},{5... | collective-permute-start | bytes 98312 | tf_op jit(solution)/shard_map/ppermute | solution.py:583
  57.5 5.2 %collective-permute-start.19 = (bf16[128,128]{1,0:T(8,128)(2,1)S(1)}, bf16[128,128]{1,0:T(8,128)(2,1)S(1)}, u32[]{:S(2)}, u32[]{:S(2)}) collective-permute-start(bf16[128,128]{1,0:T(8,128)(2,1)S(1)} %get-tuple-element.62), channel_id=1, source_target_pairs={{0,16},{4,20},{8,24},{12,28},{16,0},{20,4},{24,8},{28,12},{1,17},{... | collective-permute-start | bytes 98312 | tf_op jit(solution)/shard_map/ppermute | solution.py:583
  60.0 5.7 %collective-permute-start.20 = (bf16[128,128]{1,0:T(8,128)(2,1)S(1)}, bf16[128,128]{1,0:T(8,128)(2,1)S(1)}, u32[]{:S(2)}, u32[]{:S(2)}) collective-permute-start(bf16[128,128]{1,0:T(8,128)(2,1)S(1)} %get-tuple-element.63), channel_id=1, source_target_pairs={{0,24},{4,28},{8,16},{12,20},{16,8},{20,12},{24,0},{28,4},{1,25},{... | collective-permute-start | bytes 98312 | tf_op jit(solution)/shard_map/ppermute | solution.py:583

commit v3 on v2

--- a/solution.py
+++ b/solution.py
@@ -15,6 +15,7 @@
 lanes = 128
 vmem_bytes = 20 * 1024 * 1024
 most_bytes = 60 * 1024 * 1024
+load_bytes = 58 * 1024 * 1024
 
 def joined(part, axis, combine):
     gathered = jax.tree.map(lambda a: lax.all_gather(a, axis), part)
@@ -135,13 +136,13 @@
     return (out_query, out_key)
 
 
-def local_call(kernel, out_shape, name, grid=None, in_specs=None, out_specs=None, scratch=(), flops=0, moved=0, room=vmem_bytes):
+def local_call(kernel, out_shape, name, grid=None, in_specs=None, out_specs=None, scratch=(), flops=1, moved=0, room=vmem_bytes):
     settings = dict(
         out_shape=out_shape,
         scratch_shapes=list(scratch),
         name=name,
         compiler_params=pltpu.CompilerParams(vmem_limit_bytes=room),
-        cost_estimate=pl.CostEstimate(flops=flops, bytes_accessed=moved, transcendentals=0),
+        cost_estimate=pl.CostEstimate(flops=flops, bytes_accessed=1, transcendentals=0),
     )
     if grid is not None:
         settings["grid"] = grid
@@ -202,27 +203,58 @@
         "pack_queries",
         in_specs=[whole()],
         out_specs=whole(),
-        flops=2 * queries.size * queries.size // width,
+        flops=30_000_000_000,
     )(queries)
 
 
-def pick_kernel(own_ref, got_ref, out_ref):
+def pick_kernel(ends_ref, inner_ref, *outs):
     plane, _, _ = place()
     inner = (plane == 1) | (plane == 2)
 
+    def fill(source_ref):
+        for i, out_ref in enumerate(outs):
+            rows = out_ref.shape[0]
+            out_ref[...] = source_ref[i * rows : (i + 1) * rows, :]
+
     @pl.when(inner)
     def _():
-        out_ref[...] = got_ref[...]
+        fill(inner_ref)
 
     @pl.when(jnp.logical_not(inner))
     def _():
-        out_ref[...] = own_ref[...]
-
-
-def picked(own, got):
-    return local_call(
-        pick_kernel, bf16(own.shape), "pick_queries", in_specs=[whole()] * 2, out_specs=whole(), moved=4 * own.size
-    )(own, got)
+        fill(ends_ref)
+
+
+def picked(ends, inner, parts):
+    rows, width = ends.shape
+    return local_call(
+        pick_kernel,
+        [bf16((rows // parts, width))] * parts,
+        "pick_queries",
+        in_specs=[whole()] * 2,
+        out_specs=[whole()] * parts,
+        moved=4 * ends.size,
+    )(ends, inner)
+
+
+def parts_kernel(source_ref, *outs):
+    first = 0
+    for out_ref in outs:
+        rows = out_ref.shape[0]
+        out_ref[...] = source_ref[first : first + rows, :]
+        first += rows
+
+
+def in_parts(source):
+    rows, width = source.shape
+    large = rows * 5 // 8 // 16 * 16
+    return local_call(
+        parts_kernel,
+        [bf16((large, width)), bf16((rows - large, width))],
+        "query_parts",
+        in_specs=[whole()],
+        out_specs=[whole()] * 2,
+    )(source)
 
 
 def unpack(packed, wide_ref, slot, total, width):
@@ -266,15 +298,16 @@
 
 def mass_kernel(flip, places, rows, heads, length_ref, *refs):
     count = len(places)
-    packs = refs[:count]
-    lse_ref, key_ref, out_ref, wide_ref = refs[len(packs) :]
+    parts = (len(refs) - 4) // count
+    packs = [refs[n * parts : (n + 1) * parts] for n in range(count)]
+    lse_ref, key_ref, out_ref, wide_ref = refs[count * parts :]
     width, key_count = key_ref.shape
     tile = math.gcd(key_count, 512)
     total = rows * heads
     own_plane, own_core, _ = place()
     plane = own_plane ^ flip
     for n, other in enumerate(places):
-        unpack(packs[n][...], wide_ref, n, total, width)
+        unpack(jnp.concatenate([ref[...] for ref in packs[n]], axis=0), wide_ref, n, total, width)
         core = own_core ^ other
         context = 2 * plane + core
         lse = rows_at(lse_ref, context, rows)
@@ -286,7 +319,7 @@
                 out_ref[pl.ds(pl.multiple_of(core * rows, rows), rows), first : first + tile] = mass
 
 
-def chunk_mass(lengths, packs, lse, keys, flip, places, rows, heads, name):
+def chunk_mass(lengths, packs, lse, keys, flip, places, rows, heads, name, flops=1):
     width, key_count = keys.shape
     count = len(places)
     total = rows * heads
@@ -297,8 +330,7 @@
         in_specs=[whole()] * (len(packs) + 3),
         out_specs=whole(),
         scratch=[pltpu.VMEM((count * total, width), jnp.bfloat16)],
-        flops=2 * count * total * key_count * width,
-        moved=2 * keys.size,
+        flops=flops,
     )(lengths, *packs, lse, keys)
 
 
@@ -339,7 +371,6 @@
             pltpu.VMEM((total, width), jnp.bfloat16),
             pltpu.VMEM((4, both, key_count), jnp.float32),
         ],
-        flops=2 * total * key_count * width,
         moved=2 * keys.size,
     )(lengths, pack, lse, own, near, far, half, keys)
 
@@ -377,7 +408,6 @@
         "index_logits",
         in_specs=[whole()] * 4,
         out_specs=[whole()] * 3,
-        flops=2 * flat_query.size * key_count,
         moved=2 * index_key.size,
     )(lengths, flat_query, index_key, weight_wide)
 
@@ -520,7 +550,6 @@
         in_specs=[whole()] * (6 + len(stats)),
         out_specs=[whole()] * (partners + 2),
         scratch=[pltpu.VMEM((rows, key_count), jnp.float32), pltpu.VMEM((key_count, width), jnp.float32)],
-        flops=6 * flat * width * key_count,
         moved=8 * key_count * width,
     )(lengths, mass, logits, turned, index_key, masked, *stats)
 
@@ -586,38 +615,40 @@
         return lax.ppermute(array, "heads", [(h, h ^ e) for h in range(partners)])
 
     def mass_of(packs, *rest):
-        return chunk_mass(lengths, packs, lse, keys, *rest[:2], rows, heads, rest[2])
+        return chunk_mass(lengths, packs, lse, keys, *rest[:2], rows, heads, *rest[2:])
 
     pack = packed_queries(main_query)
-    across = planes_move(pack, [(1, 2), (2, 1), (0, 3), (3, 0)])
     near = planes_move(pack, [(0, 1), (1, 0), (2, 3), (3, 2)])
+    inner = planes_move(pack, [(1, 2), (2, 1), (0, 0), (3, 3)])
+    ends = planes_move(pack, [(0, 3), (3, 0)])
     own_pair = context_flip(pack, 1)
     lengths, lse, weight_wide, query, turned, index_key, keys = load_inputs(
         lengths, head_lse.T, index_weight, index_query, index_key, after(latent_keys, pack).T
     )
+    inner = after(inner, lse)
+    far = planes_move(inner, [(0, 2), (3, 1), (1, 0), (2, 3)])
     logits, masked, stats = index_logits(lengths, query.reshape(flat, width), index_key, weight_wide, own_rows)
-    own_mass = mass_of([pack, after(own_pair, stats)], 0, (0, 1), "mass_own")
-    across = after(across, own_mass)
-    far = planes_move(picked(pack, across), [(0, 2), (3, 1), (1, 0), (2, 3)])
-    near = after(near, own_mass)
-    near_mass = mass_of([near, context_flip(near, 1)], 1, (0, 1), "mass_near")
-    across_mass = mass_of([across, context_flip(across, 1)], 3, (0, 1), "mass_across")
+    own_mass = mass_of([pack, own_pair], 0, (0, 1), "mass_own")
+    across = picked(after(ends, own_mass, stats), inner, 2)
+    near = in_parts(after(near, stats))
+    near_mass = mass_of([*near, *(context_flip(a, 1) for a in near)], 1, (0, 1), "mass_near", 500_000_000)
+    across_mass = mass_of([*across, *(context_flip(a, 1) for a in across)], 3, (0, 1), "mass_across")
     far = after(far, near_mass, across_mass)
     far_pair = context_flip(far, 1)
     far_mass = mass_of([far], 2, (0,), "mass_far")
     shared = shared_mass(
         lengths, far_pair, lse, own_mass, near_mass, across_mass, far_mass, keys, rows, heads, partners
     )
-    mass, stats = joined_mass(stats, shared[0], [heads_flip(shared[e], e) for e in range(1, partners)])
+    mass, stats = joined_mass(stats, shared[0], [heads_flip(shared[e], e) for e in reversed(range(1, partners))])
     stats = pair_stats(stats, context_flip(stats, 1))
-    every = [stats] + [context_flip(stats, 2 * e) for e in range(1, planes)]
+    every = [stats] + [context_flip(stats, 2 * e) for e in reversed(range(1, planes))]
     *key_grads, keep, send = back_pass(
         lengths, mass, logits, turned, index_key, masked, every, partners, planes
     )
     got = context_flip(send, 1)
-    key_parts = [key_grads[0]] + [heads_flip(key_grads[e], e) for e in range(1, partners)]
+    key_parts = [key_grads[0]] + [heads_flip(key_grads[e], e) for e in reversed(range(1, partners))]
     sums = pair_sums(keep, got)
-    query_parts = [sums[0]] + [context_flip(sums[e], 2 * e) for e in range(1, planes)]
+    query_parts = [sums[0]] + [context_flip(sums[e], 2 * e) for e in reversed(range(1, planes))]
     return last_sums(key_parts, query_parts, (own_rows, index_heads // contexts, width))
 
 

time: 66.9 us -> 62.8 us (0.939)
  starting transfers between devices: 23.2 us -> 29.1 us
  local copies, waits for them, and re-layouts: 6.69 us -> 1.14 us
  waiting for transfers between devices: 21.6 us -> 17 us
    ppermute x3 -> x4, starting transfers between devices: 7.12 us -> 13.5 us  [planes_move(): lax.ppermute(array, 'context', [(2 * a + k, 2 * b + k) for a, b in pairs...]
    unnamed x14, local copies, waits for them, and re-layouts: 6.69 us -> 1.14 us
    ppermute x3 -> x4, waiting for transfers between devices: 6.91 us -> 2.98 us  [planes_move(): lax.ppermute(array, 'context', [(2 * a + k, 2 * b + k) for a, b in pairs...]
    ppermute x12 -> x14, waiting for transfers between devices: 8.61 us -> 7.08 us  [context_flip(): return lax.ppermute(array, 'context', [(c, c ^ e) for c in range(contexts)])]
    ppermute x6, waiting for transfers between devices: 6.11 us -> 6.96 us  [heads_flip(): return lax.ppermute(array, 'heads', [(h, h ^ e) for h in range(partners)])]
    ppermute x12 -> x14, starting transfers between devices: 9.02 us -> 8.46 us  [context_flip(): return lax.ppermute(array, 'context', [(c, c ^ e) for c in range(contexts)])]
  transfers between devices with their start and end apart: 21 -> 24, of which waited for: 12 -> 15; matrix products, arithmetic and copies ran while one was open for 0% -> 0% of each run, Pallas kernels for 15% -> 16%
where the time goes in v3:
time: 62.8 us; the launch traced here: 62.6 us
  starting transfers between devices  29.1 us (46%)
  waiting for transfers between devices  17 us (27%)
  Pallas kernels  14.4 us (23%)
  local copies, waits for them, and re-layouts  1.14 us (2%)
  between operations  0.91 us (1%)
    ppermute x4, starting transfers between devices, planes_move(): lax.ppermute(array, 'context', [(2 * a + k, 2 * b + k) for a, b in pairs...  13.5 us
    ppermute x14, starting transfers between devices, context_flip(): return lax.ppermute(array, 'context', [(c, c ^ e) for c in range(contexts)])  8.46 us
    ppermute x6, starting transfers between devices, heads_flip(): return lax.ppermute(array, 'heads', [(h, h ^ e) for h in range(partners)])  7.11 us
    ppermute x14, waiting for transfers between devices, context_flip(): return lax.ppermute(array, 'context', [(c, c ^ e) for c in range(contexts)])  7.08 us
    ppermute x6, waiting for transfers between devices, heads_flip(): return lax.ppermute(array, 'heads', [(h, h ^ e) for h in range(partners)])  6.96 us
    pallas_call x4, Pallas kernels, chunk_mass(): local_call(functools.partial(mass_kernel, flip, places, rows, heads), f32...  6.6 us
    ppermute x4, waiting for transfers between devices, planes_move(): lax.ppermute(array, 'context', [(2 * a + k, 2 * b + k) for a, b in pairs...  2.98 us
    pallas_call x1, Pallas kernels, back_pass(): local_call(functools.partial(back_kernel, len(stats)), [f32((key_count //...  2.22 us
  transfers between devices with their start and end apart: 24, of which 15 were waited for; matrix products, arithmetic and copies ran while one was open for 0% of the time, Pallas kernels for 16%

profile of v3, /device:TPU:0, one launch (start us, length us, event | category | flops | bytes accessed | tf_op | source)
XLA Modules:
  0.0 62.6 jit_solution(345486218731711101)
XLA Ops:
  0.7 1.1 %copy-done.6 = bf16[8,32,576]{2,1,0:T(8,128)(2,1)S(1)} copy-done((bf16[8,32,576]{2,1,0:T(8,128)(2,1)S(1)}, bf16[8,32,576]{2,1,0:T(8,128)(2,1)}, u32[]{:S(2)}) %copy-start.6) | copy-done | bytes 294936
  2.0 0.7 %collective-permute-start = (bf16[1152,128]{1,0:T(8,128)(2,1)S(1)}, bf16[1152,128]{1,0:T(8,128)(2,1)S(1)}, u32[]{:S(2)}, u32[]{:S(2)}) collective-permute-start(bf16[1152,128]{1,0:T(8,128)(2,1)S(1)} %pack_queries.1.refs_0_), channel_id=1, source_target_pairs={{8,16},{12,20},{16,8},{20,12},{0,0},{4,4},{24,24},{28,28},{9,17},{... | collective-permute-start | bytes 884744 | tf_op jit(solution)/shard_map/ppermute | solution.py:609
  2.7 5.9 %collective-permute-start.2 = (bf16[1152,128]{1,0:T(8,128)(2,1)S(1)}, bf16[1152,128]{1,0:T(8,128)(2,1)S(1)}, u32[]{:S(2)}, u32[]{:S(2)}) collective-permute-start(bf16[1152,128]{1,0:T(8,128)(2,1)S(1)} %pack_queries.1.refs_0_), channel_id=1, source_target_pairs={{0,8},{4,12},{8,0},{12,4},{16,24},{20,28},{24,16},{28,20},{1,9},{5... | collective-permute-start | bytes 884744 | tf_op jit(solution)/shard_map/ppermute | solution.py:609
  8.6 3.2 %collective-permute-start.5 = (bf16[1152,128]{1,0:T(8,128)(2,1)S(1)}, bf16[1152,128]{1,0:T(8,128)(2,1)S(1)}, u32[]{:S(2)}, u32[]{:S(2)}) collective-permute-start(bf16[1152,128]{1,0:T(8,128)(2,1)S(1)} %pack_queries.1.refs_0_), channel_id=1, source_target_pairs={{0,24},{4,28},{24,0},{28,4},{1,25},{5,29},{25,1},{29,5},{2,26},{6,... | collective-permute-start | bytes 884744 | tf_op jit(solution)/shard_map/ppermute | solution.py:609
  11.9 1.2 %load_inputs.1 = (s32[64,128]{1,0:T(8,128)S(1)}, f32[64,32]{1,0:T(8,128)S(1)}, f32[1024,128]{1,0:T(8,128)S(1)}, bf16[16,64,128]{2,1,0:T(8,128)(2,1)S(1)}, bf16[1...) custom-call(s32[64]{0:T(128)S(1)} %copy-done.5, f32[32,64]{1,0:T(8,128)S(1)} %bitcast.5, ...), custom_call_target="tpu_custom_call" | custom-call | flops 1 | bytes 1 | tf_op jit(solution)/shard_map/load_inputs/pallas_call | solution.py:449
  13.1 3.7 %collective-permute-start.1 = (bf16[1152,128]{1,0:T(8,128)(2,1)S(1)}, bf16[1152,128]{1,0:T(8,128)(2,1)S(1)}, u32[]{:S(2)}, u32[]{:S(2)}) collective-permute-start(bf16[1152,128]{1,0:T(8,128)(2,1)S(1)} %collective-permute-done.inner_ref), channel_id=1, source_target_pairs={{0,16},{4,20},{24,8},{28,12},{8,0},{12,4},{16,24},{20,28},{1,17},{... | collective-permute-start | bytes 884744 | tf_op jit(solution)/shard_map/ppermute | solution.py:609
  16.9 1.8 %index_logits.1 = (f32[16,2048]{1,0:T(8,128)S(1)}, f32[1024,2048]{1,0:T(8,128)S(1)}, f32[16,128]{1,0:T(8,128)S(1)}) custom-call(s32[64,128]{1,0:T(8,128)S(1)} %get-tuple-element.38.length_ref, bf16[1024,128]{1,0:T(8,128)(2,1)S(1)} %bitcast.4, bf16[2048,128]{1,0:T(8,128)(2,1)S(1)} %get-tuple-element.40.key_ref, f32[1024,128]{1,0:T(8,128)S(1)} %get-tuple-element.41.weight_ref), custom_call_target="tpu_custom_call" | custom-call | flops 1 | bytes 1 | tf_op jit(solution)/shard_map/index_logits/pallas_call | solution.py:405
  18.8 1.9 %mass_own.1.own_ref = f32[16,2048]{1,0:T(8,128)S(1)} custom-call(s32[64,128]{1,0:T(8,128)S(1)} %get-tuple-element.38.length_ref, bf16[1152,128]{1,0:T(8,128)(2,1)S(1)} %pack_queries.1.refs_0_, bf16[1152,128]{1,0:T(8,128)(2,1)S(1)} %collective-permute-done.6.refs_1_, f32[64,32]{1,0:T(8,128)S(1)} %get-tuple-element.43.refs_4_.refs_2_.refs_1_.lse_ref, ...), custom_call_target="tpu_custom_call" | custom-call | flops 1 | bytes 1 | tf_op jit(solution)/shard_map/mass_own/pallas_call | solution.py:326
  20.7 3.0 %collective-permute-done.5.ends_ref = bf16[1152,128]{1,0:T(8,128)(2,1)S(1)} collective-permute-done((bf16[1152,128]{1,0:T(8,128)(2,1)S(1)}, bf16[1152,128]{1,0:T(8,128)(2,1)S(1)}, u32[]{:S(2)}, u32[]{:S(2)}) %collective-permute-start.5) | collective-permute-done | bytes 294944 | tf_op jit(solution)/shard_map/ppermute | solution.py:609
  24.5 0.8 %collective-permute-done.7.refs_2_ = bf16[576,128]{1,0:T(8,128)(2,1)S(1)} collective-permute-done((bf16[576,128]{1,0:T(8,128)(2,1)S(1)}, bf16[576,128]{1,0:T(8,128)(2,1)S(1)}, u32[]{:S(2)}, u32[]{:S(2)}) %collective-permute-start.7) | collective-permute-done | bytes 147488 | tf_op jit(solution)/shard_map/ppermute | solution.py:612
  25.5 1.9 %mass_across.1.far_ref = f32[16,2048]{1,0:T(8,128)S(1)} custom-call(s32[64,128]{1,0:T(8,128)S(1)} %get-tuple-element.38.length_ref, bf16[576,128]{1,0:T(8,128)(2,1)S(1)} %get-tuple-element.50.refs_0_, bf16[576,128]{1,0:T(8,128)(2,1)S(1)} %get-tuple-element.51.refs_1_, bf16[576,128]{1,0:T(8,128)(2,1)S(1)} %collective-permute-done.7.refs_2_, ...), custom_call_target="tpu_custom_call" | custom-call | flops 1 | bytes 1 | tf_op jit(solution)/shard_map/mass_across/pallas_call | solution.py:326
  27.4 1.9 %mass_near.1.near_ref = f32[16,2048]{1,0:T(8,128)S(1)} custom-call(s32[64,128]{1,0:T(8,128)S(1)} %get-tuple-element.38.length_ref, bf16[720,128]{1,0:T(8,128)(2,1)S(1)} %get-tuple-element.46.refs_0_, bf16[432,128]{1,0:T(8,128)(2,1)S(1)} %get-tuple-element.47.refs_1_, bf16[720,128]{1,0:T(8,128)(2,1)S(1)} %collective-permute-done.3.refs_2_, ...), custom_call_target="tpu_custom_call" | custom-call | flops 500000000 | bytes 1 | tf_op jit(solution)/shard_map/mass_near/pallas_call | solution.py:326
  29.6 1.0 %mass_far.1.half_ref = f32[8,2048]{1,0:T(8,128)S(1)} custom-call(s32[64,128]{1,0:T(8,128)S(1)} %get-tuple-element.38.length_ref, bf16[1152,128]{1,0:T(8,128)(2,1)S(1)} %collective-permute-done.1.refs_0_, f32[64,32]{1,0:T(8,128)S(1)} %get-tuple-element.43.refs_4_.refs_2_.refs_1_.lse_ref, bf16[576,2048]{1,0:T(8,128)(2,1)S(1)} %get-tuple-element.48.refs_5_.refs_3_.refs_2_.key_ref), custom_call_target="tpu_custom_call" | custom-call | flops 1 | bytes 1 | tf_op jit(solution)/shard_map/mass_far/pallas_call | solution.py:326
  30.9 1.1 %mass_and_share.1 = (f32[16,2048]{1,0:T(8,128)S(1)}, bf16[16,2048]{1,0:T(8,128)(2,1)S(1)}, bf16[16,2048]{1,0:T(8,128)(2,1)S(1)}, bf16[16,2048]{1,0:T(8,128)(2,1)S(1)}) custom-call(s32[64,128]{1,0:T(8,128)S(1)} %get-tuple-element.38.length_ref, bf16[1152,128]{1,0:T(8,128)(2,1)S(1)} %collective-permute-done.9.pack_ref, ...), custom_call_target="tpu_custom_call" | custom-call | flops 1 | bytes 1 | tf_op jit(solution)/shard_map/mass_and_share/pallas_call | solution.py:364
  32.0 2.5 %collective-permute-start.10 = (bf16[16,2048]{1,0:T(8,128)(2,1)S(1)}, bf16[16,2048]{1,0:T(8,128)(2,1)S(1)}, u32[]{:S(2)}, u32[]{:S(2)}) collective-permute-start(bf16[16,2048]{1,0:T(8,128)(2,1)S(1)} %get-tuple-element.54), channel_id=1, source_target_pairs={{0,3},{1,2},{2,1},{3,0},{4,7},{5,6},{6,5},{7,4},{8,11},{9,10},{10,... | collective-permute-start | bytes 196616 | tf_op jit(solution)/shard_map/ppermute | solution.py:615
  35.5 1.7 %collective-permute-done.10.refs_0_ = bf16[16,2048]{1,0:T(8,128)(2,1)S(1)} collective-permute-done((bf16[16,2048]{1,0:T(8,128)(2,1)S(1)}, bf16[16,2048]{1,0:T(8,128)(2,1)S(1)}, u32[]{:S(2)}, u32[]{:S(2)}) %collective-permute-start.10) | collective-permute-done | bytes 65568 | tf_op jit(solution)/shard_map/ppermute | solution.py:615
  37.3 1.5 %collective-permute-done.11.refs_1_ = bf16[16,2048]{1,0:T(8,128)(2,1)S(1)} collective-permute-done((bf16[16,2048]{1,0:T(8,128)(2,1)S(1)}, bf16[16,2048]{1,0:T(8,128)(2,1)S(1)}, u32[]{:S(2)}, u32[]{:S(2)}) %collective-permute-start.11) | collective-permute-done | bytes 65568 | tf_op jit(solution)/shard_map/ppermute | solution.py:615
  39.4 1.2 %collective-permute-done.13.got_ref = f32[16,128]{1,0:T(8,128)S(1)} collective-permute-done((f32[16,128]{1,0:T(8,128)S(1)}, f32[16,128]{1,0:T(8,128)S(1)}, u32[]{:S(2)}, u32[]{:S(2)}) %collective-permute-start.13) | collective-permute-done | bytes 8224 | tf_op jit(solution)/shard_map/ppermute | solution.py:612
  40.7 3.0 %collective-permute-start.14 = (f32[16,128]{1,0:T(8,128)S(1)}, f32[16,128]{1,0:T(8,128)S(1)}, u32[]{:S(2)}, u32[]{:S(2)}) collective-permute-start(f32[16,128]{1,0:T(8,128)S(1)} %pair_stats.1.refs_0_), channel_id=1, source_target_pairs={{0,24},{4,28},{8,16},{12,20},{16,8},{20,12},{24,0},{28,4},{1,25},{... | collective-permute-start | bytes 24584 | tf_op jit(solution)/shard_map/ppermute | solution.py:612
  43.7 1.4 %collective-permute-start.16 = (f32[16,128]{1,0:T(8,128)S(1)}, f32[16,128]{1,0:T(8,128)S(1)}, u32[]{:S(2)}, u32[]{:S(2)}) collective-permute-start(f32[16,128]{1,0:T(8,128)S(1)} %pair_stats.1.refs_0_), channel_id=1, source_target_pairs={{0,8},{4,12},{8,0},{12,4},{16,24},{20,28},{24,16},{28,20},{1,9},{5... | collective-permute-start | bytes 24584 | tf_op jit(solution)/shard_map/ppermute | solution.py:612
  45.1 1.1 %collective-permute-done.14.refs_1_ = f32[16,128]{1,0:T(8,128)S(1)} collective-permute-done((f32[16,128]{1,0:T(8,128)S(1)}, f32[16,128]{1,0:T(8,128)S(1)}, u32[]{:S(2)}, u32[]{:S(2)}) %collective-permute-start.14) | collective-permute-done | bytes 8224 | tf_op jit(solution)/shard_map/ppermute | solution.py:612
  46.2 2.1 %collective-permute-done.15.refs_2_ = f32[16,128]{1,0:T(8,128)S(1)} collective-permute-done((f32[16,128]{1,0:T(8,128)S(1)}, f32[16,128]{1,0:T(8,128)S(1)}, u32[]{:S(2)}, u32[]{:S(2)}) %collective-permute-start.15) | collective-permute-done | bytes 8224 | tf_op jit(solution)/shard_map/ppermute | solution.py:612
  48.3 2.2 %index_back.1 = (f32[512,128]{1,0:T(8,128)S(1)}, bf16[512,128]{1,0:T(8,128)(2,1)S(1)}, bf16[512,128]{1,0:T(8,128)(2,1)S(1)}, bf16[512,128]{1,0:T(8,128)(2,1)S(1)...) custom-call(s32[64,128]{1,0:T(8,128)S(1)} %get-tuple-element.38.length_ref, ...), custom_call_target="tpu_custom_call" | custom-call | flops 1 | bytes 1 | tf_op jit(solution)/shard_map/index_back/pallas_call | solution.py:544
  50.6 1.6 %collective-permute-start.17 = (bf16[512,128]{1,0:T(8,128)(2,1)S(1)}, bf16[512,128]{1,0:T(8,128)(2,1)S(1)}, u32[]{:S(2)}, u32[]{:S(2)}) collective-permute-start(bf16[512,128]{1,0:T(8,128)(2,1)S(1)} %get-tuple-element.63), channel_id=1, source_target_pairs={{0,3},{1,2},{2,1},{3,0},{4,7},{5,6},{6,5},{7,4},{8,11},{9,10},{10,... | collective-permute-start | bytes 393224 | tf_op jit(solution)/shard_map/ppermute | solution.py:615
  52.2 0.9 %collective-permute-start.18 = (bf16[512,128]{1,0:T(8,128)(2,1)S(1)}, bf16[512,128]{1,0:T(8,128)(2,1)S(1)}, u32[]{:S(2)}, u32[]{:S(2)}) collective-permute-start(bf16[512,128]{1,0:T(8,128)(2,1)S(1)} %get-tuple-element.64), channel_id=1, source_target_pairs={{0,2},{1,3},{2,0},{3,1},{4,6},{5,7},{6,4},{7,5},{8,10},{9,11},{10,... | collective-permute-start | bytes 393224 | tf_op jit(solution)/shard_map/ppermute | solution.py:615
  53.0 1.1 %collective-permute-start.19 = (bf16[512,128]{1,0:T(8,128)(2,1)S(1)}, bf16[512,128]{1,0:T(8,128)(2,1)S(1)}, u32[]{:S(2)}, u32[]{:S(2)}) collective-permute-start(bf16[512,128]{1,0:T(8,128)(2,1)S(1)} %get-tuple-element.65), channel_id=1, source_target_pairs={{0,1},{1,0},{2,3},{3,2},{4,5},{5,4},{6,7},{7,6},{8,9},{9,8},{10,11... | collective-permute-start | bytes 393224 | tf_op jit(solution)/shard_map/ppermute | solution.py:615
  54.2 1.5 %collective-permute-start.21 = (bf16[128,128]{1,0:T(8,128)(2,1)S(1)}, bf16[128,128]{1,0:T(8,128)(2,1)S(1)}, u32[]{:S(2)}, u32[]{:S(2)}) collective-permute-start(bf16[128,128]{1,0:T(8,128)(2,1)S(1)} %get-tuple-element.69), channel_id=1, source_target_pairs={{0,24},{4,28},{8,16},{12,20},{16,8},{20,12},{24,0},{28,4},{1,25},{... | collective-permute-start | bytes 98312 | tf_op jit(solution)/shard_map/ppermute | solution.py:612
  56.3 1.6 %collective-permute-done.17.refs_1_ = bf16[512,128]{1,0:T(8,128)(2,1)S(1)} collective-permute-done((bf16[512,128]{1,0:T(8,128)(2,1)S(1)}, bf16[512,128]{1,0:T(8,128)(2,1)S(1)}, u32[]{:S(2)}, u32[]{:S(2)}) %collective-permute-start.17) | collective-permute-done | bytes 131104 | tf_op jit(solution)/shard_map/ppermute | solution.py:615
  57.9 0.7 %collective-permute-start.23 = (bf16[128,128]{1,0:T(8,128)(2,1)S(1)}, bf16[128,128]{1,0:T(8,128)(2,1)S(1)}, u32[]{:S(2)}, u32[]{:S(2)}) collective-permute-start(bf16[128,128]{1,0:T(8,128)(2,1)S(1)} %get-tuple-element.71), channel_id=1, source_target_pairs={{0,8},{4,12},{8,0},{12,4},{16,24},{20,28},{24,16},{28,20},{1,9},{5... | collective-permute-start | bytes 98312 | tf_op jit(solution)/shard_map/ppermute | solution.py:612
  58.6 1.6 %collective-permute-done.18.refs_2_ = bf16[512,128]{1,0:T(8,128)(2,1)S(1)} collective-permute-done((bf16[512,128]{1,0:T(8,128)(2,1)S(1)}, bf16[512,128]{1,0:T(8,128)(2,1)S(1)}, u32[]{:S(2)}, u32[]{:S(2)}) %collective-permute-start.18) | collective-permute-done | bytes 131104 | tf_op jit(solution)/shard_map/ppermute | solution.py:615
  60.5 1.3 %collective-permute-done.23.refs_7_ = bf16[128,128]{1,0:T(8,128)(2,1)S(1)} collective-permute-done((bf16[128,128]{1,0:T(8,128)(2,1)S(1)}, bf16[128,128]{1,0:T(8,128)(2,1)S(1)}, u32[]{:S(2)}, u32[]{:S(2)}) %collective-permute-start.23) | collective-permute-done | bytes 32800 | tf_op jit(solution)/shard_map/ppermute | solution.py:612
  61.8 0.8 %last_sums.1 = (f32[16,8,128]{2,1,0:T(8,128)}, f32[512,128]{1,0:T(8,128)}) custom-call(f32[512,128]{1,0:T(8,128)S(1)} %get-tuple-element.62.refs_0_, bf16[512,128]{1,0:T(8,128)(2,1)S(1)} %collective-permute-done.17.refs_1_, bf16[512,128]{1,0:T(8,128)(2,1)S(1)} %collective-permute-done.18.refs_2_, bf16[512,128]{1,0:T(8,128)(2,1)S(1)} %collective-permute-done.19.refs_3_, ...), custom_call_target="tpu_custom_call" | custom-call | flops 1 | bytes 1 | tf_op jit(solution)/shard_map/last_sums/pallas_call | solution.py:584
  (45 shorter events, 4.9 us)
Async XLA Ops:
  0.6 11.2 %copy-start = (bf16[2048,576]{0,1:T(8,128)(2,1)S(1)}, bf16[2048,576]{0,1:T(8,128)(2,1)}, u32[]{:S(2)}) copy-start(bf16[2048,576]{0,1:T(8,128)(2,1)} %param.8) | copy-start | bytes 7077892
  0.6 11.2 %copy-start.3 = (f32[64,32]{0,1:T(8,128)S(1)}, f32[64,32]{0,1:T(8,128)}, u32[]{:S(2)}) copy-start(f32[64,32]{0,1:T(8,128)} %param.9) | copy-start | bytes 24580
  0.7 11.2 %copy-start.5 = (s32[64]{0:T(128)S(1)}, s32[64]{0:T(128)}, u32[]{:S(2)}) copy-start(s32[64]{0:T(128)} %length_ref.1) | copy-start | bytes 772
  0.7 11.2 %copy-start.2 = (bf16[16,64,128]{2,1,0:T(8,128)(2,1)S(1)}, bf16[16,64,128]{2,1,0:T(8,128)(2,1)}, u32[]{:S(2)}) copy-start(bf16[16,64,128]{2,1,0:T(8,128)(2,1)} %query_hbm.1) | copy-start | bytes 786436
  0.7 11.2 %copy-start.1 = (bf16[2048,128]{1,0:T(8,128)(2,1)S(1)}, bf16[2048,128]{1,0:T(8,128)(2,1)}, u32[]{:S(2)}) copy-start(bf16[2048,128]{1,0:T(8,128)(2,1)} %key_hbm.1) | copy-start | bytes 1572868
  0.7 1.1 %copy-start.6 = (bf16[8,32,576]{2,1,0:T(8,128)(2,1)S(1)}, bf16[8,32,576]{2,1,0:T(8,128)(2,1)}, u32[]{:S(2)}) copy-start(bf16[8,32,576]{2,1,0:T(8,128)(2,1)} %query_ref.1) | copy-start | bytes 884740
  1.8 10.1 %copy-start.4 = (f32[16,64]{1,0:T(8,128)S(1)}, f32[16,64]{1,0:T(8,128)}, u32[]{:S(2)}) copy-start(f32[16,64]{1,0:T(8,128)} %weight_ref.1) | copy-start | bytes 12292
  2.0 11.1 %collective-permute-start = (bf16[1152,128]{1,0:T(8,128)(2,1)S(1)}, bf16[1152,128]{1,0:T(8,128)(2,1)S(1)}, u32[]{:S(2)}, u32[]{:S(2)}) collective-permute-start(bf16[1152,128]{1,0:T(8,128)(2,1)S(1)} %pack_queries.1.refs_0_), channel_id=1, source_target_pairs={{8,16},{12,20},{16,8},{20,12},{0,0},{4,4},{24,24},{28,28},{9,17},{... | collective-permute-start | bytes 884744 | tf_op jit(solution)/shard_map/ppermute | solution.py:609
  2.7 16.0 %collective-permute-start.2 = (bf16[1152,128]{1,0:T(8,128)(2,1)S(1)}, bf16[1152,128]{1,0:T(8,128)(2,1)S(1)}, u32[]{:S(2)}, u32[]{:S(2)}) collective-permute-start(bf16[1152,128]{1,0:T(8,128)(2,1)S(1)} %pack_queries.1.refs_0_), channel_id=1, source_target_pairs={{0,8},{4,12},{8,0},{12,4},{16,24},{20,28},{24,16},{28,20},{1,9},{5... | collective-permute-start | bytes 884744 | tf_op jit(solution)/shard_map/ppermute | solution.py:609
  8.6 10.2 %collective-permute-start.6 = (bf16[1152,128]{1,0:T(8,128)(2,1)S(1)}, bf16[1152,128]{1,0:T(8,128)(2,1)S(1)}, u32[]{:S(2)}, u32[]{:S(2)}) collective-permute-start(bf16[1152,128]{1,0:T(8,128)(2,1)S(1)} %pack_queries.1.refs_0_), channel_id=1, source_target_pairs={{0,4},{4,0},{8,12},{12,8},{16,20},{20,16},{24,28},{28,24},{1,5},{5... | collective-permute-start | bytes 884744 | tf_op jit(solution)/shard_map/ppermute | solution.py:612
  8.6 15.1 %collective-permute-start.5 = (bf16[1152,128]{1,0:T(8,128)(2,1)S(1)}, bf16[1152,128]{1,0:T(8,128)(2,1)S(1)}, u32[]{:S(2)}, u32[]{:S(2)}) collective-permute-start(bf16[1152,128]{1,0:T(8,128)(2,1)S(1)} %pack_queries.1.refs_0_), channel_id=1, source_target_pairs={{0,24},{4,28},{24,0},{28,4},{1,25},{5,29},{25,1},{29,5},{2,26},{6,... | collective-permute-start | bytes 884744 | tf_op jit(solution)/shard_map/ppermute | solution.py:609
  13.1 16.1 %collective-permute-start.1 = (bf16[1152,128]{1,0:T(8,128)(2,1)S(1)}, bf16[1152,128]{1,0:T(8,128)(2,1)S(1)}, u32[]{:S(2)}, u32[]{:S(2)}) collective-permute-start(bf16[1152,128]{1,0:T(8,128)(2,1)S(1)} %collective-permute-done.inner_ref), channel_id=1, source_target_pairs={{0,16},{4,20},{24,8},{28,12},{8,0},{12,4},{16,24},{20,28},{1,17},{... | collective-permute-start | bytes 884744 | tf_op jit(solution)/shard_map/ppermute | solution.py:609
  18.7 8.7 %collective-permute-start.3 = (bf16[720,128]{1,0:T(8,128)(2,1)S(1)}, bf16[720,128]{1,0:T(8,128)(2,1)S(1)}, u32[]{:S(2)}, u32[]{:S(2)}) collective-permute-start(bf16[720,128]{1,0:T(8,128)(2,1)S(1)} %get-tuple-element.46.refs_0_), channel_id=1, source_target_pairs={{0,4},{4,0},{8,12},{12,8},{16,20},{20,16},{24,28},{28,24},{1,5},{5... | collective-permute-start | bytes 552968 | tf_op jit(solution)/shard_map/ppermute | solution.py:612
  23.9 1.4 %collective-permute-start.7 = (bf16[576,128]{1,0:T(8,128)(2,1)S(1)}, bf16[576,128]{1,0:T(8,128)(2,1)S(1)}, u32[]{:S(2)}, u32[]{:S(2)}) collective-permute-start(bf16[576,128]{1,0:T(8,128)(2,1)S(1)} %get-tuple-element.50.refs_0_), channel_id=1, source_target_pairs={{0,4},{4,0},{8,12},{12,8},{16,20},{20,16},{24,28},{28,24},{1,5},{5... | collective-permute-start | bytes 442376 | tf_op jit(solution)/shard_map/ppermute | solution.py:612
  23.9 1.6 %collective-permute-start.8 = (bf16[576,128]{1,0:T(8,128)(2,1)S(1)}, bf16[576,128]{1,0:T(8,128)(2,1)S(1)}, u32[]{:S(2)}, u32[]{:S(2)}) collective-permute-start(bf16[576,128]{1,0:T(8,128)(2,1)S(1)} %get-tuple-element.51.refs_1_), channel_id=1, source_target_pairs={{0,4},{4,0},{8,12},{12,8},{16,20},{20,16},{24,28},{28,24},{1,5},{5... | collective-permute-start | bytes 442376 | tf_op jit(solution)/shard_map/ppermute | solution.py:612
  24.4 2.9 %collective-permute-start.4 = (bf16[432,128]{1,0:T(8,128)(2,1)S(1)}, bf16[432,128]{1,0:T(8,128)(2,1)S(1)}, u32[]{:S(2)}, u32[]{:S(2)}) collective-permute-start(bf16[432,128]{1,0:T(8,128)(2,1)S(1)} %get-tuple-element.47.refs_1_), channel_id=1, source_target_pairs={{0,4},{4,0},{8,12},{12,8},{16,20},{20,16},{24,28},{28,24},{1,5},{5... | collective-permute-start | bytes 331784 | tf_op jit(solution)/shard_map/ppermute | solution.py:612
  29.3 1.6 %collective-permute-start.9 = (bf16[1152,128]{1,0:T(8,128)(2,1)S(1)}, bf16[1152,128]{1,0:T(8,128)(2,1)S(1)}, u32[]{:S(2)}, u32[]{:S(2)}) collective-permute-start(bf16[1152,128]{1,0:T(8,128)(2,1)S(1)} %collective-permute-done.1.refs_0_), channel_id=1, source_target_pairs={{0,4},{4,0},{8,12},{12,8},{16,20},{20,16},{24,28},{28,24},{1,5},{5... | collective-permute-start | bytes 884744 | tf_op jit(solution)/shard_map/ppermute | solution.py:612
  32.0 5.3 %collective-permute-start.10 = (bf16[16,2048]{1,0:T(8,128)(2,1)S(1)}, bf16[16,2048]{1,0:T(8,128)(2,1)S(1)}, u32[]{:S(2)}, u32[]{:S(2)}) collective-permute-start(bf16[16,2048]{1,0:T(8,128)(2,1)S(1)} %get-tuple-element.54), channel_id=1, source_target_pairs={{0,3},{1,2},{2,1},{3,0},{4,7},{5,6},{6,5},{7,4},{8,11},{9,10},{10,... | collective-permute-start | bytes 196616 | tf_op jit(solution)/shard_map/ppermute | solution.py:615
  34.5 4.3 %collective-permute-start.11 = (bf16[16,2048]{1,0:T(8,128)(2,1)S(1)}, bf16[16,2048]{1,0:T(8,128)(2,1)S(1)}, u32[]{:S(2)}, u32[]{:S(2)}) collective-permute-start(bf16[16,2048]{1,0:T(8,128)(2,1)S(1)} %get-tuple-element.55), channel_id=1, source_target_pairs={{0,2},{1,3},{2,0},{3,1},{4,6},{5,7},{6,4},{7,5},{8,10},{9,11},{10,... | collective-permute-start | bytes 196616 | tf_op jit(solution)/shard_map/ppermute | solution.py:615
  35.0 4.3 %collective-permute-start.12 = (bf16[16,2048]{1,0:T(8,128)(2,1)S(1)}, bf16[16,2048]{1,0:T(8,128)(2,1)S(1)}, u32[]{:S(2)}, u32[]{:S(2)}) collective-permute-start(bf16[16,2048]{1,0:T(8,128)(2,1)S(1)} %get-tuple-element.56), channel_id=1, source_target_pairs={{0,1},{1,0},{2,3},{3,2},{4,5},{5,4},{6,7},{7,6},{8,9},{9,8},{10,11... | collective-permute-start | bytes 196616 | tf_op jit(solution)/shard_map/ppermute | solution.py:615
  39.4 1.2 %collective-permute-start.13 = (f32[16,128]{1,0:T(8,128)S(1)}, f32[16,128]{1,0:T(8,128)S(1)}, u32[]{:S(2)}, u32[]{:S(2)}) collective-permute-start(f32[16,128]{1,0:T(8,128)S(1)} %get-tuple-element.61.own_ref), channel_id=1, source_target_pairs={{0,4},{4,0},{8,12},{12,8},{16,20},{20,16},{24,28},{28,24},{1,5},{5... | collective-permute-start | bytes 24584 | tf_op jit(solution)/shard_map/ppermute | solution.py:612
  40.7 5.5 %collective-permute-start.14 = (f32[16,128]{1,0:T(8,128)S(1)}, f32[16,128]{1,0:T(8,128)S(1)}, u32[]{:S(2)}, u32[]{:S(2)}) collective-permute-start(f32[16,128]{1,0:T(8,128)S(1)} %pair_stats.1.refs_0_), channel_id=1, source_target_pairs={{0,24},{4,28},{8,16},{12,20},{16,8},{20,12},{24,0},{28,4},{1,25},{... | collective-permute-start | bytes 24584 | tf_op jit(solution)/shard_map/ppermute | solution.py:612
  43.7 4.5 %collective-permute-start.15 = (f32[16,128]{1,0:T(8,128)S(1)}, f32[16,128]{1,0:T(8,128)S(1)}, u32[]{:S(2)}, u32[]{:S(2)}) collective-permute-start(f32[16,128]{1,0:T(8,128)S(1)} %pair_stats.1.refs_0_), channel_id=1, source_target_pairs={{0,16},{4,20},{8,24},{12,28},{16,0},{20,4},{24,8},{28,12},{1,17},{... | collective-permute-start | bytes 24584 | tf_op jit(solution)/shard_map/ppermute | solution.py:612
  43.7 4.5 %collective-permute-start.16 = (f32[16,128]{1,0:T(8,128)S(1)}, f32[16,128]{1,0:T(8,128)S(1)}, u32[]{:S(2)}, u32[]{:S(2)}) collective-permute-start(f32[16,128]{1,0:T(8,128)S(1)} %pair_stats.1.refs_0_), channel_id=1, source_target_pairs={{0,8},{4,12},{8,0},{12,4},{16,24},{20,28},{24,16},{28,20},{1,9},{5... | collective-permute-start | bytes 24584 | tf_op jit(solution)/shard_map/ppermute | solution.py:612
  50.5 3.6 %collective-permute-start.20 = (bf16[4,128,128]{2,1,0:T(8,128)(2,1)S(1)}, bf16[4,128,128]{2,1,0:T(8,128)(2,1)S(1)}, u32[]{:S(2)}, u32[]{:S(2)}) collective-permute-start(bf16[4,128,128]{2,1,0:T(8,128)(2,1)S(1)} %get-tuple-element.67), channel_id=1, source_target_pairs={{0,4},{4,0},{8,12},{12,8},{16,20},{20,16},{24,28},{28,24},{1,5},{5... | collective-permute-start | bytes 393224 | tf_op jit(solution)/shard_map/ppermute | solution.py:612
  50.6 7.3 %collective-permute-start.17 = (bf16[512,128]{1,0:T(8,128)(2,1)S(1)}, bf16[512,128]{1,0:T(8,128)(2,1)S(1)}, u32[]{:S(2)}, u32[]{:S(2)}) collective-permute-start(bf16[512,128]{1,0:T(8,128)(2,1)S(1)} %get-tuple-element.63), channel_id=1, source_target_pairs={{0,3},{1,2},{2,1},{3,0},{4,7},{5,6},{6,5},{7,4},{8,11},{9,10},{10,... | collective-permute-start | bytes 393224 | tf_op jit(solution)/shard_map/ppermute | solution.py:615
  52.2 8.0 %collective-permute-start.18 = (bf16[512,128]{1,0:T(8,128)(2,1)S(1)}, bf16[512,128]{1,0:T(8,128)(2,1)S(1)}, u32[]{:S(2)}, u32[]{:S(2)}) collective-permute-start(bf16[512,128]{1,0:T(8,128)(2,1)S(1)} %get-tuple-element.64), channel_id=1, source_target_pairs={{0,2},{1,3},{2,0},{3,1},{4,6},{5,7},{6,4},{7,5},{8,10},{9,11},{10,... | collective-permute-start | bytes 393224 | tf_op jit(solution)/shard_map/ppermute | solution.py:615
  53.0 7.3 %collective-permute-start.19 = (bf16[512,128]{1,0:T(8,128)(2,1)S(1)}, bf16[512,128]{1,0:T(8,128)(2,1)S(1)}, u32[]{:S(2)}, u32[]{:S(2)}) collective-permute-start(bf16[512,128]{1,0:T(8,128)(2,1)S(1)} %get-tuple-element.65), channel_id=1, source_target_pairs={{0,1},{1,0},{2,3},{3,2},{4,5},{5,4},{6,7},{7,6},{8,9},{9,8},{10,11... | collective-permute-start | bytes 393224 | tf_op jit(solution)/shard_map/ppermute | solution.py:615
  54.2 6.1 %collective-permute-start.21 = (bf16[128,128]{1,0:T(8,128)(2,1)S(1)}, bf16[128,128]{1,0:T(8,128)(2,1)S(1)}, u32[]{:S(2)}, u32[]{:S(2)}) collective-permute-start(bf16[128,128]{1,0:T(8,128)(2,1)S(1)} %get-tuple-element.69), channel_id=1, source_target_pairs={{0,24},{4,28},{8,16},{12,20},{16,8},{20,12},{24,0},{28,4},{1,25},{... | collective-permute-start | bytes 98312 | tf_op jit(solution)/shard_map/ppermute | solution.py:612
  55.7 4.9 %collective-permute-start.22 = (bf16[128,128]{1,0:T(8,128)(2,1)S(1)}, bf16[128,128]{1,0:T(8,128)(2,1)S(1)}, u32[]{:S(2)}, u32[]{:S(2)}) collective-permute-start(bf16[128,128]{1,0:T(8,128)(2,1)S(1)} %get-tuple-element.70), channel_id=1, source_target_pairs={{0,16},{4,20},{8,24},{12,28},{16,0},{20,4},{24,8},{28,12},{1,17},{... | collective-permute-start | bytes 98312 | tf_op jit(solution)/shard_map/ppermute | solution.py:612
  57.9 3.9 %collective-permute-start.23 = (bf16[128,128]{1,0:T(8,128)(2,1)S(1)}, bf16[128,128]{1,0:T(8,128)(2,1)S(1)}, u32[]{:S(2)}, u32[]{:S(2)}) collective-permute-start(bf16[128,128]{1,0:T(8,128)(2,1)S(1)} %get-tuple-element.71), channel_id=1, source_target_pairs={{0,8},{4,12},{8,0},{12,4},{16,24},{20,28},{24,16},{28,20},{1,9},{5... | collective-permute-start | bytes 98312 | tf_op jit(solution)/shard_map/ppermute | solution.py:612

commit v4 on v3

--- a/solution.py
+++ b/solution.py
@@ -629,9 +629,9 @@
     far = planes_move(inner, [(0, 2), (3, 1), (1, 0), (2, 3)])
     logits, masked, stats = index_logits(lengths, query.reshape(flat, width), index_key, weight_wide, own_rows)
     own_mass = mass_of([pack, own_pair], 0, (0, 1), "mass_own")
-    across = picked(after(ends, own_mass, stats), inner, 2)
     near = in_parts(after(near, stats))
-    near_mass = mass_of([*near, *(context_flip(a, 1) for a in near)], 1, (0, 1), "mass_near", 500_000_000)
+    near_mass = mass_of([*near, *(context_flip(a, 1) for a in near)], 1, (0, 1), "mass_near")
+    across = picked(after(ends, own_mass, near_mass), inner, 3)
     across_mass = mass_of([*across, *(context_flip(a, 1) for a in across)], 3, (0, 1), "mass_across")
     far = after(far, near_mass, across_mass)
     far_pair = context_flip(far, 1)

time: 62.8 us -> 61.1 us (0.973)
  waiting for transfers between devices: 17 us -> 14.4 us
  starting transfers between devices: 29.1 us -> 30.1 us
    ppermute x4, waiting for transfers between devices: 2.98 us -> 1.35 us  [planes_move(): lax.ppermute(array, 'context', [(2 * a + k, 2 * b + k) for a, b in pairs...]
    ppermute x14 -> x15, starting transfers between devices: 8.46 us -> 9.48 us  [context_flip(): return lax.ppermute(array, 'context', [(c, c ^ e) for c in range(contexts)])]
    ppermute x6, waiting for transfers between devices: 6.96 us -> 6.07 us  [heads_flip(): return lax.ppermute(array, 'heads', [(h, h ^ e) for h in range(partners)])]
    ppermute x14 -> x15, waiting for transfers between devices: 7.08 us -> 6.96 us  [context_flip(): return lax.ppermute(array, 'context', [(c, c ^ e) for c in range(contexts)])]
  transfers between devices with their start and end apart: 24 -> 25, of which waited for: 15 -> 17; matrix products, arithmetic and copies ran while one was open for 0% -> 0% of each run, Pallas kernels for 16% -> 16%
where the time goes in v4:
time: 61.1 us; the launch traced here: 60.9 us
  starting transfers between devices  30.1 us (49%)
  Pallas kernels  14.4 us (24%)
  waiting for transfers between devices  14.4 us (24%)
  local copies, waits for them, and re-layouts  1.14 us (2%)
  between operations  0.9 us (1%)
    ppermute x4, starting transfers between devices, planes_move(): lax.ppermute(array, 'context', [(2 * a + k, 2 * b + k) for a, b in pairs...  13.5 us
    ppermute x15, starting transfers between devices, context_flip(): return lax.ppermute(array, 'context', [(c, c ^ e) for c in range(contexts)])  9.48 us
    ppermute x6, starting transfers between devices, heads_flip(): return lax.ppermute(array, 'heads', [(h, h ^ e) for h in range(partners)])  7.11 us
    ppermute x15, waiting for transfers between devices, context_flip(): return lax.ppermute(array, 'context', [(c, c ^ e) for c in range(contexts)])  6.96 us
    pallas_call x4, Pallas kernels, chunk_mass(): local_call(functools.partial(mass_kernel, flip, places, rows, heads), f32...  6.59 us
    ppermute x6, waiting for transfers between devices, heads_flip(): return lax.ppermute(array, 'heads', [(h, h ^ e) for h in range(partners)])  6.07 us
    pallas_call x1, Pallas kernels, back_pass(): local_call(functools.partial(back_kernel, len(stats)), [f32((key_count //...  2.22 us
    pallas_call x1, Pallas kernels, index_logits(): local_call(logits_kernel, [f32((rows, key_count)), f32((flat, key_count))...  1.84 us
  transfers between devices with their start and end apart: 25, of which 17 were waited for; matrix products, arithmetic and copies ran while one was open for 0% of the time, Pallas kernels for 16%

profile of v4, /device:TPU:0, one launch (start us, length us, event | category | flops | bytes accessed | tf_op | source)
XLA Modules:
  0.0 60.9 jit_solution(2274906249828076679)
XLA Ops:
  0.7 1.1 %copy-done.6 = bf16[8,32,576]{2,1,0:T(8,128)(2,1)S(1)} copy-done((bf16[8,32,576]{2,1,0:T(8,128)(2,1)S(1)}, bf16[8,32,576]{2,1,0:T(8,128)(2,1)}, u32[]{:S(2)}) %copy-start.6) | copy-done | bytes 294936
  2.0 0.7 %collective-permute-start = (bf16[1152,128]{1,0:T(8,128)(2,1)S(1)}, bf16[1152,128]{1,0:T(8,128)(2,1)S(1)}, u32[]{:S(2)}, u32[]{:S(2)}) collective-permute-start(bf16[1152,128]{1,0:T(8,128)(2,1)S(1)} %pack_queries.1.refs_0_), channel_id=1, source_target_pairs={{8,16},{12,20},{16,8},{20,12},{0,0},{4,4},{24,24},{28,28},{9,17},{... | collective-permute-start | bytes 884744 | tf_op jit(solution)/shard_map/ppermute | solution.py:609
  2.7 5.9 %collective-permute-start.2 = (bf16[1152,128]{1,0:T(8,128)(2,1)S(1)}, bf16[1152,128]{1,0:T(8,128)(2,1)S(1)}, u32[]{:S(2)}, u32[]{:S(2)}) collective-permute-start(bf16[1152,128]{1,0:T(8,128)(2,1)S(1)} %pack_queries.1.refs_0_), channel_id=1, source_target_pairs={{0,8},{4,12},{8,0},{12,4},{16,24},{20,28},{24,16},{28,20},{1,9},{5... | collective-permute-start | bytes 884744 | tf_op jit(solution)/shard_map/ppermute | solution.py:609
  8.6 3.2 %collective-permute-start.5 = (bf16[1152,128]{1,0:T(8,128)(2,1)S(1)}, bf16[1152,128]{1,0:T(8,128)(2,1)S(1)}, u32[]{:S(2)}, u32[]{:S(2)}) collective-permute-start(bf16[1152,128]{1,0:T(8,128)(2,1)S(1)} %pack_queries.1.refs_0_), channel_id=1, source_target_pairs={{0,24},{4,28},{24,0},{28,4},{1,25},{5,29},{25,1},{29,5},{2,26},{6,... | collective-permute-start | bytes 884744 | tf_op jit(solution)/shard_map/ppermute | solution.py:609
  11.9 1.2 %load_inputs.1 = (s32[64,128]{1,0:T(8,128)S(1)}, f32[64,32]{1,0:T(8,128)S(1)}, f32[1024,128]{1,0:T(8,128)S(1)}, bf16[16,64,128]{2,1,0:T(8,128)(2,1)S(1)}, bf16[1...) custom-call(s32[64]{0:T(128)S(1)} %copy-done.5, f32[32,64]{1,0:T(8,128)S(1)} %bitcast.5, ...), custom_call_target="tpu_custom_call" | custom-call | flops 1 | bytes 1 | tf_op jit(solution)/shard_map/load_inputs/pallas_call | solution.py:449
  13.1 3.7 %collective-permute-start.1 = (bf16[1152,128]{1,0:T(8,128)(2,1)S(1)}, bf16[1152,128]{1,0:T(8,128)(2,1)S(1)}, u32[]{:S(2)}, u32[]{:S(2)}) collective-permute-start(bf16[1152,128]{1,0:T(8,128)(2,1)S(1)} %collective-permute-done.inner_ref), channel_id=1, source_target_pairs={{0,16},{4,20},{24,8},{28,12},{8,0},{12,4},{16,24},{20,28},{1,17},{... | collective-permute-start | bytes 884744 | tf_op jit(solution)/shard_map/ppermute | solution.py:609
  16.9 1.8 %index_logits.1 = (f32[16,2048]{1,0:T(8,128)S(1)}, f32[1024,2048]{1,0:T(8,128)S(1)}, f32[16,128]{1,0:T(8,128)S(1)}) custom-call(s32[64,128]{1,0:T(8,128)S(1)} %get-tuple-element.39.length_ref, bf16[1024,128]{1,0:T(8,128)(2,1)S(1)} %bitcast.4, bf16[2048,128]{1,0:T(8,128)(2,1)S(1)} %get-tuple-element.41.key_ref, f32[1024,128]{1,0:T(8,128)S(1)} %get-tuple-element.42.weight_ref), custom_call_target="tpu_custom_call" | custom-call | flops 1 | bytes 1 | tf_op jit(solution)/shard_map/index_logits/pallas_call | solution.py:405
  19.3 1.9 %mass_own.1.own_ref = f32[16,2048]{1,0:T(8,128)S(1)} custom-call(s32[64,128]{1,0:T(8,128)S(1)} %get-tuple-element.39.length_ref, bf16[1152,128]{1,0:T(8,128)(2,1)S(1)} %pack_queries.1.refs_0_, bf16[1152,128]{1,0:T(8,128)(2,1)S(1)} %collective-permute-done.6.refs_1_, f32[64,32]{1,0:T(8,128)S(1)} %get-tuple-element.44.refs_4_.refs_2_.refs_6_.refs_1_.lse_ref, ...), custom_call_target="tpu_custom_call" | custom-call | flops 1 | bytes 1 | tf_op jit(solution)/shard_map/mass_own/pallas_call | solution.py:326
  21.2 1.9 %mass_near.1.near_ref = f32[16,2048]{1,0:T(8,128)S(1)} custom-call(s32[64,128]{1,0:T(8,128)S(1)} %get-tuple-element.39.length_ref, bf16[720,128]{1,0:T(8,128)(2,1)S(1)} %get-tuple-element.47.refs_0_, bf16[432,128]{1,0:T(8,128)(2,1)S(1)} %get-tuple-element.48.refs_1_, bf16[720,128]{1,0:T(8,128)(2,1)S(1)} %collective-permute-done.3.refs_2_, ...), custom_call_target="tpu_custom_call" | custom-call | flops 1 | bytes 1 | tf_op jit(solution)/shard_map/mass_near/pallas_call | solution.py:326
  24.5 0.7 %collective-permute-done.7.refs_3_ = bf16[384,128]{1,0:T(8,128)(2,1)S(1)} collective-permute-done((bf16[384,128]{1,0:T(8,128)(2,1)S(1)}, bf16[384,128]{1,0:T(8,128)(2,1)S(1)}, u32[]{:S(2)}, u32[]{:S(2)}) %collective-permute-start.7) | collective-permute-done | bytes 98336 | tf_op jit(solution)/shard_map/ppermute | solution.py:612
  25.7 1.9 %mass_across.1.far_ref = f32[16,2048]{1,0:T(8,128)S(1)} custom-call(s32[64,128]{1,0:T(8,128)S(1)} %get-tuple-element.39.length_ref, bf16[384,128]{1,0:T(8,128)(2,1)S(1)} %get-tuple-element.51.refs_0_, bf16[384,128]{1,0:T(8,128)(2,1)S(1)} %get-tuple-element.52.refs_1_, bf16[384,128]{1,0:T(8,128)(2,1)S(1)} %get-tuple-element.53.refs_2_, ...), custom_call_target="tpu_custom_call" | custom-call | flops 1 | bytes 1 | tf_op jit(solution)/shard_map/mass_across/pallas_call | solution.py:326
  27.6 0.7 %collective-permute-done.1.refs_0_ = bf16[1152,128]{1,0:T(8,128)(2,1)S(1)} collective-permute-done((bf16[1152,128]{1,0:T(8,128)(2,1)S(1)}, bf16[1152,128]{1,0:T(8,128)(2,1)S(1)}, u32[]{:S(2)}, u32[]{:S(2)}) %collective-permute-start.1) | collective-permute-done | bytes 294944 | tf_op jit(solution)/shard_map/ppermute | solution.py:609
  28.3 1.0 %mass_far.1.half_ref = f32[8,2048]{1,0:T(8,128)S(1)} custom-call(s32[64,128]{1,0:T(8,128)S(1)} %get-tuple-element.39.length_ref, bf16[1152,128]{1,0:T(8,128)(2,1)S(1)} %collective-permute-done.1.refs_0_, f32[64,32]{1,0:T(8,128)S(1)} %get-tuple-element.44.refs_4_.refs_2_.refs_6_.refs_1_.lse_ref, ...), custom_call_target="tpu_custom_call" | custom-call | flops 1 | bytes 1 | tf_op jit(solution)/shard_map/mass_far/pallas_call | solution.py:326
  29.9 1.1 %mass_and_share.1 = (f32[16,2048]{1,0:T(8,128)S(1)}, bf16[16,2048]{1,0:T(8,128)(2,1)S(1)}, bf16[16,2048]{1,0:T(8,128)(2,1)S(1)}, bf16[16,2048]{1,0:T(8,128)(2,1)S(1)}) custom-call(s32[64,128]{1,0:T(8,128)S(1)} %get-tuple-element.39.length_ref, bf16[1152,128]{1,0:T(8,128)(2,1)S(1)} %collective-permute-done.10.pack_ref, ...), custom_call_target="tpu_custom_call" | custom-call | flops 1 | bytes 1 | tf_op jit(solution)/shard_map/mass_and_share/pallas_call | solution.py:364
  31.0 2.5 %collective-permute-start.11 = (bf16[16,2048]{1,0:T(8,128)(2,1)S(1)}, bf16[16,2048]{1,0:T(8,128)(2,1)S(1)}, u32[]{:S(2)}, u32[]{:S(2)}) collective-permute-start(bf16[16,2048]{1,0:T(8,128)(2,1)S(1)} %get-tuple-element.56), channel_id=1, source_target_pairs={{0,3},{1,2},{2,1},{3,0},{4,7},{5,6},{6,5},{7,4},{8,11},{9,10},{10,... | collective-permute-start | bytes 196616 | tf_op jit(solution)/shard_map/ppermute | solution.py:615
  34.5 1.7 %collective-permute-done.11.refs_0_ = bf16[16,2048]{1,0:T(8,128)(2,1)S(1)} collective-permute-done((bf16[16,2048]{1,0:T(8,128)(2,1)S(1)}, bf16[16,2048]{1,0:T(8,128)(2,1)S(1)}, u32[]{:S(2)}, u32[]{:S(2)}) %collective-permute-start.11) | collective-permute-done | bytes 65568 | tf_op jit(solution)/shard_map/ppermute | solution.py:615
  36.2 1.5 %collective-permute-done.12.refs_1_ = bf16[16,2048]{1,0:T(8,128)(2,1)S(1)} collective-permute-done((bf16[16,2048]{1,0:T(8,128)(2,1)S(1)}, bf16[16,2048]{1,0:T(8,128)(2,1)S(1)}, u32[]{:S(2)}, u32[]{:S(2)}) %collective-permute-start.12) | collective-permute-done | bytes 65568 | tf_op jit(solution)/shard_map/ppermute | solution.py:615
  38.4 1.2 %collective-permute-done.14.got_ref = f32[16,128]{1,0:T(8,128)S(1)} collective-permute-done((f32[16,128]{1,0:T(8,128)S(1)}, f32[16,128]{1,0:T(8,128)S(1)}, u32[]{:S(2)}, u32[]{:S(2)}) %collective-permute-start.14) | collective-permute-done | bytes 8224 | tf_op jit(solution)/shard_map/ppermute | solution.py:612
  39.7 2.3 %collective-permute-start.15 = (f32[16,128]{1,0:T(8,128)S(1)}, f32[16,128]{1,0:T(8,128)S(1)}, u32[]{:S(2)}, u32[]{:S(2)}) collective-permute-start(f32[16,128]{1,0:T(8,128)S(1)} %pair_stats.1.refs_0_), channel_id=1, source_target_pairs={{0,24},{4,28},{8,16},{12,20},{16,8},{20,12},{24,0},{28,4},{1,25},{... | collective-permute-start | bytes 24584 | tf_op jit(solution)/shard_map/ppermute | solution.py:612
  42.4 1.7 %collective-permute-start.17 = (f32[16,128]{1,0:T(8,128)S(1)}, f32[16,128]{1,0:T(8,128)S(1)}, u32[]{:S(2)}, u32[]{:S(2)}) collective-permute-start(f32[16,128]{1,0:T(8,128)S(1)} %pair_stats.1.refs_0_), channel_id=1, source_target_pairs={{0,8},{4,12},{8,0},{12,4},{16,24},{20,28},{24,16},{28,20},{1,9},{5... | collective-permute-start | bytes 24584 | tf_op jit(solution)/shard_map/ppermute | solution.py:612
  44.1 1.1 %collective-permute-done.15.refs_1_ = f32[16,128]{1,0:T(8,128)S(1)} collective-permute-done((f32[16,128]{1,0:T(8,128)S(1)}, f32[16,128]{1,0:T(8,128)S(1)}, u32[]{:S(2)}, u32[]{:S(2)}) %collective-permute-start.15) | collective-permute-done | bytes 8224 | tf_op jit(solution)/shard_map/ppermute | solution.py:612
  45.2 1.5 %collective-permute-done.16.refs_2_ = f32[16,128]{1,0:T(8,128)S(1)} collective-permute-done((f32[16,128]{1,0:T(8,128)S(1)}, f32[16,128]{1,0:T(8,128)S(1)}, u32[]{:S(2)}, u32[]{:S(2)}) %collective-permute-start.16) | collective-permute-done | bytes 8224 | tf_op jit(solution)/shard_map/ppermute | solution.py:612
  46.6 2.2 %index_back.1 = (f32[512,128]{1,0:T(8,128)S(1)}, bf16[512,128]{1,0:T(8,128)(2,1)S(1)}, bf16[512,128]{1,0:T(8,128)(2,1)S(1)}, bf16[512,128]{1,0:T(8,128)(2,1)S(1)...) custom-call(s32[64,128]{1,0:T(8,128)S(1)} %get-tuple-element.39.length_ref, ...), custom_call_target="tpu_custom_call" | custom-call | flops 1 | bytes 1 | tf_op jit(solution)/shard_map/index_back/pallas_call | solution.py:544
  48.9 1.6 %collective-permute-start.18 = (bf16[512,128]{1,0:T(8,128)(2,1)S(1)}, bf16[512,128]{1,0:T(8,128)(2,1)S(1)}, u32[]{:S(2)}, u32[]{:S(2)}) collective-permute-start(bf16[512,128]{1,0:T(8,128)(2,1)S(1)} %get-tuple-element.65), channel_id=1, source_target_pairs={{0,3},{1,2},{2,1},{3,0},{4,7},{5,6},{6,5},{7,4},{8,11},{9,10},{10,... | collective-permute-start | bytes 393224 | tf_op jit(solution)/shard_map/ppermute | solution.py:615
  50.5 0.7 %collective-permute-start.19 = (bf16[512,128]{1,0:T(8,128)(2,1)S(1)}, bf16[512,128]{1,0:T(8,128)(2,1)S(1)}, u32[]{:S(2)}, u32[]{:S(2)}) collective-permute-start(bf16[512,128]{1,0:T(8,128)(2,1)S(1)} %get-tuple-element.66), channel_id=1, source_target_pairs={{0,2},{1,3},{2,0},{3,1},{4,6},{5,7},{6,4},{7,5},{8,10},{9,11},{10,... | collective-permute-start | bytes 393224 | tf_op jit(solution)/shard_map/ppermute | solution.py:615
  51.2 1.3 %collective-permute-start.20 = (bf16[512,128]{1,0:T(8,128)(2,1)S(1)}, bf16[512,128]{1,0:T(8,128)(2,1)S(1)}, u32[]{:S(2)}, u32[]{:S(2)}) collective-permute-start(bf16[512,128]{1,0:T(8,128)(2,1)S(1)} %get-tuple-element.67), channel_id=1, source_target_pairs={{0,1},{1,0},{2,3},{3,2},{4,5},{5,4},{6,7},{7,6},{8,9},{9,8},{10,11... | collective-permute-start | bytes 393224 | tf_op jit(solution)/shard_map/ppermute | solution.py:615
  52.5 2.0 %collective-permute-start.22 = (bf16[128,128]{1,0:T(8,128)(2,1)S(1)}, bf16[128,128]{1,0:T(8,128)(2,1)S(1)}, u32[]{:S(2)}, u32[]{:S(2)}) collective-permute-start(bf16[128,128]{1,0:T(8,128)(2,1)S(1)} %get-tuple-element.71), channel_id=1, source_target_pairs={{0,24},{4,28},{8,16},{12,20},{16,8},{20,12},{24,0},{28,4},{1,25},{... | collective-permute-start | bytes 98312 | tf_op jit(solution)/shard_map/ppermute | solution.py:612
  55.2 1.1 %collective-permute-done.18.refs_1_ = bf16[512,128]{1,0:T(8,128)(2,1)S(1)} collective-permute-done((bf16[512,128]{1,0:T(8,128)(2,1)S(1)}, bf16[512,128]{1,0:T(8,128)(2,1)S(1)}, u32[]{:S(2)}, u32[]{:S(2)}) %collective-permute-start.18) | collective-permute-done | bytes 131104 | tf_op jit(solution)/shard_map/ppermute | solution.py:615
  56.2 1.1 %collective-permute-start.24 = (bf16[128,128]{1,0:T(8,128)(2,1)S(1)}, bf16[128,128]{1,0:T(8,128)(2,1)S(1)}, u32[]{:S(2)}, u32[]{:S(2)}) collective-permute-start(bf16[128,128]{1,0:T(8,128)(2,1)S(1)} %get-tuple-element.73), channel_id=1, source_target_pairs={{0,8},{4,12},{8,0},{12,4},{16,24},{20,28},{24,16},{28,20},{1,9},{5... | collective-permute-start | bytes 98312 | tf_op jit(solution)/shard_map/ppermute | solution.py:612
  57.4 1.2 %collective-permute-done.19.refs_2_ = bf16[512,128]{1,0:T(8,128)(2,1)S(1)} collective-permute-done((bf16[512,128]{1,0:T(8,128)(2,1)S(1)}, bf16[512,128]{1,0:T(8,128)(2,1)S(1)}, u32[]{:S(2)}, u32[]{:S(2)}) %collective-permute-start.19) | collective-permute-done | bytes 131104 | tf_op jit(solution)/shard_map/ppermute | solution.py:615
  58.7 1.0 %collective-permute-done.23.refs_6_ = bf16[128,128]{1,0:T(8,128)(2,1)S(1)} collective-permute-done((bf16[128,128]{1,0:T(8,128)(2,1)S(1)}, bf16[128,128]{1,0:T(8,128)(2,1)S(1)}, u32[]{:S(2)}, u32[]{:S(2)}) %collective-permute-start.23) | collective-permute-done | bytes 32800 | tf_op jit(solution)/shard_map/ppermute | solution.py:612
  60.2 0.8 %last_sums.1 = (f32[16,8,128]{2,1,0:T(8,128)}, f32[512,128]{1,0:T(8,128)}) custom-call(f32[512,128]{1,0:T(8,128)S(1)} %get-tuple-element.64.refs_0_, bf16[512,128]{1,0:T(8,128)(2,1)S(1)} %collective-permute-done.18.refs_1_, bf16[512,128]{1,0:T(8,128)(2,1)S(1)} %collective-permute-done.19.refs_2_, bf16[512,128]{1,0:T(8,128)(2,1)S(1)} %collective-permute-done.20.refs_3_, ...), custom_call_target="tpu_custom_call" | custom-call | flops 1 | bytes 1 | tf_op jit(solution)/shard_map/last_sums/pallas_call | solution.py:584
  (47 shorter events, 6.8 us)
Async XLA Ops:
  0.6 11.2 %copy-start = (bf16[2048,576]{0,1:T(8,128)(2,1)S(1)}, bf16[2048,576]{0,1:T(8,128)(2,1)}, u32[]{:S(2)}) copy-start(bf16[2048,576]{0,1:T(8,128)(2,1)} %param.8) | copy-start | bytes 7077892
  0.6 11.2 %copy-start.3 = (f32[64,32]{0,1:T(8,128)S(1)}, f32[64,32]{0,1:T(8,128)}, u32[]{:S(2)}) copy-start(f32[64,32]{0,1:T(8,128)} %param.9) | copy-start | bytes 24580
  0.7 11.2 %copy-start.5 = (s32[64]{0:T(128)S(1)}, s32[64]{0:T(128)}, u32[]{:S(2)}) copy-start(s32[64]{0:T(128)} %length_ref.1) | copy-start | bytes 772
  0.7 11.2 %copy-start.2 = (bf16[16,64,128]{2,1,0:T(8,128)(2,1)S(1)}, bf16[16,64,128]{2,1,0:T(8,128)(2,1)}, u32[]{:S(2)}) copy-start(bf16[16,64,128]{2,1,0:T(8,128)(2,1)} %query_hbm.1) | copy-start | bytes 786436
  0.7 11.2 %copy-start.1 = (bf16[2048,128]{1,0:T(8,128)(2,1)S(1)}, bf16[2048,128]{1,0:T(8,128)(2,1)}, u32[]{:S(2)}) copy-start(bf16[2048,128]{1,0:T(8,128)(2,1)} %key_hbm.1) | copy-start | bytes 1572868
  0.7 1.1 %copy-start.6 = (bf16[8,32,576]{2,1,0:T(8,128)(2,1)S(1)}, bf16[8,32,576]{2,1,0:T(8,128)(2,1)}, u32[]{:S(2)}) copy-start(bf16[8,32,576]{2,1,0:T(8,128)(2,1)} %query_ref.1) | copy-start | bytes 884740
  1.8 10.1 %copy-start.4 = (f32[16,64]{1,0:T(8,128)S(1)}, f32[16,64]{1,0:T(8,128)}, u32[]{:S(2)}) copy-start(f32[16,64]{1,0:T(8,128)} %weight_ref.1) | copy-start | bytes 12292
  2.0 11.1 %collective-permute-start = (bf16[1152,128]{1,0:T(8,128)(2,1)S(1)}, bf16[1152,128]{1,0:T(8,128)(2,1)S(1)}, u32[]{:S(2)}, u32[]{:S(2)}) collective-permute-start(bf16[1152,128]{1,0:T(8,128)(2,1)S(1)} %pack_queries.1.refs_0_), channel_id=1, source_target_pairs={{8,16},{12,20},{16,8},{20,12},{0,0},{4,4},{24,24},{28,28},{9,17},{... | collective-permute-start | bytes 884744 | tf_op jit(solution)/shard_map/ppermute | solution.py:609
  2.7 16.0 %collective-permute-start.2 = (bf16[1152,128]{1,0:T(8,128)(2,1)S(1)}, bf16[1152,128]{1,0:T(8,128)(2,1)S(1)}, u32[]{:S(2)}, u32[]{:S(2)}) collective-permute-start(bf16[1152,128]{1,0:T(8,128)(2,1)S(1)} %pack_queries.1.refs_0_), channel_id=1, source_target_pairs={{0,8},{4,12},{8,0},{12,4},{16,24},{20,28},{24,16},{28,20},{1,9},{5... | collective-permute-start | bytes 884744 | tf_op jit(solution)/shard_map/ppermute | solution.py:609
  8.6 10.7 %collective-permute-start.6 = (bf16[1152,128]{1,0:T(8,128)(2,1)S(1)}, bf16[1152,128]{1,0:T(8,128)(2,1)S(1)}, u32[]{:S(2)}, u32[]{:S(2)}) collective-permute-start(bf16[1152,128]{1,0:T(8,128)(2,1)S(1)} %pack_queries.1.refs_0_), channel_id=1, source_target_pairs={{0,4},{4,0},{8,12},{12,8},{16,20},{20,16},{24,28},{28,24},{1,5},{5... | collective-permute-start | bytes 884744 | tf_op jit(solution)/shard_map/ppermute | solution.py:612
  8.6 15.1 %collective-permute-start.5 = (bf16[1152,128]{1,0:T(8,128)(2,1)S(1)}, bf16[1152,128]{1,0:T(8,128)(2,1)S(1)}, u32[]{:S(2)}, u32[]{:S(2)}) collective-permute-start(bf16[1152,128]{1,0:T(8,128)(2,1)S(1)} %pack_queries.1.refs_0_), channel_id=1, source_target_pairs={{0,24},{4,28},{24,0},{28,4},{1,25},{5,29},{25,1},{29,5},{2,26},{6,... | collective-permute-start | bytes 884744 | tf_op jit(solution)/shard_map/ppermute | solution.py:609
  13.1 15.2 %collective-permute-start.1 = (bf16[1152,128]{1,0:T(8,128)(2,1)S(1)}, bf16[1152,128]{1,0:T(8,128)(2,1)S(1)}, u32[]{:S(2)}, u32[]{:S(2)}) collective-permute-start(bf16[1152,128]{1,0:T(8,128)(2,1)S(1)} %collective-permute-done.inner_ref), channel_id=1, source_target_pairs={{0,16},{4,20},{24,8},{28,12},{8,0},{12,4},{16,24},{20,28},{1,17},{... | collective-permute-start | bytes 884744 | tf_op jit(solution)/shard_map/ppermute | solution.py:609
  18.7 2.5 %collective-permute-start.3 = (bf16[720,128]{1,0:T(8,128)(2,1)S(1)}, bf16[720,128]{1,0:T(8,128)(2,1)S(1)}, u32[]{:S(2)}, u32[]{:S(2)}) collective-permute-start(bf16[720,128]{1,0:T(8,128)(2,1)S(1)} %get-tuple-element.47.refs_0_), channel_id=1, source_target_pairs={{0,4},{4,0},{8,12},{12,8},{16,20},{20,16},{24,28},{28,24},{1,5},{5... | collective-permute-start | bytes 552968 | tf_op jit(solution)/shard_map/ppermute | solution.py:612
  18.8 2.4 %collective-permute-start.4 = (bf16[432,128]{1,0:T(8,128)(2,1)S(1)}, bf16[432,128]{1,0:T(8,128)(2,1)S(1)}, u32[]{:S(2)}, u32[]{:S(2)}) collective-permute-start(bf16[432,128]{1,0:T(8,128)(2,1)S(1)} %get-tuple-element.48.refs_1_), channel_id=1, source_target_pairs={{0,4},{4,0},{8,12},{12,8},{16,20},{20,16},{24,28},{28,24},{1,5},{5... | collective-permute-start | bytes 331784 | tf_op jit(solution)/shard_map/ppermute | solution.py:612
  23.9 1.4 %collective-permute-start.7 = (bf16[384,128]{1,0:T(8,128)(2,1)S(1)}, bf16[384,128]{1,0:T(8,128)(2,1)S(1)}, u32[]{:S(2)}, u32[]{:S(2)}) collective-permute-start(bf16[384,128]{1,0:T(8,128)(2,1)S(1)} %get-tuple-element.51.refs_0_), channel_id=1, source_target_pairs={{0,4},{4,0},{8,12},{12,8},{16,20},{20,16},{24,28},{28,24},{1,5},{5... | collective-permute-start | bytes 294920 | tf_op jit(solution)/shard_map/ppermute | solution.py:612
  23.9 1.4 %collective-permute-start.8 = (bf16[384,128]{1,0:T(8,128)(2,1)S(1)}, bf16[384,128]{1,0:T(8,128)(2,1)S(1)}, u32[]{:S(2)}, u32[]{:S(2)}) collective-permute-start(bf16[384,128]{1,0:T(8,128)(2,1)S(1)} %get-tuple-element.52.refs_1_), channel_id=1, source_target_pairs={{0,4},{4,0},{8,12},{12,8},{16,20},{20,16},{24,28},{28,24},{1,5},{5... | collective-permute-start | bytes 294920 | tf_op jit(solution)/shard_map/ppermute | solution.py:612
  24.4 1.3 %collective-permute-start.9 = (bf16[384,128]{1,0:T(8,128)(2,1)S(1)}, bf16[384,128]{1,0:T(8,128)(2,1)S(1)}, u32[]{:S(2)}, u32[]{:S(2)}) collective-permute-start(bf16[384,128]{1,0:T(8,128)(2,1)S(1)} %get-tuple-element.53.refs_2_), channel_id=1, source_target_pairs={{0,4},{4,0},{8,12},{12,8},{16,20},{20,16},{24,28},{28,24},{1,5},{5... | collective-permute-start | bytes 294920 | tf_op jit(solution)/shard_map/ppermute | solution.py:612
  28.3 1.6 %collective-permute-start.10 = (bf16[1152,128]{1,0:T(8,128)(2,1)S(1)}, bf16[1152,128]{1,0:T(8,128)(2,1)S(1)}, u32[]{:S(2)}, u32[]{:S(2)}) collective-permute-start(bf16[1152,128]{1,0:T(8,128)(2,1)S(1)} %collective-permute-done.1.refs_0_), channel_id=1, source_target_pairs={{0,4},{4,0},{8,12},{12,8},{16,20},{20,16},{24,28},{28,24},{1,5},{5... | collective-permute-start | bytes 884744 | tf_op jit(solution)/shard_map/ppermute | solution.py:612
  31.0 5.3 %collective-permute-start.11 = (bf16[16,2048]{1,0:T(8,128)(2,1)S(1)}, bf16[16,2048]{1,0:T(8,128)(2,1)S(1)}, u32[]{:S(2)}, u32[]{:S(2)}) collective-permute-start(bf16[16,2048]{1,0:T(8,128)(2,1)S(1)} %get-tuple-element.56), channel_id=1, source_target_pairs={{0,3},{1,2},{2,1},{3,0},{4,7},{5,6},{6,5},{7,4},{8,11},{9,10},{10,... | collective-permute-start | bytes 196616 | tf_op jit(solution)/shard_map/ppermute | solution.py:615
  33.5 4.3 %collective-permute-start.12 = (bf16[16,2048]{1,0:T(8,128)(2,1)S(1)}, bf16[16,2048]{1,0:T(8,128)(2,1)S(1)}, u32[]{:S(2)}, u32[]{:S(2)}) collective-permute-start(bf16[16,2048]{1,0:T(8,128)(2,1)S(1)} %get-tuple-element.57), channel_id=1, source_target_pairs={{0,2},{1,3},{2,0},{3,1},{4,6},{5,7},{6,4},{7,5},{8,10},{9,11},{10,... | collective-permute-start | bytes 196616 | tf_op jit(solution)/shard_map/ppermute | solution.py:615
  34.0 4.3 %collective-permute-start.13 = (bf16[16,2048]{1,0:T(8,128)(2,1)S(1)}, bf16[16,2048]{1,0:T(8,128)(2,1)S(1)}, u32[]{:S(2)}, u32[]{:S(2)}) collective-permute-start(bf16[16,2048]{1,0:T(8,128)(2,1)S(1)} %get-tuple-element.58), channel_id=1, source_target_pairs={{0,1},{1,0},{2,3},{3,2},{4,5},{5,4},{6,7},{7,6},{8,9},{9,8},{10,11... | collective-permute-start | bytes 196616 | tf_op jit(solution)/shard_map/ppermute | solution.py:615
  38.4 1.2 %collective-permute-start.14 = (f32[16,128]{1,0:T(8,128)S(1)}, f32[16,128]{1,0:T(8,128)S(1)}, u32[]{:S(2)}, u32[]{:S(2)}) collective-permute-start(f32[16,128]{1,0:T(8,128)S(1)} %get-tuple-element.63.own_ref), channel_id=1, source_target_pairs={{0,4},{4,0},{8,12},{12,8},{16,20},{20,16},{24,28},{28,24},{1,5},{5... | collective-permute-start | bytes 24584 | tf_op jit(solution)/shard_map/ppermute | solution.py:612
  39.7 5.5 %collective-permute-start.15 = (f32[16,128]{1,0:T(8,128)S(1)}, f32[16,128]{1,0:T(8,128)S(1)}, u32[]{:S(2)}, u32[]{:S(2)}) collective-permute-start(f32[16,128]{1,0:T(8,128)S(1)} %pair_stats.1.refs_0_), channel_id=1, source_target_pairs={{0,24},{4,28},{8,16},{12,20},{16,8},{20,12},{24,0},{28,4},{1,25},{... | collective-permute-start | bytes 24584 | tf_op jit(solution)/shard_map/ppermute | solution.py:612
  42.1 4.6 %collective-permute-start.16 = (f32[16,128]{1,0:T(8,128)S(1)}, f32[16,128]{1,0:T(8,128)S(1)}, u32[]{:S(2)}, u32[]{:S(2)}) collective-permute-start(f32[16,128]{1,0:T(8,128)S(1)} %pair_stats.1.refs_0_), channel_id=1, source_target_pairs={{0,16},{4,20},{8,24},{12,28},{16,0},{20,4},{24,8},{28,12},{1,17},{... | collective-permute-start | bytes 24584 | tf_op jit(solution)/shard_map/ppermute | solution.py:612
  42.4 4.2 %collective-permute-start.17 = (f32[16,128]{1,0:T(8,128)S(1)}, f32[16,128]{1,0:T(8,128)S(1)}, u32[]{:S(2)}, u32[]{:S(2)}) collective-permute-start(f32[16,128]{1,0:T(8,128)S(1)} %pair_stats.1.refs_0_), channel_id=1, source_target_pairs={{0,8},{4,12},{8,0},{12,4},{16,24},{20,28},{24,16},{28,20},{1,9},{5... | collective-permute-start | bytes 24584 | tf_op jit(solution)/shard_map/ppermute | solution.py:612
  48.9 3.6 %collective-permute-start.21 = (bf16[4,128,128]{2,1,0:T(8,128)(2,1)S(1)}, bf16[4,128,128]{2,1,0:T(8,128)(2,1)S(1)}, u32[]{:S(2)}, u32[]{:S(2)}) collective-permute-start(bf16[4,128,128]{2,1,0:T(8,128)(2,1)S(1)} %get-tuple-element.69), channel_id=1, source_target_pairs={{0,4},{4,0},{8,12},{12,8},{16,20},{20,16},{24,28},{28,24},{1,5},{5... | collective-permute-start | bytes 393224 | tf_op jit(solution)/shard_map/ppermute | solution.py:612
  48.9 7.3 %collective-permute-start.18 = (bf16[512,128]{1,0:T(8,128)(2,1)S(1)}, bf16[512,128]{1,0:T(8,128)(2,1)S(1)}, u32[]{:S(2)}, u32[]{:S(2)}) collective-permute-start(bf16[512,128]{1,0:T(8,128)(2,1)S(1)} %get-tuple-element.65), channel_id=1, source_target_pairs={{0,3},{1,2},{2,1},{3,0},{4,7},{5,6},{6,5},{7,4},{8,11},{9,10},{10,... | collective-permute-start | bytes 393224 | tf_op jit(solution)/shard_map/ppermute | solution.py:615
  50.5 8.1 %collective-permute-start.19 = (bf16[512,128]{1,0:T(8,128)(2,1)S(1)}, bf16[512,128]{1,0:T(8,128)(2,1)S(1)}, u32[]{:S(2)}, u32[]{:S(2)}) collective-permute-start(bf16[512,128]{1,0:T(8,128)(2,1)S(1)} %get-tuple-element.66), channel_id=1, source_target_pairs={{0,2},{1,3},{2,0},{3,1},{4,6},{5,7},{6,4},{7,5},{8,10},{9,11},{10,... | collective-permute-start | bytes 393224 | tf_op jit(solution)/shard_map/ppermute | solution.py:615
  51.2 7.4 %collective-permute-start.20 = (bf16[512,128]{1,0:T(8,128)(2,1)S(1)}, bf16[512,128]{1,0:T(8,128)(2,1)S(1)}, u32[]{:S(2)}, u32[]{:S(2)}) collective-permute-start(bf16[512,128]{1,0:T(8,128)(2,1)S(1)} %get-tuple-element.67), channel_id=1, source_target_pairs={{0,1},{1,0},{2,3},{3,2},{4,5},{5,4},{6,7},{7,6},{8,9},{9,8},{10,11... | collective-permute-start | bytes 393224 | tf_op jit(solution)/shard_map/ppermute | solution.py:615
  52.5 6.1 %collective-permute-start.22 = (bf16[128,128]{1,0:T(8,128)(2,1)S(1)}, bf16[128,128]{1,0:T(8,128)(2,1)S(1)}, u32[]{:S(2)}, u32[]{:S(2)}) collective-permute-start(bf16[128,128]{1,0:T(8,128)(2,1)S(1)} %get-tuple-element.71), channel_id=1, source_target_pairs={{0,24},{4,28},{8,16},{12,20},{16,8},{20,12},{24,0},{28,4},{1,25},{... | collective-permute-start | bytes 98312 | tf_op jit(solution)/shard_map/ppermute | solution.py:612
  54.5 5.2 %collective-permute-start.23 = (bf16[128,128]{1,0:T(8,128)(2,1)S(1)}, bf16[128,128]{1,0:T(8,128)(2,1)S(1)}, u32[]{:S(2)}, u32[]{:S(2)}) collective-permute-start(bf16[128,128]{1,0:T(8,128)(2,1)S(1)} %get-tuple-element.72), channel_id=1, source_target_pairs={{0,16},{4,20},{8,24},{12,28},{16,0},{20,4},{24,8},{28,12},{1,17},{... | collective-permute-start | bytes 98312 | tf_op jit(solution)/shard_map/ppermute | solution.py:612
  56.2 3.9 %collective-permute-start.24 = (bf16[128,128]{1,0:T(8,128)(2,1)S(1)}, bf16[128,128]{1,0:T(8,128)(2,1)S(1)}, u32[]{:S(2)}, u32[]{:S(2)}) collective-permute-start(bf16[128,128]{1,0:T(8,128)(2,1)S(1)} %get-tuple-element.73), channel_id=1, source_target_pairs={{0,8},{4,12},{8,0},{12,4},{16,24},{20,28},{24,16},{28,20},{1,9},{5... | collective-permute-start | bytes 98312 | tf_op jit(solution)/shard_map/ppermute | solution.py:612

commit v5 on v2

--- a/solution.py
+++ b/solution.py
@@ -15,6 +15,7 @@
 lanes = 128
 vmem_bytes = 20 * 1024 * 1024
 most_bytes = 60 * 1024 * 1024
+load_bytes = 58 * 1024 * 1024
 
 def joined(part, axis, combine):
     gathered = jax.tree.map(lambda a: lax.all_gather(a, axis), part)
@@ -135,13 +136,13 @@
     return (out_query, out_key)
 
 
-def local_call(kernel, out_shape, name, grid=None, in_specs=None, out_specs=None, scratch=(), flops=0, moved=0, room=vmem_bytes):
+def local_call(kernel, out_shape, name, grid=None, in_specs=None, out_specs=None, scratch=(), flops=1, moved=0, room=vmem_bytes):
     settings = dict(
         out_shape=out_shape,
         scratch_shapes=list(scratch),
         name=name,
         compiler_params=pltpu.CompilerParams(vmem_limit_bytes=room),
-        cost_estimate=pl.CostEstimate(flops=flops, bytes_accessed=moved, transcendentals=0),
+        cost_estimate=pl.CostEstimate(flops=flops, bytes_accessed=1, transcendentals=0),
     )
     if grid is not None:
         settings["grid"] = grid
@@ -181,78 +182,92 @@
     return pl.BlockSpec(memory_space=pltpu.HBM)
 
 
-def pack_kernel(query_ref, out_ref):
+def head_blocks(heads):
+    first = heads * 5 // 8
+    return ((0, first), (first, heads - first))
+
+
+def packed_rows(rows, heads, width):
+    return rows * heads * width // lanes
+
+
+def pack_kernel(query_ref, out_ref, *block_refs):
     rows, heads, width = query_ref.shape
-    total = rows * heads
     columns = width // lanes
-    stacked = jnp.swapaxes(query_ref[...].astype(jnp.float32), 0, 1).reshape(total, width)
-    for i in range(columns):
-        out_ref[i * total : (i + 1) * total, :] = stacked[:, i * lanes : (i + 1) * lanes].astype(jnp.bfloat16)
-    rest = stacked[:, columns * lanes :]
-    out_ref[columns * total :, :] = jnp.concatenate([rest[: total // 2], rest[total // 2 :]], axis=1).astype(
-        jnp.bfloat16
-    )
+    stacked = jnp.swapaxes(query_ref[...].astype(jnp.float32), 0, 1).reshape(rows * heads, width)
+    begin = 0
+    for (first, count), block_ref in zip(head_blocks(heads), block_refs):
+        total = rows * count
+        block = stacked[rows * first : rows * first + total]
+        rest = block[:, columns * lanes :]
+        pieces = [block[:, i * lanes : (i + 1) * lanes] for i in range(columns)]
+        pieces.append(jnp.concatenate([rest[: total // 2], rest[total // 2 :]], axis=1))
+        place = 0
+        for piece in pieces:
+            piece = piece.astype(jnp.bfloat16)
+            size = piece.shape[0]
+            out_ref[begin + place : begin + place + size, :] = piece
+            block_ref[place : place + size, :] = piece
+            place += size
+        begin += place
 
 
 def packed_queries(queries):
     rows, heads, width = queries.shape
+    blocks = [bf16((packed_rows(rows, count, width), lanes)) for _, count in head_blocks(heads)]
     return local_call(
         pack_kernel,
-        bf16((rows * heads * width // lanes, lanes)),
+        [bf16((packed_rows(rows, heads, width), lanes))] + blocks,
         "pack_queries",
         in_specs=[whole()],
-        out_specs=whole(),
-        flops=2 * queries.size * queries.size // width,
+        out_specs=[whole()] * (1 + len(blocks)),
+        flops=30_000_000_000,
     )(queries)
 
 
-def pick_kernel(own_ref, got_ref, out_ref):
+def pick_kernel(ends_ref, *refs):
+    inner_refs, out_ref = refs[:-1], refs[-1]
     plane, _, _ = place()
     inner = (plane == 1) | (plane == 2)
 
     @pl.when(inner)
     def _():
-        out_ref[...] = got_ref[...]
+        begin = 0
+        for inner_ref in inner_refs:
+            rows = inner_ref.shape[0]
+            out_ref[begin : begin + rows, :] = inner_ref[...]
+            begin += rows
 
     @pl.when(jnp.logical_not(inner))
     def _():
-        out_ref[...] = own_ref[...]
-
-
-def picked(own, got):
-    return local_call(
-        pick_kernel, bf16(own.shape), "pick_queries", in_specs=[whole()] * 2, out_specs=whole(), moved=4 * own.size
-    )(own, got)
-
-
-def unpack(packed, wide_ref, slot, total, width):
+        out_ref[...] = ends_ref[...]
+
+
+def picked(ends, inner):
+    return local_call(
+        pick_kernel,
+        bf16(ends.shape),
+        "pick_queries",
+        in_specs=[whole()] * (1 + len(inner)),
+        out_specs=whole(),
+    )(ends, *inner)
+
+
+def unpack(packed_ref, begin, wide_ref, row, total):
+    width = wide_ref.shape[1]
     columns = width // lanes
     half = total // 2
     for i in range(columns):
-        wide_ref[slot * total : (slot + 1) * total, i * lanes : (i + 1) * lanes] = packed[
-            i * total : (i + 1) * total, :
+        wide_ref[row : row + total, i * lanes : (i + 1) * lanes] = packed_ref[
+            begin + i * total : begin + (i + 1) * total, :
         ]
-    rest = packed[columns * total :, :]
-    wide_ref[slot * total : slot * total + half, columns * lanes :] = rest[:, : lanes // 2]
-    wide_ref[slot * total + half : (slot + 1) * total, columns * lanes :] = rest[:, lanes // 2 :]
+    rest = packed_ref[begin + columns * total : begin + columns * total + half, :]
+    wide_ref[row : row + half, columns * lanes :] = rest[:, : lanes // 2]
+    wide_ref[row + half : row + total, columns * lanes :] = rest[:, lanes // 2 :]
 
 
 def widened(column, width):
     return jnp.concatenate([column] * (width // lanes), axis=1)
-
-
-def shard_mass(length_ref, wide_ref, slot, lse, key_ref, context, rows, heads, first, tile):
-    total = rows * heads
-    scores = jnp.dot(
-        wide_ref[slot * total : (slot + 1) * total, :],
-        key_ref[:, first : first + tile],
-        preferred_element_type=jnp.float32,
-    )
-    summed = jnp.zeros((rows, tile), jnp.float32)
-    for h in range(heads):
-        summed = summed + jnp.exp2(scores[h * rows : (h + 1) * rows] * (main_scale * log2_e) - lse[:, h : h + 1])
-    visible = visible_tile(length_ref, context, rows, first, tile, key_ref.shape[1])
-    return jnp.where(visible, summed, 0.0)
 
 
 def rows_at(ref, index, rows):
@@ -264,84 +279,87 @@
     return positions < widened(rows_at(length_ref, block, rows), width)
 
 
-def mass_kernel(flip, places, rows, heads, length_ref, *refs):
-    count = len(places)
-    packs = refs[:count]
-    lse_ref, key_ref, out_ref, wide_ref = refs[len(packs) :]
-    width, key_count = key_ref.shape
+def chip_mass(length_ref, wide_ref, lse_ref, own_key_ref, pair_key_ref, context, heads, out_ref, before_ref=None):
+    width, key_count = own_key_ref.shape
+    first_head, head_count = heads
+    rows = wide_ref.shape[0] // head_count
     tile = math.gcd(key_count, 512)
-    total = rows * heads
-    own_plane, own_core, _ = place()
-    plane = own_plane ^ flip
-    for n, other in enumerate(places):
-        unpack(packs[n][...], wide_ref, n, total, width)
-        core = own_core ^ other
-        context = 2 * plane + core
-        lse = rows_at(lse_ref, context, rows)
+    plane, core, _ = place()
+    lse = rows_at(lse_ref, context, rows)
+    column = widened(rows_at(length_ref, context, rows), tile)
+    spread = lax.broadcasted_iota(jnp.int32, (rows, tile), 1)
+    for key_ref, half in ((own_key_ref, core), (pair_key_ref, 1 - core)):
         for first in range(0, key_count, tile):
-            mass = shard_mass(length_ref, wide_ref, n, lse, key_ref, context, rows, heads, first, tile)
-            if count == 1:
-                out_ref[:, first : first + tile] = mass
-            else:
-                out_ref[pl.ds(pl.multiple_of(core * rows, rows), rows), first : first + tile] = mass
-
-
-def chunk_mass(lengths, packs, lse, keys, flip, places, rows, heads, name):
-    width, key_count = keys.shape
-    count = len(places)
-    total = rows * heads
-    return local_call(
-        functools.partial(mass_kernel, flip, places, rows, heads),
-        f32((count * rows, key_count)),
+            scores = jnp.dot(wide_ref[...], key_ref[:, first : first + tile], preferred_element_type=jnp.float32)
+            summed = jnp.zeros((rows, tile), jnp.float32)
+            for h in range(head_count):
+                summed = summed + jnp.exp2(
+                    scores[h * rows : (h + 1) * rows] * (main_scale * log2_e)
+                    - lse[:, first_head + h : first_head + h + 1]
+                )
+            visible = (2 * plane + half) * key_count + first + spread < column
+            mass = jnp.where(visible, summed, 0.0)
+            columns = pl.ds(pl.multiple_of(half * key_count + first, tile), tile)
+            if before_ref is not None:
+                mass = mass + before_ref[:, columns]
+            out_ref[:, columns] = mass
+
+
+def mass_kernel(flip, blocks, length_ref, pack_ref, lse_ref, own_key_ref, pair_key_ref, out_ref, wide_ref):
+    plane, core, _ = place()
+    heads = (blocks[0][0], sum(count for _, count in blocks))
+    rows = wide_ref.shape[0] // heads[1]
+    begin = row = 0
+    for _, count in blocks:
+        unpack(pack_ref, begin, wide_ref, row, rows * count)
+        begin += packed_rows(rows, count, wide_ref.shape[1])
+        row += rows * count
+    chip_mass(length_ref, wide_ref, lse_ref, own_key_ref, pair_key_ref, 2 * (plane ^ flip) + core, heads, out_ref)
+
+
+def chunk_mass(lengths, pack, lse, keys, flip, blocks, rows, name, flops=1):
+    width, key_count = keys[0].shape
+    total = rows * sum(count for _, count in blocks)
+    return local_call(
+        functools.partial(mass_kernel, flip, blocks),
+        f32((rows, 2 * key_count)),
         name,
-        in_specs=[whole()] * (len(packs) + 3),
+        in_specs=[whole()] * 5,
         out_specs=whole(),
-        scratch=[pltpu.VMEM((count * total, width), jnp.bfloat16)],
-        flops=2 * count * total * key_count * width,
-        moved=2 * keys.size,
-    )(lengths, *packs, lse, keys)
-
-
-def share_kernel(rows, heads, length_ref, pack_ref, lse_ref, own_ref, near_ref, far_ref, half_ref, key_ref, *refs):
+        scratch=[pltpu.VMEM((total, width), jnp.bfloat16)],
+        flops=flops,
+    )(lengths, pack, lse, *keys)
+
+
+def share_kernel(
+    heads, length_ref, pack_ref, lse_ref, own_key_ref, pair_key_ref, own_ref, near_ref, across_ref, before_ref, *refs
+):
     outs = refs[:-2]
     wide_ref, chunks_ref = refs[-2:]
-    width, key_count = key_ref.shape
-    tile = math.gcd(key_count, 512)
-    total = rows * heads
-    unpack(pack_ref[...], wide_ref, 0, total, width)
     plane, core, group = place()
-    other = 1 - core
-    context = 2 * (plane ^ 2) + other
-    lse = rows_at(lse_ref, context, rows)
+    unpack(pack_ref, 0, wide_ref, 0, wide_ref.shape[0])
     chunks_ref[0] = own_ref[...]
     chunks_ref[1] = near_ref[...]
-    chunks_ref[3] = far_ref[...]
-    chunks_ref[2, pl.ds(pl.multiple_of(core * rows, rows), rows), :] = half_ref[...]
-    for first in range(0, key_count, tile):
-        chunks_ref[2, pl.ds(pl.multiple_of(other * rows, rows), rows), first : first + tile] = shard_mass(
-            length_ref, wide_ref, 0, lse, key_ref, context, rows, heads, first, tile
-        )
+    chunks_ref[3] = across_ref[...]
+    chip_mass(
+        length_ref, wide_ref, lse_ref, own_key_ref, pair_key_ref, 2 * (plane ^ 2) + core, heads, chunks_ref.at[2],
+        before_ref,
+    )
     for e, out_ref in enumerate(outs):
         out_ref[...] = chunks_ref[plane ^ group ^ e].astype(out_ref.dtype)
 
 
-def shared_mass(lengths, pack, lse, own, near, far, half, keys, rows, heads, partners):
-    width, key_count = keys.shape
-    total = rows * heads
-    both = 2 * rows
-    return local_call(
-        functools.partial(share_kernel, rows, heads),
-        [f32((both, key_count))] + [bf16((both, key_count))] * (partners - 1),
+def shared_mass(lengths, pack, lse, keys, own, near, across, before, heads, partners):
+    width, _ = keys[0].shape
+    rows, both = own.shape
+    return local_call(
+        functools.partial(share_kernel, heads),
+        [f32((rows, both))] + [bf16((rows, both))] * (partners - 1),
         "mass_and_share",
-        in_specs=[whole()] * 8,
+        in_specs=[whole()] * 9,
         out_specs=[whole()] * partners,
-        scratch=[
-            pltpu.VMEM((total, width), jnp.bfloat16),
-            pltpu.VMEM((4, both, key_count), jnp.float32),
-        ],
-        flops=2 * total * key_count * width,
-        moved=2 * keys.size,
-    )(lengths, pack, lse, own, near, far, half, keys)
+        scratch=[pltpu.VMEM((rows * heads[1], width), jnp.bfloat16), pltpu.VMEM((4, rows, both), jnp.float32)],
+    )(lengths, pack, lse, *keys, own, near, across, before)
 
 
 def logits_kernel(length_ref, query_ref, key_ref, weight_ref, logits_ref, masked_ref, stats_ref):
@@ -377,7 +395,6 @@
         "index_logits",
         in_specs=[whole()] * 4,
         out_specs=[whole()] * 3,
-        flops=2 * flat_query.size * key_count,
         moved=2 * index_key.size,
     )(lengths, flat_query, index_key, weight_wide)
 
@@ -436,93 +453,140 @@
 
 
 def join_kernel(stats_ref, own_ref, *refs):
-    parts, (mass_ref, out_ref) = refs[:-2], refs[-2:]
+    parts, (keep_ref, give_ref, out_ref) = refs[:-3], refs[-3:]
     mass = own_ref[...]
     for part in parts:
         mass = mass + part[...].astype(jnp.float32)
-    mass_ref[...] = mass
+    rows, both = mass.shape
+    low, high = mass[:, : both // 2], mass[:, both // 2 :]
+    _, core, _ = place()
+    keep_ref[...] = jnp.where(core == 0, low, high)
+    give_ref[...] = jnp.where(core == 0, high, low)
+    total = jnp.broadcast_to(jnp.sum(mass, axis=1, keepdims=True), (rows, lanes))
+    nothing = jnp.zeros((rows, lanes), jnp.float32)
+    totals = jnp.concatenate([jnp.where(core == 0, total, nothing), jnp.where(core == 0, nothing, total)], axis=0)
     column = lax.broadcasted_iota(jnp.int32, out_ref.shape, 1)
-    out_ref[...] = jnp.where(column == 2, jnp.sum(mass, axis=1, keepdims=True), stats_ref[...])
+    out_ref[...] = jnp.where(column == 2, totals, stats_ref[...])
 
 
 def joined_mass(stats, own, parts):
+    rows, both = own.shape
     return local_call(
         join_kernel,
-        [f32(own.shape), f32(stats.shape)],
+        [f32((rows, both // 2)), f32((rows, both // 2)), f32(stats.shape)],
         "join_mass",
         in_specs=[whole()] * (2 + len(parts)),
-        out_specs=[whole()] * 2,
-        moved=8 * own.size,
+        out_specs=[whole()] * 3,
     )(stats, own, *parts)
 
 
-def pair_stats_kernel(own_ref, got_ref, out_ref):
-    own, got = own_ref[...], got_ref[...]
-    top = jnp.maximum(own[:, 0:1], got[:, 0:1])
-    shares = own[:, 1:2] * jnp.exp(own[:, 0:1] - top) + got[:, 1:2] * jnp.exp(got[:, 0:1] - top)
-    column = lax.broadcasted_iota(jnp.int32, out_ref.shape, 1)
-    out_ref[...] = jnp.where(column == 0, top, jnp.where(column == 1, shares, own + got))
-
-
-def pair_stats(own, got):
-    return local_call(
-        pair_stats_kernel, f32(own.shape), "pair_stats", in_specs=[whole()] * 2, out_specs=whole(), moved=8 * own.size
-    )(own, got)
-
-
-def back_kernel(sources, length_ref, mass_ref, logits_ref, turned_ref, key_ref, masked_ref, *refs):
-    stats = [ref[...] for ref in refs[:sources]]
-    partners = len(refs) - sources - 4
-    key_outs = refs[sources : sources + partners]
-    keep_ref, send_ref, slope_ref, grad_ref = refs[sources + partners :]
-    rows, key_count = mass_ref.shape
-    width, flat = turned_ref.shape
-    heads = flat // rows
-    tile = math.gcd(key_count, 256)
-    _, core, group = place()
+def merge_kernel(*refs):
+    out_ref = refs[-1]
+    stats = [ref[...] for ref in refs[:-1]]
     top = functools.reduce(jnp.maximum, [s[:, 0:1] for s in stats])
     shares = sum(s[:, 1:2] * jnp.exp(s[:, 0:1] - top) for s in stats)
-    total = sum(s[:, 2:3] for s in stats)
-    visible = visible_tile(length_ref, group, rows, 0, key_count, key_count)
-    weights_exp = jnp.where(visible, jnp.exp(logits_ref[...] - top), 0.0)
-    slope_ref[...] = loss_scale * (weights_exp / shares - mass_ref[...] / total)
+    column = lax.broadcasted_iota(jnp.int32, out_ref.shape, 1)
+    out_ref[...] = jnp.where(column == 0, top, jnp.where(column == 1, shares, sum(stats)))
+
+
+def merged_stats(stats):
+    return local_call(
+        merge_kernel, f32(stats[0].shape), "merge_stats", in_specs=[whole()] * len(stats), out_specs=whole()
+    )(*stats)
+
+
+def back_rows(half, length_ref, stats_ref, mass_ref, logits_ref, turned_ref, key_ref, masked_ref, slope_ref, store):
+    rows, key_count = mass_ref.shape
+    width = key_ref.shape[1]
+    flat = turned_ref.shape[1] // 2
+    tile = math.gcd(key_count, 256)
+    stats = rows_at(stats_ref, half, rows)
+    visible = visible_tile(length_ref, 2 * lax.axis_index("heads") + half, rows, 0, key_count, key_count)
+    weights_exp = jnp.where(visible, jnp.exp(rows_at(logits_ref, half, rows) - stats[:, 0:1]), 0.0)
+    slope_ref[...] = loss_scale * (weights_exp / stats[:, 1:2] - mass_ref[...] / stats[:, 2:3])
+    begin = pl.multiple_of(half * flat, flat)
+    turned = turned_ref[:, pl.ds(begin, flat)]
     query_grad = jnp.zeros((flat, width), jnp.float32)
     for first in range(0, key_count, tile):
         keys = key_ref[first : first + tile, :]
-        slopes = jnp.broadcast_to(slope_ref[:, first : first + tile][:, None, :], (rows, heads, tile))
-        terms = (slopes.reshape(flat, tile) * masked_ref[:, first : first + tile]).astype(jnp.bfloat16)
+        slopes = jnp.broadcast_to(slope_ref[:, first : first + tile][:, None, :], (rows, flat // rows, tile))
+        masked = masked_ref[pl.ds(begin, flat), first : first + tile]
+        terms = (slopes.reshape(flat, tile) * masked).astype(jnp.bfloat16)
         query_grad = query_grad + jnp.dot(terms, keys, preferred_element_type=jnp.float32)
-        key_grad = jnp.dot(turned_ref[...], terms, preferred_element_type=jnp.float32)
-        grad_ref[first : first + tile, :] = key_grad.T
+        store(first, tile, jnp.dot(turned, terms, preferred_element_type=jnp.float32))
+    return query_grad
+
+
+def back_own_kernel(
+    length_ref, stats_ref, mass_ref, logits_ref, turned_ref, key_ref, masked_ref, query_out, key_out, slope_ref
+):
+    _, core, _ = place()
+
+    def store(first, tile, key_grad):
+        key_out[:, first : first + tile] = key_grad
+
+    query_out[...] = back_rows(
+        core, length_ref, stats_ref, mass_ref, logits_ref, turned_ref, key_ref, masked_ref, slope_ref, store
+    )
+
+
+def back_own(lengths, stats, mass, logits, turned, index_key, masked):
+    rows, key_count = mass.shape
+    width, flat = turned.shape
+    return local_call(
+        back_own_kernel,
+        [f32((flat // 2, width)), f32((width, key_count))],
+        "index_back_own",
+        in_specs=[whole()] * 7,
+        out_specs=[whole()] * 2,
+        scratch=[pltpu.VMEM((rows, key_count), jnp.float32)],
+    )(lengths, stats, mass, logits, turned, index_key, masked)
+
+
+def back_pair_kernel(
+    length_ref, stats_ref, mass_ref, logits_ref, turned_ref, key_ref, masked_ref, query_ref, before_ref, *refs
+):
+    partners = len(refs) - 4
+    key_outs = refs[:partners]
+    keep_ref, send_ref, slope_ref, grad_ref = refs[partners:]
+    key_count, width = key_ref.shape
+    _, core, group = place()
+
+    def store(first, tile, key_grad):
+        grad_ref[first : first + tile, :] = (before_ref[:, first : first + tile] + key_grad).T
+
+    other = back_rows(
+        1 - core, length_ref, stats_ref, mass_ref, logits_ref, turned_ref, key_ref, masked_ref, slope_ref, store
+    )
     block = key_count // partners
     for e, out_ref in enumerate(key_outs):
         out_ref[...] = rows_at(grad_ref, group ^ e, block).astype(out_ref.dtype)
-    planes = keep_ref.shape[0]
-    part = heads // (2 * planes)
-    split = query_grad.reshape(rows, planes, 2, part, width)
-    first_core = core == 0
-    for plane in range(planes):
-        low, high = split[:, plane, 0], split[:, plane, 1]
-        keep_ref[plane] = jnp.where(first_core, low, high).reshape(rows * part, width)
-        send_ref[plane] = jnp.where(first_core, high, low).reshape(rows * part, width).astype(jnp.bfloat16)
-
-
-def back_pass(lengths, mass, logits, turned, index_key, masked, stats, partners, planes):
+    planes, part, _ = keep_ref.shape
+    rows = mass_ref.shape[0]
+    for half, query_grad in ((core, query_ref[...]), (1 - core, other)):
+        split = query_grad.reshape(rows, planes, 2, part // (2 * rows), width)
+        place_of = pl.ds(pl.multiple_of(half * (part // 2), part // 2), part // 2)
+        for plane in range(planes):
+            low = split[:, plane, 0].reshape(part // 2, width)
+            high = split[:, plane, 1].reshape(part // 2, width)
+            keep_ref[plane, place_of, :] = jnp.where(core == 0, low, high)
+            send_ref[plane, place_of, :] = jnp.where(core == 0, high, low).astype(jnp.bfloat16)
+
+
+def back_pair(lengths, stats, mass, logits, turned, index_key, masked, query_grad, key_grad, partners, planes):
     rows, key_count = mass.shape
     width, flat = turned.shape
     part = flat // (2 * planes)
     return local_call(
-        functools.partial(back_kernel, len(stats)),
+        back_pair_kernel,
         [f32((key_count // partners, width))]
         + [bf16((key_count // partners, width))] * (partners - 1)
         + [f32((planes, part, width)), bf16((planes, part, width))],
-        "index_back",
-        in_specs=[whole()] * (6 + len(stats)),
+        "index_back_pair",
+        in_specs=[whole()] * 9,
         out_specs=[whole()] * (partners + 2),
         scratch=[pltpu.VMEM((rows, key_count), jnp.float32), pltpu.VMEM((key_count, width), jnp.float32)],
-        flops=6 * flat * width * key_count,
-        moved=8 * key_count * width,
-    )(lengths, mass, logits, turned, index_key, masked, *stats)
+    )(lengths, stats, mass, logits, turned, index_key, masked, query_grad, key_grad)
 
 
 def pair_kernel(keep_ref, got_ref, *outs):
@@ -585,39 +649,46 @@
     def heads_flip(array, e):
         return lax.ppermute(array, "heads", [(h, h ^ e) for h in range(partners)])
 
-    def mass_of(packs, *rest):
-        return chunk_mass(lengths, packs, lse, keys, *rest[:2], rows, heads, rest[2])
-
-    pack = packed_queries(main_query)
-    across = planes_move(pack, [(1, 2), (2, 1), (0, 3), (3, 0)])
+    keys_pair = context_flip(latent_keys.T, 1)
+    pack, *inner = packed_queries(main_query)
+    inner = [planes_move(block, [(1, 2), (2, 1), (0, 0), (3, 3)]) for block in inner]
     near = planes_move(pack, [(0, 1), (1, 0), (2, 3), (3, 2)])
-    own_pair = context_flip(pack, 1)
+    ends = planes_move(pack, [(0, 3), (3, 0)])
     lengths, lse, weight_wide, query, turned, index_key, keys = load_inputs(
         lengths, head_lse.T, index_weight, index_query, index_key, after(latent_keys, pack).T
     )
+    keys = (keys, keys_pair)
+
+    blocks = head_blocks(heads)
+
+    def mass_of(pack, flip, blocks, *rest):
+        return chunk_mass(lengths, pack, lse, keys, flip, blocks, rows, *rest)
+
+    inner = [after(block, lse) for block in inner]
+    far = [planes_move(block, [(0, 2), (3, 1), (1, 0), (2, 3)]) for block in inner]
     logits, masked, stats = index_logits(lengths, query.reshape(flat, width), index_key, weight_wide, own_rows)
-    own_mass = mass_of([pack, after(own_pair, stats)], 0, (0, 1), "mass_own")
-    across = after(across, own_mass)
-    far = planes_move(picked(pack, across), [(0, 2), (3, 1), (1, 0), (2, 3)])
-    near = after(near, own_mass)
-    near_mass = mass_of([near, context_flip(near, 1)], 1, (0, 1), "mass_near")
-    across_mass = mass_of([across, context_flip(across, 1)], 3, (0, 1), "mass_across")
-    far = after(far, near_mass, across_mass)
-    far_pair = context_flip(far, 1)
-    far_mass = mass_of([far], 2, (0,), "mass_far")
+    stats = merged_stats([stats, context_flip(stats, 1)])
+    own_mass = mass_of(pack, 0, blocks, "mass_own")
+    near_mass = mass_of(after(near, logits), 1, blocks, "mass_near", 100_000_000)
+    across_mass = mass_of(picked(after(ends, own_mass, near_mass), inner), 3, blocks, "mass_across", 50_000_000)
+    far_mass = mass_of(after(far[0], across_mass, stats), 2, blocks[:1], "mass_far", 1)
     shared = shared_mass(
-        lengths, far_pair, lse, own_mass, near_mass, across_mass, far_mass, keys, rows, heads, partners
-    )
-    mass, stats = joined_mass(stats, shared[0], [heads_flip(shared[e], e) for e in range(1, partners)])
-    stats = pair_stats(stats, context_flip(stats, 1))
-    every = [stats] + [context_flip(stats, 2 * e) for e in range(1, planes)]
-    *key_grads, keep, send = back_pass(
-        lengths, mass, logits, turned, index_key, masked, every, partners, planes
+        lengths, after(far[1], far_mass), lse, keys, own_mass, near_mass, across_mass, far_mass, blocks[1], partners
+    )
+    keep_mass, give_mass, stats = joined_mass(
+        stats, shared[0], [heads_flip(shared[e], e) for e in (*reversed(range(1, partners - 1)), partners - 1)]
+    )
+    got_mass = context_flip(give_mass, 1)
+    stats = merged_stats([stats] + [context_flip(stats, 2 * e) for e in reversed(range(1, planes))])
+    back = (logits, turned, index_key, masked)
+    query_grad, key_grad = back_own(lengths, stats, keep_mass, *back)
+    *key_grads, keep, send = back_pair(
+        lengths, context_flip(stats, 1), got_mass, *back, query_grad, key_grad, partners, planes
     )
     got = context_flip(send, 1)
-    key_parts = [key_grads[0]] + [heads_flip(key_grads[e], e) for e in range(1, partners)]
+    key_parts = [key_grads[0]] + [heads_flip(key_grads[e], e) for e in reversed(range(1, partners))]
     sums = pair_sums(keep, got)
-    query_parts = [sums[0]] + [context_flip(sums[e], 2 * e) for e in range(1, planes)]
+    query_parts = [sums[0]] + [context_flip(sums[e], 2 * e) for e in reversed(range(1, planes))]
     return last_sums(key_parts, query_parts, (own_rows, index_heads // contexts, width))
 
 

time: 66.9 us -> 59.8 us (0.89)
  waiting for transfers between devices: 21.6 us -> 13.4 us
  starting transfers between devices: 23.2 us -> 29.1 us
  local copies, waits for them, and re-layouts: 6.69 us -> 1.28 us
  Pallas kernels: 14.2 us -> 15 us
    ppermute x3 -> x6, starting transfers between devices: 7.12 us -> 13 us  [planes_move(): lax.ppermute(array, 'context', [(2 * a + k, 2 * b + k) for a, b in pairs...]
    unnamed x14, local copies, waits for them, and re-layouts: 6.69 us -> 1.28 us
    ppermute x3 -> x6, waiting for transfers between devices: 6.91 us -> 1.68 us  [planes_move(): lax.ppermute(array, 'context', [(2 * a + k, 2 * b + k) for a, b in pairs...]
    ppermute x12 -> x11, waiting for transfers between devices: 8.61 us -> 5.78 us  [context_flip(): return lax.ppermute(array, 'context', [(c, c ^ e) for c in range(contexts)])]
    pallas_call x10 -> x12, Pallas kernels: 10.3 us -> 11.1 us  [the longest x4 6.8 us: chunk_mass(): local_call(functools.partial(mass_kernel, flip, blocks), f32((rows, 2 * k...]
    ppermute x12 -> x11, starting transfers between devices: 9.02 us -> 9.03 us  [context_flip(): return lax.ppermute(array, 'context', [(c, c ^ e) for c in range(contexts)])]
  transfers between devices with their start and end apart: 21 -> 23, of which waited for: 12 -> 15; matrix products, arithmetic and copies ran while one was open for 0% -> 0% of each run, Pallas kernels for 15% -> 20%
where the time goes in v5:
time: 59.8 us; the launch traced here: 59.6 us
  starting transfers between devices  29.1 us (49%)
  Pallas kernels  15 us (25%)
  waiting for transfers between devices  13.4 us (22%)
  local copies, waits for them, and re-layouts  1.28 us (2%)
  between operations  0.88 us (1%)
    ppermute x6, starting transfers between devices, planes_move(): lax.ppermute(array, 'context', [(2 * a + k, 2 * b + k) for a, b in pairs...  13 us
    ppermute x11, starting transfers between devices, context_flip(): return lax.ppermute(array, 'context', [(c, c ^ e) for c in range(contexts)])  9.03 us
    ppermute x6, starting transfers between devices, heads_flip(): return lax.ppermute(array, 'heads', [(h, h ^ e) for h in range(partners)])  7.04 us
    pallas_call x4, Pallas kernels, chunk_mass(): local_call(functools.partial(mass_kernel, flip, blocks), f32((rows, 2 * k...  6.8 us
    ppermute x6, waiting for transfers between devices, heads_flip(): return lax.ppermute(array, 'heads', [(h, h ^ e) for h in range(partners)])  5.96 us
    ppermute x11, waiting for transfers between devices, context_flip(): return lax.ppermute(array, 'context', [(c, c ^ e) for c in range(contexts)])  5.78 us
    pallas_call x1, Pallas kernels, index_logits(): local_call(logits_kernel, [f32((rows, key_count)), f32((flat, key_count))...  1.84 us
    ppermute x6, waiting for transfers between devices, planes_move(): lax.ppermute(array, 'context', [(2 * a + k, 2 * b + k) for a, b in pairs...  1.68 us
  transfers between devices with their start and end apart: 23, of which 15 were waited for; matrix products, arithmetic and copies ran while one was open for 0% of the time, Pallas kernels for 20%

profile of v5, /device:TPU:0, one launch (start us, length us, event | category | flops | bytes accessed | tf_op | source)
XLA Modules:
  0.0 59.6 jit_solution(12258198377102554600)
XLA Ops:
  1.2 1.3 %copy-done.6 = bf16[8,32,576]{2,1,0:T(8,128)(2,1)S(1)} copy-done((bf16[8,32,576]{2,1,0:T(8,128)(2,1)S(1)}, bf16[8,32,576]{2,1,0:T(8,128)(2,1)}, u32[]{:S(2)}) %copy-start.6) | copy-done | bytes 294936
  2.6 0.7 %collective-permute-start.3 = (bf16[720,128]{1,0:T(8,128)(2,1)S(1)}, bf16[720,128]{1,0:T(8,128)(2,1)S(1)}, u32[]{:S(2)}, u32[]{:S(2)}) collective-permute-start(bf16[720,128]{1,0:T(8,128)(2,1)S(1)} %get-tuple-element.51), channel_id=1, source_target_pairs={{8,16},{12,20},{16,8},{20,12},{0,0},{4,4},{24,24},{28,28},{9,17},{... | collective-permute-start | bytes 552968 | tf_op jit(solution)/shard_map/ppermute | solution.py:644
  3.3 5.3 %collective-permute-start.7 = (bf16[1152,128]{1,0:T(8,128)(2,1)S(1)}, bf16[1152,128]{1,0:T(8,128)(2,1)S(1)}, u32[]{:S(2)}, u32[]{:S(2)}) collective-permute-start(bf16[1152,128]{1,0:T(8,128)(2,1)S(1)} %get-tuple-element.41.pack_ref), channel_id=1, source_target_pairs={{0,8},{4,12},{8,0},{12,4},{16,24},{20,28},{24,16},{28,20},{1,9},{5... | collective-permute-start | bytes 884744 | tf_op jit(solution)/shard_map/ppermute | solution.py:644
  8.7 3.2 %collective-permute-start.5 = (bf16[1152,128]{1,0:T(8,128)(2,1)S(1)}, bf16[1152,128]{1,0:T(8,128)(2,1)S(1)}, u32[]{:S(2)}, u32[]{:S(2)}) collective-permute-start(bf16[1152,128]{1,0:T(8,128)(2,1)S(1)} %get-tuple-element.41.pack_ref), channel_id=1, source_target_pairs={{0,24},{4,28},{24,0},{28,4},{1,25},{5,29},{25,1},{29,5},{2,26},{6,... | collective-permute-start | bytes 884744 | tf_op jit(solution)/shard_map/ppermute | solution.py:644
  12.6 1.2 %load_inputs.1 = (s32[64,128]{1,0:T(8,128)S(1)}, f32[64,32]{1,0:T(8,128)S(1)}, f32[1024,128]{1,0:T(8,128)S(1)}, bf16[16,64,128]{2,1,0:T(8,128)(2,1)S(1)}, bf16[1...) custom-call(s32[64]{0:T(128)S(1)} %copy-done.5, f32[32,64]{1,0:T(8,128)S(1)} %bitcast.7, ...), custom_call_target="tpu_custom_call" | custom-call | flops 1 | bytes 1 | tf_op jit(solution)/shard_map/load_inputs/pallas_call | solution.py:436
  13.9 1.5 %collective-permute-start.4 = (bf16[720,128]{1,0:T(8,128)(2,1)S(1)}, bf16[720,128]{1,0:T(8,128)(2,1)S(1)}, u32[]{:S(2)}, u32[]{:S(2)}) collective-permute-start(bf16[720,128]{1,0:T(8,128)(2,1)S(1)} %collective-permute-done.3.refs_0_), channel_id=1, source_target_pairs={{0,16},{4,20},{24,8},{28,12},{8,0},{12,4},{16,24},{20,28},{1,17},{... | collective-permute-start | bytes 552968 | tf_op jit(solution)/shard_map/ppermute | solution.py:644
  15.4 1.8 %index_logits.1 = (f32[16,2048]{1,0:T(8,128)S(1)}, f32[1024,2048]{1,0:T(8,128)S(1)}, f32[16,128]{1,0:T(8,128)S(1)}) custom-call(s32[64,128]{1,0:T(8,128)S(1)} %get-tuple-element.43.length_ref, bf16[1024,128]{1,0:T(8,128)(2,1)S(1)} %bitcast.6, bf16[2048,128]{1,0:T(8,128)(2,1)S(1)} %get-tuple-element.45.key_ref, f32[1024,128]{1,0:T(8,128)S(1)} %get-tuple-element.46.weight_ref), custom_call_target="tpu_custom_call" | custom-call | flops 1 | bytes 1 | tf_op jit(solution)/shard_map/index_logits/pallas_call | solution.py:392
  17.3 1.2 %collective-permute-done.refs_1_ = f32[16,128]{1,0:T(8,128)S(1)} collective-permute-done((f32[16,128]{1,0:T(8,128)S(1)}, f32[16,128]{1,0:T(8,128)S(1)}, u32[]{:S(2)}, u32[]{:S(2)}) %collective-permute-start) | collective-permute-done | bytes 8224 | tf_op jit(solution)/shard_map/ppermute | solution.py:647
  18.5 1.5 %collective-permute-start.2 = (bf16[432,128]{1,0:T(8,128)(2,1)S(1)}, bf16[432,128]{1,0:T(8,128)(2,1)S(1)}, u32[]{:S(2)}, u32[]{:S(2)}) collective-permute-start(bf16[432,128]{1,0:T(8,128)(2,1)S(1)} %collective-permute-done.1.refs_1_), channel_id=1, source_target_pairs={{0,16},{4,20},{24,8},{28,12},{8,0},{12,4},{16,24},{20,28},{1,17},{... | collective-permute-start | bytes 331784 | tf_op jit(solution)/shard_map/ppermute | solution.py:644
  20.2 1.8 %mass_own.1.own_ref = f32[8,4096]{1,0:T(8,128)S(1)} custom-call(s32[64,128]{1,0:T(8,128)S(1)} %get-tuple-element.43.length_ref, bf16[1152,128]{1,0:T(8,128)(2,1)S(1)} %get-tuple-element.41.pack_ref, f32[64,32]{1,0:T(8,128)S(1)} %get-tuple-element.49.lse_ref, bf16[576,2048]{1,0:T(8,128)(2,1)S(1)} %get-tuple-element.53.own_key_ref, ...), custom_call_target="tpu_custom_call" | custom-call | flops 1 | bytes 1 | tf_op jit(solution)/shard_map/mass_own/pallas_call | solution.py:323
  22.0 1.8 %mass_near.1.near_ref = f32[8,4096]{1,0:T(8,128)S(1)} custom-call(s32[64,128]{1,0:T(8,128)S(1)} %get-tuple-element.43.length_ref, bf16[1152,128]{1,0:T(8,128)(2,1)S(1)} %collective-permute-done.7.pack_ref, f32[64,32]{1,0:T(8,128)S(1)} %get-tuple-element.49.lse_ref, bf16[576,2048]{1,0:T(8,128)(2,1)S(1)} %get-tuple-element.53.own_key_ref, ...), custom_call_target="tpu_custom_call" | custom-call | flops 100000000 | bytes 1 | tf_op jit(solution)/shard_map/mass_near/pallas_call | solution.py:323
  24.4 1.8 %mass_across.1.across_ref = f32[8,4096]{1,0:T(8,128)S(1)} custom-call(s32[64,128]{1,0:T(8,128)S(1)} %get-tuple-element.43.length_ref, bf16[1152,128]{1,0:T(8,128)(2,1)S(1)} %pick_queries.1.pack_ref, f32[64,32]{1,0:T(8,128)S(1)} %get-tuple-element.49.lse_ref, bf16[576,2048]{1,0:T(8,128)(2,1)S(1)} %get-tuple-element.53.own_key_ref, ...), custom_call_target="tpu_custom_call" | custom-call | flops 50000000 | bytes 1 | tf_op jit(solution)/shard_map/mass_across/pallas_call | solution.py:323
  26.2 1.1 %collective-permute-done.4.pack_ref = bf16[720,128]{1,0:T(8,128)(2,1)S(1)} collective-permute-done((bf16[720,128]{1,0:T(8,128)(2,1)S(1)}, bf16[720,128]{1,0:T(8,128)(2,1)S(1)}, u32[]{:S(2)}, u32[]{:S(2)}) %collective-permute-start.4) | collective-permute-done | bytes 184352 | tf_op jit(solution)/shard_map/ppermute | solution.py:644
  27.3 1.3 %mass_far.1.before_ref = f32[8,4096]{1,0:T(8,128)S(1)} custom-call(s32[64,128]{1,0:T(8,128)S(1)} %get-tuple-element.43.length_ref, bf16[720,128]{1,0:T(8,128)(2,1)S(1)} %collective-permute-done.4.pack_ref, f32[64,32]{1,0:T(8,128)S(1)} %get-tuple-element.49.lse_ref, bf16[576,2048]{1,0:T(8,128)(2,1)S(1)} %get-tuple-element.53.own_key_ref, ...), custom_call_target="tpu_custom_call" | custom-call | flops 1 | bytes 1 | tf_op jit(solution)/shard_map/mass_far/pallas_call | solution.py:323
  28.9 1.1 %mass_and_share.1 = (f32[8,4096]{1,0:T(8,128)S(1)}, bf16[8,4096]{1,0:T(8,128)(2,1)S(1)}, bf16[8,4096]{1,0:T(8,128)(2,1)S(1)}, bf16[8,4096]{1,0:T(8,128)(2,1)S(1)}) custom-call(s32[64,128]{1,0:T(8,128)S(1)} %get-tuple-element.43.length_ref, bf16[432,128]{1,0:T(8,128)(2,1)S(1)} %collective-permute-done.2.pack_ref, f32[64,32]{1,0:T(8,128)S(1)} %get-tuple-element.49.lse_ref, ...), custom_call_target="tpu_custom_call" | custom-call | flops 1 | bytes 1 | tf_op jit(solution)/shard_map/mass_and_share/pallas_call | solution.py:355
  30.0 2.5 %collective-permute-start.10 = (bf16[8,4096]{1,0:T(8,128)(2,1)S(1)}, bf16[8,4096]{1,0:T(8,128)(2,1)S(1)}, u32[]{:S(2)}, u32[]{:S(2)}) collective-permute-start(bf16[8,4096]{1,0:T(8,128)(2,1)S(1)} %get-tuple-element.62), channel_id=1, source_target_pairs={{0,3},{1,2},{2,1},{3,0},{4,7},{5,6},{6,5},{7,4},{8,11},{9,10},{10,... | collective-permute-start | bytes 196616 | tf_op jit(solution)/shard_map/ppermute | solution.py:650
  33.6 1.8 %collective-permute-done.10.refs_2_ = bf16[8,4096]{1,0:T(8,128)(2,1)S(1)} collective-permute-done((bf16[8,4096]{1,0:T(8,128)(2,1)S(1)}, bf16[8,4096]{1,0:T(8,128)(2,1)S(1)}, u32[]{:S(2)}, u32[]{:S(2)}) %collective-permute-start.10) | collective-permute-done | bytes 65568 | tf_op jit(solution)/shard_map/ppermute | solution.py:650
  35.3 1.4 %collective-permute-done.8.refs_0_ = bf16[8,4096]{1,0:T(8,128)(2,1)S(1)} collective-permute-done((bf16[8,4096]{1,0:T(8,128)(2,1)S(1)}, bf16[8,4096]{1,0:T(8,128)(2,1)S(1)}, u32[]{:S(2)}, u32[]{:S(2)}) %collective-permute-start.8) | collective-permute-done | bytes 65568 | tf_op jit(solution)/shard_map/ppermute | solution.py:650
  37.4 2.5 %collective-permute-start.11 = (f32[16,128]{1,0:T(8,128)S(1)}, f32[16,128]{1,0:T(8,128)S(1)}, u32[]{:S(2)}, u32[]{:S(2)}) collective-permute-start(f32[16,128]{1,0:T(8,128)S(1)} %get-tuple-element.63.refs_0_), channel_id=1, source_target_pairs={{0,24},{4,28},{8,16},{12,20},{16,8},{20,12},{24,0},{28,4},{1,25},{... | collective-permute-start | bytes 24584 | tf_op jit(solution)/shard_map/ppermute | solution.py:647
  40.5 1.4 %collective-permute-start.13 = (f32[16,128]{1,0:T(8,128)S(1)}, f32[16,128]{1,0:T(8,128)S(1)}, u32[]{:S(2)}, u32[]{:S(2)}) collective-permute-start(f32[16,128]{1,0:T(8,128)S(1)} %get-tuple-element.63.refs_0_), channel_id=1, source_target_pairs={{0,8},{4,12},{8,0},{12,4},{16,24},{20,28},{24,16},{28,20},{1,9},{5... | collective-permute-start | bytes 24584 | tf_op jit(solution)/shard_map/ppermute | solution.py:647
  41.9 1.1 %collective-permute-done.11.refs_1_ = f32[16,128]{1,0:T(8,128)S(1)} collective-permute-done((f32[16,128]{1,0:T(8,128)S(1)}, f32[16,128]{1,0:T(8,128)S(1)}, u32[]{:S(2)}, u32[]{:S(2)}) %collective-permute-start.11) | collective-permute-done | bytes 8224 | tf_op jit(solution)/shard_map/ppermute | solution.py:647
  42.9 1.6 %collective-permute-done.12.refs_2_ = f32[16,128]{1,0:T(8,128)S(1)} collective-permute-done((f32[16,128]{1,0:T(8,128)S(1)}, f32[16,128]{1,0:T(8,128)S(1)}, u32[]{:S(2)}, u32[]{:S(2)}) %collective-permute-start.12) | collective-permute-done | bytes 8224 | tf_op jit(solution)/shard_map/ppermute | solution.py:647
  44.7 1.1 %index_back_own.1 = (f32[512,128]{1,0:T(8,128)S(1)}, f32[128,2048]{1,0:T(8,128)S(1)}) custom-call(s32[64,128]{1,0:T(8,128)S(1)} %get-tuple-element.43.length_ref, f32[16,128]{1,0:T(8,128)S(1)} %merge_stats.3.stats_ref, f32[8,2048]{1,0:T(8,128)S(1)} %get-tuple-element.67.mass_ref, f32[16,2048]{1,0:T(8,128)S(1)} %get-tuple-element.54.logits_ref, ...), custom_call_target="tpu_custom_call" | custom-call | flops 1 | bytes 1 | tf_op jit(solution)/shard_map/index_back_own/pallas_call | solution.py:536
  45.9 1.2 %index_back_pair.1 = (f32[512,128]{1,0:T(8,128)S(1)}, bf16[512,128]{1,0:T(8,128)(2,1)S(1)}, bf16[512,128]{1,0:T(8,128)(2,1)S(1)}, bf16[512,128]{1,0:T(8,128)(2,1...) custom-call(s32[64,128]{1,0:T(8,128)S(1)} %get-tuple-element.43.length_ref, ...), custom_call_target="tpu_custom_call" | custom-call | flops 1 | bytes 1 | tf_op jit(solution)/shard_map/index_back_pair/pallas_call | solution.py:580
  47.7 1.5 %collective-permute-start.16 = (bf16[512,128]{1,0:T(8,128)(2,1)S(1)}, bf16[512,128]{1,0:T(8,128)(2,1)S(1)}, u32[]{:S(2)}, u32[]{:S(2)}) collective-permute-start(bf16[512,128]{1,0:T(8,128)(2,1)S(1)} %get-tuple-element.71), channel_id=1, source_target_pairs={{0,3},{1,2},{2,1},{3,0},{4,7},{5,6},{6,5},{7,4},{8,11},{9,10},{10,... | collective-permute-start | bytes 393224 | tf_op jit(solution)/shard_map/ppermute | solution.py:650
  49.7 1.5 %collective-permute-start.18 = (bf16[512,128]{1,0:T(8,128)(2,1)S(1)}, bf16[512,128]{1,0:T(8,128)(2,1)S(1)}, u32[]{:S(2)}, u32[]{:S(2)}) collective-permute-start(bf16[512,128]{1,0:T(8,128)(2,1)S(1)} %get-tuple-element.73), channel_id=1, source_target_pairs={{0,1},{1,0},{2,3},{3,2},{4,5},{5,4},{6,7},{7,6},{8,9},{9,8},{10,11... | collective-permute-start | bytes 393224 | tf_op jit(solution)/shard_map/ppermute | solution.py:650
  51.2 2.1 %collective-permute-start.20 = (bf16[128,128]{1,0:T(8,128)(2,1)S(1)}, bf16[128,128]{1,0:T(8,128)(2,1)S(1)}, u32[]{:S(2)}, u32[]{:S(2)}) collective-permute-start(bf16[128,128]{1,0:T(8,128)(2,1)S(1)} %get-tuple-element.77), channel_id=1, source_target_pairs={{0,24},{4,28},{8,16},{12,20},{16,8},{20,12},{24,0},{28,4},{1,25},{... | collective-permute-start | bytes 98312 | tf_op jit(solution)/shard_map/ppermute | solution.py:647
  53.7 1.2 %collective-permute-done.16.refs_1_ = bf16[512,128]{1,0:T(8,128)(2,1)S(1)} collective-permute-done((bf16[512,128]{1,0:T(8,128)(2,1)S(1)}, bf16[512,128]{1,0:T(8,128)(2,1)S(1)}, u32[]{:S(2)}, u32[]{:S(2)}) %collective-permute-start.16) | collective-permute-done | bytes 131104 | tf_op jit(solution)/shard_map/ppermute | solution.py:650
  54.9 1.0 %collective-permute-start.22 = (bf16[128,128]{1,0:T(8,128)(2,1)S(1)}, bf16[128,128]{1,0:T(8,128)(2,1)S(1)}, u32[]{:S(2)}, u32[]{:S(2)}) collective-permute-start(bf16[128,128]{1,0:T(8,128)(2,1)S(1)} %get-tuple-element.79), channel_id=1, source_target_pairs={{0,8},{4,12},{8,0},{12,4},{16,24},{20,28},{24,16},{28,20},{1,9},{5... | collective-permute-start | bytes 98312 | tf_op jit(solution)/shard_map/ppermute | solution.py:647
  55.9 0.9 %collective-permute-done.17.refs_2_ = bf16[512,128]{1,0:T(8,128)(2,1)S(1)} collective-permute-done((bf16[512,128]{1,0:T(8,128)(2,1)S(1)}, bf16[512,128]{1,0:T(8,128)(2,1)S(1)}, u32[]{:S(2)}, u32[]{:S(2)}) %collective-permute-start.17) | collective-permute-done | bytes 131104 | tf_op jit(solution)/shard_map/ppermute | solution.py:650
  57.0 1.5 %collective-permute-done.21.refs_6_ = bf16[128,128]{1,0:T(8,128)(2,1)S(1)} collective-permute-done((bf16[128,128]{1,0:T(8,128)(2,1)S(1)}, bf16[128,128]{1,0:T(8,128)(2,1)S(1)}, u32[]{:S(2)}, u32[]{:S(2)}) %collective-permute-start.21) | collective-permute-done | bytes 32800 | tf_op jit(solution)/shard_map/ppermute | solution.py:647
  58.8 0.8 %last_sums.1 = (f32[16,8,128]{2,1,0:T(8,128)}, f32[512,128]{1,0:T(8,128)}) custom-call(f32[512,128]{1,0:T(8,128)S(1)} %get-tuple-element.70.refs_0_, bf16[512,128]{1,0:T(8,128)(2,1)S(1)} %collective-permute-done.16.refs_1_, bf16[512,128]{1,0:T(8,128)(2,1)S(1)} %collective-permute-done.17.refs_2_, bf16[512,128]{1,0:T(8,128)(2,1)S(1)} %collective-permute-done.18.refs_3_, ...), custom_call_target="tpu_custom_call" | custom-call | flops 1 | bytes 1 | tf_op jit(solution)/shard_map/last_sums/pallas_call | solution.py:619
  (44 shorter events, 6.8 us)
Async XLA Ops:
  0.6 12.0 %copy-start = (bf16[2048,576]{0,1:T(8,128)(2,1)S(1)}, bf16[2048,576]{0,1:T(8,128)(2,1)}, u32[]{:S(2)}) copy-start(bf16[2048,576]{0,1:T(8,128)(2,1)} %param.8) | copy-start | bytes 7077892
  0.6 12.0 %copy-start.1 = (bf16[2048,128]{1,0:T(8,128)(2,1)S(1)}, bf16[2048,128]{1,0:T(8,128)(2,1)}, u32[]{:S(2)}) copy-start(bf16[2048,128]{1,0:T(8,128)(2,1)} %key_hbm.1) | copy-start | bytes 1572868
  0.7 12.0 %copy-start.2 = (bf16[16,64,128]{2,1,0:T(8,128)(2,1)S(1)}, bf16[16,64,128]{2,1,0:T(8,128)(2,1)}, u32[]{:S(2)}) copy-start(bf16[16,64,128]{2,1,0:T(8,128)(2,1)} %query_hbm.1) | copy-start | bytes 786436
  0.7 12.0 %copy-start.3 = (f32[64,32]{0,1:T(8,128)S(1)}, f32[64,32]{0,1:T(8,128)}, u32[]{:S(2)}) copy-start(f32[64,32]{0,1:T(8,128)} %param.9) | copy-start | bytes 24580
  0.7 12.0 %copy-start.4 = (f32[16,64]{1,0:T(8,128)S(1)}, f32[16,64]{1,0:T(8,128)}, u32[]{:S(2)}) copy-start(f32[16,64]{1,0:T(8,128)} %weight_ref.1) | copy-start | bytes 12292
  0.7 12.0 %copy-start.5 = (s32[64]{0:T(128)S(1)}, s32[64]{0:T(128)}, u32[]{:S(2)}) copy-start(s32[64]{0:T(128)} %length_ref.1) | copy-start | bytes 772
  0.7 19.5 %collective-permute-start.6 = (bf16[576,2048]{1,0:T(8,128)(2,1)}, bf16[576,2048]{1,0:T(8,128)(2,1)S(1)}, u32[]{:S(2)}, u32[]{:S(2)}) collective-permute-start(bf16[576,2048]{1,0:T(8,128)(2,1)} %bitcast.4), channel_id=1, source_target_pairs={{0,4},{4,0},{8,12},{12,8},{16,20},{20,16},{24,28},{28,24},{1,5},{5... | collective-permute-start | bytes 7077896 | tf_op jit(solution)/shard_map/ppermute | solution.py:647
  1.2 1.3 %copy-start.6 = (bf16[8,32,576]{2,1,0:T(8,128)(2,1)S(1)}, bf16[8,32,576]{2,1,0:T(8,128)(2,1)}, u32[]{:S(2)}) copy-start(bf16[8,32,576]{2,1,0:T(8,128)(2,1)} %query_ref.1) | copy-start | bytes 884740
  2.6 11.2 %collective-permute-start.3 = (bf16[720,128]{1,0:T(8,128)(2,1)S(1)}, bf16[720,128]{1,0:T(8,128)(2,1)S(1)}, u32[]{:S(2)}, u32[]{:S(2)}) collective-permute-start(bf16[720,128]{1,0:T(8,128)(2,1)S(1)} %get-tuple-element.51), channel_id=1, source_target_pairs={{8,16},{12,20},{16,8},{20,12},{0,0},{4,4},{24,24},{28,28},{9,17},{... | collective-permute-start | bytes 552968 | tf_op jit(solution)/shard_map/ppermute | solution.py:644
  3.3 16.8 %collective-permute-start.7 = (bf16[1152,128]{1,0:T(8,128)(2,1)S(1)}, bf16[1152,128]{1,0:T(8,128)(2,1)S(1)}, u32[]{:S(2)}, u32[]{:S(2)}) collective-permute-start(bf16[1152,128]{1,0:T(8,128)(2,1)S(1)} %get-tuple-element.41.pack_ref), channel_id=1, source_target_pairs={{0,8},{4,12},{8,0},{12,4},{16,24},{20,28},{24,16},{28,20},{1,9},{5... | collective-permute-start | bytes 884744 | tf_op jit(solution)/shard_map/ppermute | solution.py:644
  8.7 15.5 %collective-permute-start.5 = (bf16[1152,128]{1,0:T(8,128)(2,1)S(1)}, bf16[1152,128]{1,0:T(8,128)(2,1)S(1)}, u32[]{:S(2)}, u32[]{:S(2)}) collective-permute-start(bf16[1152,128]{1,0:T(8,128)(2,1)S(1)} %get-tuple-element.41.pack_ref), channel_id=1, source_target_pairs={{0,24},{4,28},{24,0},{28,4},{1,25},{5,29},{25,1},{29,5},{2,26},{6,... | collective-permute-start | bytes 884744 | tf_op jit(solution)/shard_map/ppermute | solution.py:644
  11.9 5.4 %collective-permute-start.1 = (bf16[432,128]{1,0:T(8,128)(2,1)S(1)}, bf16[432,128]{1,0:T(8,128)(2,1)S(1)}, u32[]{:S(2)}, u32[]{:S(2)}) collective-permute-start(bf16[432,128]{1,0:T(8,128)(2,1)S(1)} %get-tuple-element.48), channel_id=1, source_target_pairs={{8,16},{12,20},{16,8},{20,12},{0,0},{4,4},{24,24},{28,28},{9,17},{... | collective-permute-start | bytes 331784 | tf_op jit(solution)/shard_map/ppermute | solution.py:644
  13.9 13.4 %collective-permute-start.4 = (bf16[720,128]{1,0:T(8,128)(2,1)S(1)}, bf16[720,128]{1,0:T(8,128)(2,1)S(1)}, u32[]{:S(2)}, u32[]{:S(2)}) collective-permute-start(bf16[720,128]{1,0:T(8,128)(2,1)S(1)} %collective-permute-done.3.refs_0_), channel_id=1, source_target_pairs={{0,16},{4,20},{24,8},{28,12},{8,0},{12,4},{16,24},{20,28},{1,17},{... | collective-permute-start | bytes 552968 | tf_op jit(solution)/shard_map/ppermute | solution.py:644
  17.3 1.2 %collective-permute-start = (f32[16,128]{1,0:T(8,128)S(1)}, f32[16,128]{1,0:T(8,128)S(1)}, u32[]{:S(2)}, u32[]{:S(2)}) collective-permute-start(f32[16,128]{1,0:T(8,128)S(1)} %get-tuple-element.47.refs_0_), channel_id=1, source_target_pairs={{0,4},{4,0},{8,12},{12,8},{16,20},{20,16},{24,28},{28,24},{1,5},{5... | collective-permute-start | bytes 24584 | tf_op jit(solution)/shard_map/ppermute | solution.py:647
  18.5 10.4 %collective-permute-start.2 = (bf16[432,128]{1,0:T(8,128)(2,1)S(1)}, bf16[432,128]{1,0:T(8,128)(2,1)S(1)}, u32[]{:S(2)}, u32[]{:S(2)}) collective-permute-start(bf16[432,128]{1,0:T(8,128)(2,1)S(1)} %collective-permute-done.1.refs_1_), channel_id=1, source_target_pairs={{0,16},{4,20},{24,8},{28,12},{8,0},{12,4},{16,24},{20,28},{1,17},{... | collective-permute-start | bytes 331784 | tf_op jit(solution)/shard_map/ppermute | solution.py:644
  30.0 5.3 %collective-permute-start.10 = (bf16[8,4096]{1,0:T(8,128)(2,1)S(1)}, bf16[8,4096]{1,0:T(8,128)(2,1)S(1)}, u32[]{:S(2)}, u32[]{:S(2)}) collective-permute-start(bf16[8,4096]{1,0:T(8,128)(2,1)S(1)} %get-tuple-element.62), channel_id=1, source_target_pairs={{0,3},{1,2},{2,1},{3,0},{4,7},{5,6},{6,5},{7,4},{8,11},{9,10},{10,... | collective-permute-start | bytes 196616 | tf_op jit(solution)/shard_map/ppermute | solution.py:650
  32.5 4.3 %collective-permute-start.8 = (bf16[8,4096]{1,0:T(8,128)(2,1)S(1)}, bf16[8,4096]{1,0:T(8,128)(2,1)S(1)}, u32[]{:S(2)}, u32[]{:S(2)}) collective-permute-start(bf16[8,4096]{1,0:T(8,128)(2,1)S(1)} %get-tuple-element.60), channel_id=1, source_target_pairs={{0,2},{1,3},{2,0},{3,1},{4,6},{5,7},{6,4},{7,5},{8,10},{9,11},{10,... | collective-permute-start | bytes 196616 | tf_op jit(solution)/shard_map/ppermute | solution.py:650
  33.0 4.3 %collective-permute-start.9 = (bf16[8,4096]{1,0:T(8,128)(2,1)S(1)}, bf16[8,4096]{1,0:T(8,128)(2,1)S(1)}, u32[]{:S(2)}, u32[]{:S(2)}) collective-permute-start(bf16[8,4096]{1,0:T(8,128)(2,1)S(1)} %get-tuple-element.61), channel_id=1, source_target_pairs={{0,1},{1,0},{2,3},{3,2},{4,5},{5,4},{6,7},{7,6},{8,9},{9,8},{10,11... | collective-permute-start | bytes 196616 | tf_op jit(solution)/shard_map/ppermute | solution.py:650
  37.4 8.5 %collective-permute-start.15 = (f32[8,2048]{1,0:T(8,128)S(1)}, f32[8,2048]{1,0:T(8,128)S(1)}, u32[]{:S(2)}, u32[]{:S(2)}) collective-permute-start(f32[8,2048]{1,0:T(8,128)S(1)} %get-tuple-element.64), channel_id=1, source_target_pairs={{0,4},{4,0},{8,12},{12,8},{16,20},{20,16},{24,28},{28,24},{1,5},{5... | collective-permute-start | bytes 196616 | tf_op jit(solution)/shard_map/ppermute | solution.py:647
  37.4 5.5 %collective-permute-start.11 = (f32[16,128]{1,0:T(8,128)S(1)}, f32[16,128]{1,0:T(8,128)S(1)}, u32[]{:S(2)}, u32[]{:S(2)}) collective-permute-start(f32[16,128]{1,0:T(8,128)S(1)} %get-tuple-element.63.refs_0_), channel_id=1, source_target_pairs={{0,24},{4,28},{8,16},{12,20},{16,8},{20,12},{24,0},{28,4},{1,25},{... | collective-permute-start | bytes 24584 | tf_op jit(solution)/shard_map/ppermute | solution.py:647
  40.0 4.6 %collective-permute-start.12 = (f32[16,128]{1,0:T(8,128)S(1)}, f32[16,128]{1,0:T(8,128)S(1)}, u32[]{:S(2)}, u32[]{:S(2)}) collective-permute-start(f32[16,128]{1,0:T(8,128)S(1)} %get-tuple-element.63.refs_0_), channel_id=1, source_target_pairs={{0,16},{4,20},{8,24},{12,28},{16,0},{20,4},{24,8},{28,12},{1,17},{... | collective-permute-start | bytes 24584 | tf_op jit(solution)/shard_map/ppermute | solution.py:647
  40.5 4.1 %collective-permute-start.13 = (f32[16,128]{1,0:T(8,128)S(1)}, f32[16,128]{1,0:T(8,128)S(1)}, u32[]{:S(2)}, u32[]{:S(2)}) collective-permute-start(f32[16,128]{1,0:T(8,128)S(1)} %get-tuple-element.63.refs_0_), channel_id=1, source_target_pairs={{0,8},{4,12},{8,0},{12,4},{16,24},{20,28},{24,16},{28,20},{1,9},{5... | collective-permute-start | bytes 24584 | tf_op jit(solution)/shard_map/ppermute | solution.py:647
  44.7 1.2 %collective-permute-start.14 = (f32[16,128]{1,0:T(8,128)S(1)}, f32[16,128]{1,0:T(8,128)S(1)}, u32[]{:S(2)}, u32[]{:S(2)}) collective-permute-start(f32[16,128]{1,0:T(8,128)S(1)} %merge_stats.3.stats_ref), channel_id=1, source_target_pairs={{0,4},{4,0},{8,12},{12,8},{16,20},{20,16},{24,28},{28,24},{1,5},{5... | collective-permute-start | bytes 24584 | tf_op jit(solution)/shard_map/ppermute | solution.py:647
  47.1 4.0 %collective-permute-start.19 = (bf16[4,128,128]{2,1,0:T(8,128)(2,1)S(1)}, bf16[4,128,128]{2,1,0:T(8,128)(2,1)S(1)}, u32[]{:S(2)}, u32[]{:S(2)}) collective-permute-start(bf16[4,128,128]{2,1,0:T(8,128)(2,1)S(1)} %get-tuple-element.75), channel_id=1, source_target_pairs={{0,4},{4,0},{8,12},{12,8},{16,20},{20,16},{24,28},{28,24},{1,5},{5... | collective-permute-start | bytes 393224 | tf_op jit(solution)/shard_map/ppermute | solution.py:647
  47.7 7.3 %collective-permute-start.16 = (bf16[512,128]{1,0:T(8,128)(2,1)S(1)}, bf16[512,128]{1,0:T(8,128)(2,1)S(1)}, u32[]{:S(2)}, u32[]{:S(2)}) collective-permute-start(bf16[512,128]{1,0:T(8,128)(2,1)S(1)} %get-tuple-element.71), channel_id=1, source_target_pairs={{0,3},{1,2},{2,1},{3,0},{4,7},{5,6},{6,5},{7,4},{8,11},{9,10},{10,... | collective-permute-start | bytes 393224 | tf_op jit(solution)/shard_map/ppermute | solution.py:650
  49.2 7.7 %collective-permute-start.17 = (bf16[512,128]{1,0:T(8,128)(2,1)S(1)}, bf16[512,128]{1,0:T(8,128)(2,1)S(1)}, u32[]{:S(2)}, u32[]{:S(2)}) collective-permute-start(bf16[512,128]{1,0:T(8,128)(2,1)S(1)} %get-tuple-element.72), channel_id=1, source_target_pairs={{0,2},{1,3},{2,0},{3,1},{4,6},{5,7},{6,4},{7,5},{8,10},{9,11},{10,... | collective-permute-start | bytes 393224 | tf_op jit(solution)/shard_map/ppermute | solution.py:650
  49.7 7.3 %collective-permute-start.18 = (bf16[512,128]{1,0:T(8,128)(2,1)S(1)}, bf16[512,128]{1,0:T(8,128)(2,1)S(1)}, u32[]{:S(2)}, u32[]{:S(2)}) collective-permute-start(bf16[512,128]{1,0:T(8,128)(2,1)S(1)} %get-tuple-element.73), channel_id=1, source_target_pairs={{0,1},{1,0},{2,3},{3,2},{4,5},{5,4},{6,7},{7,6},{8,9},{9,8},{10,11... | collective-permute-start | bytes 393224 | tf_op jit(solution)/shard_map/ppermute | solution.py:650
  51.2 5.8 %collective-permute-start.20 = (bf16[128,128]{1,0:T(8,128)(2,1)S(1)}, bf16[128,128]{1,0:T(8,128)(2,1)S(1)}, u32[]{:S(2)}, u32[]{:S(2)}) collective-permute-start(bf16[128,128]{1,0:T(8,128)(2,1)S(1)} %get-tuple-element.77), channel_id=1, source_target_pairs={{0,24},{4,28},{8,16},{12,20},{16,8},{20,12},{24,0},{28,4},{1,25},{... | collective-permute-start | bytes 98312 | tf_op jit(solution)/shard_map/ppermute | solution.py:647
  53.3 5.1 %collective-permute-start.21 = (bf16[128,128]{1,0:T(8,128)(2,1)S(1)}, bf16[128,128]{1,0:T(8,128)(2,1)S(1)}, u32[]{:S(2)}, u32[]{:S(2)}) collective-permute-start(bf16[128,128]{1,0:T(8,128)(2,1)S(1)} %get-tuple-element.78), channel_id=1, source_target_pairs={{0,16},{4,20},{8,24},{12,28},{16,0},{20,4},{24,8},{28,12},{1,17},{... | collective-permute-start | bytes 98312 | tf_op jit(solution)/shard_map/ppermute | solution.py:647
  54.9 3.9 %collective-permute-start.22 = (bf16[128,128]{1,0:T(8,128)(2,1)S(1)}, bf16[128,128]{1,0:T(8,128)(2,1)S(1)}, u32[]{:S(2)}, u32[]{:S(2)}) collective-permute-start(bf16[128,128]{1,0:T(8,128)(2,1)S(1)} %get-tuple-element.79), channel_id=1, source_target_pairs={{0,8},{4,12},{8,0},{12,4},{16,24},{20,28},{24,16},{28,20},{1,9},{5... | collective-permute-start | bytes 98312 | tf_op jit(solution)/shard_map/ppermute | solution.py:647

commit v6 on v5

--- a/solution.py
+++ b/solution.py
@@ -686,7 +686,7 @@
         lengths, context_flip(stats, 1), got_mass, *back, query_grad, key_grad, partners, planes
     )
     got = context_flip(send, 1)
-    key_parts = [key_grads[0]] + [heads_flip(key_grads[e], e) for e in reversed(range(1, partners))]
+    key_parts = [key_grads[0]] + [heads_flip(key_grads[e], e) for e in range(1, partners)]
     sums = pair_sums(keep, got)
     query_parts = [sums[0]] + [context_flip(sums[e], 2 * e) for e in reversed(range(1, planes))]
     return last_sums(key_parts, query_parts, (own_rows, index_heads // contexts, width))

time: 59.8 us -> 59.4 us (level)
  waiting for transfers between devices: 13.4 us -> 12.4 us
  starting transfers between devices: 29.1 us -> 29.7 us
    ppermute x6, waiting for transfers between devices: 5.96 us -> 5.28 us  [heads_flip(): return lax.ppermute(array, 'heads', [(h, h ^ e) for h in range(partners)])]
    ppermute x11, starting transfers between devices: 9.03 us -> 9.66 us  [context_flip(): return lax.ppermute(array, 'context', [(c, c ^ e) for c in range(contexts)])]
  transfers between devices with their start and end apart: 23 -> 23, of which waited for: 15 -> 14; matrix products, arithmetic and copies ran while one was open for 0% -> 0% of each run, Pallas kernels for 20% -> 20%
where the time goes in v6:
time: 59.4 us; the launch traced here: 59.2 us
  starting transfers between devices  29.7 us (50%)
  Pallas kernels  15 us (25%)
  waiting for transfers between devices  12.4 us (21%)
  local copies, waits for them, and re-layouts  1.28 us (2%)
  between operations  0.88 us (1%)
    ppermute x6, starting transfers between devices, planes_move(): lax.ppermute(array, 'context', [(2 * a + k, 2 * b + k) for a, b in pairs...  13 us
    ppermute x11, starting transfers between devices, context_flip(): return lax.ppermute(array, 'context', [(c, c ^ e) for c in range(contexts)])  9.66 us
    ppermute x6, starting transfers between devices, heads_flip(): return lax.ppermute(array, 'heads', [(h, h ^ e) for h in range(partners)])  7.04 us
    pallas_call x4, Pallas kernels, chunk_mass(): local_call(functools.partial(mass_kernel, flip, blocks), f32((rows, 2 * k...  6.8 us
    ppermute x11, waiting for transfers between devices, context_flip(): return lax.ppermute(array, 'context', [(c, c ^ e) for c in range(contexts)])  5.41 us
    ppermute x6, waiting for transfers between devices, heads_flip(): return lax.ppermute(array, 'heads', [(h, h ^ e) for h in range(partners)])  5.28 us
    pallas_call x1, Pallas kernels, index_logits(): local_call(logits_kernel, [f32((rows, key_count)), f32((flat, key_count))...  1.84 us
    ppermute x6, waiting for transfers between devices, planes_move(): lax.ppermute(array, 'context', [(2 * a + k, 2 * b + k) for a, b in pairs...  1.68 us
  transfers between devices with their start and end apart: 23, of which 14 were waited for; matrix products, arithmetic and copies ran while one was open for 0% of the time, Pallas kernels for 20%

profile of v6, /device:TPU:0, one launch (start us, length us, event | category | flops | bytes accessed | tf_op | source)
XLA Modules:
  0.0 59.2 jit_solution(2555669878929274622)
XLA Ops:
  1.2 1.3 %copy-done.6 = bf16[8,32,576]{2,1,0:T(8,128)(2,1)S(1)} copy-done((bf16[8,32,576]{2,1,0:T(8,128)(2,1)S(1)}, bf16[8,32,576]{2,1,0:T(8,128)(2,1)}, u32[]{:S(2)}) %copy-start.6) | copy-done | bytes 294936
  2.6 0.7 %collective-permute-start.3 = (bf16[720,128]{1,0:T(8,128)(2,1)S(1)}, bf16[720,128]{1,0:T(8,128)(2,1)S(1)}, u32[]{:S(2)}, u32[]{:S(2)}) collective-permute-start(bf16[720,128]{1,0:T(8,128)(2,1)S(1)} %get-tuple-element.51), channel_id=1, source_target_pairs={{8,16},{12,20},{16,8},{20,12},{0,0},{4,4},{24,24},{28,28},{9,17},{... | collective-permute-start | bytes 552968 | tf_op jit(solution)/shard_map/ppermute | solution.py:644
  3.3 5.3 %collective-permute-start.7 = (bf16[1152,128]{1,0:T(8,128)(2,1)S(1)}, bf16[1152,128]{1,0:T(8,128)(2,1)S(1)}, u32[]{:S(2)}, u32[]{:S(2)}) collective-permute-start(bf16[1152,128]{1,0:T(8,128)(2,1)S(1)} %get-tuple-element.41.pack_ref), channel_id=1, source_target_pairs={{0,8},{4,12},{8,0},{12,4},{16,24},{20,28},{24,16},{28,20},{1,9},{5... | collective-permute-start | bytes 884744 | tf_op jit(solution)/shard_map/ppermute | solution.py:644
  8.7 3.2 %collective-permute-start.5 = (bf16[1152,128]{1,0:T(8,128)(2,1)S(1)}, bf16[1152,128]{1,0:T(8,128)(2,1)S(1)}, u32[]{:S(2)}, u32[]{:S(2)}) collective-permute-start(bf16[1152,128]{1,0:T(8,128)(2,1)S(1)} %get-tuple-element.41.pack_ref), channel_id=1, source_target_pairs={{0,24},{4,28},{24,0},{28,4},{1,25},{5,29},{25,1},{29,5},{2,26},{6,... | collective-permute-start | bytes 884744 | tf_op jit(solution)/shard_map/ppermute | solution.py:644
  11.9 0.7 %collective-permute-start.1 = (bf16[432,128]{1,0:T(8,128)(2,1)S(1)}, bf16[432,128]{1,0:T(8,128)(2,1)S(1)}, u32[]{:S(2)}, u32[]{:S(2)}) collective-permute-start(bf16[432,128]{1,0:T(8,128)(2,1)S(1)} %get-tuple-element.48), channel_id=1, source_target_pairs={{8,16},{12,20},{16,8},{20,12},{0,0},{4,4},{24,24},{28,28},{9,17},{... | collective-permute-start | bytes 331784 | tf_op jit(solution)/shard_map/ppermute | solution.py:644
  12.6 1.2 %load_inputs.1 = (s32[64,128]{1,0:T(8,128)S(1)}, f32[64,32]{1,0:T(8,128)S(1)}, f32[1024,128]{1,0:T(8,128)S(1)}, bf16[16,64,128]{2,1,0:T(8,128)(2,1)S(1)}, bf16[1...) custom-call(s32[64]{0:T(128)S(1)} %copy-done.5, f32[32,64]{1,0:T(8,128)S(1)} %bitcast.7, ...), custom_call_target="tpu_custom_call" | custom-call | flops 1 | bytes 1 | tf_op jit(solution)/shard_map/load_inputs/pallas_call | solution.py:436
  13.9 1.5 %collective-permute-start.4 = (bf16[720,128]{1,0:T(8,128)(2,1)S(1)}, bf16[720,128]{1,0:T(8,128)(2,1)S(1)}, u32[]{:S(2)}, u32[]{:S(2)}) collective-permute-start(bf16[720,128]{1,0:T(8,128)(2,1)S(1)} %collective-permute-done.3.refs_0_), channel_id=1, source_target_pairs={{0,16},{4,20},{24,8},{28,12},{8,0},{12,4},{16,24},{20,28},{1,17},{... | collective-permute-start | bytes 552968 | tf_op jit(solution)/shard_map/ppermute | solution.py:644
  15.4 1.8 %index_logits.1 = (f32[16,2048]{1,0:T(8,128)S(1)}, f32[1024,2048]{1,0:T(8,128)S(1)}, f32[16,128]{1,0:T(8,128)S(1)}) custom-call(s32[64,128]{1,0:T(8,128)S(1)} %get-tuple-element.43.length_ref, bf16[1024,128]{1,0:T(8,128)(2,1)S(1)} %bitcast.6, bf16[2048,128]{1,0:T(8,128)(2,1)S(1)} %get-tuple-element.45.key_ref, f32[1024,128]{1,0:T(8,128)S(1)} %get-tuple-element.46.weight_ref), custom_call_target="tpu_custom_call" | custom-call | flops 1 | bytes 1 | tf_op jit(solution)/shard_map/index_logits/pallas_call | solution.py:392
  17.3 1.2 %collective-permute-done.refs_1_ = f32[16,128]{1,0:T(8,128)S(1)} collective-permute-done((f32[16,128]{1,0:T(8,128)S(1)}, f32[16,128]{1,0:T(8,128)S(1)}, u32[]{:S(2)}, u32[]{:S(2)}) %collective-permute-start) | collective-permute-done | bytes 8224 | tf_op jit(solution)/shard_map/ppermute | solution.py:647
  18.5 1.5 %collective-permute-start.2 = (bf16[432,128]{1,0:T(8,128)(2,1)S(1)}, bf16[432,128]{1,0:T(8,128)(2,1)S(1)}, u32[]{:S(2)}, u32[]{:S(2)}) collective-permute-start(bf16[432,128]{1,0:T(8,128)(2,1)S(1)} %collective-permute-done.1.refs_1_), channel_id=1, source_target_pairs={{0,16},{4,20},{24,8},{28,12},{8,0},{12,4},{16,24},{20,28},{1,17},{... | collective-permute-start | bytes 331784 | tf_op jit(solution)/shard_map/ppermute | solution.py:644
  20.2 1.8 %mass_own.1.own_ref = f32[8,4096]{1,0:T(8,128)S(1)} custom-call(s32[64,128]{1,0:T(8,128)S(1)} %get-tuple-element.43.length_ref, bf16[1152,128]{1,0:T(8,128)(2,1)S(1)} %get-tuple-element.41.pack_ref, f32[64,32]{1,0:T(8,128)S(1)} %get-tuple-element.49.lse_ref, bf16[576,2048]{1,0:T(8,128)(2,1)S(1)} %get-tuple-element.53.own_key_ref, ...), custom_call_target="tpu_custom_call" | custom-call | flops 1 | bytes 1 | tf_op jit(solution)/shard_map/mass_own/pallas_call | solution.py:323
  22.0 1.8 %mass_near.1.near_ref = f32[8,4096]{1,0:T(8,128)S(1)} custom-call(s32[64,128]{1,0:T(8,128)S(1)} %get-tuple-element.43.length_ref, bf16[1152,128]{1,0:T(8,128)(2,1)S(1)} %collective-permute-done.7.pack_ref, f32[64,32]{1,0:T(8,128)S(1)} %get-tuple-element.49.lse_ref, bf16[576,2048]{1,0:T(8,128)(2,1)S(1)} %get-tuple-element.53.own_key_ref, ...), custom_call_target="tpu_custom_call" | custom-call | flops 100000000 | bytes 1 | tf_op jit(solution)/shard_map/mass_near/pallas_call | solution.py:323
  24.4 1.8 %mass_across.1.across_ref = f32[8,4096]{1,0:T(8,128)S(1)} custom-call(s32[64,128]{1,0:T(8,128)S(1)} %get-tuple-element.43.length_ref, bf16[1152,128]{1,0:T(8,128)(2,1)S(1)} %pick_queries.1.pack_ref, f32[64,32]{1,0:T(8,128)S(1)} %get-tuple-element.49.lse_ref, bf16[576,2048]{1,0:T(8,128)(2,1)S(1)} %get-tuple-element.53.own_key_ref, ...), custom_call_target="tpu_custom_call" | custom-call | flops 50000000 | bytes 1 | tf_op jit(solution)/shard_map/mass_across/pallas_call | solution.py:323
  26.2 1.1 %collective-permute-done.4.pack_ref = bf16[720,128]{1,0:T(8,128)(2,1)S(1)} collective-permute-done((bf16[720,128]{1,0:T(8,128)(2,1)S(1)}, bf16[720,128]{1,0:T(8,128)(2,1)S(1)}, u32[]{:S(2)}, u32[]{:S(2)}) %collective-permute-start.4) | collective-permute-done | bytes 184352 | tf_op jit(solution)/shard_map/ppermute | solution.py:644
  27.3 1.3 %mass_far.1.before_ref = f32[8,4096]{1,0:T(8,128)S(1)} custom-call(s32[64,128]{1,0:T(8,128)S(1)} %get-tuple-element.43.length_ref, bf16[720,128]{1,0:T(8,128)(2,1)S(1)} %collective-permute-done.4.pack_ref, f32[64,32]{1,0:T(8,128)S(1)} %get-tuple-element.49.lse_ref, bf16[576,2048]{1,0:T(8,128)(2,1)S(1)} %get-tuple-element.53.own_key_ref, ...), custom_call_target="tpu_custom_call" | custom-call | flops 1 | bytes 1 | tf_op jit(solution)/shard_map/mass_far/pallas_call | solution.py:323
  28.9 1.1 %mass_and_share.1 = (f32[8,4096]{1,0:T(8,128)S(1)}, bf16[8,4096]{1,0:T(8,128)(2,1)S(1)}, bf16[8,4096]{1,0:T(8,128)(2,1)S(1)}, bf16[8,4096]{1,0:T(8,128)(2,1)S(1)}) custom-call(s32[64,128]{1,0:T(8,128)S(1)} %get-tuple-element.43.length_ref, bf16[432,128]{1,0:T(8,128)(2,1)S(1)} %collective-permute-done.2.pack_ref, f32[64,32]{1,0:T(8,128)S(1)} %get-tuple-element.49.lse_ref, ...), custom_call_target="tpu_custom_call" | custom-call | flops 1 | bytes 1 | tf_op jit(solution)/shard_map/mass_and_share/pallas_call | solution.py:355
  30.0 2.5 %collective-permute-start.10 = (bf16[8,4096]{1,0:T(8,128)(2,1)S(1)}, bf16[8,4096]{1,0:T(8,128)(2,1)S(1)}, u32[]{:S(2)}, u32[]{:S(2)}) collective-permute-start(bf16[8,4096]{1,0:T(8,128)(2,1)S(1)} %get-tuple-element.62), channel_id=1, source_target_pairs={{0,3},{1,2},{2,1},{3,0},{4,7},{5,6},{6,5},{7,4},{8,11},{9,10},{10,... | collective-permute-start | bytes 196616 | tf_op jit(solution)/shard_map/ppermute | solution.py:650
  33.6 1.8 %collective-permute-done.10.refs_2_ = bf16[8,4096]{1,0:T(8,128)(2,1)S(1)} collective-permute-done((bf16[8,4096]{1,0:T(8,128)(2,1)S(1)}, bf16[8,4096]{1,0:T(8,128)(2,1)S(1)}, u32[]{:S(2)}, u32[]{:S(2)}) %collective-permute-start.10) | collective-permute-done | bytes 65568 | tf_op jit(solution)/shard_map/ppermute | solution.py:650
  35.3 1.4 %collective-permute-done.8.refs_0_ = bf16[8,4096]{1,0:T(8,128)(2,1)S(1)} collective-permute-done((bf16[8,4096]{1,0:T(8,128)(2,1)S(1)}, bf16[8,4096]{1,0:T(8,128)(2,1)S(1)}, u32[]{:S(2)}, u32[]{:S(2)}) %collective-permute-start.8) | collective-permute-done | bytes 65568 | tf_op jit(solution)/shard_map/ppermute | solution.py:650
  37.4 2.5 %collective-permute-start.11 = (f32[16,128]{1,0:T(8,128)S(1)}, f32[16,128]{1,0:T(8,128)S(1)}, u32[]{:S(2)}, u32[]{:S(2)}) collective-permute-start(f32[16,128]{1,0:T(8,128)S(1)} %get-tuple-element.63.refs_0_), channel_id=1, source_target_pairs={{0,24},{4,28},{8,16},{12,20},{16,8},{20,12},{24,0},{28,4},{1,25},{... | collective-permute-start | bytes 24584 | tf_op jit(solution)/shard_map/ppermute | solution.py:647
  40.5 1.4 %collective-permute-start.13 = (f32[16,128]{1,0:T(8,128)S(1)}, f32[16,128]{1,0:T(8,128)S(1)}, u32[]{:S(2)}, u32[]{:S(2)}) collective-permute-start(f32[16,128]{1,0:T(8,128)S(1)} %get-tuple-element.63.refs_0_), channel_id=1, source_target_pairs={{0,8},{4,12},{8,0},{12,4},{16,24},{20,28},{24,16},{28,20},{1,9},{5... | collective-permute-start | bytes 24584 | tf_op jit(solution)/shard_map/ppermute | solution.py:647
  41.9 1.1 %collective-permute-done.11.refs_1_ = f32[16,128]{1,0:T(8,128)S(1)} collective-permute-done((f32[16,128]{1,0:T(8,128)S(1)}, f32[16,128]{1,0:T(8,128)S(1)}, u32[]{:S(2)}, u32[]{:S(2)}) %collective-permute-start.11) | collective-permute-done | bytes 8224 | tf_op jit(solution)/shard_map/ppermute | solution.py:647
  42.9 1.6 %collective-permute-done.12.refs_2_ = f32[16,128]{1,0:T(8,128)S(1)} collective-permute-done((f32[16,128]{1,0:T(8,128)S(1)}, f32[16,128]{1,0:T(8,128)S(1)}, u32[]{:S(2)}, u32[]{:S(2)}) %collective-permute-start.12) | collective-permute-done | bytes 8224 | tf_op jit(solution)/shard_map/ppermute | solution.py:647
  44.7 1.1 %index_back_own.1 = (f32[512,128]{1,0:T(8,128)S(1)}, f32[128,2048]{1,0:T(8,128)S(1)}) custom-call(s32[64,128]{1,0:T(8,128)S(1)} %get-tuple-element.43.length_ref, f32[16,128]{1,0:T(8,128)S(1)} %merge_stats.3.stats_ref, f32[8,2048]{1,0:T(8,128)S(1)} %get-tuple-element.67.mass_ref, f32[16,2048]{1,0:T(8,128)S(1)} %get-tuple-element.54.logits_ref, ...), custom_call_target="tpu_custom_call" | custom-call | flops 1 | bytes 1 | tf_op jit(solution)/shard_map/index_back_own/pallas_call | solution.py:536
  45.9 1.2 %index_back_pair.1 = (f32[512,128]{1,0:T(8,128)S(1)}, bf16[512,128]{1,0:T(8,128)(2,1)S(1)}, bf16[512,128]{1,0:T(8,128)(2,1)S(1)}, bf16[512,128]{1,0:T(8,128)(2,1...) custom-call(s32[64,128]{1,0:T(8,128)S(1)} %get-tuple-element.43.length_ref, ...), custom_call_target="tpu_custom_call" | custom-call | flops 1 | bytes 1 | tf_op jit(solution)/shard_map/index_back_pair/pallas_call | solution.py:580
  48.2 1.5 %collective-permute-start.17 = (bf16[512,128]{1,0:T(8,128)(2,1)S(1)}, bf16[512,128]{1,0:T(8,128)(2,1)S(1)}, u32[]{:S(2)}, u32[]{:S(2)}) collective-permute-start(bf16[512,128]{1,0:T(8,128)(2,1)S(1)} %get-tuple-element.72), channel_id=1, source_target_pairs={{0,2},{1,3},{2,0},{3,1},{4,6},{5,7},{6,4},{7,5},{8,10},{9,11},{10,... | collective-permute-start | bytes 393224 | tf_op jit(solution)/shard_map/ppermute | solution.py:650
  49.7 1.4 %collective-permute-start.18 = (bf16[512,128]{1,0:T(8,128)(2,1)S(1)}, bf16[512,128]{1,0:T(8,128)(2,1)S(1)}, u32[]{:S(2)}, u32[]{:S(2)}) collective-permute-start(bf16[512,128]{1,0:T(8,128)(2,1)S(1)} %get-tuple-element.73), channel_id=1, source_target_pairs={{0,3},{1,2},{2,1},{3,0},{4,7},{5,6},{6,5},{7,4},{8,11},{9,10},{10,... | collective-permute-start | bytes 393224 | tf_op jit(solution)/shard_map/ppermute | solution.py:650
  51.2 2.1 %collective-permute-start.20 = (bf16[128,128]{1,0:T(8,128)(2,1)S(1)}, bf16[128,128]{1,0:T(8,128)(2,1)S(1)}, u32[]{:S(2)}, u32[]{:S(2)}) collective-permute-start(bf16[128,128]{1,0:T(8,128)(2,1)S(1)} %get-tuple-element.77), channel_id=1, source_target_pairs={{0,24},{4,28},{8,16},{12,20},{16,8},{20,12},{24,0},{28,4},{1,25},{... | collective-permute-start | bytes 98312 | tf_op jit(solution)/shard_map/ppermute | solution.py:647
  54.0 1.6 %collective-permute-start.22 = (bf16[128,128]{1,0:T(8,128)(2,1)S(1)}, bf16[128,128]{1,0:T(8,128)(2,1)S(1)}, u32[]{:S(2)}, u32[]{:S(2)}) collective-permute-start(bf16[128,128]{1,0:T(8,128)(2,1)S(1)} %get-tuple-element.79), channel_id=1, source_target_pairs={{0,8},{4,12},{8,0},{12,4},{16,24},{20,28},{24,16},{28,20},{1,9},{5... | collective-permute-start | bytes 98312 | tf_op jit(solution)/shard_map/ppermute | solution.py:647
  55.6 1.3 %collective-permute-done.18.refs_3_ = bf16[512,128]{1,0:T(8,128)(2,1)S(1)} collective-permute-done((bf16[512,128]{1,0:T(8,128)(2,1)S(1)}, bf16[512,128]{1,0:T(8,128)(2,1)S(1)}, u32[]{:S(2)}, u32[]{:S(2)}) %collective-permute-start.18) | collective-permute-done | bytes 131104 | tf_op jit(solution)/shard_map/ppermute | solution.py:650
  57.0 1.5 %collective-permute-done.21.refs_6_ = bf16[128,128]{1,0:T(8,128)(2,1)S(1)} collective-permute-done((bf16[128,128]{1,0:T(8,128)(2,1)S(1)}, bf16[128,128]{1,0:T(8,128)(2,1)S(1)}, u32[]{:S(2)}, u32[]{:S(2)}) %collective-permute-start.21) | collective-permute-done | bytes 32800 | tf_op jit(solution)/shard_map/ppermute | solution.py:647
  58.4 0.8 %last_sums.1 = (f32[16,8,128]{2,1,0:T(8,128)}, f32[512,128]{1,0:T(8,128)}) custom-call(f32[512,128]{1,0:T(8,128)S(1)} %get-tuple-element.70.refs_0_, bf16[512,128]{1,0:T(8,128)(2,1)S(1)} %collective-permute-done.16.refs_1_, bf16[512,128]{1,0:T(8,128)(2,1)S(1)} %collective-permute-done.17.refs_2_, bf16[512,128]{1,0:T(8,128)(2,1)S(1)} %collective-permute-done.18.refs_3_, ...), custom_call_target="tpu_custom_call" | custom-call | flops 1 | bytes 1 | tf_op jit(solution)/shard_map/last_sums/pallas_call | solution.py:619
  (44 shorter events, 6.0 us)
Async XLA Ops:
  0.6 12.0 %copy-start = (bf16[2048,576]{0,1:T(8,128)(2,1)S(1)}, bf16[2048,576]{0,1:T(8,128)(2,1)}, u32[]{:S(2)}) copy-start(bf16[2048,576]{0,1:T(8,128)(2,1)} %param.8) | copy-start | bytes 7077892
  0.6 12.0 %copy-start.1 = (bf16[2048,128]{1,0:T(8,128)(2,1)S(1)}, bf16[2048,128]{1,0:T(8,128)(2,1)}, u32[]{:S(2)}) copy-start(bf16[2048,128]{1,0:T(8,128)(2,1)} %key_hbm.1) | copy-start | bytes 1572868
  0.7 12.0 %copy-start.2 = (bf16[16,64,128]{2,1,0:T(8,128)(2,1)S(1)}, bf16[16,64,128]{2,1,0:T(8,128)(2,1)}, u32[]{:S(2)}) copy-start(bf16[16,64,128]{2,1,0:T(8,128)(2,1)} %query_hbm.1) | copy-start | bytes 786436
  0.7 12.0 %copy-start.3 = (f32[64,32]{0,1:T(8,128)S(1)}, f32[64,32]{0,1:T(8,128)}, u32[]{:S(2)}) copy-start(f32[64,32]{0,1:T(8,128)} %param.9) | copy-start | bytes 24580
  0.7 12.0 %copy-start.4 = (f32[16,64]{1,0:T(8,128)S(1)}, f32[16,64]{1,0:T(8,128)}, u32[]{:S(2)}) copy-start(f32[16,64]{1,0:T(8,128)} %weight_ref.1) | copy-start | bytes 12292
  0.7 12.0 %copy-start.5 = (s32[64]{0:T(128)S(1)}, s32[64]{0:T(128)}, u32[]{:S(2)}) copy-start(s32[64]{0:T(128)} %length_ref.1) | copy-start | bytes 772
  0.7 19.5 %collective-permute-start.6 = (bf16[576,2048]{1,0:T(8,128)(2,1)}, bf16[576,2048]{1,0:T(8,128)(2,1)S(1)}, u32[]{:S(2)}, u32[]{:S(2)}) collective-permute-start(bf16[576,2048]{1,0:T(8,128)(2,1)} %bitcast.4), channel_id=1, source_target_pairs={{0,4},{4,0},{8,12},{12,8},{16,20},{20,16},{24,28},{28,24},{1,5},{5... | collective-permute-start | bytes 7077896 | tf_op jit(solution)/shard_map/ppermute | solution.py:647
  1.2 1.3 %copy-start.6 = (bf16[8,32,576]{2,1,0:T(8,128)(2,1)S(1)}, bf16[8,32,576]{2,1,0:T(8,128)(2,1)}, u32[]{:S(2)}) copy-start(bf16[8,32,576]{2,1,0:T(8,128)(2,1)} %query_ref.1) | copy-start | bytes 884740
  2.6 11.2 %collective-permute-start.3 = (bf16[720,128]{1,0:T(8,128)(2,1)S(1)}, bf16[720,128]{1,0:T(8,128)(2,1)S(1)}, u32[]{:S(2)}, u32[]{:S(2)}) collective-permute-start(bf16[720,128]{1,0:T(8,128)(2,1)S(1)} %get-tuple-element.51), channel_id=1, source_target_pairs={{8,16},{12,20},{16,8},{20,12},{0,0},{4,4},{24,24},{28,28},{9,17},{... | collective-permute-start | bytes 552968 | tf_op jit(solution)/shard_map/ppermute | solution.py:644
  3.3 16.8 %collective-permute-start.7 = (bf16[1152,128]{1,0:T(8,128)(2,1)S(1)}, bf16[1152,128]{1,0:T(8,128)(2,1)S(1)}, u32[]{:S(2)}, u32[]{:S(2)}) collective-permute-start(bf16[1152,128]{1,0:T(8,128)(2,1)S(1)} %get-tuple-element.41.pack_ref), channel_id=1, source_target_pairs={{0,8},{4,12},{8,0},{12,4},{16,24},{20,28},{24,16},{28,20},{1,9},{5... | collective-permute-start | bytes 884744 | tf_op jit(solution)/shard_map/ppermute | solution.py:644
  8.7 15.5 %collective-permute-start.5 = (bf16[1152,128]{1,0:T(8,128)(2,1)S(1)}, bf16[1152,128]{1,0:T(8,128)(2,1)S(1)}, u32[]{:S(2)}, u32[]{:S(2)}) collective-permute-start(bf16[1152,128]{1,0:T(8,128)(2,1)S(1)} %get-tuple-element.41.pack_ref), channel_id=1, source_target_pairs={{0,24},{4,28},{24,0},{28,4},{1,25},{5,29},{25,1},{29,5},{2,26},{6,... | collective-permute-start | bytes 884744 | tf_op jit(solution)/shard_map/ppermute | solution.py:644
  11.9 5.4 %collective-permute-start.1 = (bf16[432,128]{1,0:T(8,128)(2,1)S(1)}, bf16[432,128]{1,0:T(8,128)(2,1)S(1)}, u32[]{:S(2)}, u32[]{:S(2)}) collective-permute-start(bf16[432,128]{1,0:T(8,128)(2,1)S(1)} %get-tuple-element.48), channel_id=1, source_target_pairs={{8,16},{12,20},{16,8},{20,12},{0,0},{4,4},{24,24},{28,28},{9,17},{... | collective-permute-start | bytes 331784 | tf_op jit(solution)/shard_map/ppermute | solution.py:644
  13.9 13.4 %collective-permute-start.4 = (bf16[720,128]{1,0:T(8,128)(2,1)S(1)}, bf16[720,128]{1,0:T(8,128)(2,1)S(1)}, u32[]{:S(2)}, u32[]{:S(2)}) collective-permute-start(bf16[720,128]{1,0:T(8,128)(2,1)S(1)} %collective-permute-done.3.refs_0_), channel_id=1, source_target_pairs={{0,16},{4,20},{24,8},{28,12},{8,0},{12,4},{16,24},{20,28},{1,17},{... | collective-permute-start | bytes 552968 | tf_op jit(solution)/shard_map/ppermute | solution.py:644
  17.3 1.2 %collective-permute-start = (f32[16,128]{1,0:T(8,128)S(1)}, f32[16,128]{1,0:T(8,128)S(1)}, u32[]{:S(2)}, u32[]{:S(2)}) collective-permute-start(f32[16,128]{1,0:T(8,128)S(1)} %get-tuple-element.47.refs_0_), channel_id=1, source_target_pairs={{0,4},{4,0},{8,12},{12,8},{16,20},{20,16},{24,28},{28,24},{1,5},{5... | collective-permute-start | bytes 24584 | tf_op jit(solution)/shard_map/ppermute | solution.py:647
  18.5 10.4 %collective-permute-start.2 = (bf16[432,128]{1,0:T(8,128)(2,1)S(1)}, bf16[432,128]{1,0:T(8,128)(2,1)S(1)}, u32[]{:S(2)}, u32[]{:S(2)}) collective-permute-start(bf16[432,128]{1,0:T(8,128)(2,1)S(1)} %collective-permute-done.1.refs_1_), channel_id=1, source_target_pairs={{0,16},{4,20},{24,8},{28,12},{8,0},{12,4},{16,24},{20,28},{1,17},{... | collective-permute-start | bytes 331784 | tf_op jit(solution)/shard_map/ppermute | solution.py:644
  30.0 5.3 %collective-permute-start.10 = (bf16[8,4096]{1,0:T(8,128)(2,1)S(1)}, bf16[8,4096]{1,0:T(8,128)(2,1)S(1)}, u32[]{:S(2)}, u32[]{:S(2)}) collective-permute-start(bf16[8,4096]{1,0:T(8,128)(2,1)S(1)} %get-tuple-element.62), channel_id=1, source_target_pairs={{0,3},{1,2},{2,1},{3,0},{4,7},{5,6},{6,5},{7,4},{8,11},{9,10},{10,... | collective-permute-start | bytes 196616 | tf_op jit(solution)/shard_map/ppermute | solution.py:650
  32.5 4.3 %collective-permute-start.8 = (bf16[8,4096]{1,0:T(8,128)(2,1)S(1)}, bf16[8,4096]{1,0:T(8,128)(2,1)S(1)}, u32[]{:S(2)}, u32[]{:S(2)}) collective-permute-start(bf16[8,4096]{1,0:T(8,128)(2,1)S(1)} %get-tuple-element.60), channel_id=1, source_target_pairs={{0,2},{1,3},{2,0},{3,1},{4,6},{5,7},{6,4},{7,5},{8,10},{9,11},{10,... | collective-permute-start | bytes 196616 | tf_op jit(solution)/shard_map/ppermute | solution.py:650
  33.0 4.3 %collective-permute-start.9 = (bf16[8,4096]{1,0:T(8,128)(2,1)S(1)}, bf16[8,4096]{1,0:T(8,128)(2,1)S(1)}, u32[]{:S(2)}, u32[]{:S(2)}) collective-permute-start(bf16[8,4096]{1,0:T(8,128)(2,1)S(1)} %get-tuple-element.61), channel_id=1, source_target_pairs={{0,1},{1,0},{2,3},{3,2},{4,5},{5,4},{6,7},{7,6},{8,9},{9,8},{10,11... | collective-permute-start | bytes 196616 | tf_op jit(solution)/shard_map/ppermute | solution.py:650
  37.4 8.5 %collective-permute-start.15 = (f32[8,2048]{1,0:T(8,128)S(1)}, f32[8,2048]{1,0:T(8,128)S(1)}, u32[]{:S(2)}, u32[]{:S(2)}) collective-permute-start(f32[8,2048]{1,0:T(8,128)S(1)} %get-tuple-element.64), channel_id=1, source_target_pairs={{0,4},{4,0},{8,12},{12,8},{16,20},{20,16},{24,28},{28,24},{1,5},{5... | collective-permute-start | bytes 196616 | tf_op jit(solution)/shard_map/ppermute | solution.py:647
  37.4 5.5 %collective-permute-start.11 = (f32[16,128]{1,0:T(8,128)S(1)}, f32[16,128]{1,0:T(8,128)S(1)}, u32[]{:S(2)}, u32[]{:S(2)}) collective-permute-start(f32[16,128]{1,0:T(8,128)S(1)} %get-tuple-element.63.refs_0_), channel_id=1, source_target_pairs={{0,24},{4,28},{8,16},{12,20},{16,8},{20,12},{24,0},{28,4},{1,25},{... | collective-permute-start | bytes 24584 | tf_op jit(solution)/shard_map/ppermute | solution.py:647
  40.0 4.6 %collective-permute-start.12 = (f32[16,128]{1,0:T(8,128)S(1)}, f32[16,128]{1,0:T(8,128)S(1)}, u32[]{:S(2)}, u32[]{:S(2)}) collective-permute-start(f32[16,128]{1,0:T(8,128)S(1)} %get-tuple-element.63.refs_0_), channel_id=1, source_target_pairs={{0,16},{4,20},{8,24},{12,28},{16,0},{20,4},{24,8},{28,12},{1,17},{... | collective-permute-start | bytes 24584 | tf_op jit(solution)/shard_map/ppermute | solution.py:647
  40.5 4.1 %collective-permute-start.13 = (f32[16,128]{1,0:T(8,128)S(1)}, f32[16,128]{1,0:T(8,128)S(1)}, u32[]{:S(2)}, u32[]{:S(2)}) collective-permute-start(f32[16,128]{1,0:T(8,128)S(1)} %get-tuple-element.63.refs_0_), channel_id=1, source_target_pairs={{0,8},{4,12},{8,0},{12,4},{16,24},{20,28},{24,16},{28,20},{1,9},{5... | collective-permute-start | bytes 24584 | tf_op jit(solution)/shard_map/ppermute | solution.py:647
  44.7 1.2 %collective-permute-start.14 = (f32[16,128]{1,0:T(8,128)S(1)}, f32[16,128]{1,0:T(8,128)S(1)}, u32[]{:S(2)}, u32[]{:S(2)}) collective-permute-start(f32[16,128]{1,0:T(8,128)S(1)} %merge_stats.3.stats_ref), channel_id=1, source_target_pairs={{0,4},{4,0},{8,12},{12,8},{16,20},{20,16},{24,28},{28,24},{1,5},{5... | collective-permute-start | bytes 24584 | tf_op jit(solution)/shard_map/ppermute | solution.py:647
  47.1 4.0 %collective-permute-start.19 = (bf16[4,128,128]{2,1,0:T(8,128)(2,1)S(1)}, bf16[4,128,128]{2,1,0:T(8,128)(2,1)S(1)}, u32[]{:S(2)}, u32[]{:S(2)}) collective-permute-start(bf16[4,128,128]{2,1,0:T(8,128)(2,1)S(1)} %get-tuple-element.75), channel_id=1, source_target_pairs={{0,4},{4,0},{8,12},{12,8},{16,20},{20,16},{24,28},{28,24},{1,5},{5... | collective-permute-start | bytes 393224 | tf_op jit(solution)/shard_map/ppermute | solution.py:647
  47.7 6.4 %collective-permute-start.16 = (bf16[512,128]{1,0:T(8,128)(2,1)S(1)}, bf16[512,128]{1,0:T(8,128)(2,1)S(1)}, u32[]{:S(2)}, u32[]{:S(2)}) collective-permute-start(bf16[512,128]{1,0:T(8,128)(2,1)S(1)} %get-tuple-element.71), channel_id=1, source_target_pairs={{0,1},{1,0},{2,3},{3,2},{4,5},{5,4},{6,7},{7,6},{8,9},{9,8},{10,11... | collective-permute-start | bytes 393224 | tf_op jit(solution)/shard_map/ppermute | solution.py:650
  48.2 7.4 %collective-permute-start.17 = (bf16[512,128]{1,0:T(8,128)(2,1)S(1)}, bf16[512,128]{1,0:T(8,128)(2,1)S(1)}, u32[]{:S(2)}, u32[]{:S(2)}) collective-permute-start(bf16[512,128]{1,0:T(8,128)(2,1)S(1)} %get-tuple-element.72), channel_id=1, source_target_pairs={{0,2},{1,3},{2,0},{3,1},{4,6},{5,7},{6,4},{7,5},{8,10},{9,11},{10,... | collective-permute-start | bytes 393224 | tf_op jit(solution)/shard_map/ppermute | solution.py:650
  49.7 7.2 %collective-permute-start.18 = (bf16[512,128]{1,0:T(8,128)(2,1)S(1)}, bf16[512,128]{1,0:T(8,128)(2,1)S(1)}, u32[]{:S(2)}, u32[]{:S(2)}) collective-permute-start(bf16[512,128]{1,0:T(8,128)(2,1)S(1)} %get-tuple-element.73), channel_id=1, source_target_pairs={{0,3},{1,2},{2,1},{3,0},{4,7},{5,6},{6,5},{7,4},{8,11},{9,10},{10,... | collective-permute-start | bytes 393224 | tf_op jit(solution)/shard_map/ppermute | solution.py:650
  51.2 5.8 %collective-permute-start.20 = (bf16[128,128]{1,0:T(8,128)(2,1)S(1)}, bf16[128,128]{1,0:T(8,128)(2,1)S(1)}, u32[]{:S(2)}, u32[]{:S(2)}) collective-permute-start(bf16[128,128]{1,0:T(8,128)(2,1)S(1)} %get-tuple-element.77), channel_id=1, source_target_pairs={{0,24},{4,28},{8,16},{12,20},{16,8},{20,12},{24,0},{28,4},{1,25},{... | collective-permute-start | bytes 98312 | tf_op jit(solution)/shard_map/ppermute | solution.py:647
  53.3 5.1 %collective-permute-start.21 = (bf16[128,128]{1,0:T(8,128)(2,1)S(1)}, bf16[128,128]{1,0:T(8,128)(2,1)S(1)}, u32[]{:S(2)}, u32[]{:S(2)}) collective-permute-start(bf16[128,128]{1,0:T(8,128)(2,1)S(1)} %get-tuple-element.78), channel_id=1, source_target_pairs={{0,16},{4,20},{8,24},{12,28},{16,0},{20,4},{24,8},{28,12},{1,17},{... | collective-permute-start | bytes 98312 | tf_op jit(solution)/shard_map/ppermute | solution.py:647
  54.0 4.4 %collective-permute-start.22 = (bf16[128,128]{1,0:T(8,128)(2,1)S(1)}, bf16[128,128]{1,0:T(8,128)(2,1)S(1)}, u32[]{:S(2)}, u32[]{:S(2)}) collective-permute-start(bf16[128,128]{1,0:T(8,128)(2,1)S(1)} %get-tuple-element.79), channel_id=1, source_target_pairs={{0,8},{4,12},{8,0},{12,4},{16,24},{20,28},{24,16},{28,20},{1,9},{5... | collective-permute-start | bytes 98312 | tf_op jit(solution)/shard_map/ppermute | solution.py:647

commit v7 on v6

--- a/solution.py
+++ b/solution.py
@@ -14,8 +14,6 @@
 log2_e = math.log2(math.e)
 lanes = 128
 vmem_bytes = 20 * 1024 * 1024
-most_bytes = 60 * 1024 * 1024
-load_bytes = 58 * 1024 * 1024
 
 def joined(part, axis, combine):
     gathered = jax.tree.map(lambda a: lax.all_gather(a, axis), part)
@@ -136,21 +134,17 @@
     return (out_query, out_key)
 
 
-def local_call(kernel, out_shape, name, grid=None, in_specs=None, out_specs=None, scratch=(), flops=1, moved=0, room=vmem_bytes):
-    settings = dict(
+def local_call(kernel, out_shape, name, in_specs, out_specs, scratch=(), flops=1):
+    return pl.pallas_call(
+        kernel,
         out_shape=out_shape,
+        in_specs=in_specs,
+        out_specs=out_specs,
         scratch_shapes=list(scratch),
         name=name,
-        compiler_params=pltpu.CompilerParams(vmem_limit_bytes=room),
+        compiler_params=pltpu.CompilerParams(vmem_limit_bytes=vmem_bytes),
         cost_estimate=pl.CostEstimate(flops=flops, bytes_accessed=1, transcendentals=0),
     )
-    if grid is not None:
-        settings["grid"] = grid
-    if in_specs is not None:
-        settings["in_specs"] = in_specs
-    if out_specs is not None:
-        settings["out_specs"] = out_specs
-    return pl.pallas_call(kernel, **settings)
 
 
 def whole():
@@ -159,10 +153,6 @@
 
 def scalars():
     return pl.BlockSpec(memory_space=pltpu.SMEM)
-
-
-def fixed(shape):
-    return pl.BlockSpec(shape, lambda step: (0,) * len(shape))
 
 
 def f32(shape):
@@ -317,7 +307,7 @@
     chip_mass(length_ref, wide_ref, lse_ref, own_key_ref, pair_key_ref, 2 * (plane ^ flip) + core, heads, out_ref)
 
 
-def chunk_mass(lengths, pack, lse, keys, flip, blocks, rows, name, flops=1):
+def chunk_mass(lengths, pack, lse, keys, flip, blocks, rows, name):
     width, key_count = keys[0].shape
     total = rows * sum(count for _, count in blocks)
     return local_call(
@@ -327,7 +317,6 @@
         in_specs=[whole()] * 5,
         out_specs=whole(),
         scratch=[pltpu.VMEM((total, width), jnp.bfloat16)],
-        flops=flops,
     )(lengths, pack, lse, *keys)
 
 
@@ -395,7 +384,6 @@
         "index_logits",
         in_specs=[whole()] * 4,
         out_specs=[whole()] * 3,
-        moved=2 * index_key.size,
     )(lengths, flat_query, index_key, weight_wide)
 
 
@@ -448,7 +436,6 @@
         in_specs=[scalars(), whole(), whole(), hbm(), hbm(), hbm()],
         out_specs=[whole()] * 7,
         scratch=[pltpu.SemaphoreType.DMA((3,))],
-        moved=4 * (key.size + latent.size),
     )(lengths, lse, weights, query, key, latent)
 
 
@@ -604,7 +591,6 @@
         "pair_sums",
         in_specs=[whole(), whole()],
         out_specs=[whole()] * planes,
-        moved=8 * keep.size,
     )(keep, got)
 
 
@@ -622,7 +608,6 @@
         "last_sums",
         in_specs=[whole()] * (len(key_parts) + len(query_parts)),
         out_specs=[whole()] * 2,
-        moved=8 * key_parts[0].size,
     )(*key_parts, *query_parts)
 
 
@@ -664,14 +649,14 @@
     def mass_of(pack, flip, blocks, *rest):
         return chunk_mass(lengths, pack, lse, keys, flip, blocks, rows, *rest)
 
-    inner = [after(block, lse) for block in inner]
+    inner[1] = after(inner[1], lse)
     far = [planes_move(block, [(0, 2), (3, 1), (1, 0), (2, 3)]) for block in inner]
     logits, masked, stats = index_logits(lengths, query.reshape(flat, width), index_key, weight_wide, own_rows)
     stats = merged_stats([stats, context_flip(stats, 1)])
     own_mass = mass_of(pack, 0, blocks, "mass_own")
-    near_mass = mass_of(after(near, logits), 1, blocks, "mass_near", 100_000_000)
-    across_mass = mass_of(picked(after(ends, own_mass, near_mass), inner), 3, blocks, "mass_across", 50_000_000)
-    far_mass = mass_of(after(far[0], across_mass, stats), 2, blocks[:1], "mass_far", 1)
+    near_mass = mass_of(after(near, logits), 1, blocks, "mass_near")
+    across_mass = mass_of(picked(after(ends, own_mass, near_mass), inner), 3, blocks, "mass_across")
+    far_mass = mass_of(after(far[0], across_mass, stats), 2, blocks[:1], "mass_far")
     shared = shared_mass(
         lengths, after(far[1], far_mass), lse, keys, own_mass, near_mass, across_mass, far_mass, blocks[1], partners
     )

time: 59.4 us -> 59.1 us (level)
  waiting for transfers between devices: 12.4 us -> 11.4 us
  starting transfers between devices: 29.7 us -> 30.4 us
    ppermute x11, waiting for transfers between devices: 5.41 us -> 4.11 us  [context_flip(): return lax.ppermute(array, 'context', [(c, c ^ e) for c in range(contexts)])]
where the time goes in v7:
time: 59.1 us; the launch traced here: 58.9 us
  starting transfers between devices  30.4 us (51%)
  Pallas kernels  15 us (25%)
  waiting for transfers between devices  11.4 us (19%)
  local copies, waits for them, and re-layouts  1.28 us (2%)
  between operations  0.87 us (1%)
    ppermute x6, starting transfers between devices, planes_move(): lax.ppermute(array, 'context', [(2 * a + k, 2 * b + k) for a, b in pairs...  13.5 us
    ppermute x11, starting transfers between devices, context_flip(): return lax.ppermute(array, 'context', [(c, c ^ e) for c in range(contexts)])  9.9 us
    ppermute x6, starting transfers between devices, heads_flip(): return lax.ppermute(array, 'heads', [(h, h ^ e) for h in range(partners)])  7.04 us
    pallas_call x4, Pallas kernels, chunk_mass(): local_call(functools.partial(mass_kernel, flip, blocks), f32((rows, 2 * k...  6.81 us
    ppermute x6, waiting for transfers between devices, heads_flip(): return lax.ppermute(array, 'heads', [(h, h ^ e) for h in range(partners)])  5.06 us
    ppermute x11, waiting for transfers between devices, context_flip(): return lax.ppermute(array, 'context', [(c, c ^ e) for c in range(contexts)])  4.11 us
    ppermute x6, waiting for transfers between devices, planes_move(): lax.ppermute(array, 'context', [(2 * a + k, 2 * b + k) for a, b in pairs...  2.2 us
    pallas_call x1, Pallas kernels, index_logits(): local_call(logits_kernel, [f32((rows, key_count)), f32((flat, key_count))...  1.85 us
  transfers between devices with their start and end apart: 23, of which 14 were waited for; matrix products, arithmetic and copies ran while one was open for 0% of the time, Pallas kernels for 20%

profile of v7, /device:TPU:0, one launch (start us, length us, event | category | flops | bytes accessed | tf_op | source)
XLA Modules:
  0.0 58.9 jit_solution(15070256434479351696)
XLA Ops:
  1.2 1.3 %copy-done.6 = bf16[8,32,576]{2,1,0:T(8,128)(2,1)S(1)} copy-done((bf16[8,32,576]{2,1,0:T(8,128)(2,1)S(1)}, bf16[8,32,576]{2,1,0:T(8,128)(2,1)}, u32[]{:S(2)}) %copy-start.6) | copy-done | bytes 294936
  2.6 0.7 %collective-permute-start.3 = (bf16[720,128]{1,0:T(8,128)(2,1)S(1)}, bf16[720,128]{1,0:T(8,128)(2,1)S(1)}, u32[]{:S(2)}, u32[]{:S(2)}) collective-permute-start(bf16[720,128]{1,0:T(8,128)(2,1)S(1)} %get-tuple-element.50), channel_id=1, source_target_pairs={{8,16},{12,20},{16,8},{20,12},{0,0},{4,4},{24,24},{28,28},{9,17},{... | collective-permute-start | bytes 552968 | tf_op jit(solution)/shard_map/ppermute | solution.py:629
  3.3 5.3 %collective-permute-start.7 = (bf16[1152,128]{1,0:T(8,128)(2,1)S(1)}, bf16[1152,128]{1,0:T(8,128)(2,1)S(1)}, u32[]{:S(2)}, u32[]{:S(2)}) collective-permute-start(bf16[1152,128]{1,0:T(8,128)(2,1)S(1)} %get-tuple-element.40.pack_ref), channel_id=1, source_target_pairs={{0,8},{4,12},{8,0},{12,4},{16,24},{20,28},{24,16},{28,20},{1,9},{5... | collective-permute-start | bytes 884744 | tf_op jit(solution)/shard_map/ppermute | solution.py:629
  8.7 3.2 %collective-permute-start.5 = (bf16[1152,128]{1,0:T(8,128)(2,1)S(1)}, bf16[1152,128]{1,0:T(8,128)(2,1)S(1)}, u32[]{:S(2)}, u32[]{:S(2)}) collective-permute-start(bf16[1152,128]{1,0:T(8,128)(2,1)S(1)} %get-tuple-element.40.pack_ref), channel_id=1, source_target_pairs={{0,24},{4,28},{24,0},{28,4},{1,25},{5,29},{25,1},{29,5},{2,26},{6,... | collective-permute-start | bytes 884744 | tf_op jit(solution)/shard_map/ppermute | solution.py:629
  12.6 2.8 %collective-permute-start.4 = (bf16[720,128]{1,0:T(8,128)(2,1)S(1)}, bf16[720,128]{1,0:T(8,128)(2,1)S(1)}, u32[]{:S(2)}, u32[]{:S(2)}) collective-permute-start(bf16[720,128]{1,0:T(8,128)(2,1)S(1)} %collective-permute-done.3.refs_0_), channel_id=1, source_target_pairs={{0,16},{4,20},{24,8},{28,12},{8,0},{12,4},{16,24},{20,28},{1,17},{... | collective-permute-start | bytes 552968 | tf_op jit(solution)/shard_map/ppermute | solution.py:629
  15.5 1.2 %load_inputs.1 = (s32[64,128]{1,0:T(8,128)S(1)}, f32[64,32]{1,0:T(8,128)S(1)}, f32[1024,128]{1,0:T(8,128)S(1)}, bf16[16,64,128]{2,1,0:T(8,128)(2,1)S(1)}, bf16[1...) custom-call(s32[64]{0:T(128)S(1)} %copy-done.5, f32[32,64]{1,0:T(8,128)S(1)} %bitcast.7, ...), custom_call_target="tpu_custom_call" | custom-call | flops 1 | bytes 1 | tf_op jit(solution)/shard_map/load_inputs/pallas_call | solution.py:424
  16.7 0.7 %collective-permute-start.2 = (bf16[432,128]{1,0:T(8,128)(2,1)S(1)}, bf16[432,128]{1,0:T(8,128)(2,1)S(1)}, u32[]{:S(2)}, u32[]{:S(2)}) collective-permute-start(bf16[432,128]{1,0:T(8,128)(2,1)S(1)} %collective-permute-done.1.refs_1_), channel_id=1, source_target_pairs={{0,16},{4,20},{24,8},{28,12},{8,0},{12,4},{16,24},{20,28},{1,17},{... | collective-permute-start | bytes 331784 | tf_op jit(solution)/shard_map/ppermute | solution.py:629
  17.5 1.8 %index_logits.1 = (f32[16,2048]{1,0:T(8,128)S(1)}, f32[1024,2048]{1,0:T(8,128)S(1)}, f32[16,128]{1,0:T(8,128)S(1)}) custom-call(s32[64,128]{1,0:T(8,128)S(1)} %get-tuple-element.42.length_ref, bf16[1024,128]{1,0:T(8,128)(2,1)S(1)} %bitcast.6, bf16[2048,128]{1,0:T(8,128)(2,1)S(1)} %get-tuple-element.44.key_ref, f32[1024,128]{1,0:T(8,128)S(1)} %get-tuple-element.45.weight_ref), custom_call_target="tpu_custom_call" | custom-call | flops 1 | bytes 1 | tf_op jit(solution)/shard_map/index_logits/pallas_call | solution.py:381
  19.3 1.8 %mass_own.1.own_ref = f32[8,4096]{1,0:T(8,128)S(1)} custom-call(s32[64,128]{1,0:T(8,128)S(1)} %get-tuple-element.42.length_ref, bf16[1152,128]{1,0:T(8,128)(2,1)S(1)} %get-tuple-element.40.pack_ref, f32[64,32]{1,0:T(8,128)S(1)} %get-tuple-element.48.lse_ref, bf16[576,2048]{1,0:T(8,128)(2,1)S(1)} %get-tuple-element.51.own_key_ref, ...), custom_call_target="tpu_custom_call" | custom-call | flops 1 | bytes 1 | tf_op jit(solution)/shard_map/mass_own/pallas_call | solution.py:313
  21.2 1.8 %mass_near.1.near_ref = f32[8,4096]{1,0:T(8,128)S(1)} custom-call(s32[64,128]{1,0:T(8,128)S(1)} %get-tuple-element.42.length_ref, bf16[1152,128]{1,0:T(8,128)(2,1)S(1)} %collective-permute-done.7.pack_ref, f32[64,32]{1,0:T(8,128)S(1)} %get-tuple-element.48.lse_ref, bf16[576,2048]{1,0:T(8,128)(2,1)S(1)} %get-tuple-element.51.own_key_ref, ...), custom_call_target="tpu_custom_call" | custom-call | flops 1 | bytes 1 | tf_op jit(solution)/shard_map/mass_near/pallas_call | solution.py:313
  23.0 1.1 %collective-permute-done.5.ends_ref = bf16[1152,128]{1,0:T(8,128)(2,1)S(1)} collective-permute-done((bf16[1152,128]{1,0:T(8,128)(2,1)S(1)}, bf16[1152,128]{1,0:T(8,128)(2,1)S(1)}, u32[]{:S(2)}, u32[]{:S(2)}) %collective-permute-start.5) | collective-permute-done | bytes 294944 | tf_op jit(solution)/shard_map/ppermute | solution.py:629
  24.5 1.8 %mass_across.1.across_ref = f32[8,4096]{1,0:T(8,128)S(1)} custom-call(s32[64,128]{1,0:T(8,128)S(1)} %get-tuple-element.42.length_ref, bf16[1152,128]{1,0:T(8,128)(2,1)S(1)} %pick_queries.1.pack_ref, f32[64,32]{1,0:T(8,128)S(1)} %get-tuple-element.48.lse_ref, bf16[576,2048]{1,0:T(8,128)(2,1)S(1)} %get-tuple-element.51.own_key_ref, ...), custom_call_target="tpu_custom_call" | custom-call | flops 1 | bytes 1 | tf_op jit(solution)/shard_map/mass_across/pallas_call | solution.py:313
  26.7 1.3 %mass_far.1.before_ref = f32[8,4096]{1,0:T(8,128)S(1)} custom-call(s32[64,128]{1,0:T(8,128)S(1)} %get-tuple-element.42.length_ref, bf16[720,128]{1,0:T(8,128)(2,1)S(1)} %collective-permute-done.4.pack_ref, f32[64,32]{1,0:T(8,128)S(1)} %get-tuple-element.48.lse_ref, bf16[576,2048]{1,0:T(8,128)(2,1)S(1)} %get-tuple-element.51.own_key_ref, ...), custom_call_target="tpu_custom_call" | custom-call | flops 1 | bytes 1 | tf_op jit(solution)/shard_map/mass_far/pallas_call | solution.py:313
  28.0 0.7 %collective-permute-done.2.pack_ref = bf16[432,128]{1,0:T(8,128)(2,1)S(1)} collective-permute-done((bf16[432,128]{1,0:T(8,128)(2,1)S(1)}, bf16[432,128]{1,0:T(8,128)(2,1)S(1)}, u32[]{:S(2)}, u32[]{:S(2)}) %collective-permute-start.2) | collective-permute-done | bytes 110624 | tf_op jit(solution)/shard_map/ppermute | solution.py:629
  28.7 1.1 %mass_and_share.1 = (f32[8,4096]{1,0:T(8,128)S(1)}, bf16[8,4096]{1,0:T(8,128)(2,1)S(1)}, bf16[8,4096]{1,0:T(8,128)(2,1)S(1)}, bf16[8,4096]{1,0:T(8,128)(2,1)S(1)}) custom-call(s32[64,128]{1,0:T(8,128)S(1)} %get-tuple-element.42.length_ref, bf16[432,128]{1,0:T(8,128)(2,1)S(1)} %collective-permute-done.2.pack_ref, f32[64,32]{1,0:T(8,128)S(1)} %get-tuple-element.48.lse_ref, ...), custom_call_target="tpu_custom_call" | custom-call | flops 1 | bytes 1 | tf_op jit(solution)/shard_map/mass_and_share/pallas_call | solution.py:344
  29.8 2.5 %collective-permute-start.10 = (bf16[8,4096]{1,0:T(8,128)(2,1)S(1)}, bf16[8,4096]{1,0:T(8,128)(2,1)S(1)}, u32[]{:S(2)}, u32[]{:S(2)}) collective-permute-start(bf16[8,4096]{1,0:T(8,128)(2,1)S(1)} %get-tuple-element.60), channel_id=1, source_target_pairs={{0,3},{1,2},{2,1},{3,0},{4,7},{5,6},{6,5},{7,4},{8,11},{9,10},{10,... | collective-permute-start | bytes 196616 | tf_op jit(solution)/shard_map/ppermute | solution.py:635
  33.4 1.7 %collective-permute-done.10.refs_2_ = bf16[8,4096]{1,0:T(8,128)(2,1)S(1)} collective-permute-done((bf16[8,4096]{1,0:T(8,128)(2,1)S(1)}, bf16[8,4096]{1,0:T(8,128)(2,1)S(1)}, u32[]{:S(2)}, u32[]{:S(2)}) %collective-permute-start.10) | collective-permute-done | bytes 65568 | tf_op jit(solution)/shard_map/ppermute | solution.py:635
  35.1 1.5 %collective-permute-done.8.refs_0_ = bf16[8,4096]{1,0:T(8,128)(2,1)S(1)} collective-permute-done((bf16[8,4096]{1,0:T(8,128)(2,1)S(1)}, bf16[8,4096]{1,0:T(8,128)(2,1)S(1)}, u32[]{:S(2)}, u32[]{:S(2)}) %collective-permute-start.8) | collective-permute-done | bytes 65568 | tf_op jit(solution)/shard_map/ppermute | solution.py:635
  37.3 1.5 %collective-permute-start.11 = (f32[16,128]{1,0:T(8,128)S(1)}, f32[16,128]{1,0:T(8,128)S(1)}, u32[]{:S(2)}, u32[]{:S(2)}) collective-permute-start(f32[16,128]{1,0:T(8,128)S(1)} %get-tuple-element.61.refs_0_), channel_id=1, source_target_pairs={{0,24},{4,28},{8,16},{12,20},{16,8},{20,12},{24,0},{28,4},{1,25},{... | collective-permute-start | bytes 24584 | tf_op jit(solution)/shard_map/ppermute | solution.py:632
  38.8 1.7 %collective-permute-start.12 = (f32[16,128]{1,0:T(8,128)S(1)}, f32[16,128]{1,0:T(8,128)S(1)}, u32[]{:S(2)}, u32[]{:S(2)}) collective-permute-start(f32[16,128]{1,0:T(8,128)S(1)} %get-tuple-element.61.refs_0_), channel_id=1, source_target_pairs={{0,16},{4,20},{8,24},{12,28},{16,0},{20,4},{24,8},{28,12},{1,17},{... | collective-permute-start | bytes 24584 | tf_op jit(solution)/shard_map/ppermute | solution.py:632
  40.5 1.2 %collective-permute-start.13 = (f32[16,128]{1,0:T(8,128)S(1)}, f32[16,128]{1,0:T(8,128)S(1)}, u32[]{:S(2)}, u32[]{:S(2)}) collective-permute-start(f32[16,128]{1,0:T(8,128)S(1)} %get-tuple-element.61.refs_0_), channel_id=1, source_target_pairs={{0,8},{4,12},{8,0},{12,4},{16,24},{20,28},{24,16},{28,20},{1,9},{5... | collective-permute-start | bytes 24584 | tf_op jit(solution)/shard_map/ppermute | solution.py:632
  41.7 1.1 %collective-permute-done.11.refs_1_ = f32[16,128]{1,0:T(8,128)S(1)} collective-permute-done((f32[16,128]{1,0:T(8,128)S(1)}, f32[16,128]{1,0:T(8,128)S(1)}, u32[]{:S(2)}, u32[]{:S(2)}) %collective-permute-start.11) | collective-permute-done | bytes 8224 | tf_op jit(solution)/shard_map/ppermute | solution.py:632
  43.3 0.8 %collective-permute-done.13.refs_3_ = f32[16,128]{1,0:T(8,128)S(1)} collective-permute-done((f32[16,128]{1,0:T(8,128)S(1)}, f32[16,128]{1,0:T(8,128)S(1)}, u32[]{:S(2)}, u32[]{:S(2)}) %collective-permute-start.13) | collective-permute-done | bytes 8224 | tf_op jit(solution)/shard_map/ppermute | solution.py:632
  44.3 1.1 %index_back_own.1 = (f32[512,128]{1,0:T(8,128)S(1)}, f32[128,2048]{1,0:T(8,128)S(1)}) custom-call(s32[64,128]{1,0:T(8,128)S(1)} %get-tuple-element.42.length_ref, f32[16,128]{1,0:T(8,128)S(1)} %merge_stats.3.stats_ref, f32[8,2048]{1,0:T(8,128)S(1)} %get-tuple-element.65.mass_ref, f32[16,2048]{1,0:T(8,128)S(1)} %get-tuple-element.52.logits_ref, ...), custom_call_target="tpu_custom_call" | custom-call | flops 1 | bytes 1 | tf_op jit(solution)/shard_map/index_back_own/pallas_call | solution.py:523
  45.5 1.2 %index_back_pair.1 = (f32[512,128]{1,0:T(8,128)S(1)}, bf16[512,128]{1,0:T(8,128)(2,1)S(1)}, bf16[512,128]{1,0:T(8,128)(2,1)S(1)}, bf16[512,128]{1,0:T(8,128)(2,1...) custom-call(s32[64,128]{1,0:T(8,128)S(1)} %get-tuple-element.42.length_ref, ...), custom_call_target="tpu_custom_call" | custom-call | flops 1 | bytes 1 | tf_op jit(solution)/shard_map/index_back_pair/pallas_call | solution.py:567
  47.8 1.5 %collective-permute-start.17 = (bf16[512,128]{1,0:T(8,128)(2,1)S(1)}, bf16[512,128]{1,0:T(8,128)(2,1)S(1)}, u32[]{:S(2)}, u32[]{:S(2)}) collective-permute-start(bf16[512,128]{1,0:T(8,128)(2,1)S(1)} %get-tuple-element.70), channel_id=1, source_target_pairs={{0,2},{1,3},{2,0},{3,1},{4,6},{5,7},{6,4},{7,5},{8,10},{9,11},{10,... | collective-permute-start | bytes 393224 | tf_op jit(solution)/shard_map/ppermute | solution.py:635
  49.3 1.4 %collective-permute-start.18 = (bf16[512,128]{1,0:T(8,128)(2,1)S(1)}, bf16[512,128]{1,0:T(8,128)(2,1)S(1)}, u32[]{:S(2)}, u32[]{:S(2)}) collective-permute-start(bf16[512,128]{1,0:T(8,128)(2,1)S(1)} %get-tuple-element.71), channel_id=1, source_target_pairs={{0,3},{1,2},{2,1},{3,0},{4,7},{5,6},{6,5},{7,4},{8,11},{9,10},{10,... | collective-permute-start | bytes 393224 | tf_op jit(solution)/shard_map/ppermute | solution.py:635
  50.8 2.5 %collective-permute-start.20 = (bf16[128,128]{1,0:T(8,128)(2,1)S(1)}, bf16[128,128]{1,0:T(8,128)(2,1)S(1)}, u32[]{:S(2)}, u32[]{:S(2)}) collective-permute-start(bf16[128,128]{1,0:T(8,128)(2,1)S(1)} %get-tuple-element.75), channel_id=1, source_target_pairs={{0,24},{4,28},{8,16},{12,20},{16,8},{20,12},{24,0},{28,4},{1,25},{... | collective-permute-start | bytes 98312 | tf_op jit(solution)/shard_map/ppermute | solution.py:632
  53.6 1.6 %collective-permute-start.22 = (bf16[128,128]{1,0:T(8,128)(2,1)S(1)}, bf16[128,128]{1,0:T(8,128)(2,1)S(1)}, u32[]{:S(2)}, u32[]{:S(2)}) collective-permute-start(bf16[128,128]{1,0:T(8,128)(2,1)S(1)} %get-tuple-element.77), channel_id=1, source_target_pairs={{0,8},{4,12},{8,0},{12,4},{16,24},{20,28},{24,16},{28,20},{1,9},{5... | collective-permute-start | bytes 98312 | tf_op jit(solution)/shard_map/ppermute | solution.py:632
  55.2 1.3 %collective-permute-done.18.refs_3_ = bf16[512,128]{1,0:T(8,128)(2,1)S(1)} collective-permute-done((bf16[512,128]{1,0:T(8,128)(2,1)S(1)}, bf16[512,128]{1,0:T(8,128)(2,1)S(1)}, u32[]{:S(2)}, u32[]{:S(2)}) %collective-permute-start.18) | collective-permute-done | bytes 131104 | tf_op jit(solution)/shard_map/ppermute | solution.py:635
  56.6 1.6 %collective-permute-done.21.refs_6_ = bf16[128,128]{1,0:T(8,128)(2,1)S(1)} collective-permute-done((bf16[128,128]{1,0:T(8,128)(2,1)S(1)}, bf16[128,128]{1,0:T(8,128)(2,1)S(1)}, u32[]{:S(2)}, u32[]{:S(2)}) %collective-permute-start.21) | collective-permute-done | bytes 32800 | tf_op jit(solution)/shard_map/ppermute | solution.py:632
  58.1 0.8 %last_sums.1 = (f32[16,8,128]{2,1,0:T(8,128)}, f32[512,128]{1,0:T(8,128)}) custom-call(f32[512,128]{1,0:T(8,128)S(1)} %get-tuple-element.68.refs_0_, bf16[512,128]{1,0:T(8,128)(2,1)S(1)} %collective-permute-done.16.refs_1_, bf16[512,128]{1,0:T(8,128)(2,1)S(1)} %collective-permute-done.17.refs_2_, bf16[512,128]{1,0:T(8,128)(2,1)S(1)} %collective-permute-done.18.refs_3_, ...), custom_call_target="tpu_custom_call" | custom-call | flops 1 | bytes 1 | tf_op jit(solution)/shard_map/last_sums/pallas_call | solution.py:605
  (44 shorter events, 5.9 us)
Async XLA Ops:
  0.6 14.8 %copy-start = (bf16[2048,576]{0,1:T(8,128)(2,1)S(1)}, bf16[2048,576]{0,1:T(8,128)(2,1)}, u32[]{:S(2)}) copy-start(bf16[2048,576]{0,1:T(8,128)(2,1)} %param.8) | copy-start | bytes 7077892
  0.6 14.8 %copy-start.1 = (bf16[2048,128]{1,0:T(8,128)(2,1)S(1)}, bf16[2048,128]{1,0:T(8,128)(2,1)}, u32[]{:S(2)}) copy-start(bf16[2048,128]{1,0:T(8,128)(2,1)} %key_hbm.1) | copy-start | bytes 1572868
  0.7 14.8 %copy-start.2 = (bf16[16,64,128]{2,1,0:T(8,128)(2,1)S(1)}, bf16[16,64,128]{2,1,0:T(8,128)(2,1)}, u32[]{:S(2)}) copy-start(bf16[16,64,128]{2,1,0:T(8,128)(2,1)} %query_hbm.1) | copy-start | bytes 786436
  0.7 14.8 %copy-start.3 = (f32[64,32]{0,1:T(8,128)S(1)}, f32[64,32]{0,1:T(8,128)}, u32[]{:S(2)}) copy-start(f32[64,32]{0,1:T(8,128)} %param.9) | copy-start | bytes 24580
  0.7 14.8 %copy-start.4 = (f32[16,64]{1,0:T(8,128)S(1)}, f32[16,64]{1,0:T(8,128)}, u32[]{:S(2)}) copy-start(f32[16,64]{1,0:T(8,128)} %weight_ref.1) | copy-start | bytes 12292
  0.7 14.8 %copy-start.5 = (s32[64]{0:T(128)S(1)}, s32[64]{0:T(128)}, u32[]{:S(2)}) copy-start(s32[64]{0:T(128)} %length_ref.1) | copy-start | bytes 772
  0.7 18.6 %collective-permute-start.6 = (bf16[576,2048]{1,0:T(8,128)(2,1)}, bf16[576,2048]{1,0:T(8,128)(2,1)S(1)}, u32[]{:S(2)}, u32[]{:S(2)}) collective-permute-start(bf16[576,2048]{1,0:T(8,128)(2,1)} %bitcast.4), channel_id=1, source_target_pairs={{0,4},{4,0},{8,12},{12,8},{16,20},{20,16},{24,28},{28,24},{1,5},{5... | collective-permute-start | bytes 7077896 | tf_op jit(solution)/shard_map/ppermute | solution.py:632
  1.2 1.3 %copy-start.6 = (bf16[8,32,576]{2,1,0:T(8,128)(2,1)S(1)}, bf16[8,32,576]{2,1,0:T(8,128)(2,1)}, u32[]{:S(2)}) copy-start(bf16[8,32,576]{2,1,0:T(8,128)(2,1)} %query_ref.1) | copy-start | bytes 884740
  2.6 9.9 %collective-permute-start.3 = (bf16[720,128]{1,0:T(8,128)(2,1)S(1)}, bf16[720,128]{1,0:T(8,128)(2,1)S(1)}, u32[]{:S(2)}, u32[]{:S(2)}) collective-permute-start(bf16[720,128]{1,0:T(8,128)(2,1)S(1)} %get-tuple-element.50), channel_id=1, source_target_pairs={{8,16},{12,20},{16,8},{20,12},{0,0},{4,4},{24,24},{28,28},{9,17},{... | collective-permute-start | bytes 552968 | tf_op jit(solution)/shard_map/ppermute | solution.py:629
  3.3 16.0 %collective-permute-start.7 = (bf16[1152,128]{1,0:T(8,128)(2,1)S(1)}, bf16[1152,128]{1,0:T(8,128)(2,1)S(1)}, u32[]{:S(2)}, u32[]{:S(2)}) collective-permute-start(bf16[1152,128]{1,0:T(8,128)(2,1)S(1)} %get-tuple-element.40.pack_ref), channel_id=1, source_target_pairs={{0,8},{4,12},{8,0},{12,4},{16,24},{20,28},{24,16},{28,20},{1,9},{5... | collective-permute-start | bytes 884744 | tf_op jit(solution)/shard_map/ppermute | solution.py:629
  8.7 15.5 %collective-permute-start.5 = (bf16[1152,128]{1,0:T(8,128)(2,1)S(1)}, bf16[1152,128]{1,0:T(8,128)(2,1)S(1)}, u32[]{:S(2)}, u32[]{:S(2)}) collective-permute-start(bf16[1152,128]{1,0:T(8,128)(2,1)S(1)} %get-tuple-element.40.pack_ref), channel_id=1, source_target_pairs={{0,24},{4,28},{24,0},{28,4},{1,25},{5,29},{25,1},{29,5},{2,26},{6,... | collective-permute-start | bytes 884744 | tf_op jit(solution)/shard_map/ppermute | solution.py:629
  11.9 4.8 %collective-permute-start.1 = (bf16[432,128]{1,0:T(8,128)(2,1)S(1)}, bf16[432,128]{1,0:T(8,128)(2,1)S(1)}, u32[]{:S(2)}, u32[]{:S(2)}) collective-permute-start(bf16[432,128]{1,0:T(8,128)(2,1)S(1)} %get-tuple-element.47), channel_id=1, source_target_pairs={{8,16},{12,20},{16,8},{20,12},{0,0},{4,4},{24,24},{28,28},{9,17},{... | collective-permute-start | bytes 331784 | tf_op jit(solution)/shard_map/ppermute | solution.py:629
  12.6 14.1 %collective-permute-start.4 = (bf16[720,128]{1,0:T(8,128)(2,1)S(1)}, bf16[720,128]{1,0:T(8,128)(2,1)S(1)}, u32[]{:S(2)}, u32[]{:S(2)}) collective-permute-start(bf16[720,128]{1,0:T(8,128)(2,1)S(1)} %collective-permute-done.3.refs_0_), channel_id=1, source_target_pairs={{0,16},{4,20},{24,8},{28,12},{8,0},{12,4},{16,24},{20,28},{1,17},{... | collective-permute-start | bytes 552968 | tf_op jit(solution)/shard_map/ppermute | solution.py:629
  16.7 12.0 %collective-permute-start.2 = (bf16[432,128]{1,0:T(8,128)(2,1)S(1)}, bf16[432,128]{1,0:T(8,128)(2,1)S(1)}, u32[]{:S(2)}, u32[]{:S(2)}) collective-permute-start(bf16[432,128]{1,0:T(8,128)(2,1)S(1)} %collective-permute-done.1.refs_1_), channel_id=1, source_target_pairs={{0,16},{4,20},{24,8},{28,12},{8,0},{12,4},{16,24},{20,28},{1,17},{... | collective-permute-start | bytes 331784 | tf_op jit(solution)/shard_map/ppermute | solution.py:629
  19.3 5.1 %collective-permute-start = (f32[16,128]{1,0:T(8,128)S(1)}, f32[16,128]{1,0:T(8,128)S(1)}, u32[]{:S(2)}, u32[]{:S(2)}) collective-permute-start(f32[16,128]{1,0:T(8,128)S(1)} %get-tuple-element.46.refs_0_), channel_id=1, source_target_pairs={{0,4},{4,0},{8,12},{12,8},{16,20},{20,16},{24,28},{28,24},{1,5},{5... | collective-permute-start | bytes 24584 | tf_op jit(solution)/shard_map/ppermute | solution.py:632
  29.8 5.3 %collective-permute-start.10 = (bf16[8,4096]{1,0:T(8,128)(2,1)S(1)}, bf16[8,4096]{1,0:T(8,128)(2,1)S(1)}, u32[]{:S(2)}, u32[]{:S(2)}) collective-permute-start(bf16[8,4096]{1,0:T(8,128)(2,1)S(1)} %get-tuple-element.60), channel_id=1, source_target_pairs={{0,3},{1,2},{2,1},{3,0},{4,7},{5,6},{6,5},{7,4},{8,11},{9,10},{10,... | collective-permute-start | bytes 196616 | tf_op jit(solution)/shard_map/ppermute | solution.py:635
  32.4 4.3 %collective-permute-start.8 = (bf16[8,4096]{1,0:T(8,128)(2,1)S(1)}, bf16[8,4096]{1,0:T(8,128)(2,1)S(1)}, u32[]{:S(2)}, u32[]{:S(2)}) collective-permute-start(bf16[8,4096]{1,0:T(8,128)(2,1)S(1)} %get-tuple-element.58), channel_id=1, source_target_pairs={{0,2},{1,3},{2,0},{3,1},{4,6},{5,7},{6,4},{7,5},{8,10},{9,11},{10,... | collective-permute-start | bytes 196616 | tf_op jit(solution)/shard_map/ppermute | solution.py:635
  32.9 4.3 %collective-permute-start.9 = (bf16[8,4096]{1,0:T(8,128)(2,1)S(1)}, bf16[8,4096]{1,0:T(8,128)(2,1)S(1)}, u32[]{:S(2)}, u32[]{:S(2)}) collective-permute-start(bf16[8,4096]{1,0:T(8,128)(2,1)S(1)} %get-tuple-element.59), channel_id=1, source_target_pairs={{0,1},{1,0},{2,3},{3,2},{4,5},{5,4},{6,7},{7,6},{8,9},{9,8},{10,11... | collective-permute-start | bytes 196616 | tf_op jit(solution)/shard_map/ppermute | solution.py:635
  37.3 8.2 %collective-permute-start.15 = (f32[8,2048]{1,0:T(8,128)S(1)}, f32[8,2048]{1,0:T(8,128)S(1)}, u32[]{:S(2)}, u32[]{:S(2)}) collective-permute-start(f32[8,2048]{1,0:T(8,128)S(1)} %get-tuple-element.62), channel_id=1, source_target_pairs={{0,4},{4,0},{8,12},{12,8},{16,20},{20,16},{24,28},{28,24},{1,5},{5... | collective-permute-start | bytes 196616 | tf_op jit(solution)/shard_map/ppermute | solution.py:632
  37.3 5.5 %collective-permute-start.11 = (f32[16,128]{1,0:T(8,128)S(1)}, f32[16,128]{1,0:T(8,128)S(1)}, u32[]{:S(2)}, u32[]{:S(2)}) collective-permute-start(f32[16,128]{1,0:T(8,128)S(1)} %get-tuple-element.61.refs_0_), channel_id=1, source_target_pairs={{0,24},{4,28},{8,16},{12,20},{16,8},{20,12},{24,0},{28,4},{1,25},{... | collective-permute-start | bytes 24584 | tf_op jit(solution)/shard_map/ppermute | solution.py:632
  38.8 4.5 %collective-permute-start.12 = (f32[16,128]{1,0:T(8,128)S(1)}, f32[16,128]{1,0:T(8,128)S(1)}, u32[]{:S(2)}, u32[]{:S(2)}) collective-permute-start(f32[16,128]{1,0:T(8,128)S(1)} %get-tuple-element.61.refs_0_), channel_id=1, source_target_pairs={{0,16},{4,20},{8,24},{12,28},{16,0},{20,4},{24,8},{28,12},{1,17},{... | collective-permute-start | bytes 24584 | tf_op jit(solution)/shard_map/ppermute | solution.py:632
  40.5 3.7 %collective-permute-start.13 = (f32[16,128]{1,0:T(8,128)S(1)}, f32[16,128]{1,0:T(8,128)S(1)}, u32[]{:S(2)}, u32[]{:S(2)}) collective-permute-start(f32[16,128]{1,0:T(8,128)S(1)} %get-tuple-element.61.refs_0_), channel_id=1, source_target_pairs={{0,8},{4,12},{8,0},{12,4},{16,24},{20,28},{24,16},{28,20},{1,9},{5... | collective-permute-start | bytes 24584 | tf_op jit(solution)/shard_map/ppermute | solution.py:632
  44.3 1.2 %collective-permute-start.14 = (f32[16,128]{1,0:T(8,128)S(1)}, f32[16,128]{1,0:T(8,128)S(1)}, u32[]{:S(2)}, u32[]{:S(2)}) collective-permute-start(f32[16,128]{1,0:T(8,128)S(1)} %merge_stats.3.stats_ref), channel_id=1, source_target_pairs={{0,4},{4,0},{8,12},{12,8},{16,20},{20,16},{24,28},{28,24},{1,5},{5... | collective-permute-start | bytes 24584 | tf_op jit(solution)/shard_map/ppermute | solution.py:632
  46.7 4.0 %collective-permute-start.19 = (bf16[4,128,128]{2,1,0:T(8,128)(2,1)S(1)}, bf16[4,128,128]{2,1,0:T(8,128)(2,1)S(1)}, u32[]{:S(2)}, u32[]{:S(2)}) collective-permute-start(bf16[4,128,128]{2,1,0:T(8,128)(2,1)S(1)} %get-tuple-element.73), channel_id=1, source_target_pairs={{0,4},{4,0},{8,12},{12,8},{16,20},{20,16},{24,28},{28,24},{1,5},{5... | collective-permute-start | bytes 393224 | tf_op jit(solution)/shard_map/ppermute | solution.py:632
  47.3 6.4 %collective-permute-start.16 = (bf16[512,128]{1,0:T(8,128)(2,1)S(1)}, bf16[512,128]{1,0:T(8,128)(2,1)S(1)}, u32[]{:S(2)}, u32[]{:S(2)}) collective-permute-start(bf16[512,128]{1,0:T(8,128)(2,1)S(1)} %get-tuple-element.69), channel_id=1, source_target_pairs={{0,1},{1,0},{2,3},{3,2},{4,5},{5,4},{6,7},{7,6},{8,9},{9,8},{10,11... | collective-permute-start | bytes 393224 | tf_op jit(solution)/shard_map/ppermute | solution.py:635
  47.8 7.5 %collective-permute-start.17 = (bf16[512,128]{1,0:T(8,128)(2,1)S(1)}, bf16[512,128]{1,0:T(8,128)(2,1)S(1)}, u32[]{:S(2)}, u32[]{:S(2)}) collective-permute-start(bf16[512,128]{1,0:T(8,128)(2,1)S(1)} %get-tuple-element.70), channel_id=1, source_target_pairs={{0,2},{1,3},{2,0},{3,1},{4,6},{5,7},{6,4},{7,5},{8,10},{9,11},{10,... | collective-permute-start | bytes 393224 | tf_op jit(solution)/shard_map/ppermute | solution.py:635
  49.3 7.2 %collective-permute-start.18 = (bf16[512,128]{1,0:T(8,128)(2,1)S(1)}, bf16[512,128]{1,0:T(8,128)(2,1)S(1)}, u32[]{:S(2)}, u32[]{:S(2)}) collective-permute-start(bf16[512,128]{1,0:T(8,128)(2,1)S(1)} %get-tuple-element.71), channel_id=1, source_target_pairs={{0,3},{1,2},{2,1},{3,0},{4,7},{5,6},{6,5},{7,4},{8,11},{9,10},{10,... | collective-permute-start | bytes 393224 | tf_op jit(solution)/shard_map/ppermute | solution.py:635
  50.8 5.8 %collective-permute-start.20 = (bf16[128,128]{1,0:T(8,128)(2,1)S(1)}, bf16[128,128]{1,0:T(8,128)(2,1)S(1)}, u32[]{:S(2)}, u32[]{:S(2)}) collective-permute-start(bf16[128,128]{1,0:T(8,128)(2,1)S(1)} %get-tuple-element.75), channel_id=1, source_target_pairs={{0,24},{4,28},{8,16},{12,20},{16,8},{20,12},{24,0},{28,4},{1,25},{... | collective-permute-start | bytes 98312 | tf_op jit(solution)/shard_map/ppermute | solution.py:632
  53.3 4.8 %collective-permute-start.21 = (bf16[128,128]{1,0:T(8,128)(2,1)S(1)}, bf16[128,128]{1,0:T(8,128)(2,1)S(1)}, u32[]{:S(2)}, u32[]{:S(2)}) collective-permute-start(bf16[128,128]{1,0:T(8,128)(2,1)S(1)} %get-tuple-element.76), channel_id=1, source_target_pairs={{0,16},{4,20},{8,24},{12,28},{16,0},{20,4},{24,8},{28,12},{1,17},{... | collective-permute-start | bytes 98312 | tf_op jit(solution)/shard_map/ppermute | solution.py:632
  53.6 4.5 %collective-permute-start.22 = (bf16[128,128]{1,0:T(8,128)(2,1)S(1)}, bf16[128,128]{1,0:T(8,128)(2,1)S(1)}, u32[]{:S(2)}, u32[]{:S(2)}) collective-permute-start(bf16[128,128]{1,0:T(8,128)(2,1)S(1)} %get-tuple-element.77), channel_id=1, source_target_pairs={{0,8},{4,12},{8,0},{12,4},{16,24},{20,28},{24,16},{28,20},{1,9},{5... | collective-permute-start | bytes 98312 | tf_op jit(solution)/shard_map/ppermute | solution.py:632

commit v8 on v7

--- a/solution.py
+++ b/solution.py
@@ -594,21 +594,13 @@
     )(keep, got)
 
 
-def last_kernel(key_parts, *refs):
-    query_out, key_out = refs[-2:]
-    key_refs, query_refs = refs[:key_parts], refs[key_parts:-2]
-    key_out[...] = sum(ref[...].astype(jnp.float32) for ref in key_refs)
-    query_out[...] = sum(ref[...].astype(jnp.float32) for ref in query_refs).reshape(query_out.shape)
-
-
-def last_sums(key_parts, query_parts, query_shape):
-    return local_call(
-        functools.partial(last_kernel, len(key_parts)),
-        [f32(query_shape), f32(key_parts[0].shape)],
-        "last_sums",
-        in_specs=[whole()] * (len(key_parts) + len(query_parts)),
-        out_specs=[whole()] * 2,
-    )(*key_parts, *query_parts)
+def sum_kernel(*refs):
+    out_ref = refs[-1]
+    out_ref[...] = sum(ref[...].astype(jnp.float32) for ref in refs[:-1]).reshape(out_ref.shape)
+
+
+def summed(parts, shape, name):
+    return local_call(sum_kernel, f32(shape), name, in_specs=[whole()] * len(parts), out_specs=whole())(*parts)
 
 
 def after(array, *others):
@@ -670,11 +662,13 @@
     *key_grads, keep, send = back_pair(
         lengths, context_flip(stats, 1), got_mass, *back, query_grad, key_grad, partners, planes
     )
-    got = context_flip(send, 1)
+    sums = pair_sums(keep, context_flip(send, 1))
+    key_grads[-1] = after(key_grads[-1], sums[0])
     key_parts = [key_grads[0]] + [heads_flip(key_grads[e], e) for e in range(1, partners)]
-    sums = pair_sums(keep, got)
     query_parts = [sums[0]] + [context_flip(sums[e], 2 * e) for e in reversed(range(1, planes))]
-    return last_sums(key_parts, query_parts, (own_rows, index_heads // contexts, width))
+    out_key = summed(key_parts, key_parts[0].shape, "key_sums")
+    query_parts[1] = after(query_parts[1], out_key)
+    return summed(query_parts, (own_rows, index_heads // contexts, width), "query_sums"), out_key
 
 
 def fits(mesh):

time: 59.1 us -> 59 us (level)
  waiting for transfers between devices: 11.4 us -> 10.5 us
  Pallas kernels: 15 us -> 15.6 us
    ppermute x11, waiting for transfers between devices: 4.11 us -> 3.35 us  [context_flip(): return lax.ppermute(array, 'context', [(c, c ^ e) for c in range(contexts)])]
    pallas_call x1 -> x2, Pallas kernels: 0.78 us -> 1.41 us  [summed(): local_call(sum_kernel, f32(shape), name, in_specs=[whole()] * len(parts),...]
  transfers between devices with their start and end apart: 23 -> 23, of which waited for: 14 -> 12; matrix products, arithmetic and copies ran while one was open for 0% -> 0% of each run, Pallas kernels for 20% -> 21%
where the time goes in v8:
time: 59 us; the launch traced here: 58.8 us
  starting transfers between devices  30.5 us (52%)
  Pallas kernels  15.6 us (26%)
  waiting for transfers between devices  10.5 us (18%)
  local copies, waits for them, and re-layouts  1.28 us (2%)
  between operations  0.87 us (1%)
    ppermute x6, starting transfers between devices, planes_move(): lax.ppermute(array, 'context', [(2 * a + k, 2 * b + k) for a, b in pairs...  13.5 us
    ppermute x11, starting transfers between devices, context_flip(): return lax.ppermute(array, 'context', [(c, c ^ e) for c in range(contexts)])  9.9 us
    ppermute x6, starting transfers between devices, heads_flip(): return lax.ppermute(array, 'heads', [(h, h ^ e) for h in range(partners)])  7.11 us
    pallas_call x4, Pallas kernels, chunk_mass(): local_call(functools.partial(mass_kernel, flip, blocks), f32((rows, 2 * k...  6.81 us
    ppermute x6, waiting for transfers between devices, heads_flip(): return lax.ppermute(array, 'heads', [(h, h ^ e) for h in range(partners)])  5 us
    ppermute x11, waiting for transfers between devices, context_flip(): return lax.ppermute(array, 'context', [(c, c ^ e) for c in range(contexts)])  3.35 us
    ppermute x6, waiting for transfers between devices, planes_move(): lax.ppermute(array, 'context', [(2 * a + k, 2 * b + k) for a, b in pairs...  2.2 us
    pallas_call x1, Pallas kernels, index_logits(): local_call(logits_kernel, [f32((rows, key_count)), f32((flat, key_count))...  1.85 us
  transfers between devices with their start and end apart: 23, of which 12 were waited for; matrix products, arithmetic and copies ran while one was open for 0% of the time, Pallas kernels for 21%

profile of v8, /device:TPU:0, one launch (start us, length us, event | category | flops | bytes accessed | tf_op | source)
XLA Modules:
  0.0 58.8 jit_solution(7146037262760274257)
XLA Ops:
  1.2 1.3 %copy-done.6 = bf16[8,32,576]{2,1,0:T(8,128)(2,1)S(1)} copy-done((bf16[8,32,576]{2,1,0:T(8,128)(2,1)S(1)}, bf16[8,32,576]{2,1,0:T(8,128)(2,1)}, u32[]{:S(2)}) %copy-start.6) | copy-done | bytes 294936
  2.6 0.7 %collective-permute-start.3 = (bf16[720,128]{1,0:T(8,128)(2,1)S(1)}, bf16[720,128]{1,0:T(8,128)(2,1)S(1)}, u32[]{:S(2)}, u32[]{:S(2)}) collective-permute-start(bf16[720,128]{1,0:T(8,128)(2,1)S(1)} %get-tuple-element.52), channel_id=1, source_target_pairs={{8,16},{12,20},{16,8},{20,12},{0,0},{4,4},{24,24},{28,28},{9,17},{... | collective-permute-start | bytes 552968 | tf_op jit(solution)/shard_map/ppermute | solution.py:621
  3.3 5.3 %collective-permute-start.7 = (bf16[1152,128]{1,0:T(8,128)(2,1)S(1)}, bf16[1152,128]{1,0:T(8,128)(2,1)S(1)}, u32[]{:S(2)}, u32[]{:S(2)}) collective-permute-start(bf16[1152,128]{1,0:T(8,128)(2,1)S(1)} %get-tuple-element.42.pack_ref), channel_id=1, source_target_pairs={{0,8},{4,12},{8,0},{12,4},{16,24},{20,28},{24,16},{28,20},{1,9},{5... | collective-permute-start | bytes 884744 | tf_op jit(solution)/shard_map/ppermute | solution.py:621
  8.7 3.2 %collective-permute-start.5 = (bf16[1152,128]{1,0:T(8,128)(2,1)S(1)}, bf16[1152,128]{1,0:T(8,128)(2,1)S(1)}, u32[]{:S(2)}, u32[]{:S(2)}) collective-permute-start(bf16[1152,128]{1,0:T(8,128)(2,1)S(1)} %get-tuple-element.42.pack_ref), channel_id=1, source_target_pairs={{0,24},{4,28},{24,0},{28,4},{1,25},{5,29},{25,1},{29,5},{2,26},{6,... | collective-permute-start | bytes 884744 | tf_op jit(solution)/shard_map/ppermute | solution.py:621
  12.6 2.8 %collective-permute-start.4 = (bf16[720,128]{1,0:T(8,128)(2,1)S(1)}, bf16[720,128]{1,0:T(8,128)(2,1)S(1)}, u32[]{:S(2)}, u32[]{:S(2)}) collective-permute-start(bf16[720,128]{1,0:T(8,128)(2,1)S(1)} %collective-permute-done.3.refs_0_), channel_id=1, source_target_pairs={{0,16},{4,20},{24,8},{28,12},{8,0},{12,4},{16,24},{20,28},{1,17},{... | collective-permute-start | bytes 552968 | tf_op jit(solution)/shard_map/ppermute | solution.py:621
  15.5 1.2 %load_inputs.1 = (s32[64,128]{1,0:T(8,128)S(1)}, f32[64,32]{1,0:T(8,128)S(1)}, f32[1024,128]{1,0:T(8,128)S(1)}, bf16[16,64,128]{2,1,0:T(8,128)(2,1)S(1)}, bf16[1...) custom-call(s32[64]{0:T(128)S(1)} %copy-done.5, f32[32,64]{1,0:T(8,128)S(1)} %bitcast.7, ...), custom_call_target="tpu_custom_call" | custom-call | flops 1 | bytes 1 | tf_op jit(solution)/shard_map/load_inputs/pallas_call | solution.py:424
  16.7 0.7 %collective-permute-start.2 = (bf16[432,128]{1,0:T(8,128)(2,1)S(1)}, bf16[432,128]{1,0:T(8,128)(2,1)S(1)}, u32[]{:S(2)}, u32[]{:S(2)}) collective-permute-start(bf16[432,128]{1,0:T(8,128)(2,1)S(1)} %collective-permute-done.1.refs_1_), channel_id=1, source_target_pairs={{0,16},{4,20},{24,8},{28,12},{8,0},{12,4},{16,24},{20,28},{1,17},{... | collective-permute-start | bytes 331784 | tf_op jit(solution)/shard_map/ppermute | solution.py:621
  17.5 1.8 %index_logits.1 = (f32[16,2048]{1,0:T(8,128)S(1)}, f32[1024,2048]{1,0:T(8,128)S(1)}, f32[16,128]{1,0:T(8,128)S(1)}) custom-call(s32[64,128]{1,0:T(8,128)S(1)} %get-tuple-element.44.length_ref, bf16[1024,128]{1,0:T(8,128)(2,1)S(1)} %bitcast.6, bf16[2048,128]{1,0:T(8,128)(2,1)S(1)} %get-tuple-element.46.key_ref, f32[1024,128]{1,0:T(8,128)S(1)} %get-tuple-element.47.weight_ref), custom_call_target="tpu_custom_call" | custom-call | flops 1 | bytes 1 | tf_op jit(solution)/shard_map/index_logits/pallas_call | solution.py:381
  19.3 1.8 %mass_own.1.own_ref = f32[8,4096]{1,0:T(8,128)S(1)} custom-call(s32[64,128]{1,0:T(8,128)S(1)} %get-tuple-element.44.length_ref, bf16[1152,128]{1,0:T(8,128)(2,1)S(1)} %get-tuple-element.42.pack_ref, f32[64,32]{1,0:T(8,128)S(1)} %get-tuple-element.50.lse_ref, bf16[576,2048]{1,0:T(8,128)(2,1)S(1)} %get-tuple-element.53.own_key_ref, ...), custom_call_target="tpu_custom_call" | custom-call | flops 1 | bytes 1 | tf_op jit(solution)/shard_map/mass_own/pallas_call | solution.py:313
  21.2 1.8 %mass_near.1.near_ref = f32[8,4096]{1,0:T(8,128)S(1)} custom-call(s32[64,128]{1,0:T(8,128)S(1)} %get-tuple-element.44.length_ref, bf16[1152,128]{1,0:T(8,128)(2,1)S(1)} %collective-permute-done.7.pack_ref, f32[64,32]{1,0:T(8,128)S(1)} %get-tuple-element.50.lse_ref, bf16[576,2048]{1,0:T(8,128)(2,1)S(1)} %get-tuple-element.53.own_key_ref, ...), custom_call_target="tpu_custom_call" | custom-call | flops 1 | bytes 1 | tf_op jit(solution)/shard_map/mass_near/pallas_call | solution.py:313
  23.0 1.1 %collective-permute-done.5.ends_ref = bf16[1152,128]{1,0:T(8,128)(2,1)S(1)} collective-permute-done((bf16[1152,128]{1,0:T(8,128)(2,1)S(1)}, bf16[1152,128]{1,0:T(8,128)(2,1)S(1)}, u32[]{:S(2)}, u32[]{:S(2)}) %collective-permute-start.5) | collective-permute-done | bytes 294944 | tf_op jit(solution)/shard_map/ppermute | solution.py:621
  24.5 1.8 %mass_across.1.across_ref = f32[8,4096]{1,0:T(8,128)S(1)} custom-call(s32[64,128]{1,0:T(8,128)S(1)} %get-tuple-element.44.length_ref, bf16[1152,128]{1,0:T(8,128)(2,1)S(1)} %pick_queries.1.pack_ref, f32[64,32]{1,0:T(8,128)S(1)} %get-tuple-element.50.lse_ref, bf16[576,2048]{1,0:T(8,128)(2,1)S(1)} %get-tuple-element.53.own_key_ref, ...), custom_call_target="tpu_custom_call" | custom-call | flops 1 | bytes 1 | tf_op jit(solution)/shard_map/mass_across/pallas_call | solution.py:313
  26.7 1.3 %mass_far.1.before_ref = f32[8,4096]{1,0:T(8,128)S(1)} custom-call(s32[64,128]{1,0:T(8,128)S(1)} %get-tuple-element.44.length_ref, bf16[720,128]{1,0:T(8,128)(2,1)S(1)} %collective-permute-done.4.pack_ref, f32[64,32]{1,0:T(8,128)S(1)} %get-tuple-element.50.lse_ref, bf16[576,2048]{1,0:T(8,128)(2,1)S(1)} %get-tuple-element.53.own_key_ref, ...), custom_call_target="tpu_custom_call" | custom-call | flops 1 | bytes 1 | tf_op jit(solution)/shard_map/mass_far/pallas_call | solution.py:313
  28.0 0.7 %collective-permute-done.2.pack_ref = bf16[432,128]{1,0:T(8,128)(2,1)S(1)} collective-permute-done((bf16[432,128]{1,0:T(8,128)(2,1)S(1)}, bf16[432,128]{1,0:T(8,128)(2,1)S(1)}, u32[]{:S(2)}, u32[]{:S(2)}) %collective-permute-start.2) | collective-permute-done | bytes 110624 | tf_op jit(solution)/shard_map/ppermute | solution.py:621
  28.7 1.1 %mass_and_share.1 = (f32[8,4096]{1,0:T(8,128)S(1)}, bf16[8,4096]{1,0:T(8,128)(2,1)S(1)}, bf16[8,4096]{1,0:T(8,128)(2,1)S(1)}, bf16[8,4096]{1,0:T(8,128)(2,1)S(1)}) custom-call(s32[64,128]{1,0:T(8,128)S(1)} %get-tuple-element.44.length_ref, bf16[432,128]{1,0:T(8,128)(2,1)S(1)} %collective-permute-done.2.pack_ref, f32[64,32]{1,0:T(8,128)S(1)} %get-tuple-element.50.lse_ref, ...), custom_call_target="tpu_custom_call" | custom-call | flops 1 | bytes 1 | tf_op jit(solution)/shard_map/mass_and_share/pallas_call | solution.py:344
  29.8 2.5 %collective-permute-start.10 = (bf16[8,4096]{1,0:T(8,128)(2,1)S(1)}, bf16[8,4096]{1,0:T(8,128)(2,1)S(1)}, u32[]{:S(2)}, u32[]{:S(2)}) collective-permute-start(bf16[8,4096]{1,0:T(8,128)(2,1)S(1)} %get-tuple-element.62), channel_id=1, source_target_pairs={{0,3},{1,2},{2,1},{3,0},{4,7},{5,6},{6,5},{7,4},{8,11},{9,10},{10,... | collective-permute-start | bytes 196616 | tf_op jit(solution)/shard_map/ppermute | solution.py:627
  33.4 1.7 %collective-permute-done.10.refs_2_ = bf16[8,4096]{1,0:T(8,128)(2,1)S(1)} collective-permute-done((bf16[8,4096]{1,0:T(8,128)(2,1)S(1)}, bf16[8,4096]{1,0:T(8,128)(2,1)S(1)}, u32[]{:S(2)}, u32[]{:S(2)}) %collective-permute-start.10) | collective-permute-done | bytes 65568 | tf_op jit(solution)/shard_map/ppermute | solution.py:627
  35.1 1.5 %collective-permute-done.8.refs_0_ = bf16[8,4096]{1,0:T(8,128)(2,1)S(1)} collective-permute-done((bf16[8,4096]{1,0:T(8,128)(2,1)S(1)}, bf16[8,4096]{1,0:T(8,128)(2,1)S(1)}, u32[]{:S(2)}, u32[]{:S(2)}) %collective-permute-start.8) | collective-permute-done | bytes 65568 | tf_op jit(solution)/shard_map/ppermute | solution.py:627
  37.3 1.5 %collective-permute-start.11 = (f32[16,128]{1,0:T(8,128)S(1)}, f32[16,128]{1,0:T(8,128)S(1)}, u32[]{:S(2)}, u32[]{:S(2)}) collective-permute-start(f32[16,128]{1,0:T(8,128)S(1)} %get-tuple-element.63.refs_0_), channel_id=1, source_target_pairs={{0,24},{4,28},{8,16},{12,20},{16,8},{20,12},{24,0},{28,4},{1,25},{... | collective-permute-start | bytes 24584 | tf_op jit(solution)/shard_map/ppermute | solution.py:624
  38.8 1.7 %collective-permute-start.12 = (f32[16,128]{1,0:T(8,128)S(1)}, f32[16,128]{1,0:T(8,128)S(1)}, u32[]{:S(2)}, u32[]{:S(2)}) collective-permute-start(f32[16,128]{1,0:T(8,128)S(1)} %get-tuple-element.63.refs_0_), channel_id=1, source_target_pairs={{0,16},{4,20},{8,24},{12,28},{16,0},{20,4},{24,8},{28,12},{1,17},{... | collective-permute-start | bytes 24584 | tf_op jit(solution)/shard_map/ppermute | solution.py:624
  40.5 1.2 %collective-permute-start.13 = (f32[16,128]{1,0:T(8,128)S(1)}, f32[16,128]{1,0:T(8,128)S(1)}, u32[]{:S(2)}, u32[]{:S(2)}) collective-permute-start(f32[16,128]{1,0:T(8,128)S(1)} %get-tuple-element.63.refs_0_), channel_id=1, source_target_pairs={{0,8},{4,12},{8,0},{12,4},{16,24},{20,28},{24,16},{28,20},{1,9},{5... | collective-permute-start | bytes 24584 | tf_op jit(solution)/shard_map/ppermute | solution.py:624
  41.7 1.1 %collective-permute-done.11.refs_1_ = f32[16,128]{1,0:T(8,128)S(1)} collective-permute-done((f32[16,128]{1,0:T(8,128)S(1)}, f32[16,128]{1,0:T(8,128)S(1)}, u32[]{:S(2)}, u32[]{:S(2)}) %collective-permute-start.11) | collective-permute-done | bytes 8224 | tf_op jit(solution)/shard_map/ppermute | solution.py:624
  43.3 0.8 %collective-permute-done.13.refs_3_ = f32[16,128]{1,0:T(8,128)S(1)} collective-permute-done((f32[16,128]{1,0:T(8,128)S(1)}, f32[16,128]{1,0:T(8,128)S(1)}, u32[]{:S(2)}, u32[]{:S(2)}) %collective-permute-start.13) | collective-permute-done | bytes 8224 | tf_op jit(solution)/shard_map/ppermute | solution.py:624
  44.3 1.1 %index_back_own.1 = (f32[512,128]{1,0:T(8,128)S(1)}, f32[128,2048]{1,0:T(8,128)S(1)}) custom-call(s32[64,128]{1,0:T(8,128)S(1)} %get-tuple-element.44.length_ref, f32[16,128]{1,0:T(8,128)S(1)} %merge_stats.3.stats_ref, f32[8,2048]{1,0:T(8,128)S(1)} %get-tuple-element.67.mass_ref, f32[16,2048]{1,0:T(8,128)S(1)} %get-tuple-element.54.logits_ref, ...), custom_call_target="tpu_custom_call" | custom-call | flops 1 | bytes 1 | tf_op jit(solution)/shard_map/index_back_own/pallas_call | solution.py:523
  45.5 1.2 %index_back_pair.1 = (f32[512,128]{1,0:T(8,128)S(1)}, bf16[512,128]{1,0:T(8,128)(2,1)S(1)}, bf16[512,128]{1,0:T(8,128)(2,1)S(1)}, bf16[512,128]{1,0:T(8,128)(2,1...) custom-call(s32[64,128]{1,0:T(8,128)S(1)} %get-tuple-element.44.length_ref, ...), custom_call_target="tpu_custom_call" | custom-call | flops 1 | bytes 1 | tf_op jit(solution)/shard_map/index_back_pair/pallas_call | solution.py:567
  47.8 1.5 %collective-permute-start.19 = (bf16[512,128]{1,0:T(8,128)(2,1)S(1)}, bf16[512,128]{1,0:T(8,128)(2,1)S(1)}, u32[]{:S(2)}, u32[]{:S(2)}) collective-permute-start(bf16[512,128]{1,0:T(8,128)(2,1)S(1)} %get-tuple-element.76), channel_id=1, source_target_pairs={{0,2},{1,3},{2,0},{3,1},{4,6},{5,7},{6,4},{7,5},{8,10},{9,11},{10,... | collective-permute-start | bytes 393224 | tf_op jit(solution)/shard_map/ppermute | solution.py:627
  49.4 1.5 %collective-permute-start.20 = (bf16[512,128]{1,0:T(8,128)(2,1)S(1)}, bf16[512,128]{1,0:T(8,128)(2,1)S(1)}, u32[]{:S(2)}, u32[]{:S(2)}) collective-permute-start(bf16[512,128]{1,0:T(8,128)(2,1)S(1)} %get-tuple-element.78), channel_id=1, source_target_pairs={{0,3},{1,2},{2,1},{3,0},{4,7},{5,6},{6,5},{7,4},{8,11},{9,10},{10,... | collective-permute-start | bytes 393224 | tf_op jit(solution)/shard_map/ppermute | solution.py:627
  50.8 2.5 %collective-permute-start.17 = (bf16[128,128]{1,0:T(8,128)(2,1)S(1)}, bf16[128,128]{1,0:T(8,128)(2,1)S(1)}, u32[]{:S(2)}, u32[]{:S(2)}) collective-permute-start(bf16[128,128]{1,0:T(8,128)(2,1)S(1)} %get-tuple-element.73), channel_id=1, source_target_pairs={{0,24},{4,28},{8,16},{12,20},{16,8},{20,12},{24,0},{28,4},{1,25},{... | collective-permute-start | bytes 98312 | tf_op jit(solution)/shard_map/ppermute | solution.py:624
  53.6 1.7 %collective-permute-start.22 = (bf16[128,128]{1,0:T(8,128)(2,1)S(1)}, bf16[128,128]{1,0:T(8,128)(2,1)S(1)}, u32[]{:S(2)}, u32[]{:S(2)}) collective-permute-start(bf16[128,128]{1,0:T(8,128)(2,1)S(1)} %get-tuple-element.81), channel_id=1, source_target_pairs={{0,8},{4,12},{8,0},{12,4},{16,24},{20,28},{24,16},{28,20},{1,9},{5... | collective-permute-start | bytes 98312 | tf_op jit(solution)/shard_map/ppermute | solution.py:624
  55.2 1.3 %collective-permute-done.20.refs_3_ = bf16[512,128]{1,0:T(8,128)(2,1)S(1)} collective-permute-done((bf16[512,128]{1,0:T(8,128)(2,1)S(1)}, bf16[512,128]{1,0:T(8,128)(2,1)S(1)}, u32[]{:S(2)}, u32[]{:S(2)}) %collective-permute-start.20) | collective-permute-done | bytes 131104 | tf_op jit(solution)/shard_map/ppermute | solution.py:627
  56.5 0.8 %key_sums.1 = f32[512,128]{1,0:T(8,128)} custom-call(f32[512,128]{1,0:T(8,128)S(1)} %get-tuple-element.74.refs_0_, bf16[512,128]{1,0:T(8,128)(2,1)S(1)} %collective-permute-done.18.refs_1_, bf16[512,128]{1,0:T(8,128)(2,1)S(1)} %collective-permute-done.19.refs_2_, bf16[512,128]{1,0:T(8,128)(2,1)S(1)} %collective-permute-done.20.refs_3_), custom_call_target="tpu_custom_call" | custom-call | flops 1 | bytes 1 | tf_op jit(solution)/shard_map/key_sums/pallas_call | solution.py:603
  57.3 0.9 %collective-permute-done.21.refs_2_ = bf16[128,128]{1,0:T(8,128)(2,1)S(1)} collective-permute-done((bf16[128,128]{1,0:T(8,128)(2,1)S(1)}, bf16[128,128]{1,0:T(8,128)(2,1)S(1)}, u32[]{:S(2)}, u32[]{:S(2)}) %collective-permute-start.21) | collective-permute-done | bytes 32800 | tf_op jit(solution)/shard_map/ppermute | solution.py:624
  (45 shorter events, 6.5 us)
Async XLA Ops:
  0.6 14.8 %copy-start = (bf16[2048,576]{0,1:T(8,128)(2,1)S(1)}, bf16[2048,576]{0,1:T(8,128)(2,1)}, u32[]{:S(2)}) copy-start(bf16[2048,576]{0,1:T(8,128)(2,1)} %param.8) | copy-start | bytes 7077892
  0.6 14.8 %copy-start.1 = (bf16[2048,128]{1,0:T(8,128)(2,1)S(1)}, bf16[2048,128]{1,0:T(8,128)(2,1)}, u32[]{:S(2)}) copy-start(bf16[2048,128]{1,0:T(8,128)(2,1)} %key_hbm.1) | copy-start | bytes 1572868
  0.7 14.8 %copy-start.2 = (bf16[16,64,128]{2,1,0:T(8,128)(2,1)S(1)}, bf16[16,64,128]{2,1,0:T(8,128)(2,1)}, u32[]{:S(2)}) copy-start(bf16[16,64,128]{2,1,0:T(8,128)(2,1)} %query_hbm.1) | copy-start | bytes 786436
  0.7 14.8 %copy-start.3 = (f32[64,32]{0,1:T(8,128)S(1)}, f32[64,32]{0,1:T(8,128)}, u32[]{:S(2)}) copy-start(f32[64,32]{0,1:T(8,128)} %param.9) | copy-start | bytes 24580
  0.7 14.8 %copy-start.4 = (f32[16,64]{1,0:T(8,128)S(1)}, f32[16,64]{1,0:T(8,128)}, u32[]{:S(2)}) copy-start(f32[16,64]{1,0:T(8,128)} %weight_ref.1) | copy-start | bytes 12292
  0.7 14.8 %copy-start.5 = (s32[64]{0:T(128)S(1)}, s32[64]{0:T(128)}, u32[]{:S(2)}) copy-start(s32[64]{0:T(128)} %length_ref.1) | copy-start | bytes 772
  0.7 18.6 %collective-permute-start.6 = (bf16[576,2048]{1,0:T(8,128)(2,1)}, bf16[576,2048]{1,0:T(8,128)(2,1)S(1)}, u32[]{:S(2)}, u32[]{:S(2)}) collective-permute-start(bf16[576,2048]{1,0:T(8,128)(2,1)} %bitcast.4), channel_id=1, source_target_pairs={{0,4},{4,0},{8,12},{12,8},{16,20},{20,16},{24,28},{28,24},{1,5},{5... | collective-permute-start | bytes 7077896 | tf_op jit(solution)/shard_map/ppermute | solution.py:624
  1.2 1.3 %copy-start.6 = (bf16[8,32,576]{2,1,0:T(8,128)(2,1)S(1)}, bf16[8,32,576]{2,1,0:T(8,128)(2,1)}, u32[]{:S(2)}) copy-start(bf16[8,32,576]{2,1,0:T(8,128)(2,1)} %query_ref.1) | copy-start | bytes 884740
  2.6 9.9 %collective-permute-start.3 = (bf16[720,128]{1,0:T(8,128)(2,1)S(1)}, bf16[720,128]{1,0:T(8,128)(2,1)S(1)}, u32[]{:S(2)}, u32[]{:S(2)}) collective-permute-start(bf16[720,128]{1,0:T(8,128)(2,1)S(1)} %get-tuple-element.52), channel_id=1, source_target_pairs={{8,16},{12,20},{16,8},{20,12},{0,0},{4,4},{24,24},{28,28},{9,17},{... | collective-permute-start | bytes 552968 | tf_op jit(solution)/shard_map/ppermute | solution.py:621
  3.3 16.0 %collective-permute-start.7 = (bf16[1152,128]{1,0:T(8,128)(2,1)S(1)}, bf16[1152,128]{1,0:T(8,128)(2,1)S(1)}, u32[]{:S(2)}, u32[]{:S(2)}) collective-permute-start(bf16[1152,128]{1,0:T(8,128)(2,1)S(1)} %get-tuple-element.42.pack_ref), channel_id=1, source_target_pairs={{0,8},{4,12},{8,0},{12,4},{16,24},{20,28},{24,16},{28,20},{1,9},{5... | collective-permute-start | bytes 884744 | tf_op jit(solution)/shard_map/ppermute | solution.py:621
  8.7 15.5 %collective-permute-start.5 = (bf16[1152,128]{1,0:T(8,128)(2,1)S(1)}, bf16[1152,128]{1,0:T(8,128)(2,1)S(1)}, u32[]{:S(2)}, u32[]{:S(2)}) collective-permute-start(bf16[1152,128]{1,0:T(8,128)(2,1)S(1)} %get-tuple-element.42.pack_ref), channel_id=1, source_target_pairs={{0,24},{4,28},{24,0},{28,4},{1,25},{5,29},{25,1},{29,5},{2,26},{6,... | collective-permute-start | bytes 884744 | tf_op jit(solution)/shard_map/ppermute | solution.py:621
  11.9 4.8 %collective-permute-start.1 = (bf16[432,128]{1,0:T(8,128)(2,1)S(1)}, bf16[432,128]{1,0:T(8,128)(2,1)S(1)}, u32[]{:S(2)}, u32[]{:S(2)}) collective-permute-start(bf16[432,128]{1,0:T(8,128)(2,1)S(1)} %get-tuple-element.49), channel_id=1, source_target_pairs={{8,16},{12,20},{16,8},{20,12},{0,0},{4,4},{24,24},{28,28},{9,17},{... | collective-permute-start | bytes 331784 | tf_op jit(solution)/shard_map/ppermute | solution.py:621
  12.6 14.1 %collective-permute-start.4 = (bf16[720,128]{1,0:T(8,128)(2,1)S(1)}, bf16[720,128]{1,0:T(8,128)(2,1)S(1)}, u32[]{:S(2)}, u32[]{:S(2)}) collective-permute-start(bf16[720,128]{1,0:T(8,128)(2,1)S(1)} %collective-permute-done.3.refs_0_), channel_id=1, source_target_pairs={{0,16},{4,20},{24,8},{28,12},{8,0},{12,4},{16,24},{20,28},{1,17},{... | collective-permute-start | bytes 552968 | tf_op jit(solution)/shard_map/ppermute | solution.py:621
  16.7 12.0 %collective-permute-start.2 = (bf16[432,128]{1,0:T(8,128)(2,1)S(1)}, bf16[432,128]{1,0:T(8,128)(2,1)S(1)}, u32[]{:S(2)}, u32[]{:S(2)}) collective-permute-start(bf16[432,128]{1,0:T(8,128)(2,1)S(1)} %collective-permute-done.1.refs_1_), channel_id=1, source_target_pairs={{0,16},{4,20},{24,8},{28,12},{8,0},{12,4},{16,24},{20,28},{1,17},{... | collective-permute-start | bytes 331784 | tf_op jit(solution)/shard_map/ppermute | solution.py:621
  19.3 5.1 %collective-permute-start = (f32[16,128]{1,0:T(8,128)S(1)}, f32[16,128]{1,0:T(8,128)S(1)}, u32[]{:S(2)}, u32[]{:S(2)}) collective-permute-start(f32[16,128]{1,0:T(8,128)S(1)} %get-tuple-element.48.refs_0_), channel_id=1, source_target_pairs={{0,4},{4,0},{8,12},{12,8},{16,20},{20,16},{24,28},{28,24},{1,5},{5... | collective-permute-start | bytes 24584 | tf_op jit(solution)/shard_map/ppermute | solution.py:624
  29.8 5.3 %collective-permute-start.10 = (bf16[8,4096]{1,0:T(8,128)(2,1)S(1)}, bf16[8,4096]{1,0:T(8,128)(2,1)S(1)}, u32[]{:S(2)}, u32[]{:S(2)}) collective-permute-start(bf16[8,4096]{1,0:T(8,128)(2,1)S(1)} %get-tuple-element.62), channel_id=1, source_target_pairs={{0,3},{1,2},{2,1},{3,0},{4,7},{5,6},{6,5},{7,4},{8,11},{9,10},{10,... | collective-permute-start | bytes 196616 | tf_op jit(solution)/shard_map/ppermute | solution.py:627
  32.4 4.3 %collective-permute-start.8 = (bf16[8,4096]{1,0:T(8,128)(2,1)S(1)}, bf16[8,4096]{1,0:T(8,128)(2,1)S(1)}, u32[]{:S(2)}, u32[]{:S(2)}) collective-permute-start(bf16[8,4096]{1,0:T(8,128)(2,1)S(1)} %get-tuple-element.60), channel_id=1, source_target_pairs={{0,2},{1,3},{2,0},{3,1},{4,6},{5,7},{6,4},{7,5},{8,10},{9,11},{10,... | collective-permute-start | bytes 196616 | tf_op jit(solution)/shard_map/ppermute | solution.py:627
  32.9 4.3 %collective-permute-start.9 = (bf16[8,4096]{1,0:T(8,128)(2,1)S(1)}, bf16[8,4096]{1,0:T(8,128)(2,1)S(1)}, u32[]{:S(2)}, u32[]{:S(2)}) collective-permute-start(bf16[8,4096]{1,0:T(8,128)(2,1)S(1)} %get-tuple-element.61), channel_id=1, source_target_pairs={{0,1},{1,0},{2,3},{3,2},{4,5},{5,4},{6,7},{7,6},{8,9},{9,8},{10,11... | collective-permute-start | bytes 196616 | tf_op jit(solution)/shard_map/ppermute | solution.py:627
  37.3 8.2 %collective-permute-start.15 = (f32[8,2048]{1,0:T(8,128)S(1)}, f32[8,2048]{1,0:T(8,128)S(1)}, u32[]{:S(2)}, u32[]{:S(2)}) collective-permute-start(f32[8,2048]{1,0:T(8,128)S(1)} %get-tuple-element.64), channel_id=1, source_target_pairs={{0,4},{4,0},{8,12},{12,8},{16,20},{20,16},{24,28},{28,24},{1,5},{5... | collective-permute-start | bytes 196616 | tf_op jit(solution)/shard_map/ppermute | solution.py:624
  37.3 5.5 %collective-permute-start.11 = (f32[16,128]{1,0:T(8,128)S(1)}, f32[16,128]{1,0:T(8,128)S(1)}, u32[]{:S(2)}, u32[]{:S(2)}) collective-permute-start(f32[16,128]{1,0:T(8,128)S(1)} %get-tuple-element.63.refs_0_), channel_id=1, source_target_pairs={{0,24},{4,28},{8,16},{12,20},{16,8},{20,12},{24,0},{28,4},{1,25},{... | collective-permute-start | bytes 24584 | tf_op jit(solution)/shard_map/ppermute | solution.py:624
  38.8 4.5 %collective-permute-start.12 = (f32[16,128]{1,0:T(8,128)S(1)}, f32[16,128]{1,0:T(8,128)S(1)}, u32[]{:S(2)}, u32[]{:S(2)}) collective-permute-start(f32[16,128]{1,0:T(8,128)S(1)} %get-tuple-element.63.refs_0_), channel_id=1, source_target_pairs={{0,16},{4,20},{8,24},{12,28},{16,0},{20,4},{24,8},{28,12},{1,17},{... | collective-permute-start | bytes 24584 | tf_op jit(solution)/shard_map/ppermute | solution.py:624
  40.5 3.7 %collective-permute-start.13 = (f32[16,128]{1,0:T(8,128)S(1)}, f32[16,128]{1,0:T(8,128)S(1)}, u32[]{:S(2)}, u32[]{:S(2)}) collective-permute-start(f32[16,128]{1,0:T(8,128)S(1)} %get-tuple-element.63.refs_0_), channel_id=1, source_target_pairs={{0,8},{4,12},{8,0},{12,4},{16,24},{20,28},{24,16},{28,20},{1,9},{5... | collective-permute-start | bytes 24584 | tf_op jit(solution)/shard_map/ppermute | solution.py:624
  44.3 1.2 %collective-permute-start.14 = (f32[16,128]{1,0:T(8,128)S(1)}, f32[16,128]{1,0:T(8,128)S(1)}, u32[]{:S(2)}, u32[]{:S(2)}) collective-permute-start(f32[16,128]{1,0:T(8,128)S(1)} %merge_stats.3.stats_ref), channel_id=1, source_target_pairs={{0,4},{4,0},{8,12},{12,8},{16,20},{20,16},{24,28},{28,24},{1,5},{5... | collective-permute-start | bytes 24584 | tf_op jit(solution)/shard_map/ppermute | solution.py:624
  46.7 2.6 %collective-permute-start.16 = (bf16[4,128,128]{2,1,0:T(8,128)(2,1)S(1)}, bf16[4,128,128]{2,1,0:T(8,128)(2,1)S(1)}, u32[]{:S(2)}, u32[]{:S(2)}) collective-permute-start(bf16[4,128,128]{2,1,0:T(8,128)(2,1)S(1)} %get-tuple-element.71), channel_id=1, source_target_pairs={{0,4},{4,0},{8,12},{12,8},{16,20},{20,16},{24,28},{28,24},{1,5},{5... | collective-permute-start | bytes 393224 | tf_op jit(solution)/shard_map/ppermute | solution.py:624
  47.3 6.3 %collective-permute-start.18 = (bf16[512,128]{1,0:T(8,128)(2,1)S(1)}, bf16[512,128]{1,0:T(8,128)(2,1)S(1)}, u32[]{:S(2)}, u32[]{:S(2)}) collective-permute-start(bf16[512,128]{1,0:T(8,128)(2,1)S(1)} %get-tuple-element.75), channel_id=1, source_target_pairs={{0,1},{1,0},{2,3},{3,2},{4,5},{5,4},{6,7},{7,6},{8,9},{9,8},{10,11... | collective-permute-start | bytes 393224 | tf_op jit(solution)/shard_map/ppermute | solution.py:627
  47.8 7.5 %collective-permute-start.19 = (bf16[512,128]{1,0:T(8,128)(2,1)S(1)}, bf16[512,128]{1,0:T(8,128)(2,1)S(1)}, u32[]{:S(2)}, u32[]{:S(2)}) collective-permute-start(bf16[512,128]{1,0:T(8,128)(2,1)S(1)} %get-tuple-element.76), channel_id=1, source_target_pairs={{0,2},{1,3},{2,0},{3,1},{4,6},{5,7},{6,4},{7,5},{8,10},{9,11},{10,... | collective-permute-start | bytes 393224 | tf_op jit(solution)/shard_map/ppermute | solution.py:627
  49.4 7.2 %collective-permute-start.20 = (bf16[512,128]{1,0:T(8,128)(2,1)S(1)}, bf16[512,128]{1,0:T(8,128)(2,1)S(1)}, u32[]{:S(2)}, u32[]{:S(2)}) collective-permute-start(bf16[512,128]{1,0:T(8,128)(2,1)S(1)} %get-tuple-element.78), channel_id=1, source_target_pairs={{0,3},{1,2},{2,1},{3,0},{4,7},{5,6},{6,5},{7,4},{8,11},{9,10},{10,... | collective-permute-start | bytes 393224 | tf_op jit(solution)/shard_map/ppermute | solution.py:627
  50.8 6.4 %collective-permute-start.17 = (bf16[128,128]{1,0:T(8,128)(2,1)S(1)}, bf16[128,128]{1,0:T(8,128)(2,1)S(1)}, u32[]{:S(2)}, u32[]{:S(2)}) collective-permute-start(bf16[128,128]{1,0:T(8,128)(2,1)S(1)} %get-tuple-element.73), channel_id=1, source_target_pairs={{0,24},{4,28},{8,16},{12,20},{16,8},{20,12},{24,0},{28,4},{1,25},{... | collective-permute-start | bytes 98312 | tf_op jit(solution)/shard_map/ppermute | solution.py:624
  53.3 4.8 %collective-permute-start.21 = (bf16[128,128]{1,0:T(8,128)(2,1)S(1)}, bf16[128,128]{1,0:T(8,128)(2,1)S(1)}, u32[]{:S(2)}, u32[]{:S(2)}) collective-permute-start(bf16[128,128]{1,0:T(8,128)(2,1)S(1)} %get-tuple-element.80), channel_id=1, source_target_pairs={{0,16},{4,20},{8,24},{12,28},{16,0},{20,4},{24,8},{28,12},{1,17},{... | collective-permute-start | bytes 98312 | tf_op jit(solution)/shard_map/ppermute | solution.py:624
  53.6 4.6 %collective-permute-start.22 = (bf16[128,128]{1,0:T(8,128)(2,1)S(1)}, bf16[128,128]{1,0:T(8,128)(2,1)S(1)}, u32[]{:S(2)}, u32[]{:S(2)}) collective-permute-start(bf16[128,128]{1,0:T(8,128)(2,1)S(1)} %get-tuple-element.81), channel_id=1, source_target_pairs={{0,8},{4,12},{8,0},{12,4},{16,24},{20,28},{24,16},{28,20},{1,9},{5... | collective-permute-start | bytes 98312 | tf_op jit(solution)/shard_map/ppermute | solution.py:624

commit v9 on v8

--- a/solution.py
+++ b/solution.py
@@ -13,7 +13,7 @@
 masked_low = -1e30
 log2_e = math.log2(math.e)
 lanes = 128
-vmem_bytes = 20 * 1024 * 1024
+vmem_bytes = 32 * 1024 * 1024
 
 def joined(part, axis, combine):
     gathered = jax.tree.map(lambda a: lax.all_gather(a, axis), part)

time: 59 us -> 59 us (level)
  no operation moved by 1% of the time
where the time goes in v9:
time: 59 us; the launch traced here: 58.8 us
  starting transfers between devices  30.5 us (52%)
  Pallas kernels  15.6 us (26%)
  waiting for transfers between devices  10.5 us (18%)
  local copies, waits for them, and re-layouts  1.28 us (2%)
  between operations  0.87 us (1%)
    ppermute x6, starting transfers between devices, planes_move(): lax.ppermute(array, 'context', [(2 * a + k, 2 * b + k) for a, b in pairs...  13.5 us
    ppermute x11, starting transfers between devices, context_flip(): return lax.ppermute(array, 'context', [(c, c ^ e) for c in range(contexts)])  9.9 us
    ppermute x6, starting transfers between devices, heads_flip(): return lax.ppermute(array, 'heads', [(h, h ^ e) for h in range(partners)])  7.11 us
    pallas_call x4, Pallas kernels, chunk_mass(): local_call(functools.partial(mass_kernel, flip, blocks), f32((rows, 2 * k...  6.81 us
    ppermute x6, waiting for transfers between devices, heads_flip(): return lax.ppermute(array, 'heads', [(h, h ^ e) for h in range(partners)])  5 us
    ppermute x11, waiting for transfers between devices, context_flip(): return lax.ppermute(array, 'context', [(c, c ^ e) for c in range(contexts)])  3.35 us
    ppermute x6, waiting for transfers between devices, planes_move(): lax.ppermute(array, 'context', [(2 * a + k, 2 * b + k) for a, b in pairs...  2.2 us
    pallas_call x1, Pallas kernels, index_logits(): local_call(logits_kernel, [f32((rows, key_count)), f32((flat, key_count))...  1.85 us
  transfers between devices with their start and end apart: 23, of which 12 were waited for; matrix products, arithmetic and copies ran while one was open for 0% of the time, Pallas kernels for 21%

profile of v9, /device:TPU:0, one launch (start us, length us, event | category | flops | bytes accessed | tf_op | source)
XLA Modules:
  0.0 58.8 jit_solution(18090606650329917492)
XLA Ops:
  1.2 1.3 %copy-done.6 = bf16[8,32,576]{2,1,0:T(8,128)(2,1)S(1)} copy-done((bf16[8,32,576]{2,1,0:T(8,128)(2,1)S(1)}, bf16[8,32,576]{2,1,0:T(8,128)(2,1)}, u32[]{:S(2)}) %copy-start.6) | copy-done | bytes 294936
  2.6 0.7 %collective-permute-start.3 = (bf16[720,128]{1,0:T(8,128)(2,1)S(1)}, bf16[720,128]{1,0:T(8,128)(2,1)S(1)}, u32[]{:S(2)}, u32[]{:S(2)}) collective-permute-start(bf16[720,128]{1,0:T(8,128)(2,1)S(1)} %get-tuple-element.52), channel_id=1, source_target_pairs={{8,16},{12,20},{16,8},{20,12},{0,0},{4,4},{24,24},{28,28},{9,17},{... | collective-permute-start | bytes 552968 | tf_op jit(solution)/shard_map/ppermute | solution.py:621
  3.3 5.3 %collective-permute-start.7 = (bf16[1152,128]{1,0:T(8,128)(2,1)S(1)}, bf16[1152,128]{1,0:T(8,128)(2,1)S(1)}, u32[]{:S(2)}, u32[]{:S(2)}) collective-permute-start(bf16[1152,128]{1,0:T(8,128)(2,1)S(1)} %get-tuple-element.42.pack_ref), channel_id=1, source_target_pairs={{0,8},{4,12},{8,0},{12,4},{16,24},{20,28},{24,16},{28,20},{1,9},{5... | collective-permute-start | bytes 884744 | tf_op jit(solution)/shard_map/ppermute | solution.py:621
  8.7 3.2 %collective-permute-start.5 = (bf16[1152,128]{1,0:T(8,128)(2,1)S(1)}, bf16[1152,128]{1,0:T(8,128)(2,1)S(1)}, u32[]{:S(2)}, u32[]{:S(2)}) collective-permute-start(bf16[1152,128]{1,0:T(8,128)(2,1)S(1)} %get-tuple-element.42.pack_ref), channel_id=1, source_target_pairs={{0,24},{4,28},{24,0},{28,4},{1,25},{5,29},{25,1},{29,5},{2,26},{6,... | collective-permute-start | bytes 884744 | tf_op jit(solution)/shard_map/ppermute | solution.py:621
  12.6 2.8 %collective-permute-start.4 = (bf16[720,128]{1,0:T(8,128)(2,1)S(1)}, bf16[720,128]{1,0:T(8,128)(2,1)S(1)}, u32[]{:S(2)}, u32[]{:S(2)}) collective-permute-start(bf16[720,128]{1,0:T(8,128)(2,1)S(1)} %collective-permute-done.3.refs_0_), channel_id=1, source_target_pairs={{0,16},{4,20},{24,8},{28,12},{8,0},{12,4},{16,24},{20,28},{1,17},{... | collective-permute-start | bytes 552968 | tf_op jit(solution)/shard_map/ppermute | solution.py:621
  15.5 1.2 %load_inputs.1 = (s32[64,128]{1,0:T(8,128)S(1)}, f32[64,32]{1,0:T(8,128)S(1)}, f32[1024,128]{1,0:T(8,128)S(1)}, bf16[16,64,128]{2,1,0:T(8,128)(2,1)S(1)}, bf16[1...) custom-call(s32[64]{0:T(128)S(1)} %copy-done.5, f32[32,64]{1,0:T(8,128)S(1)} %bitcast.7, ...), custom_call_target="tpu_custom_call" | custom-call | flops 1 | bytes 1 | tf_op jit(solution)/shard_map/load_inputs/pallas_call | solution.py:424
  16.7 0.7 %collective-permute-start.2 = (bf16[432,128]{1,0:T(8,128)(2,1)S(1)}, bf16[432,128]{1,0:T(8,128)(2,1)S(1)}, u32[]{:S(2)}, u32[]{:S(2)}) collective-permute-start(bf16[432,128]{1,0:T(8,128)(2,1)S(1)} %collective-permute-done.1.refs_1_), channel_id=1, source_target_pairs={{0,16},{4,20},{24,8},{28,12},{8,0},{12,4},{16,24},{20,28},{1,17},{... | collective-permute-start | bytes 331784 | tf_op jit(solution)/shard_map/ppermute | solution.py:621
  17.5 1.8 %index_logits.1 = (f32[16,2048]{1,0:T(8,128)S(1)}, f32[1024,2048]{1,0:T(8,128)S(1)}, f32[16,128]{1,0:T(8,128)S(1)}) custom-call(s32[64,128]{1,0:T(8,128)S(1)} %get-tuple-element.44.length_ref, bf16[1024,128]{1,0:T(8,128)(2,1)S(1)} %bitcast.6, bf16[2048,128]{1,0:T(8,128)(2,1)S(1)} %get-tuple-element.46.key_ref, f32[1024,128]{1,0:T(8,128)S(1)} %get-tuple-element.47.weight_ref), custom_call_target="tpu_custom_call" | custom-call | flops 1 | bytes 1 | tf_op jit(solution)/shard_map/index_logits/pallas_call | solution.py:381
  19.3 1.8 %mass_own.1.own_ref = f32[8,4096]{1,0:T(8,128)S(1)} custom-call(s32[64,128]{1,0:T(8,128)S(1)} %get-tuple-element.44.length_ref, bf16[1152,128]{1,0:T(8,128)(2,1)S(1)} %get-tuple-element.42.pack_ref, f32[64,32]{1,0:T(8,128)S(1)} %get-tuple-element.50.lse_ref, bf16[576,2048]{1,0:T(8,128)(2,1)S(1)} %get-tuple-element.53.own_key_ref, ...), custom_call_target="tpu_custom_call" | custom-call | flops 1 | bytes 1 | tf_op jit(solution)/shard_map/mass_own/pallas_call | solution.py:313
  21.2 1.8 %mass_near.1.near_ref = f32[8,4096]{1,0:T(8,128)S(1)} custom-call(s32[64,128]{1,0:T(8,128)S(1)} %get-tuple-element.44.length_ref, bf16[1152,128]{1,0:T(8,128)(2,1)S(1)} %collective-permute-done.7.pack_ref, f32[64,32]{1,0:T(8,128)S(1)} %get-tuple-element.50.lse_ref, bf16[576,2048]{1,0:T(8,128)(2,1)S(1)} %get-tuple-element.53.own_key_ref, ...), custom_call_target="tpu_custom_call" | custom-call | flops 1 | bytes 1 | tf_op jit(solution)/shard_map/mass_near/pallas_call | solution.py:313
  23.0 1.1 %collective-permute-done.5.ends_ref = bf16[1152,128]{1,0:T(8,128)(2,1)S(1)} collective-permute-done((bf16[1152,128]{1,0:T(8,128)(2,1)S(1)}, bf16[1152,128]{1,0:T(8,128)(2,1)S(1)}, u32[]{:S(2)}, u32[]{:S(2)}) %collective-permute-start.5) | collective-permute-done | bytes 294944 | tf_op jit(solution)/shard_map/ppermute | solution.py:621
  24.5 1.8 %mass_across.1.across_ref = f32[8,4096]{1,0:T(8,128)S(1)} custom-call(s32[64,128]{1,0:T(8,128)S(1)} %get-tuple-element.44.length_ref, bf16[1152,128]{1,0:T(8,128)(2,1)S(1)} %pick_queries.1.pack_ref, f32[64,32]{1,0:T(8,128)S(1)} %get-tuple-element.50.lse_ref, bf16[576,2048]{1,0:T(8,128)(2,1)S(1)} %get-tuple-element.53.own_key_ref, ...), custom_call_target="tpu_custom_call" | custom-call | flops 1 | bytes 1 | tf_op jit(solution)/shard_map/mass_across/pallas_call | solution.py:313
  26.7 1.3 %mass_far.1.before_ref = f32[8,4096]{1,0:T(8,128)S(1)} custom-call(s32[64,128]{1,0:T(8,128)S(1)} %get-tuple-element.44.length_ref, bf16[720,128]{1,0:T(8,128)(2,1)S(1)} %collective-permute-done.4.pack_ref, f32[64,32]{1,0:T(8,128)S(1)} %get-tuple-element.50.lse_ref, bf16[576,2048]{1,0:T(8,128)(2,1)S(1)} %get-tuple-element.53.own_key_ref, ...), custom_call_target="tpu_custom_call" | custom-call | flops 1 | bytes 1 | tf_op jit(solution)/shard_map/mass_far/pallas_call | solution.py:313
  28.0 0.7 %collective-permute-done.2.pack_ref = bf16[432,128]{1,0:T(8,128)(2,1)S(1)} collective-permute-done((bf16[432,128]{1,0:T(8,128)(2,1)S(1)}, bf16[432,128]{1,0:T(8,128)(2,1)S(1)}, u32[]{:S(2)}, u32[]{:S(2)}) %collective-permute-start.2) | collective-permute-done | bytes 110624 | tf_op jit(solution)/shard_map/ppermute | solution.py:621
  28.7 1.1 %mass_and_share.1 = (f32[8,4096]{1,0:T(8,128)S(1)}, bf16[8,4096]{1,0:T(8,128)(2,1)S(1)}, bf16[8,4096]{1,0:T(8,128)(2,1)S(1)}, bf16[8,4096]{1,0:T(8,128)(2,1)S(1)}) custom-call(s32[64,128]{1,0:T(8,128)S(1)} %get-tuple-element.44.length_ref, bf16[432,128]{1,0:T(8,128)(2,1)S(1)} %collective-permute-done.2.pack_ref, f32[64,32]{1,0:T(8,128)S(1)} %get-tuple-element.50.lse_ref, ...), custom_call_target="tpu_custom_call" | custom-call | flops 1 | bytes 1 | tf_op jit(solution)/shard_map/mass_and_share/pallas_call | solution.py:344
  29.8 2.5 %collective-permute-start.10 = (bf16[8,4096]{1,0:T(8,128)(2,1)S(1)}, bf16[8,4096]{1,0:T(8,128)(2,1)S(1)}, u32[]{:S(2)}, u32[]{:S(2)}) collective-permute-start(bf16[8,4096]{1,0:T(8,128)(2,1)S(1)} %get-tuple-element.62), channel_id=1, source_target_pairs={{0,3},{1,2},{2,1},{3,0},{4,7},{5,6},{6,5},{7,4},{8,11},{9,10},{10,... | collective-permute-start | bytes 196616 | tf_op jit(solution)/shard_map/ppermute | solution.py:627
  33.4 1.7 %collective-permute-done.10.refs_2_ = bf16[8,4096]{1,0:T(8,128)(2,1)S(1)} collective-permute-done((bf16[8,4096]{1,0:T(8,128)(2,1)S(1)}, bf16[8,4096]{1,0:T(8,128)(2,1)S(1)}, u32[]{:S(2)}, u32[]{:S(2)}) %collective-permute-start.10) | collective-permute-done | bytes 65568 | tf_op jit(solution)/shard_map/ppermute | solution.py:627
  35.1 1.5 %collective-permute-done.8.refs_0_ = bf16[8,4096]{1,0:T(8,128)(2,1)S(1)} collective-permute-done((bf16[8,4096]{1,0:T(8,128)(2,1)S(1)}, bf16[8,4096]{1,0:T(8,128)(2,1)S(1)}, u32[]{:S(2)}, u32[]{:S(2)}) %collective-permute-start.8) | collective-permute-done | bytes 65568 | tf_op jit(solution)/shard_map/ppermute | solution.py:627
  37.3 1.5 %collective-permute-start.11 = (f32[16,128]{1,0:T(8,128)S(1)}, f32[16,128]{1,0:T(8,128)S(1)}, u32[]{:S(2)}, u32[]{:S(2)}) collective-permute-start(f32[16,128]{1,0:T(8,128)S(1)} %get-tuple-element.63.refs_0_), channel_id=1, source_target_pairs={{0,24},{4,28},{8,16},{12,20},{16,8},{20,12},{24,0},{28,4},{1,25},{... | collective-permute-start | bytes 24584 | tf_op jit(solution)/shard_map/ppermute | solution.py:624
  38.8 1.7 %collective-permute-start.12 = (f32[16,128]{1,0:T(8,128)S(1)}, f32[16,128]{1,0:T(8,128)S(1)}, u32[]{:S(2)}, u32[]{:S(2)}) collective-permute-start(f32[16,128]{1,0:T(8,128)S(1)} %get-tuple-element.63.refs_0_), channel_id=1, source_target_pairs={{0,16},{4,20},{8,24},{12,28},{16,0},{20,4},{24,8},{28,12},{1,17},{... | collective-permute-start | bytes 24584 | tf_op jit(solution)/shard_map/ppermute | solution.py:624
  40.5 1.2 %collective-permute-start.13 = (f32[16,128]{1,0:T(8,128)S(1)}, f32[16,128]{1,0:T(8,128)S(1)}, u32[]{:S(2)}, u32[]{:S(2)}) collective-permute-start(f32[16,128]{1,0:T(8,128)S(1)} %get-tuple-element.63.refs_0_), channel_id=1, source_target_pairs={{0,8},{4,12},{8,0},{12,4},{16,24},{20,28},{24,16},{28,20},{1,9},{5... | collective-permute-start | bytes 24584 | tf_op jit(solution)/shard_map/ppermute | solution.py:624
  41.7 1.1 %collective-permute-done.11.refs_1_ = f32[16,128]{1,0:T(8,128)S(1)} collective-permute-done((f32[16,128]{1,0:T(8,128)S(1)}, f32[16,128]{1,0:T(8,128)S(1)}, u32[]{:S(2)}, u32[]{:S(2)}) %collective-permute-start.11) | collective-permute-done | bytes 8224 | tf_op jit(solution)/shard_map/ppermute | solution.py:624
  43.3 0.8 %collective-permute-done.13.refs_3_ = f32[16,128]{1,0:T(8,128)S(1)} collective-permute-done((f32[16,128]{1,0:T(8,128)S(1)}, f32[16,128]{1,0:T(8,128)S(1)}, u32[]{:S(2)}, u32[]{:S(2)}) %collective-permute-start.13) | collective-permute-done | bytes 8224 | tf_op jit(solution)/shard_map/ppermute | solution.py:624
  44.3 1.1 %index_back_own.1 = (f32[512,128]{1,0:T(8,128)S(1)}, f32[128,2048]{1,0:T(8,128)S(1)}) custom-call(s32[64,128]{1,0:T(8,128)S(1)} %get-tuple-element.44.length_ref, f32[16,128]{1,0:T(8,128)S(1)} %merge_stats.3.stats_ref, f32[8,2048]{1,0:T(8,128)S(1)} %get-tuple-element.67.mass_ref, f32[16,2048]{1,0:T(8,128)S(1)} %get-tuple-element.54.logits_ref, ...), custom_call_target="tpu_custom_call" | custom-call | flops 1 | bytes 1 | tf_op jit(solution)/shard_map/index_back_own/pallas_call | solution.py:523
  45.5 1.2 %index_back_pair.1 = (f32[512,128]{1,0:T(8,128)S(1)}, bf16[512,128]{1,0:T(8,128)(2,1)S(1)}, bf16[512,128]{1,0:T(8,128)(2,1)S(1)}, bf16[512,128]{1,0:T(8,128)(2,1...) custom-call(s32[64,128]{1,0:T(8,128)S(1)} %get-tuple-element.44.length_ref, ...), custom_call_target="tpu_custom_call" | custom-call | flops 1 | bytes 1 | tf_op jit(solution)/shard_map/index_back_pair/pallas_call | solution.py:567
  47.8 1.5 %collective-permute-start.19 = (bf16[512,128]{1,0:T(8,128)(2,1)S(1)}, bf16[512,128]{1,0:T(8,128)(2,1)S(1)}, u32[]{:S(2)}, u32[]{:S(2)}) collective-permute-start(bf16[512,128]{1,0:T(8,128)(2,1)S(1)} %get-tuple-element.76), channel_id=1, source_target_pairs={{0,2},{1,3},{2,0},{3,1},{4,6},{5,7},{6,4},{7,5},{8,10},{9,11},{10,... | collective-permute-start | bytes 393224 | tf_op jit(solution)/shard_map/ppermute | solution.py:627
  49.4 1.5 %collective-permute-start.20 = (bf16[512,128]{1,0:T(8,128)(2,1)S(1)}, bf16[512,128]{1,0:T(8,128)(2,1)S(1)}, u32[]{:S(2)}, u32[]{:S(2)}) collective-permute-start(bf16[512,128]{1,0:T(8,128)(2,1)S(1)} %get-tuple-element.78), channel_id=1, source_target_pairs={{0,3},{1,2},{2,1},{3,0},{4,7},{5,6},{6,5},{7,4},{8,11},{9,10},{10,... | collective-permute-start | bytes 393224 | tf_op jit(solution)/shard_map/ppermute | solution.py:627
  50.8 2.5 %collective-permute-start.17 = (bf16[128,128]{1,0:T(8,128)(2,1)S(1)}, bf16[128,128]{1,0:T(8,128)(2,1)S(1)}, u32[]{:S(2)}, u32[]{:S(2)}) collective-permute-start(bf16[128,128]{1,0:T(8,128)(2,1)S(1)} %get-tuple-element.73), channel_id=1, source_target_pairs={{0,24},{4,28},{8,16},{12,20},{16,8},{20,12},{24,0},{28,4},{1,25},{... | collective-permute-start | bytes 98312 | tf_op jit(solution)/shard_map/ppermute | solution.py:624
  53.6 1.7 %collective-permute-start.22 = (bf16[128,128]{1,0:T(8,128)(2,1)S(1)}, bf16[128,128]{1,0:T(8,128)(2,1)S(1)}, u32[]{:S(2)}, u32[]{:S(2)}) collective-permute-start(bf16[128,128]{1,0:T(8,128)(2,1)S(1)} %get-tuple-element.81), channel_id=1, source_target_pairs={{0,8},{4,12},{8,0},{12,4},{16,24},{20,28},{24,16},{28,20},{1,9},{5... | collective-permute-start | bytes 98312 | tf_op jit(solution)/shard_map/ppermute | solution.py:624
  55.2 1.3 %collective-permute-done.20.refs_3_ = bf16[512,128]{1,0:T(8,128)(2,1)S(1)} collective-permute-done((bf16[512,128]{1,0:T(8,128)(2,1)S(1)}, bf16[512,128]{1,0:T(8,128)(2,1)S(1)}, u32[]{:S(2)}, u32[]{:S(2)}) %collective-permute-start.20) | collective-permute-done | bytes 131104 | tf_op jit(solution)/shard_map/ppermute | solution.py:627
  56.5 0.8 %key_sums.1 = f32[512,128]{1,0:T(8,128)} custom-call(f32[512,128]{1,0:T(8,128)S(1)} %get-tuple-element.74.refs_0_, bf16[512,128]{1,0:T(8,128)(2,1)S(1)} %collective-permute-done.18.refs_1_, bf16[512,128]{1,0:T(8,128)(2,1)S(1)} %collective-permute-done.19.refs_2_, bf16[512,128]{1,0:T(8,128)(2,1)S(1)} %collective-permute-done.20.refs_3_), custom_call_target="tpu_custom_call" | custom-call | flops 1 | bytes 1 | tf_op jit(solution)/shard_map/key_sums/pallas_call | solution.py:603
  57.3 0.9 %collective-permute-done.21.refs_2_ = bf16[128,128]{1,0:T(8,128)(2,1)S(1)} collective-permute-done((bf16[128,128]{1,0:T(8,128)(2,1)S(1)}, bf16[128,128]{1,0:T(8,128)(2,1)S(1)}, u32[]{:S(2)}, u32[]{:S(2)}) %collective-permute-start.21) | collective-permute-done | bytes 32800 | tf_op jit(solution)/shard_map/ppermute | solution.py:624
  (45 shorter events, 6.5 us)
Async XLA Ops:
  0.6 14.8 %copy-start = (bf16[2048,576]{0,1:T(8,128)(2,1)S(1)}, bf16[2048,576]{0,1:T(8,128)(2,1)}, u32[]{:S(2)}) copy-start(bf16[2048,576]{0,1:T(8,128)(2,1)} %param.8) | copy-start | bytes 7077892
  0.6 14.8 %copy-start.1 = (bf16[2048,128]{1,0:T(8,128)(2,1)S(1)}, bf16[2048,128]{1,0:T(8,128)(2,1)}, u32[]{:S(2)}) copy-start(bf16[2048,128]{1,0:T(8,128)(2,1)} %key_hbm.1) | copy-start | bytes 1572868
  0.7 14.8 %copy-start.2 = (bf16[16,64,128]{2,1,0:T(8,128)(2,1)S(1)}, bf16[16,64,128]{2,1,0:T(8,128)(2,1)}, u32[]{:S(2)}) copy-start(bf16[16,64,128]{2,1,0:T(8,128)(2,1)} %query_hbm.1) | copy-start | bytes 786436
  0.7 14.8 %copy-start.3 = (f32[64,32]{0,1:T(8,128)S(1)}, f32[64,32]{0,1:T(8,128)}, u32[]{:S(2)}) copy-start(f32[64,32]{0,1:T(8,128)} %param.9) | copy-start | bytes 24580
  0.7 14.8 %copy-start.4 = (f32[16,64]{1,0:T(8,128)S(1)}, f32[16,64]{1,0:T(8,128)}, u32[]{:S(2)}) copy-start(f32[16,64]{1,0:T(8,128)} %weight_ref.1) | copy-start | bytes 12292
  0.7 14.8 %copy-start.5 = (s32[64]{0:T(128)S(1)}, s32[64]{0:T(128)}, u32[]{:S(2)}) copy-start(s32[64]{0:T(128)} %length_ref.1) | copy-start | bytes 772
  0.7 18.6 %collective-permute-start.6 = (bf16[576,2048]{1,0:T(8,128)(2,1)}, bf16[576,2048]{1,0:T(8,128)(2,1)S(1)}, u32[]{:S(2)}, u32[]{:S(2)}) collective-permute-start(bf16[576,2048]{1,0:T(8,128)(2,1)} %bitcast.4), channel_id=1, source_target_pairs={{0,4},{4,0},{8,12},{12,8},{16,20},{20,16},{24,28},{28,24},{1,5},{5... | collective-permute-start | bytes 7077896 | tf_op jit(solution)/shard_map/ppermute | solution.py:624
  1.2 1.3 %copy-start.6 = (bf16[8,32,576]{2,1,0:T(8,128)(2,1)S(1)}, bf16[8,32,576]{2,1,0:T(8,128)(2,1)}, u32[]{:S(2)}) copy-start(bf16[8,32,576]{2,1,0:T(8,128)(2,1)} %query_ref.1) | copy-start | bytes 884740
  2.6 9.9 %collective-permute-start.3 = (bf16[720,128]{1,0:T(8,128)(2,1)S(1)}, bf16[720,128]{1,0:T(8,128)(2,1)S(1)}, u32[]{:S(2)}, u32[]{:S(2)}) collective-permute-start(bf16[720,128]{1,0:T(8,128)(2,1)S(1)} %get-tuple-element.52), channel_id=1, source_target_pairs={{8,16},{12,20},{16,8},{20,12},{0,0},{4,4},{24,24},{28,28},{9,17},{... | collective-permute-start | bytes 552968 | tf_op jit(solution)/shard_map/ppermute | solution.py:621
  3.3 16.0 %collective-permute-start.7 = (bf16[1152,128]{1,0:T(8,128)(2,1)S(1)}, bf16[1152,128]{1,0:T(8,128)(2,1)S(1)}, u32[]{:S(2)}, u32[]{:S(2)}) collective-permute-start(bf16[1152,128]{1,0:T(8,128)(2,1)S(1)} %get-tuple-element.42.pack_ref), channel_id=1, source_target_pairs={{0,8},{4,12},{8,0},{12,4},{16,24},{20,28},{24,16},{28,20},{1,9},{5... | collective-permute-start | bytes 884744 | tf_op jit(solution)/shard_map/ppermute | solution.py:621
  8.7 15.5 %collective-permute-start.5 = (bf16[1152,128]{1,0:T(8,128)(2,1)S(1)}, bf16[1152,128]{1,0:T(8,128)(2,1)S(1)}, u32[]{:S(2)}, u32[]{:S(2)}) collective-permute-start(bf16[1152,128]{1,0:T(8,128)(2,1)S(1)} %get-tuple-element.42.pack_ref), channel_id=1, source_target_pairs={{0,24},{4,28},{24,0},{28,4},{1,25},{5,29},{25,1},{29,5},{2,26},{6,... | collective-permute-start | bytes 884744 | tf_op jit(solution)/shard_map/ppermute | solution.py:621
  11.9 4.8 %collective-permute-start.1 = (bf16[432,128]{1,0:T(8,128)(2,1)S(1)}, bf16[432,128]{1,0:T(8,128)(2,1)S(1)}, u32[]{:S(2)}, u32[]{:S(2)}) collective-permute-start(bf16[432,128]{1,0:T(8,128)(2,1)S(1)} %get-tuple-element.49), channel_id=1, source_target_pairs={{8,16},{12,20},{16,8},{20,12},{0,0},{4,4},{24,24},{28,28},{9,17},{... | collective-permute-start | bytes 331784 | tf_op jit(solution)/shard_map/ppermute | solution.py:621
  12.6 14.1 %collective-permute-start.4 = (bf16[720,128]{1,0:T(8,128)(2,1)S(1)}, bf16[720,128]{1,0:T(8,128)(2,1)S(1)}, u32[]{:S(2)}, u32[]{:S(2)}) collective-permute-start(bf16[720,128]{1,0:T(8,128)(2,1)S(1)} %collective-permute-done.3.refs_0_), channel_id=1, source_target_pairs={{0,16},{4,20},{24,8},{28,12},{8,0},{12,4},{16,24},{20,28},{1,17},{... | collective-permute-start | bytes 552968 | tf_op jit(solution)/shard_map/ppermute | solution.py:621
  16.7 12.0 %collective-permute-start.2 = (bf16[432,128]{1,0:T(8,128)(2,1)S(1)}, bf16[432,128]{1,0:T(8,128)(2,1)S(1)}, u32[]{:S(2)}, u32[]{:S(2)}) collective-permute-start(bf16[432,128]{1,0:T(8,128)(2,1)S(1)} %collective-permute-done.1.refs_1_), channel_id=1, source_target_pairs={{0,16},{4,20},{24,8},{28,12},{8,0},{12,4},{16,24},{20,28},{1,17},{... | collective-permute-start | bytes 331784 | tf_op jit(solution)/shard_map/ppermute | solution.py:621
  19.3 5.1 %collective-permute-start = (f32[16,128]{1,0:T(8,128)S(1)}, f32[16,128]{1,0:T(8,128)S(1)}, u32[]{:S(2)}, u32[]{:S(2)}) collective-permute-start(f32[16,128]{1,0:T(8,128)S(1)} %get-tuple-element.48.refs_0_), channel_id=1, source_target_pairs={{0,4},{4,0},{8,12},{12,8},{16,20},{20,16},{24,28},{28,24},{1,5},{5... | collective-permute-start | bytes 24584 | tf_op jit(solution)/shard_map/ppermute | solution.py:624
  29.8 5.3 %collective-permute-start.10 = (bf16[8,4096]{1,0:T(8,128)(2,1)S(1)}, bf16[8,4096]{1,0:T(8,128)(2,1)S(1)}, u32[]{:S(2)}, u32[]{:S(2)}) collective-permute-start(bf16[8,4096]{1,0:T(8,128)(2,1)S(1)} %get-tuple-element.62), channel_id=1, source_target_pairs={{0,3},{1,2},{2,1},{3,0},{4,7},{5,6},{6,5},{7,4},{8,11},{9,10},{10,... | collective-permute-start | bytes 196616 | tf_op jit(solution)/shard_map/ppermute | solution.py:627
  32.4 4.3 %collective-permute-start.8 = (bf16[8,4096]{1,0:T(8,128)(2,1)S(1)}, bf16[8,4096]{1,0:T(8,128)(2,1)S(1)}, u32[]{:S(2)}, u32[]{:S(2)}) collective-permute-start(bf16[8,4096]{1,0:T(8,128)(2,1)S(1)} %get-tuple-element.60), channel_id=1, source_target_pairs={{0,2},{1,3},{2,0},{3,1},{4,6},{5,7},{6,4},{7,5},{8,10},{9,11},{10,... | collective-permute-start | bytes 196616 | tf_op jit(solution)/shard_map/ppermute | solution.py:627
  32.9 4.3 %collective-permute-start.9 = (bf16[8,4096]{1,0:T(8,128)(2,1)S(1)}, bf16[8,4096]{1,0:T(8,128)(2,1)S(1)}, u32[]{:S(2)}, u32[]{:S(2)}) collective-permute-start(bf16[8,4096]{1,0:T(8,128)(2,1)S(1)} %get-tuple-element.61), channel_id=1, source_target_pairs={{0,1},{1,0},{2,3},{3,2},{4,5},{5,4},{6,7},{7,6},{8,9},{9,8},{10,11... | collective-permute-start | bytes 196616 | tf_op jit(solution)/shard_map/ppermute | solution.py:627
  37.3 8.2 %collective-permute-start.15 = (f32[8,2048]{1,0:T(8,128)S(1)}, f32[8,2048]{1,0:T(8,128)S(1)}, u32[]{:S(2)}, u32[]{:S(2)}) collective-permute-start(f32[8,2048]{1,0:T(8,128)S(1)} %get-tuple-element.64), channel_id=1, source_target_pairs={{0,4},{4,0},{8,12},{12,8},{16,20},{20,16},{24,28},{28,24},{1,5},{5... | collective-permute-start | bytes 196616 | tf_op jit(solution)/shard_map/ppermute | solution.py:624
  37.3 5.5 %collective-permute-start.11 = (f32[16,128]{1,0:T(8,128)S(1)}, f32[16,128]{1,0:T(8,128)S(1)}, u32[]{:S(2)}, u32[]{:S(2)}) collective-permute-start(f32[16,128]{1,0:T(8,128)S(1)} %get-tuple-element.63.refs_0_), channel_id=1, source_target_pairs={{0,24},{4,28},{8,16},{12,20},{16,8},{20,12},{24,0},{28,4},{1,25},{... | collective-permute-start | bytes 24584 | tf_op jit(solution)/shard_map/ppermute | solution.py:624
  38.8 4.5 %collective-permute-start.12 = (f32[16,128]{1,0:T(8,128)S(1)}, f32[16,128]{1,0:T(8,128)S(1)}, u32[]{:S(2)}, u32[]{:S(2)}) collective-permute-start(f32[16,128]{1,0:T(8,128)S(1)} %get-tuple-element.63.refs_0_), channel_id=1, source_target_pairs={{0,16},{4,20},{8,24},{12,28},{16,0},{20,4},{24,8},{28,12},{1,17},{... | collective-permute-start | bytes 24584 | tf_op jit(solution)/shard_map/ppermute | solution.py:624
  40.5 3.7 %collective-permute-start.13 = (f32[16,128]{1,0:T(8,128)S(1)}, f32[16,128]{1,0:T(8,128)S(1)}, u32[]{:S(2)}, u32[]{:S(2)}) collective-permute-start(f32[16,128]{1,0:T(8,128)S(1)} %get-tuple-element.63.refs_0_), channel_id=1, source_target_pairs={{0,8},{4,12},{8,0},{12,4},{16,24},{20,28},{24,16},{28,20},{1,9},{5... | collective-permute-start | bytes 24584 | tf_op jit(solution)/shard_map/ppermute | solution.py:624
  44.3 1.2 %collective-permute-start.14 = (f32[16,128]{1,0:T(8,128)S(1)}, f32[16,128]{1,0:T(8,128)S(1)}, u32[]{:S(2)}, u32[]{:S(2)}) collective-permute-start(f32[16,128]{1,0:T(8,128)S(1)} %merge_stats.3.stats_ref), channel_id=1, source_target_pairs={{0,4},{4,0},{8,12},{12,8},{16,20},{20,16},{24,28},{28,24},{1,5},{5... | collective-permute-start | bytes 24584 | tf_op jit(solution)/shard_map/ppermute | solution.py:624
  46.7 2.6 %collective-permute-start.16 = (bf16[4,128,128]{2,1,0:T(8,128)(2,1)S(1)}, bf16[4,128,128]{2,1,0:T(8,128)(2,1)S(1)}, u32[]{:S(2)}, u32[]{:S(2)}) collective-permute-start(bf16[4,128,128]{2,1,0:T(8,128)(2,1)S(1)} %get-tuple-element.71), channel_id=1, source_target_pairs={{0,4},{4,0},{8,12},{12,8},{16,20},{20,16},{24,28},{28,24},{1,5},{5... | collective-permute-start | bytes 393224 | tf_op jit(solution)/shard_map/ppermute | solution.py:624
  47.3 6.3 %collective-permute-start.18 = (bf16[512,128]{1,0:T(8,128)(2,1)S(1)}, bf16[512,128]{1,0:T(8,128)(2,1)S(1)}, u32[]{:S(2)}, u32[]{:S(2)}) collective-permute-start(bf16[512,128]{1,0:T(8,128)(2,1)S(1)} %get-tuple-element.75), channel_id=1, source_target_pairs={{0,1},{1,0},{2,3},{3,2},{4,5},{5,4},{6,7},{7,6},{8,9},{9,8},{10,11... | collective-permute-start | bytes 393224 | tf_op jit(solution)/shard_map/ppermute | solution.py:627
  47.8 7.5 %collective-permute-start.19 = (bf16[512,128]{1,0:T(8,128)(2,1)S(1)}, bf16[512,128]{1,0:T(8,128)(2,1)S(1)}, u32[]{:S(2)}, u32[]{:S(2)}) collective-permute-start(bf16[512,128]{1,0:T(8,128)(2,1)S(1)} %get-tuple-element.76), channel_id=1, source_target_pairs={{0,2},{1,3},{2,0},{3,1},{4,6},{5,7},{6,4},{7,5},{8,10},{9,11},{10,... | collective-permute-start | bytes 393224 | tf_op jit(solution)/shard_map/ppermute | solution.py:627
  49.4 7.2 %collective-permute-start.20 = (bf16[512,128]{1,0:T(8,128)(2,1)S(1)}, bf16[512,128]{1,0:T(8,128)(2,1)S(1)}, u32[]{:S(2)}, u32[]{:S(2)}) collective-permute-start(bf16[512,128]{1,0:T(8,128)(2,1)S(1)} %get-tuple-element.78), channel_id=1, source_target_pairs={{0,3},{1,2},{2,1},{3,0},{4,7},{5,6},{6,5},{7,4},{8,11},{9,10},{10,... | collective-permute-start | bytes 393224 | tf_op jit(solution)/shard_map/ppermute | solution.py:627
  50.8 6.4 %collective-permute-start.17 = (bf16[128,128]{1,0:T(8,128)(2,1)S(1)}, bf16[128,128]{1,0:T(8,128)(2,1)S(1)}, u32[]{:S(2)}, u32[]{:S(2)}) collective-permute-start(bf16[128,128]{1,0:T(8,128)(2,1)S(1)} %get-tuple-element.73), channel_id=1, source_target_pairs={{0,24},{4,28},{8,16},{12,20},{16,8},{20,12},{24,0},{28,4},{1,25},{... | collective-permute-start | bytes 98312 | tf_op jit(solution)/shard_map/ppermute | solution.py:624
  53.3 4.8 %collective-permute-start.21 = (bf16[128,128]{1,0:T(8,128)(2,1)S(1)}, bf16[128,128]{1,0:T(8,128)(2,1)S(1)}, u32[]{:S(2)}, u32[]{:S(2)}) collective-permute-start(bf16[128,128]{1,0:T(8,128)(2,1)S(1)} %get-tuple-element.80), channel_id=1, source_target_pairs={{0,16},{4,20},{8,24},{12,28},{16,0},{20,4},{24,8},{28,12},{1,17},{... | collective-permute-start | bytes 98312 | tf_op jit(solution)/shard_map/ppermute | solution.py:624
  53.6 4.6 %collective-permute-start.22 = (bf16[128,128]{1,0:T(8,128)(2,1)S(1)}, bf16[128,128]{1,0:T(8,128)(2,1)S(1)}, u32[]{:S(2)}, u32[]{:S(2)}) collective-permute-start(bf16[128,128]{1,0:T(8,128)(2,1)S(1)} %get-tuple-element.81), channel_id=1, source_target_pairs={{0,8},{4,12},{8,0},{12,4},{16,24},{20,28},{24,16},{28,20},{1,9},{5... | collective-permute-start | bytes 98312 | tf_op jit(solution)/shard_map/ppermute | solution.py:624
